TPU v7x, 32 devices: a whole 2x2x4 slice. The times are simulated.
32 devices in a mesh: row: 4 (over x, core), col: 2 (over y), seq: 4 (over z).
Axes of the slice: x: 2, y: 2, z: 4, core: 2. Of those that a mesh axis runs over, the one named last changes fastest.
Arguments:
- left_piece: bfloat16 [512, 32, 256], P('seq', None, 'row'), may hold values from -6 to 6
- right_piece: bfloat16 [512, 32, 256], P('seq', 'row', 'col'), may hold values from -6 to 6
- proj_weight: bfloat16 [1024, 128], replicated, may hold values from -4 to 4
- proj_bias: float32 [128], replicated, may hold values from -3 to 3
- pair_rep: bfloat16 [256, 256, 128], P(('row', 'seq'), 'col'), may hold values from -6 to 6
- norm_gain: float32 [128], replicated, may hold values from 0.5 to 1.5
- up_weight: bfloat16 [128, 512], replicated, may hold values from -0.5 to 0.5
- up_bias: float32 [512], replicated, may hold values from -3 to 3
- down_weight: bfloat16 [512, 128], replicated, may hold values from -0.25 to 0.25
- down_bias: float32 [128], replicated, may hold values from -3 to 3
Outputs:
- refined: bfloat16 [256, 256, 128], P(('row', 'seq'), 'col')
All inputs are finite; a program needn't handle non-finite values.
Results may differ from a plain program's by a relative error of at most 0.0085.
Values may be sent and summed in bfloat16 or wider, within the bound.
No kernel may reach another device: no remote copies, remote signals or barrier semaphores. Data moves between devices by JAX's collectives and lax.ppermute only.
A program may use at most 64 MiB of HBM per device.

v0:
```python
import jax
import jax.numpy as jnp
from jax import lax
from jax.sharding import PartitionSpec as P

epsilon = 1e-05


def project_block(row_slab, right_all, proj_weight):
    seq_count, channels, row_count = row_slab.shape
    columns = right_all.shape[2]
    left_mat = row_slab.reshape(seq_count, channels * row_count)
    right_mat = right_all.reshape(seq_count, channels * columns)
    outer_prod = lax.dot_general(
        left_mat, right_mat, (((0,), (0,)), ((), ())), preferred_element_type=jnp.float32
    ).astype(jnp.bfloat16)
    outer_prod = outer_prod.reshape(channels, row_count, channels, columns).transpose(1, 3, 0, 2)
    outer_prod = outer_prod.reshape(row_count * columns, channels * channels)
    result = jnp.dot(outer_prod, proj_weight, preferred_element_type=jnp.float32)
    return result.reshape(row_count, columns, proj_weight.shape[1])


def project_rows(row_slab, right_all, proj_weight):
    seq_count, channels, row_count = row_slab.shape
    sub_rows = 8
    pieces = row_slab.reshape(seq_count, channels, row_count // sub_rows, sub_rows)
    pieces = jnp.moveaxis(pieces, 2, 0)
    result = lax.map(lambda portion: project_block(portion, right_all, proj_weight), pieces)
    return result.reshape(row_count, right_all.shape[2], proj_weight.shape[1])


def transition(middle, norm_gain, up_weight, up_bias, down_weight, down_bias):
    row_count, columns, channels = middle.shape
    values = middle.astype(jnp.float32).reshape(row_count * columns, channels)
    center = jnp.mean(values, axis=1, keepdims=True)
    spread = jnp.mean(jnp.square(values - center), axis=1, keepdims=True)
    normed = ((values - center) * lax.rsqrt(spread + epsilon) * norm_gain).astype(jnp.bfloat16)
    hidden = jnp.maximum(
        jnp.dot(normed, up_weight, preferred_element_type=jnp.float32) + up_bias, 0.0
    ).astype(jnp.bfloat16)
    result = values + jnp.dot(hidden, down_weight, preferred_element_type=jnp.float32) + down_bias
    return result.astype(jnp.bfloat16).reshape(row_count, columns, channels)


def gather_right(right_part):
    return lax.all_gather(right_part, "row", axis=1, tiled=True)


def move_cols(tile):
    return lax.all_to_all(tile, "col", split_axis=0, concat_axis=2, tiled=True)


def on_device(
    left_piece,
    right_piece,
    proj_weight,
    proj_bias,
    pair_rep,
    norm_gain,
    up_weight,
    up_bias,
    down_weight,
    down_bias,
):
    own_rows = pair_rep.shape[0]
    columns = pair_rep.shape[1]
    channels = pair_rep.shape[2]
    groups = lax.axis_size("seq")
    group_len = left_piece.shape[0]
    piece_channels = left_piece.shape[1]
    seq_total = group_len * groups
    split_left = left_piece.reshape(group_len, piece_channels, groups, own_rows)
    left_own = lax.all_to_all(split_left, "seq", split_axis=2, concat_axis=0, tiled=True)
    left_own = left_own.reshape(groups * group_len, piece_channels, own_rows)
    right_seq = lax.all_gather(right_piece, "seq", axis=0, tiled=True)
    right_all = gather_right(right_seq)
    summed = jnp.zeros((own_rows, columns, channels), jnp.float32)
    for group_id in range(groups):
        row_slab = left_own[group_id * group_len : (group_id + 1) * group_len]
        right_group = right_all[group_id * group_len : (group_id + 1) * group_len]
        summed = summed + project_rows(row_slab, right_group, proj_weight)
    update = (summed / seq_total + proj_bias).astype(jnp.bfloat16)
    col_count = lax.axis_size("col")
    rowseq_count = lax.axis_size(("row", "seq"))
    run_len = own_rows // col_count
    section_one = move_cols(update.reshape(col_count, run_len, columns, channels))
    section_two = lax.all_to_all(
        section_one.reshape(run_len, rowseq_count, own_rows, channels),
        ("row", "seq"),
        split_axis=1,
        concat_axis=0,
        tiled=True,
    )
    section_three = move_cols(
        section_two.reshape(col_count, rowseq_count // col_count, 1, run_len, own_rows, channels)
    )
    mirrored = section_three.reshape(columns, own_rows, channels).transpose(1, 0, 2)
    middle = (
        pair_rep.astype(jnp.float32)
        + 0.5 * (update.astype(jnp.float32) + mirrored.astype(jnp.float32))
    ).astype(jnp.bfloat16)
    return transition(middle, norm_gain, up_weight, up_bias, down_weight, down_bias)


def solution(mesh):
    in_specs = (
        P("seq", None, "row"),
        P("seq", "row", "col"),
        P(),
        P(),
        P(("row", "seq"), "col", None),
        P(),
        P(),
        P(),
        P(),
        P(),
    )
    out_specs = P(("row", "seq"), "col", None)
    return jax.shard_map(
        on_device, mesh=mesh, in_specs=in_specs, out_specs=out_specs, check_vma=False
    )
```

profile of v0, /device:TPU:3, one launch (start us, length us, event | category | flops | bytes accessed | tf_op | source)
XLA Modules:
  0.0 155.5 jit_solution(7148563249127097135)
XLA Ops:
  6.5 0.7 all-gather.3.cloned.1.call-update
  7.3 0.0 all-gather.5.cloned.1.call-start
  7.3 30.7 %all-gather.3.cloned.1.call-done = bf16[512,8,128]{2,1,0:T(8,128)(2,1)} async-done(((bf16[128,8,128]{2,1,0:T(8,128)(2,1)}), bf16[512,8,128]{2,1,0:T(8,128)(2,1)}) %all-gather.3.cloned.1.call-update) | async-done | bytes 1048592 | tf_op jit(solution)/shard_map/all_gather | solution.py:75
  38.0 0.0 all-gather.5.cloned.1.call-update
  38.0 1.9 %copy.56 = bf16[128,32,4,16]{0,3,1,2:T(8,128)(2,1)} copy(bf16[128,32,4,16]{0,3,2,1:T(8,128)(2,1)} %bitcast.216) | data formatting | bytes 1048576 | tf_op jit(solution)/shard_map/reshape | solution.py:72
  39.9 3.5 %all-to-all-start = ((bf16[128,32,4,16]{0,3,1,2:T(8,128)(2,1)}), bf16[128,32,4,16]{0,3,1,2:T(8,128)(2,1)S(1)}, u32[]{:S(2)}, u32[]{:S(2)}) async-start(bf16[128,32,4,16]{0,3,1,2:T(8,128)(2,1)} %copy.56), calls=%async_computation | async-start | bytes 1048576 | tf_op jit(solution)/shard_map/all_to_all | solution.py:73
  43.4 14.0 %all-to-all-done = bf16[128,32,4,16]{0,3,1,2:T(8,128)(2,1)S(1)} async-done(((bf16[128,32,4,16]{0,3,1,2:T(8,128)(2,1)}), bf16[128,32,4,16]{0,3,1,2:T(8,128)(2,1)S(1)}, u32[]{:S(2)}, u32[]{:S(2)}) %all-to-all-start) | async-done | bytes 524320 | tf_op jit(solution)/shard_map/all_to_all | solution.py:73
  57.3 0.8 slice_bitcast_fusion.2
  58.1 15.4 %all-gather.5.cloned.1.call-done = bf16[512,32,128]{2,1,0:T(8,128)(2,1)} async-done(((bf16[512,8,128]{2,1,0:T(8,128)(2,1)}), bf16[512,32,128]{2,1,0:T(8,128)(2,1)}) %all-gather.5.cloned.1.call-update) | async-done | bytes 4194320 | tf_op jit(solution)/shard_map/all_gather | solution.py:46
  73.5 4.0 %fusion.68 = (bf16[128,32,128]{2,1,0:T(8,128)(2,1)S(1)}, bf16[128,32,128]{2,1,0:T(8,128)(2,1)S(1)}, bf16[128,32,128]{2,1,0:T(8,128)(2,1)S(1)}, bf16[128,32,128]{2,1,0:T(8,128)(2,1)}) fusion(bf16[512,32,128]{2,1,0:T(8,128)(2,1)} %all-gather.5.cloned.1.call-done), kind=kLoop, calls=%fused_computation.71 | loop fusion | bytes 8388608 | tf_op jit(solution)/shard_map/slice | solution.py:80
  77.5 1.1 broadcast.40.clone.2
  78.5 7.3 %while.40 = (s32[]{:T(128)}, f32[2,8,128,128]{3,2,1,0:T(8,128)}, bf16[2,128,32,8]{1,3,0,2:T(8,128)(2,1)}, bf16[128,32,128]{2,1,0:T(8,128)(2,1)}, bf16[1024,128]{1,0:T(8,128)(2,1)}, /*index=5*/s32[]{:T(128)}) while((s32[]{:T(128)}, f32[2,8,128,128]{3,2,1,0:T(8,128)}, bf16[2,128,32,8]{1,3,0,2:T(8,128)(2,1)}, bf16[128,32,128]{2,1,0:T(8,128)(2,1)}, ...), condition=%wide.region_1.2_spmd, body=%wide.region_0.1_spmd.sunk | while | flops 537919488 | bytes 7144545 | solution.py:28
  78.5 2.0 %convolution_convert_fusion.8 = bf16[256,4096]{1,0:T(8,128)(2,1)S(1)} fusion(bf16[16,8,32,128]{3,2,1,0:T(8,128)(2,1)} %bitcast.209, bf16[2,128,32,8]{1,3,0,2:T(8,128)(2,1)} %get-tuple-element.405, s32[]{:T(128)} %get-tuple-element.397), kind=kOutput, calls=%fused_computation.clone.1 | convolution fusion | flops 269484032 | bytes 3211776 | tf_op jit(solution)/shard_map/while/body/eval_jaxpr/dot_general | solution.py:14
  80.6 1.6 %fusion.96 = f32[2,8,128,128]{3,2,1,0:T(8,128)} fusion(f32[2,8,128,128]{3,2,1,0:T(8,128)} %get-tuple-element.398, s32[]{:T(128)} %get-tuple-element.397, bf16[8,128,1024]{1,0,2:T(8,128)(2,1)S(1)} %bitcast.202, bf16[1024,128]{1,0:T(8,128)(2,1)S(1)} %copy-done.4), kind=kOutput, calls=%fused_computation.4.clone.1 | convolution fusion | flops 268435456 | bytes 2884096 | tf_op jit(solution)/shard_map/while/body/eval_jaxpr/dot_general | solution.py:19
  82.2 2.0 %convolution_convert_fusion.8 = bf16[256,4096]{1,0:T(8,128)(2,1)S(1)} fusion(bf16[16,8,32,128]{3,2,1,0:T(8,128)(2,1)} %bitcast.209, bf16[2,128,32,8]{1,3,0,2:T(8,128)(2,1)} %get-tuple-element.405, s32[]{:T(128)} %get-tuple-element.397), kind=kOutput, calls=%fused_computation.clone.1 | convolution fusion | flops 269484032 | bytes 3211776 | tf_op jit(solution)/shard_map/while/body/eval_jaxpr/dot_general | solution.py:14
  84.2 1.6 %fusion.96 = f32[2,8,128,128]{3,2,1,0:T(8,128)} fusion(f32[2,8,128,128]{3,2,1,0:T(8,128)} %get-tuple-element.398, s32[]{:T(128)} %get-tuple-element.397, bf16[8,128,1024]{1,0,2:T(8,128)(2,1)S(1)} %bitcast.202, bf16[1024,128]{1,0:T(8,128)(2,1)S(1)} %copy-done.4), kind=kOutput, calls=%fused_computation.4.clone.1 | convolution fusion | flops 268435456 | bytes 2884096 | tf_op jit(solution)/shard_map/while/body/eval_jaxpr/dot_general | solution.py:19
  85.8 1.1 broadcast.40.clone.3
  86.9 6.4 %while.41 = (s32[]{:T(128)}, f32[2,8,128,128]{3,2,1,0:T(8,128)}, bf16[2,128,32,8]{1,3,0,2:T(8,128)(2,1)}, bf16[128,32,128]{2,1,0:T(8,128)(2,1)S(1)}, bf16[1024,128]{1,0:T(8,128)(2,1)}, /*index=5*/s32[]{:T(128)}) while((s32[]{:T(128)}, f32[2,8,128,128]{3,2,1,0:T(8,128)}, bf16[2,128,32,8]{1,3,0,2:T(8,128)(2,1)}, ...), condition=%wide.region_3.4_spmd, body=%wide.region_2.3_spmd.sunk | while | flops 537919488 | bytes 7144545 | solution.py:28
  86.9 1.6 %convolution_convert_fusion.9 = bf16[256,4096]{1,0:T(8,128)(2,1)S(1)} fusion(bf16[16,8,32,128]{3,2,1,0:T(8,128)(2,1)S(1)} %bitcast.208, bf16[2,128,32,8]{1,3,0,2:T(8,128)(2,1)} %get-tuple-element.423, s32[]{:T(128)} %get-tuple-element.415), kind=kOutput, calls=%fused_computation.11.clone.1 | convolution fusion | flops 269484032 | bytes 3211776 | tf_op jit(solution)/shard_map/while/body/eval_jaxpr/dot_general | solution.py:14
  88.6 1.6 %fusion.101 = f32[2,8,128,128]{3,2,1,0:T(8,128)} fusion(f32[2,8,128,128]{3,2,1,0:T(8,128)} %get-tuple-element.416, s32[]{:T(128)} %get-tuple-element.415, bf16[8,128,1024]{1,0,2:T(8,128)(2,1)S(1)} %bitcast.203, bf16[1024,128]{1,0:T(8,128)(2,1)S(1)} %copy-done.5), kind=kOutput, calls=%fused_computation.15.clone.1 | convolution fusion | flops 268435456 | bytes 2884096 | tf_op jit(solution)/shard_map/while/body/eval_jaxpr/dot_general | solution.py:19
  90.1 1.6 %convolution_convert_fusion.9 = bf16[256,4096]{1,0:T(8,128)(2,1)S(1)} fusion(bf16[16,8,32,128]{3,2,1,0:T(8,128)(2,1)S(1)} %bitcast.208, bf16[2,128,32,8]{1,3,0,2:T(8,128)(2,1)} %get-tuple-element.423, s32[]{:T(128)} %get-tuple-element.415), kind=kOutput, calls=%fused_computation.11.clone.1 | convolution fusion | flops 269484032 | bytes 3211776 | tf_op jit(solution)/shard_map/while/body/eval_jaxpr/dot_general | solution.py:14
  91.8 1.6 %fusion.101 = f32[2,8,128,128]{3,2,1,0:T(8,128)} fusion(f32[2,8,128,128]{3,2,1,0:T(8,128)} %get-tuple-element.416, s32[]{:T(128)} %get-tuple-element.415, bf16[8,128,1024]{1,0,2:T(8,128)(2,1)S(1)} %bitcast.203, bf16[1024,128]{1,0:T(8,128)(2,1)S(1)} %copy-done.5), kind=kOutput, calls=%fused_computation.15.clone.1 | convolution fusion | flops 268435456 | bytes 2884096 | tf_op jit(solution)/shard_map/while/body/eval_jaxpr/dot_general | solution.py:19
  93.3 0.1 broadcast.40.clone.1
  93.4 3.5 %while.42 = (s32[]{:T(128)}, f32[2,8,128,128]{3,2,1,0:T(8,128)S(1)}, bf16[2,128,32,8]{1,3,0,2:T(8,128)(2,1)S(1)}, bf16[128,32,128]{2,1,0:T(8,128)(2,1)S(1)}, bf16[1024,128]{1,0:T(8,128)(2,1)}, /*index=5*/s32[]{:T(128)}) while((s32[]{:T(128)}, f32[2,8,128,128]{3,2,1,0:T(8,128)S(1)}, bf16[2,128,32,8]{1,3,0,2:T(8,128)(2,1)S(1)}, ...), condition=%wide.region_5.6_spmd, body=%wide.region_4.5_spmd.sunk | while | flops 537919488 | bytes 7143529 | solution.py:28
  93.5 0.0 copy-start.6
  93.5 0.7 convolution_convert_fusion.10
  94.2 0.2 copy-done.6
  94.4 0.8 fusion.106
  95.2 0.8 convolution_convert_fusion.10
  96.0 0.2 copy-done.6
  96.2 0.8 fusion.106
  97.0 0.1 broadcast.40.clone
  97.1 3.5 %while.43 = (s32[]{:T(128)}, f32[2,8,128,128]{3,2,1,0:T(8,128)S(1)}, bf16[2,128,32,8]{1,3,0,2:T(8,128)(2,1)S(1)}, bf16[128,32,128]{2,1,0:T(8,128)(2,1)S(1)}, bf16[1024,128]{1,0:T(8,128)(2,1)}, /*index=5*/s32[]{:T(128)}) while((s32[]{:T(128)}, f32[2,8,128,128]{3,2,1,0:T(8,128)S(1)}, bf16[2,128,32,8]{1,3,0,2:T(8,128)(2,1)S(1)}, ...), condition=%wide.region_7.8_spmd, body=%wide.region_6.7_spmd.sunk | while | flops 537919488 | bytes 7143529 | solution.py:28
  97.1 0.7 convolution_convert_fusion.11
  97.8 0.2 copy-done.7
  98.0 0.8 fusion.111
  98.8 0.8 convolution_convert_fusion.11
  99.6 0.2 copy-done.7
  99.8 0.8 fusion.111
  100.6 1.9 %add_convert_fusion = (bf16[2,8,128,128]{3,2,1,0:T(8,128)(2,1)S(1)}, f32[2,8,128,128]{3,2,1,0:T(8,128)S(1)}) fusion(f32[128]{0:T(128)S(1)} %copy-done.2, f32[2,8,128,128]{3,2,1,0:T(8,128)S(1)} %get-tuple-element.116, f32[2,8,128,128]{3,2,1,0:T(8,128)S(1)} %get-tuple-element.115, f32[2,8,128,128]{3,2,1,0:T(8,128)} %get-tuple-element.113, ...), kind=kLoop, calls=%fused_computation.59 | loop fusion | flops 1572864 | bytes 5767680 | tf_op jit(solution)/shard_map/convert_element_type | solution.py:82
  102.5 10.1 %all_to_all.54 = bf16[2,8,128,128]{3,2,1,0:T(8,128)(2,1)S(1)} all-to-all(bf16[2,8,128,128]{3,2,1,0:T(8,128)(2,1)S(1)} %get-tuple-element.219), channel_id=1, replica_groups=mesh['row'=4,'col'=2,'seq'=4] {'col'}, dimensions={0} | all-to-all | bytes 1048576 | tf_op jit(solution)/shard_map/all_to_all | solution.py:50
  112.6 21.6 %all_to_all.55 = bf16[8,16,16,128]{3,2,0,1:T(8,128)(2,1)S(1)} all-to-all(bf16[8,16,16,128]{3,2,0,1:T(8,128)(2,1)S(1)} %copy.62), channel_id=1, replica_groups=mesh['row'=4,'col'=2,'seq'=4] {'row','seq'}, dimensions={1} | all-to-all | bytes 1048576 | tf_op jit(solution)/shard_map/all_to_all | solution.py:87
  134.3 10.3 %all_to_all.56 = bf16[2,8,1,8,16,128]{5,4,3,1,2,0:T(8,128)(2,1)S(1)} all-to-all(bf16[2,8,1,8,16,128]{5,4,3,1,2,0:T(8,128)(2,1)S(1)} %bitcast.215), channel_id=1, replica_groups=mesh['row'=4,'col'=2,'seq'=4] {'col'}, dimensions={0} | all-to-all | bytes 1048576 | tf_op jit(solution)/shard_map/all_to_all | solution.py:50
  144.6 0.1 bitcast_convert_fusion
  144.8 0.5 convert_reduce_fusion
  145.3 0.6 multiply_reduce_fusion
  146.0 0.6 fusion.60
  146.6 2.0 %fusion.57 = bf16[2048,128]{1,0:T(8,128)(2,1)} fusion(bf16[512,128]{1,0:T(8,128)(2,1)S(1)} %copy-done, bf16[2048,128]{1,0:T(8,128)(2,1)S(1)} %fusion.60, bf16[128,512]{1,0:T(8,128)(2,1)S(1)} %copy-done.8, f32[512]{0:T(512)S(1)} %copy-done.9, f32[128]{0:T(128)S(1)} %copy-done.10, bf16[2048,128]{1,0:T(8,128)(2,1)S(1)} %bitcast.210), kind=kOutput, calls=%fused_computation.47 | convolution fusion | flops 541065216 | bytes 1837568 | tf_op jit(solution)/shard_map/dot_general | solution.py:41
  (30 shorter events, 0.2 us)
Async XLA Ops:
  6.5 140.1 %copy-start = (bf16[512,128]{1,0:T(8,128)(2,1)S(1)}, bf16[512,128]{1,0:T(8,128)(2,1)}, u32[]{:S(2)}) copy-start(bf16[512,128]{1,0:T(8,128)(2,1)} %param.26) | copy-start | bytes 393220
  6.5 31.4 %all-gather.3.cloned.1.call-start = ((), (), s32[]{:S(2)}) async-start(), calls=%async_computation.4 | async-start | bytes 1310720 | tf_op jit(solution)/shard_map/all_gather | solution.py:75
  7.3 66.2 %all-gather.5.cloned.1.call-start = ((), (), s32[]{:S(2)}) async-start(), calls=%async_computation.5 | async-start | bytes 5242880 | tf_op jit(solution)/shard_map/all_gather | solution.py:46
  39.9 17.5 %all-to-all-start = ((bf16[128,32,4,16]{0,3,1,2:T(8,128)(2,1)}), bf16[128,32,4,16]{0,3,1,2:T(8,128)(2,1)S(1)}, u32[]{:S(2)}, u32[]{:S(2)}) async-start(bf16[128,32,4,16]{0,3,1,2:T(8,128)(2,1)} %copy.56), calls=%async_computation | async-start | bytes 1048576 | tf_op jit(solution)/shard_map/all_to_all | solution.py:73
  78.5 2.0 %copy-start.4 = (bf16[1024,128]{1,0:T(8,128)(2,1)S(1)}, bf16[1024,128]{1,0:T(8,128)(2,1)}, u32[]{:S(2)}) copy-start(bf16[1024,128]{1,0:T(8,128)(2,1)} %get-tuple-element.407) | copy-start | bytes 786436 | tf_op jit(solution)/shard_map/while
  82.2 2.0 %copy-start.4 = (bf16[1024,128]{1,0:T(8,128)(2,1)S(1)}, bf16[1024,128]{1,0:T(8,128)(2,1)}, u32[]{:S(2)}) copy-start(bf16[1024,128]{1,0:T(8,128)(2,1)} %get-tuple-element.407) | copy-start | bytes 786436 | tf_op jit(solution)/shard_map/while
  86.9 1.6 %copy-start.5 = (bf16[1024,128]{1,0:T(8,128)(2,1)S(1)}, bf16[1024,128]{1,0:T(8,128)(2,1)}, u32[]{:S(2)}) copy-start(bf16[1024,128]{1,0:T(8,128)(2,1)} %get-tuple-element.425) | copy-start | bytes 786436 | tf_op jit(solution)/shard_map/while
  90.1 1.6 %copy-start.5 = (bf16[1024,128]{1,0:T(8,128)(2,1)S(1)}, bf16[1024,128]{1,0:T(8,128)(2,1)}, u32[]{:S(2)}) copy-start(bf16[1024,128]{1,0:T(8,128)(2,1)} %get-tuple-element.425) | copy-start | bytes 786436 | tf_op jit(solution)/shard_map/while
  93.5 1.0 copy-start.6
  95.2 1.0 copy-start.6
  97.1 3.5 %copy-start.2 = (f32[128]{0:T(128)S(1)}, f32[128]{0:T(128)}, u32[]{:S(2)}) copy-start(f32[128]{0:T(128)} %param.21) | copy-start | bytes 1540
  97.1 1.0 copy-start.7
  98.8 1.0 copy-start.7
  112.6 32.1 %copy-start.1 = (bf16[16,128,128]{2,1,0:T(8,128)(2,1)S(1)}, bf16[16,128,128]{2,1,0:T(8,128)(2,1)}, u32[]{:S(2)}) copy-start(bf16[16,128,128]{2,1,0:T(8,128)(2,1)} %param.22) | copy-start | bytes 1572868
  144.7 1.3 copy-start.3
  144.7 1.9 %copy-start.8 = (bf16[128,512]{1,0:T(8,128)(2,1)S(1)}, bf16[128,512]{1,0:T(8,128)(2,1)}, u32[]{:S(2)}) copy-start(bf16[128,512]{1,0:T(8,128)(2,1)} %param.24) | copy-start | bytes 393220
  144.7 1.9 %copy-start.9 = (f32[512]{0:T(512)S(1)}, f32[512]{0:T(512)}, u32[]{:S(2)}) copy-start(f32[512]{0:T(512)} %param.25) | copy-start | bytes 6148
  144.7 1.9 %copy-start.10 = (f32[128]{0:T(128)S(1)}, f32[128]{0:T(128)}, u32[]{:S(2)}) copy-start(f32[128]{0:T(128)} %param.27) | copy-start | bytes 1540
Sparse Core Ops, SparseCore 0:
  8.9 29.0 all-gather.2
  39.5 33.9 all-gather.4
where the time goes:
time: 158 us; the launch traced here: 155 us
  waiting for transfers between devices  60.8 us (38%)
  blocking collectives  42 us (27%)
  matrix products  21.8 us (14%)
  between operations  13.6 us (9%)
  local copies, waits for them, and re-layouts  9.86 us (6%)
  other arithmetic  3.76 us (2%)
  starting transfers between devices  3.51 us (2%)
    all_gather x1, waiting for transfers between devices, on_device(): right_seq = lax.all_gather(right_piece, 'seq', axis=0, tiled=True)  30.7 us
    all_to_all x1, blocking collectives, on_device(): lax.all_to_all(section_one.reshape(run_len, rowseq_count, own_rows, chann...  21.6 us
    all_to_all x2, blocking collectives, move_cols(): return lax.all_to_all(tile, 'col', split_axis=0, concat_axis=2, tiled=True)  20.4 us
    all_gather x1, waiting for transfers between devices, gather_right(): return lax.all_gather(right_part, 'row', axis=1, tiled=True)  15.4 us
    all_to_all x1, waiting for transfers between devices, on_device(): lax.all_to_all(split_left, 'seq', split_axis=2, concat_axis=0, tiled=True)  14 us
    dot_general x8, matrix products, project_block(): lax.dot_general(left_mat, right_mat, (((0,), (0,)), ((), ())), preferred_...  10.3 us
    dot_general x8, matrix products, project_block(): jnp.dot(outer_prod, proj_weight, preferred_element_type=jnp.float32)  9.4 us
    slice x1, local copies, waits for them, and re-layouts, on_device(): right_group = right_all[group_id * group_len:(group_id + 1) * group_len]  3.97 us
  transfers between devices with their start and end apart: 3, of which 3 were waited for; matrix products, arithmetic and copies ran while one was open for 2% of the time, Pallas kernels for 0%

commit v1 on v0

v1 whole, which is shorter than its diff:
```python
import functools

import jax
import jax.numpy as jnp
from jax import lax
from jax.experimental import pallas as pl
from jax.experimental.pallas import tpu as pltpu
from jax.sharding import PartitionSpec as P

epsilon = 1e-05
axes = ("row", "col", "seq")


def update_kernel(groups, xs, seq_total, *refs):
    place_ref = refs[0]
    left_refs = refs[1:3]
    right_refs = refs[3 : 3 + groups * xs]
    weight_ref, bias_ref = refs[3 + groups * xs : 5 + groups * xs]
    own_ref, other_ref = refs[5 + groups * xs : 7 + groups * xs]
    mirror_refs = refs[7 + groups * xs : 7 + groups * xs + groups]
    outer_ref, update_ref = refs[7 + groups * xs + groups :]
    own_rows, channels, group_len = left_refs[0].shape[1:]
    per = right_refs[0].shape[0]
    lanes = right_refs[0].shape[2]
    half = lanes // 2
    pair_channels = weight_ref.shape[0] // 2
    block = 8
    lane_low = lax.broadcasted_iota(jnp.int32, (pair_channels, lanes), 1) < half
    bias = bias_ref[...]

    def right_tile(item):
        dx, rest = divmod(item, per)
        return jnp.concatenate(
            [right_refs[dz * xs + dx][rest] for dz in range(groups)], axis=0
        )

    for side in range(2):
        left_ref = left_refs[side]

        @pl.loop(0, own_rows // block)
        def _(step):
            start = step * block
            left = jnp.concatenate(
                [
                    left_ref[dz, pl.ds(start, block)].reshape(block * channels, group_len)
                    for dz in range(groups)
                ],
                axis=1,
            )
            for pair in range(xs * per // 2):
                right = jnp.concatenate(
                    [right_tile(2 * pair), right_tile(2 * pair + 1)], axis=1
                )
                outer = jnp.dot(left, right, preferred_element_type=jnp.float32)
                outer = outer.astype(jnp.bfloat16)
                for part in range(2):
                    item = 2 * pair + part
                    outer_ref[:, item * channels : (item + 1) * channels, :] = outer[
                        :, part * lanes : (part + 1) * lanes
                    ].reshape(block, channels, lanes)
            for two in range(block // 2):
                both = jnp.concatenate([outer_ref[2 * two], outer_ref[2 * two + 1]], axis=1)
                proj = jnp.dot(weight_ref[...], both, preferred_element_type=jnp.float32)
                a0 = proj[:pair_channels, :lanes]
                a1 = proj[:pair_channels, lanes:]
                b0 = proj[pair_channels:, :lanes]
                b1 = proj[pair_channels:, lanes:]
                cell = jnp.where(lane_low, a0, b1) + pltpu.roll(
                    jnp.where(lane_low, a1, b0), half, 1
                )
                cell = cell.T / seq_total + bias
                update_ref[pl.ds(side * own_rows + start + 2 * two, 2)] = cell.astype(
                    jnp.bfloat16
                ).reshape(2, half, pair_channels)

    own_ref[...] = update_ref[:own_rows]
    other_ref[...] = update_ref[own_rows:]
    run = half // groups
    for dz in range(groups):
        begin = pl.multiple_of((place_ref[1] ^ dz) * run, run)
        mirror_refs[dz][...] = update_ref[:, pl.ds(begin, run), :]


def finish_kernel(groups, *refs):
    place_ref, pair_ref, own_ref, other_ref = refs[:4]
    mirror_refs = refs[4 : 4 + groups]
    gain_ref, up_ref, up_bias_ref, down_ref, down_bias_ref = refs[4 + groups : 9 + groups]
    out_ref, middle_ref = refs[9 + groups :]
    own_rows, columns, pair_channels = pair_ref.shape
    half = columns // 2
    run = half // groups
    for side in range(2):
        direct_ref = (own_ref, other_ref)[side]
        for dz in range(groups):
            local = pl.multiple_of((place_ref[1] ^ dz) * run, run)
            begin = pl.multiple_of((place_ref[0] ^ side) * half + local, run)
            mirrored = mirror_refs[dz][side * own_rows : (side + 1) * own_rows]
            mirrored = jnp.swapaxes(mirrored.astype(jnp.float32), 0, 1)
            direct = direct_ref[:, pl.ds(local, run), :].astype(jnp.float32)
            residual = pair_ref[:, pl.ds(begin, run), :].astype(jnp.float32)
            middle_ref[:, pl.ds(begin, run), :] = (
                residual + 0.5 * (direct + mirrored)
            ).astype(jnp.bfloat16)

    block = 4

    @pl.loop(0, own_rows // block)
    def _(step):
        values = middle_ref[pl.ds(step * block, block)].astype(jnp.float32)
        values = values.reshape(block * columns, pair_channels)
        center = jnp.mean(values, axis=1, keepdims=True)
        moved = values - center
        spread = jnp.mean(jnp.square(moved), axis=1, keepdims=True)
        normed = (moved * lax.rsqrt(spread + epsilon) * gain_ref[...]).astype(jnp.bfloat16)
        hidden = jnp.maximum(
            jnp.dot(normed, up_ref[...], preferred_element_type=jnp.float32)
            + up_bias_ref[...],
            0.0,
        ).astype(jnp.bfloat16)
        result = (
            values
            + jnp.dot(hidden, down_ref[...], preferred_element_type=jnp.float32)
            + down_bias_ref[...]
        )
        out_ref[pl.ds(step * block, block)] = result.astype(jnp.bfloat16).reshape(
            block, columns, pair_channels
        )


def on_device(
    left_piece,
    right_piece,
    proj_weight,
    proj_bias,
    pair_rep,
    norm_gain,
    up_weight,
    up_bias,
    down_weight,
    down_bias,
):
    rows = lax.axis_size("row")
    cols = lax.axis_size("col")
    groups = lax.axis_size("seq")
    xs = rows // 2
    row, col, seq = (lax.axis_index(name) for name in axes)
    core = row % 2
    own_rows, columns, pair_channels = pair_rep.shape
    group_len, channels, _ = left_piece.shape
    part_channels = right_piece.shape[1]
    half = columns // 2
    e1 = part_channels // 2
    seq_total = group_len * groups

    def swap(value, name, size, flip):
        return lax.ppermute(value, name, [(i, i ^ flip) for i in range(size)])

    right = right_piece.reshape(group_len, e1, 2, 2, half).transpose(3, 1, 0, 2, 4)
    right = right.reshape(2, e1, group_len, 2 * half)
    kept = lax.dynamic_index_in_dim(right, core, 0, False)
    sent = lax.dynamic_index_in_dim(right, 1 - core, 0, False)
    base = jnp.concatenate([kept, swap(sent, "row", rows, 1)], axis=0)

    left = left_piece.transpose(2, 1, 0).reshape(groups, own_rows, channels, group_len)

    rights = []
    bases = [base] + [swap(base, "seq", groups, dz) for dz in range(1, groups)]
    for item in bases:
        rights.append(item)
        for dx in range(1, xs):
            rights.append(swap(item, "row", rows, 2 * dx))
    lefts = []
    for dz in range(groups):
        piece = lax.dynamic_index_in_dim(left, seq ^ dz, 0, False)
        lefts.append(swap(piece, "seq", groups, dz) if dz > 0 else piece)
    left_own = jnp.stack(lefts)
    left_other = swap(left_own, "row", rows, 1)

    weight = proj_weight.reshape(channels, rows, e1, 2, pair_channels)
    weight = weight.transpose(1, 3, 4, 2, 0)
    weight = jnp.stack(
        [lax.dynamic_index_in_dim(weight, row ^ m, 0, False) for m in range(rows)], axis=2
    )
    weight = weight.reshape(2 * pair_channels, channels * channels // 2)

    place = jnp.stack([core, seq]).astype(jnp.int32)
    vmem = pl.BlockSpec(memory_space=pltpu.VMEM)
    smem = pl.BlockSpec(memory_space=pltpu.SMEM)
    bf16 = jnp.bfloat16
    run = half // groups
    count = 5 + groups * xs
    outs = pl.pallas_call(
        functools.partial(update_kernel, groups, xs, seq_total),
        out_shape=[jax.ShapeDtypeStruct((own_rows, half, pair_channels), bf16)] * 2
        + [jax.ShapeDtypeStruct((2 * own_rows, run, pair_channels), bf16)] * groups,
        in_specs=[smem] + [vmem] * (count - 1),
        out_specs=[vmem] * (2 + groups),
        scratch_shapes=[
            pltpu.VMEM((8, channels * channels // 2, 2 * half), bf16),
            pltpu.VMEM((2 * own_rows, half, pair_channels), bf16),
        ],
        compiler_params=pltpu.CompilerParams(vmem_limit_bytes=40 * 1024 * 1024),
        name="update",
    )(place, left_own, left_other, *rights, weight, proj_bias.reshape(1, pair_channels))
    update_own, update_other = outs[:2]
    update_other = swap(update_other, "row", rows, 1)

    mirrors = []
    for dz in range(groups):
        pairs = []
        for r in range(rows):
            for c in range(cols):
                for q in range(groups):
                    source = (r * cols + c) * groups + q
                    target = ((2 * c + r % 2) * cols + r // 2) * groups + (q ^ dz)
                    pairs.append((source, target))
        mirrors.append(lax.ppermute(outs[2 + dz], axes, pairs))

    return pl.pallas_call(
        functools.partial(finish_kernel, groups),
        out_shape=jax.ShapeDtypeStruct(pair_rep.shape, bf16),
        in_specs=[smem] + [vmem] * (8 + groups),
        out_specs=vmem,
        scratch_shapes=[pltpu.VMEM(pair_rep.shape, bf16)],
        compiler_params=pltpu.CompilerParams(vmem_limit_bytes=40 * 1024 * 1024),
        name="finish",
    )(
        place,
        pair_rep,
        update_own,
        update_other,
        *mirrors,
        norm_gain.reshape(1, -1),
        up_weight,
        up_bias.reshape(1, -1),
        down_weight,
        down_bias.reshape(1, -1),
    )


def solution(mesh):
    in_specs = (
        P("seq", None, "row"),
        P("seq", "row", "col"),
        P(),
        P(),
        P(("row", "seq"), "col", None),
        P(),
        P(),
        P(),
        P(),
        P(),
    )
    out_specs = P(("row", "seq"), "col", None)
    return jax.shard_map(
        on_device, mesh=mesh, in_specs=in_specs, out_specs=out_specs, check_vma=False
    )
```

time: 158 us -> 86.4 us (0.55)
  the two profiles are of different devices: /device:TPU:3 before, /device:TPU:12 now
where the time goes in v1:
time: 86.4 us; the launch traced here: 86.2 us
  waiting for transfers between devices  47.3 us (55%)
  starting transfers between devices  22.2 us (26%)
  Pallas kernels  10.2 us (12%)
  local copies, waits for them, and re-layouts  5.48 us (6%)
    ppermute x13, waiting for transfers between devices, swap(): return lax.ppermute(value, name, [(i, i ^ flip) for i in range(size)])  35.6 us
    ppermute x13, starting transfers between devices, swap(): return lax.ppermute(value, name, [(i, i ^ flip) for i in range(size)])  12.6 us
    ppermute x4, waiting for transfers between devices, on_device(): mirrors.append(lax.ppermute(outs[2 + dz], axes, pairs))  11.8 us
    ppermute x4, starting transfers between devices, on_device(): mirrors.append(lax.ppermute(outs[2 + dz], axes, pairs))  9.62 us
    pallas_call x1, Pallas kernels, on_device(): pl.pallas_call(functools.partial(update_kernel, groups, xs, seq_total), o...  5.45 us
    pallas_call x1, Pallas kernels, on_device(): pl.pallas_call(functools.partial(finish_kernel, groups), out_shape=jax.Sh...  4.76 us
    unnamed x20, local copies, waits for them, and re-layouts  3.32 us
  transfers between devices with their start and end apart: 17, of which 10 were waited for; matrix products, arithmetic and copies ran while one was open for 4% of the time, Pallas kernels for 0%

profile of v1, /device:TPU:12, one launch (start us, length us, event | category | flops | bytes accessed | tf_op | source)
XLA Modules:
  0.0 86.2 jit_solution(6150087303780144569)
XLA Ops:
  0.0 1.1 %copy.18 = bf16[128,8,128]{0,2,1:T(8,128)(2,1)S(1)} copy(bf16[128,8,128]{2,1,0:T(8,128)(2,1)} %param.11) | data formatting | bytes 524288 | tf_op args[1]
  1.2 0.0 copy-start.7
  1.2 0.1 copy.21
  1.4 0.1 collective-permute-start.4
  1.5 0.8 copy-done.7
  2.2 0.3 copy.17
  2.6 0.0 copy-start.8
  2.7 1.6 %collective-permute-start.2 = (bf16[16,32,128]{2,1,0:T(8,128)(2,1)S(1)}, bf16[16,32,128]{2,1,0:T(8,128)(2,1)S(1)}, u32[]{:S(2)}, u32[]{:S(2)}) collective-permute-start(bf16[16,32,128]{2,1,0:T(8,128)(2,1)S(1)} %get-tuple-element.18), channel_id=1, source_target_pairs={{0,3},{1,2},{2,1},{3,0},{4,7},{5,6},{6,5},{7,4},{8,11},{9,10},{10,... | collective-permute-start | bytes 393224 | tf_op jit(solution)/shard_map/ppermute | solution.py:156
  4.3 1.2 %collective-permute-start.1 = (bf16[16,32,128]{2,1,0:T(8,128)(2,1)S(1)}, bf16[16,32,128]{2,1,0:T(8,128)(2,1)S(1)}, u32[]{:S(2)}, u32[]{:S(2)}) collective-permute-start(bf16[16,32,128]{2,1,0:T(8,128)(2,1)S(1)} %get-tuple-element.19), channel_id=1, source_target_pairs={{0,2},{1,3},{2,0},{3,1},{4,6},{5,7},{6,4},{7,5},{8,10},{9,11},{10,... | collective-permute-start | bytes 393224 | tf_op jit(solution)/shard_map/ppermute | solution.py:156
  5.5 1.2 %collective-permute-start = (bf16[16,32,128]{2,1,0:T(8,128)(2,1)S(1)}, bf16[16,32,128]{2,1,0:T(8,128)(2,1)S(1)}, u32[]{:S(2)}, u32[]{:S(2)}) collective-permute-start(bf16[16,32,128]{2,1,0:T(8,128)(2,1)S(1)} %get-tuple-element.20), channel_id=1, source_target_pairs={{0,1},{1,0},{2,3},{3,2},{4,5},{5,4},{6,7},{7,6},{8,9},{9,8},{10,11... | collective-permute-start | bytes 393224 | tf_op jit(solution)/shard_map/ppermute | solution.py:156
  6.8 0.2 constant_dynamic-slice_fusion.3
  7.0 0.1 copy.20
  7.1 0.0 collective-permute-done.4
  7.1 1.5 %collective-permute-start.10 = (bf16[8,128,128]{2,1,0:T(8,128)(2,1)S(1)}, bf16[8,128,128]{2,1,0:T(8,128)(2,1)S(1)}, u32[]{:S(2)}, u32[]{:S(2)}) collective-permute-start(bf16[8,128,128]{2,1,0:T(8,128)(2,1)S(1)} %pad_maximum_fusion.1.refs_3_), channel_id=1, source_target_pairs={{0,3},{1,2},{2,1},{3,0},{4,7},{5,6},{6,5},{7,4},{8,11},{9,10},{10,... | collective-permute-start | bytes 786440 | tf_op jit(solution)/shard_map/ppermute | solution.py:156
  8.7 1.7 %collective-permute-start.8 = (bf16[8,128,128]{2,1,0:T(8,128)(2,1)S(1)}, bf16[8,128,128]{2,1,0:T(8,128)(2,1)S(1)}, u32[]{:S(2)}, u32[]{:S(2)}) collective-permute-start(bf16[8,128,128]{2,1,0:T(8,128)(2,1)S(1)} %pad_maximum_fusion.1.refs_3_), channel_id=1, source_target_pairs={{0,2},{1,3},{2,0},{3,1},{4,6},{5,7},{6,4},{7,5},{8,10},{9,11},{10,... | collective-permute-start | bytes 786440 | tf_op jit(solution)/shard_map/ppermute | solution.py:156
  10.4 5.2 %collective-permute-done.2 = bf16[16,32,128]{2,1,0:T(8,128)(2,1)S(1)} collective-permute-done((bf16[16,32,128]{2,1,0:T(8,128)(2,1)S(1)}, bf16[16,32,128]{2,1,0:T(8,128)(2,1)S(1)}, u32[]{:S(2)}, u32[]{:S(2)}) %collective-permute-start.2) | collective-permute-done | bytes 131104 | tf_op jit(solution)/shard_map/ppermute | solution.py:156
  15.6 12.3 %collective-permute-done.1 = bf16[16,32,128]{2,1,0:T(8,128)(2,1)S(1)} collective-permute-done((bf16[16,32,128]{2,1,0:T(8,128)(2,1)S(1)}, bf16[16,32,128]{2,1,0:T(8,128)(2,1)S(1)}, u32[]{:S(2)}, u32[]{:S(2)}) %collective-permute-start.1) | collective-permute-done | bytes 131104 | tf_op jit(solution)/shard_map/ppermute | solution.py:156
  27.9 0.1 pad_maximum_fusion.refs_1_
  27.9 0.1 collective-permute-start.3
  28.0 0.1 copy_bitcast_fusion.3
  28.1 1.6 %collective-permute-start.5 = (bf16[8,128,128]{2,1,0:T(8,128)(2,1)S(1)}, bf16[8,128,128]{2,1,0:T(8,128)(2,1)S(1)}, u32[]{:S(2)}, u32[]{:S(2)}) collective-permute-start(bf16[8,128,128]{2,1,0:T(8,128)(2,1)S(1)} %pad_maximum_fusion.1.refs_3_), channel_id=1, source_target_pairs={{0,16},{8,24},{16,0},{24,8},{1,17},{9,25},{17,1},{25,9},{2,18},{10... | collective-permute-start | bytes 786440 | tf_op jit(solution)/shard_map/ppermute | solution.py:156
  29.7 4.5 %collective-permute-done.10.refs_9_ = bf16[8,128,128]{2,1,0:T(8,128)(2,1)S(1)} collective-permute-done((bf16[8,128,128]{2,1,0:T(8,128)(2,1)S(1)}, bf16[8,128,128]{2,1,0:T(8,128)(2,1)S(1)}, u32[]{:S(2)}, u32[]{:S(2)}) %collective-permute-start.10) | collective-permute-done | bytes 262176 | tf_op jit(solution)/shard_map/ppermute | solution.py:156
  34.2 1.5 %collective-permute-start.11 = (bf16[8,128,128]{2,1,0:T(8,128)(2,1)S(1)}, bf16[8,128,128]{2,1,0:T(8,128)(2,1)S(1)}, u32[]{:S(2)}, u32[]{:S(2)}) collective-permute-start(bf16[8,128,128]{2,1,0:T(8,128)(2,1)S(1)} %collective-permute-done.10.refs_9_), channel_id=1, source_target_pairs={{0,16},{8,24},{16,0},{24,8},{1,17},{9,25},{17,1},{25,9},{2,18},{10... | collective-permute-start | bytes 786440 | tf_op jit(solution)/shard_map/ppermute | solution.py:156
  35.7 2.3 %collective-permute-done.8.refs_7_ = bf16[8,128,128]{2,1,0:T(8,128)(2,1)S(1)} collective-permute-done((bf16[8,128,128]{2,1,0:T(8,128)(2,1)S(1)}, bf16[8,128,128]{2,1,0:T(8,128)(2,1)S(1)}, u32[]{:S(2)}, u32[]{:S(2)}) %collective-permute-start.8) | collective-permute-done | bytes 262176 | tf_op jit(solution)/shard_map/ppermute | solution.py:156
  38.0 1.5 %collective-permute-start.9 = (bf16[8,128,128]{2,1,0:T(8,128)(2,1)S(1)}, bf16[8,128,128]{2,1,0:T(8,128)(2,1)S(1)}, u32[]{:S(2)}, u32[]{:S(2)}) collective-permute-start(bf16[8,128,128]{2,1,0:T(8,128)(2,1)S(1)} %collective-permute-done.8.refs_7_), channel_id=1, source_target_pairs={{0,16},{8,24},{16,0},{24,8},{1,17},{9,25},{17,1},{25,9},{2,18},{10... | collective-permute-start | bytes 786440 | tf_op jit(solution)/shard_map/ppermute | solution.py:156
  39.4 0.5 collective-permute-start.7
  40.0 0.1 copy_bitcast_fusion.1
  40.1 0.5 pad_maximum_fusion.2
  40.6 0.7 copy.37
  41.3 1.1 %copy.26.refs_11_ = bf16[256,512]{1,0:T(8,128)(2,1)S(1)} copy(bf16[256,512]{0,1:T(8,128)(2,1)} %bitcast.54) | data formatting | bytes 524288 | tf_op jit(solution)/shard_map/reshape | solution.py:184
  42.4 0.1 pad_add_fusion.refs_0_
  42.5 0.0 collective-permute-done.5.refs_4_
  42.5 1.0 %collective-permute-done.11.refs_10_ = bf16[8,128,128]{2,1,0:T(8,128)(2,1)S(1)} collective-permute-done((bf16[8,128,128]{2,1,0:T(8,128)(2,1)S(1)}, bf16[8,128,128]{2,1,0:T(8,128)(2,1)S(1)}, u32[]{:S(2)}, u32[]{:S(2)}) %collective-permute-start.11) | collective-permute-done | bytes 262176 | tf_op jit(solution)/shard_map/ppermute | solution.py:156
  43.4 5.6 %collective-permute-done.9.refs_8_ = bf16[8,128,128]{2,1,0:T(8,128)(2,1)S(1)} collective-permute-done((bf16[8,128,128]{2,1,0:T(8,128)(2,1)S(1)}, bf16[8,128,128]{2,1,0:T(8,128)(2,1)S(1)}, u32[]{:S(2)}, u32[]{:S(2)}) %collective-permute-start.9) | collective-permute-done | bytes 262176 | tf_op jit(solution)/shard_map/ppermute | solution.py:156
  49.1 4.7 %collective-permute-done.7.refs_6_ = bf16[8,128,128]{2,1,0:T(8,128)(2,1)S(1)} collective-permute-done((bf16[8,128,128]{2,1,0:T(8,128)(2,1)S(1)}, bf16[8,128,128]{2,1,0:T(8,128)(2,1)S(1)}, u32[]{:S(2)}, u32[]{:S(2)}) %collective-permute-start.7) | collective-permute-done | bytes 262176 | tf_op jit(solution)/shard_map/ppermute | solution.py:156
  53.7 0.0 copy-start.1
  53.8 0.0 copy-start.2
  53.8 5.5 %update.1 = (bf16[16,64,128]{2,1,0:T(8,128)(2,1)S(1)}, bf16[16,64,128]{2,1,0:T(8,128)(2,1)S(1)}, bf16[32,16,128]{2,1,0:T(8,128)(2,1)S(1)}, bf16[32,16,128]{2,1,0...) custom-call(s32[2]{0:T(128)S(1)} %pad_add_fusion.refs_0_, ...), custom_call_target="tpu_custom_call" | custom-call | tf_op jit(solution)/shard_map/update/pallas_call | solution.py:192
  59.2 0.1 collective-permute-start.12
  59.3 3.3 %collective-permute-start.13 = (bf16[32,16,128]{2,1,0:T(8,128)(2,1)S(1)}, bf16[32,16,128]{2,1,0:T(8,128)(2,1)S(1)}, u32[]{:S(2)}, u32[]{:S(2)}) collective-permute-start(bf16[32,16,128]{2,1,0:T(8,128)(2,1)S(1)} %get-tuple-element.13), channel_id=1, source_target_pairs={{0,0},{1,1},{2,2},{3,3},{4,16},{5,17},{6,18},{7,19},{8,8},{9,9},{1... | collective-permute-start | bytes 393224 | tf_op jit(solution)/shard_map/ppermute | solution.py:217
  62.7 3.2 %collective-permute-start.14 = (bf16[32,16,128]{2,1,0:T(8,128)(2,1)S(1)}, bf16[32,16,128]{2,1,0:T(8,128)(2,1)S(1)}, u32[]{:S(2)}, u32[]{:S(2)}) collective-permute-start(bf16[32,16,128]{2,1,0:T(8,128)(2,1)S(1)} %get-tuple-element.14), channel_id=1, source_target_pairs={{0,1},{1,0},{2,3},{3,2},{4,17},{5,16},{6,19},{7,18},{8,9},{9,8},{1... | collective-permute-start | bytes 393224 | tf_op jit(solution)/shard_map/ppermute | solution.py:217
  65.8 1.3 %collective-permute-start.15 = (bf16[32,16,128]{2,1,0:T(8,128)(2,1)S(1)}, bf16[32,16,128]{2,1,0:T(8,128)(2,1)S(1)}, u32[]{:S(2)}, u32[]{:S(2)}) collective-permute-start(bf16[32,16,128]{2,1,0:T(8,128)(2,1)S(1)} %get-tuple-element.15), channel_id=1, source_target_pairs={{0,2},{1,3},{2,0},{3,1},{4,18},{5,19},{6,16},{7,17},{8,10},{9,11},... | collective-permute-start | bytes 393224 | tf_op jit(solution)/shard_map/ppermute | solution.py:217
  67.1 1.8 %collective-permute-start.16 = (bf16[32,16,128]{2,1,0:T(8,128)(2,1)S(1)}, bf16[32,16,128]{2,1,0:T(8,128)(2,1)S(1)}, u32[]{:S(2)}, u32[]{:S(2)}) collective-permute-start(bf16[32,16,128]{2,1,0:T(8,128)(2,1)S(1)} %get-tuple-element.16), channel_id=1, source_target_pairs={{0,3},{1,2},{2,1},{3,0},{4,19},{5,18},{6,17},{7,16},{8,11},{9,10},... | collective-permute-start | bytes 393224 | tf_op jit(solution)/shard_map/ppermute | solution.py:217
  68.9 1.9 %collective-permute-done.13.refs_4_ = bf16[32,16,128]{2,1,0:T(8,128)(2,1)S(1)} collective-permute-done((bf16[32,16,128]{2,1,0:T(8,128)(2,1)S(1)}, bf16[32,16,128]{2,1,0:T(8,128)(2,1)S(1)}, u32[]{:S(2)}, u32[]{:S(2)}) %collective-permute-start.13) | collective-permute-done | bytes 131104 | tf_op jit(solution)/shard_map/ppermute | solution.py:217
  70.8 5.9 %collective-permute-done.15.refs_6_ = bf16[32,16,128]{2,1,0:T(8,128)(2,1)S(1)} collective-permute-done((bf16[32,16,128]{2,1,0:T(8,128)(2,1)S(1)}, bf16[32,16,128]{2,1,0:T(8,128)(2,1)S(1)}, u32[]{:S(2)}, u32[]{:S(2)}) %collective-permute-start.15) | collective-permute-done | bytes 131104 | tf_op jit(solution)/shard_map/ppermute | solution.py:217
  76.7 4.1 %collective-permute-done.16.refs_7_ = bf16[32,16,128]{2,1,0:T(8,128)(2,1)S(1)} collective-permute-done((bf16[32,16,128]{2,1,0:T(8,128)(2,1)S(1)}, bf16[32,16,128]{2,1,0:T(8,128)(2,1)S(1)}, u32[]{:S(2)}, u32[]{:S(2)}) %collective-permute-start.16) | collective-permute-done | bytes 131104 | tf_op jit(solution)/shard_map/ppermute | solution.py:217
  80.8 0.6 copy-done.3
  81.4 4.8 %finish.1 = bf16[16,128,128]{2,1,0:T(8,128)(2,1)} custom-call(s32[2]{0:T(128)S(1)} %pad_add_fusion.refs_0_, bf16[16,128,128]{2,1,0:T(8,128)(2,1)S(1)} %copy-done, bf16[16,64,128]{2,1,0:T(8,128)(2,1)S(1)} %get-tuple-element.11.refs_2_, bf16[16,64,128]{2,1,0:T(8,128)(2,1)S(1)} %collective-permute-done.12.refs_3_, ...), custom_call_target="tpu_custom_call" | custom-call | tf_op jit(solution)/shard_map/finish/pallas_call | solution.py:219
  (22 shorter events, 0.2 us)
Async XLA Ops:
  1.2 1.0 %copy-start.7 = (bf16[128,32,64]{0,2,1:T(8,128)(2,1)S(1)}, bf16[128,32,64]{0,2,1:T(8,128)(2,1)}, u32[]{:S(2)}) copy-start(bf16[128,32,64]{0,2,1:T(8,128)(2,1)} %param.10) | copy-start | bytes 1572868
  1.4 5.7 %collective-permute-start.4 = (bf16[4,128,128]{2,1,0:T(8,128)(2,1)S(1)}, bf16[4,128,128]{2,1,0:T(8,128)(2,1)S(1)}, u32[]{:S(2)}, u32[]{:S(2)}) collective-permute-start(bf16[4,128,128]{2,1,0:T(8,128)(2,1)S(1)} %bitcast.59), channel_id=1, source_target_pairs={{0,8},{8,0},{16,24},{24,16},{1,9},{9,1},{17,25},{25,17},{2,10},{10... | collective-permute-start | bytes 393224 | tf_op jit(solution)/shard_map/ppermute | solution.py:156
  2.6 4.2 %copy-start.8 = (bf16[1024,128]{1,0:T(8,128)(2,1)S(1)}, bf16[1024,128]{1,0:T(8,128)(2,1)}, u32[]{:S(2)}) copy-start(bf16[1024,128]{1,0:T(8,128)(2,1)} %param.12) | copy-start | bytes 786436
  2.7 12.9 %collective-permute-start.2 = (bf16[16,32,128]{2,1,0:T(8,128)(2,1)S(1)}, bf16[16,32,128]{2,1,0:T(8,128)(2,1)S(1)}, u32[]{:S(2)}, u32[]{:S(2)}) collective-permute-start(bf16[16,32,128]{2,1,0:T(8,128)(2,1)S(1)} %get-tuple-element.18), channel_id=1, source_target_pairs={{0,3},{1,2},{2,1},{3,0},{4,7},{5,6},{6,5},{7,4},{8,11},{9,10},{10,... | collective-permute-start | bytes 393224 | tf_op jit(solution)/shard_map/ppermute | solution.py:156
  4.3 23.6 %collective-permute-start.1 = (bf16[16,32,128]{2,1,0:T(8,128)(2,1)S(1)}, bf16[16,32,128]{2,1,0:T(8,128)(2,1)S(1)}, u32[]{:S(2)}, u32[]{:S(2)}) collective-permute-start(bf16[16,32,128]{2,1,0:T(8,128)(2,1)S(1)} %get-tuple-element.19), channel_id=1, source_target_pairs={{0,2},{1,3},{2,0},{3,1},{4,6},{5,7},{6,4},{7,5},{8,10},{9,11},{10,... | collective-permute-start | bytes 393224 | tf_op jit(solution)/shard_map/ppermute | solution.py:156
  5.5 22.3 %collective-permute-start = (bf16[16,32,128]{2,1,0:T(8,128)(2,1)S(1)}, bf16[16,32,128]{2,1,0:T(8,128)(2,1)S(1)}, u32[]{:S(2)}, u32[]{:S(2)}) collective-permute-start(bf16[16,32,128]{2,1,0:T(8,128)(2,1)S(1)} %get-tuple-element.20), channel_id=1, source_target_pairs={{0,1},{1,0},{2,3},{3,2},{4,5},{5,4},{6,7},{7,6},{8,9},{9,8},{10,11... | collective-permute-start | bytes 393224 | tf_op jit(solution)/shard_map/ppermute | solution.py:156
  7.1 27.1 %collective-permute-start.10 = (bf16[8,128,128]{2,1,0:T(8,128)(2,1)S(1)}, bf16[8,128,128]{2,1,0:T(8,128)(2,1)S(1)}, u32[]{:S(2)}, u32[]{:S(2)}) collective-permute-start(bf16[8,128,128]{2,1,0:T(8,128)(2,1)S(1)} %pad_maximum_fusion.1.refs_3_), channel_id=1, source_target_pairs={{0,3},{1,2},{2,1},{3,0},{4,7},{5,6},{6,5},{7,4},{8,11},{9,10},{10,... | collective-permute-start | bytes 786440 | tf_op jit(solution)/shard_map/ppermute | solution.py:156
  8.7 29.3 %collective-permute-start.8 = (bf16[8,128,128]{2,1,0:T(8,128)(2,1)S(1)}, bf16[8,128,128]{2,1,0:T(8,128)(2,1)S(1)}, u32[]{:S(2)}, u32[]{:S(2)}) collective-permute-start(bf16[8,128,128]{2,1,0:T(8,128)(2,1)S(1)} %pad_maximum_fusion.1.refs_3_), channel_id=1, source_target_pairs={{0,2},{1,3},{2,0},{3,1},{4,6},{5,7},{6,4},{7,5},{8,10},{9,11},{10,... | collective-permute-start | bytes 786440 | tf_op jit(solution)/shard_map/ppermute | solution.py:156
  15.6 23.9 %collective-permute-start.6 = (bf16[8,128,128]{2,1,0:T(8,128)(2,1)S(1)}, bf16[8,128,128]{2,1,0:T(8,128)(2,1)S(1)}, u32[]{:S(2)}, u32[]{:S(2)}) collective-permute-start(bf16[8,128,128]{2,1,0:T(8,128)(2,1)S(1)} %pad_maximum_fusion.1.refs_3_), channel_id=1, source_target_pairs={{0,1},{1,0},{2,3},{3,2},{4,5},{5,4},{6,7},{7,6},{8,9},{9,8},{10,11... | collective-permute-start | bytes 786440 | tf_op jit(solution)/shard_map/ppermute | solution.py:156
  27.9 25.8 %collective-permute-start.3 = (bf16[4,16,32,128]{3,2,1,0:T(8,128)(2,1)S(1)}, bf16[4,16,32,128]{3,2,1,0:T(8,128)(2,1)S(1)}, u32[]{:S(2)}, u32[]{:S(2)}) collective-permute-start(bf16[4,16,32,128]{3,2,1,0:T(8,128)(2,1)S(1)} %pad_maximum_fusion.refs_1_), channel_id=1, source_target_pairs={{0,8},{8,0},{16,24},{24,16},{1,9},{9,1},{17,25},{25,17},{2,10},{10... | collective-permute-start | bytes 1572872 | tf_op jit(solution)/shard_map/ppermute | solution.py:156
  28.1 14.4 %collective-permute-start.5 = (bf16[8,128,128]{2,1,0:T(8,128)(2,1)S(1)}, bf16[8,128,128]{2,1,0:T(8,128)(2,1)S(1)}, u32[]{:S(2)}, u32[]{:S(2)}) collective-permute-start(bf16[8,128,128]{2,1,0:T(8,128)(2,1)S(1)} %pad_maximum_fusion.1.refs_3_), channel_id=1, source_target_pairs={{0,16},{8,24},{16,0},{24,8},{1,17},{9,25},{17,1},{25,9},{2,18},{10... | collective-permute-start | bytes 786440 | tf_op jit(solution)/shard_map/ppermute | solution.py:156
  34.2 9.2 %collective-permute-start.11 = (bf16[8,128,128]{2,1,0:T(8,128)(2,1)S(1)}, bf16[8,128,128]{2,1,0:T(8,128)(2,1)S(1)}, u32[]{:S(2)}, u32[]{:S(2)}) collective-permute-start(bf16[8,128,128]{2,1,0:T(8,128)(2,1)S(1)} %collective-permute-done.10.refs_9_), channel_id=1, source_target_pairs={{0,16},{8,24},{16,0},{24,8},{1,17},{9,25},{17,1},{25,9},{2,18},{10... | collective-permute-start | bytes 786440 | tf_op jit(solution)/shard_map/ppermute | solution.py:156
  38.0 11.1 %collective-permute-start.9 = (bf16[8,128,128]{2,1,0:T(8,128)(2,1)S(1)}, bf16[8,128,128]{2,1,0:T(8,128)(2,1)S(1)}, u32[]{:S(2)}, u32[]{:S(2)}) collective-permute-start(bf16[8,128,128]{2,1,0:T(8,128)(2,1)S(1)} %collective-permute-done.8.refs_7_), channel_id=1, source_target_pairs={{0,16},{8,24},{16,0},{24,8},{1,17},{9,25},{17,1},{25,9},{2,18},{10... | collective-permute-start | bytes 786440 | tf_op jit(solution)/shard_map/ppermute | solution.py:156
  39.4 14.3 %collective-permute-start.7 = (bf16[8,128,128]{2,1,0:T(8,128)(2,1)S(1)}, bf16[8,128,128]{2,1,0:T(8,128)(2,1)S(1)}, u32[]{:S(2)}, u32[]{:S(2)}) collective-permute-start(bf16[8,128,128]{2,1,0:T(8,128)(2,1)S(1)} %collective-permute-done.6.refs_5_), channel_id=1, source_target_pairs={{0,16},{8,24},{16,0},{24,8},{1,17},{9,25},{17,1},{25,9},{2,18},{10... | collective-permute-start | bytes 786440 | tf_op jit(solution)/shard_map/ppermute | solution.py:156
  42.5 11.3 %copy-start.4 = (f32[128]{0:T(128)S(1)}, f32[128]{0:T(128)}, u32[]{:S(2)}) copy-start(f32[128]{0:T(128)} %param.13) | copy-start | bytes 1540
  53.7 27.0 %copy-start = (bf16[16,128,128]{2,1,0:T(8,128)(2,1)S(1)}, bf16[16,128,128]{2,1,0:T(8,128)(2,1)}, u32[]{:S(2)}) copy-start(bf16[16,128,128]{2,1,0:T(8,128)(2,1)} %refs_1_.1) | copy-start | bytes 1572868
  53.7 27.0 %copy-start.1 = (bf16[128,512]{1,0:T(8,128)(2,1)S(1)}, bf16[128,512]{1,0:T(8,128)(2,1)}, u32[]{:S(2)}) copy-start(bf16[128,512]{1,0:T(8,128)(2,1)} %refs_9_.1) | copy-start | bytes 393220
  53.8 27.0 %copy-start.2 = (bf16[512,128]{1,0:T(8,128)(2,1)S(1)}, bf16[512,128]{1,0:T(8,128)(2,1)}, u32[]{:S(2)}) copy-start(bf16[512,128]{1,0:T(8,128)(2,1)} %refs_11_.1) | copy-start | bytes 393220
  59.2 21.5 %collective-permute-start.12 = (bf16[16,64,128]{2,1,0:T(8,128)(2,1)S(1)}, bf16[16,64,128]{2,1,0:T(8,128)(2,1)S(1)}, u32[]{:S(2)}, u32[]{:S(2)}) collective-permute-start(bf16[16,64,128]{2,1,0:T(8,128)(2,1)S(1)} %get-tuple-element.12), channel_id=1, source_target_pairs={{0,8},{8,0},{16,24},{24,16},{1,9},{9,1},{17,25},{25,17},{2,10},{10... | collective-permute-start | bytes 786440 | tf_op jit(solution)/shard_map/ppermute | solution.py:156
  59.3 11.5 %collective-permute-start.13 = (bf16[32,16,128]{2,1,0:T(8,128)(2,1)S(1)}, bf16[32,16,128]{2,1,0:T(8,128)(2,1)S(1)}, u32[]{:S(2)}, u32[]{:S(2)}) collective-permute-start(bf16[32,16,128]{2,1,0:T(8,128)(2,1)S(1)} %get-tuple-element.13), channel_id=1, source_target_pairs={{0,0},{1,1},{2,2},{3,3},{4,16},{5,17},{6,18},{7,19},{8,8},{9,9},{1... | collective-permute-start | bytes 393224 | tf_op jit(solution)/shard_map/ppermute | solution.py:217
  62.7 8.1 %collective-permute-start.14 = (bf16[32,16,128]{2,1,0:T(8,128)(2,1)S(1)}, bf16[32,16,128]{2,1,0:T(8,128)(2,1)S(1)}, u32[]{:S(2)}, u32[]{:S(2)}) collective-permute-start(bf16[32,16,128]{2,1,0:T(8,128)(2,1)S(1)} %get-tuple-element.14), channel_id=1, source_target_pairs={{0,1},{1,0},{2,3},{3,2},{4,17},{5,16},{6,19},{7,18},{8,9},{9,8},{1... | collective-permute-start | bytes 393224 | tf_op jit(solution)/shard_map/ppermute | solution.py:217
  65.8 10.8 %collective-permute-start.15 = (bf16[32,16,128]{2,1,0:T(8,128)(2,1)S(1)}, bf16[32,16,128]{2,1,0:T(8,128)(2,1)S(1)}, u32[]{:S(2)}, u32[]{:S(2)}) collective-permute-start(bf16[32,16,128]{2,1,0:T(8,128)(2,1)S(1)} %get-tuple-element.15), channel_id=1, source_target_pairs={{0,2},{1,3},{2,0},{3,1},{4,18},{5,19},{6,16},{7,17},{8,10},{9,11},... | collective-permute-start | bytes 393224 | tf_op jit(solution)/shard_map/ppermute | solution.py:217
  67.1 13.6 %collective-permute-start.16 = (bf16[32,16,128]{2,1,0:T(8,128)(2,1)S(1)}, bf16[32,16,128]{2,1,0:T(8,128)(2,1)S(1)}, u32[]{:S(2)}, u32[]{:S(2)}) collective-permute-start(bf16[32,16,128]{2,1,0:T(8,128)(2,1)S(1)} %get-tuple-element.16), channel_id=1, source_target_pairs={{0,3},{1,2},{2,1},{3,0},{4,19},{5,18},{6,17},{7,16},{8,11},{9,10},... | collective-permute-start | bytes 393224 | tf_op jit(solution)/shard_map/ppermute | solution.py:217
  80.7 0.7 copy-start.3
  80.7 0.7 copy-start.5
  80.7 0.7 copy-start.6

commit v2 on v1

--- a/solution.py
+++ b/solution.py
@@ -11,27 +11,30 @@
 axes = ("row", "col", "seq")
 
 
-def update_kernel(groups, xs, seq_total, *refs):
-    place_ref = refs[0]
-    left_refs = refs[1:3]
-    right_refs = refs[3 : 3 + groups * xs]
-    weight_ref, bias_ref = refs[3 + groups * xs : 5 + groups * xs]
-    own_ref, other_ref = refs[5 + groups * xs : 7 + groups * xs]
-    mirror_refs = refs[7 + groups * xs : 7 + groups * xs + groups]
-    outer_ref, update_ref = refs[7 + groups * xs + groups :]
-    own_rows, channels, group_len = left_refs[0].shape[1:]
-    per = right_refs[0].shape[0]
-    lanes = right_refs[0].shape[2]
+def update_kernel(groups, own_rows, seq_total, last, *refs):
+    left_refs = refs[:2]
+    position = 2
+    if last:
+        place_ref, bias_ref, partial_ref = refs[2:5]
+        position = 5
+    weight_ref = refs[position]
+    outs = groups + 2 if last else 1
+    scratch = 2 if last else 1
+    right_refs = refs[position + 1 : len(refs) - outs - scratch]
+    out_refs = refs[len(refs) - outs - scratch : len(refs) - scratch]
+    outer_ref = refs[len(refs) - scratch]
+    channels, group_len = left_refs[0].shape[2:]
+    per, _, lanes = right_refs[0].shape
+    sources = len(right_refs) // groups
     half = lanes // 2
     pair_channels = weight_ref.shape[0] // 2
     block = 8
     lane_low = lax.broadcasted_iota(jnp.int32, (pair_channels, lanes), 1) < half
-    bias = bias_ref[...]
 
     def right_tile(item):
         dx, rest = divmod(item, per)
         return jnp.concatenate(
-            [right_refs[dz * xs + dx][rest] for dz in range(groups)], axis=0
+            [right_refs[dz * sources + dx][rest] for dz in range(groups)], axis=0
         )
 
     for side in range(2):
@@ -47,7 +50,7 @@
                 ],
                 axis=1,
             )
-            for pair in range(xs * per // 2):
+            for pair in range(sources * per // 2):
                 right = jnp.concatenate(
                     [right_tile(2 * pair), right_tile(2 * pair + 1)], axis=1
                 )
@@ -68,17 +71,23 @@
                 cell = jnp.where(lane_low, a0, b1) + pltpu.roll(
                     jnp.where(lane_low, a1, b0), half, 1
                 )
-                cell = cell.T / seq_total + bias
-                update_ref[pl.ds(side * own_rows + start + 2 * two, 2)] = cell.astype(
-                    jnp.bfloat16
-                ).reshape(2, half, pair_channels)
-
-    own_ref[...] = update_ref[:own_rows]
-    other_ref[...] = update_ref[own_rows:]
-    run = half // groups
-    for dz in range(groups):
-        begin = pl.multiple_of((place_ref[1] ^ dz) * run, run)
-        mirror_refs[dz][...] = update_ref[:, pl.ds(begin, run), :]
+                index = (side * own_rows + start) // 2 + two
+                if last:
+                    cell = (cell + partial_ref[index]).T / seq_total + bias_ref[...]
+                    refs[-1][pl.ds(2 * index, 2)] = cell.astype(jnp.bfloat16).reshape(
+                        2, half, pair_channels
+                    )
+                else:
+                    out_refs[0][index] = cell
+
+    if last:
+        update_ref = refs[-1]
+        out_refs[0][...] = update_ref[:own_rows]
+        out_refs[1][...] = update_ref[own_rows:]
+        run = half // groups
+        for dz in range(groups):
+            begin = pl.multiple_of((place_ref[1] ^ dz) * run, run)
+            out_refs[2 + dz][...] = update_ref[:, pl.ds(begin, run), :]
 
 
 def finish_kernel(groups, *refs):
@@ -108,9 +117,17 @@
     def _(step):
         values = middle_ref[pl.ds(step * block, block)].astype(jnp.float32)
         values = values.reshape(block * columns, pair_channels)
-        center = jnp.mean(values, axis=1, keepdims=True)
+        ones = jnp.full((pair_channels, pair_channels), 1.0 / pair_channels, jnp.bfloat16)
+        center = jnp.dot(
+            values.astype(jnp.bfloat16), ones, preferred_element_type=jnp.float32
+        )
         moved = values - center
-        spread = jnp.mean(jnp.square(moved), axis=1, keepdims=True)
+        square = jnp.square(moved)
+        high = square.astype(jnp.bfloat16)
+        low = (square - high.astype(jnp.float32)).astype(jnp.bfloat16)
+        spread = jnp.dot(high, ones, preferred_element_type=jnp.float32) + jnp.dot(
+            low, ones, preferred_element_type=jnp.float32
+        )
         normed = (moved * lax.rsqrt(spread + epsilon) * gain_ref[...]).astype(jnp.bfloat16)
         hidden = jnp.maximum(
             jnp.dot(normed, up_ref[...], preferred_element_type=jnp.float32)
@@ -155,26 +172,56 @@
     def swap(value, name, size, flip):
         return lax.ppermute(value, name, [(i, i ^ flip) for i in range(size)])
 
+    share = own_rows // cols
+    left = left_piece.transpose(2, 1, 0).reshape(groups, cols, share, channels, group_len)
+    left = lax.dynamic_index_in_dim(left, col, 1, False)
+    lefts = []
+    for dz in range(groups):
+        piece = lax.dynamic_index_in_dim(left, seq ^ dz, 0, False)
+        lefts.append(swap(piece, "seq", groups, dz) if dz > 0 else piece)
+    left = jnp.stack(lefts)
+    shares = [left] + [swap(left, "col", cols, dy) for dy in range(1, cols)]
+    stacked = jnp.stack(shares)
+    stacked = jnp.stack(
+        [lax.dynamic_index_in_dim(stacked, col ^ dy, 0, False) for dy in range(cols)], axis=1
+    )
+    left_own = stacked.reshape(groups, own_rows, channels, group_len)
+    left_other = swap(left_own, "row", rows, 1)
+
     right = right_piece.reshape(group_len, e1, 2, 2, half).transpose(3, 1, 0, 2, 4)
     right = right.reshape(2, e1, group_len, 2 * half)
     kept = lax.dynamic_index_in_dim(right, core, 0, False)
     sent = lax.dynamic_index_in_dim(right, 1 - core, 0, False)
     base = jnp.concatenate([kept, swap(sent, "row", rows, 1)], axis=0)
 
-    left = left_piece.transpose(2, 1, 0).reshape(groups, own_rows, channels, group_len)
-
-    rights = []
-    bases = [base] + [swap(base, "seq", groups, dz) for dz in range(1, groups)]
-    for item in bases:
-        rights.append(item)
-        for dx in range(1, xs):
-            rights.append(swap(item, "row", rows, 2 * dx))
-    lefts = []
-    for dz in range(groups):
-        piece = lax.dynamic_index_in_dim(left, seq ^ dz, 0, False)
-        lefts.append(swap(piece, "seq", groups, dz) if dz > 0 else piece)
-    left_own = jnp.stack(lefts)
-    left_other = swap(left_own, "row", rows, 1)
+    def cross(value):
+        return [value] + [swap(value, "row", rows, 2 * dx) for dx in range(1, xs)]
+
+    if groups == 4:
+        middle = jnp.logical_or(seq == 1, seq == 2)
+        near = swap(base, "seq", groups, 1)
+        inner = lax.ppermute(base, "seq", [(1, 2), (2, 1)])
+        first = cross(base)
+        near_held, _ = lax.optimization_barrier((near, first[-1]))
+        across = lax.ppermute(near, "seq", [(1, 2), (2, 1)])
+        outward = lax.ppermute(inner, "seq", [(1, 0), (2, 3)])
+        second = cross(near_held)
+        farther = lax.ppermute(across, "seq", [(1, 0), (2, 3)])
+        block_a = jnp.where(middle, inner, outward)
+        block_b = jnp.where(middle, across, farther)
+        block_a, _ = lax.optimization_barrier((block_a, second[-1]))
+        third = cross(block_a)
+        block_b, _ = lax.optimization_barrier((block_b, third[-1]))
+        fourth = cross(block_b)
+        rights = first + second + third + fourth
+        swapped = jnp.concatenate([left_own[:2], left_own[3:], left_own[2:3]])
+        left_own = jnp.where(middle, swapped, left_own)
+        swapped = jnp.concatenate([left_other[:2], left_other[3:], left_other[2:3]])
+        left_other = jnp.where(middle, swapped, left_other)
+    else:
+        rights = cross(base)
+        for dz in range(1, groups):
+            rights += cross(swap(base, "seq", groups, dz))
 
     weight = proj_weight.reshape(channels, rows, e1, 2, pair_channels)
     weight = weight.transpose(1, 3, 4, 2, 0)
@@ -182,26 +229,45 @@
         [lax.dynamic_index_in_dim(weight, row ^ m, 0, False) for m in range(rows)], axis=2
     )
     weight = weight.reshape(2 * pair_channels, channels * channels // 2)
+    split = channels * channels // 2 // xs
 
     place = jnp.stack([core, seq]).astype(jnp.int32)
     vmem = pl.BlockSpec(memory_space=pltpu.VMEM)
     smem = pl.BlockSpec(memory_space=pltpu.SMEM)
     bf16 = jnp.bfloat16
     run = half // groups
-    count = 5 + groups * xs
+    params = pltpu.CompilerParams(vmem_limit_bytes=40 * 1024 * 1024)
+    partial = pl.pallas_call(
+        functools.partial(update_kernel, groups, own_rows, seq_total, False),
+        out_shape=jax.ShapeDtypeStruct((own_rows, pair_channels, 2 * half), jnp.float32),
+        in_specs=[vmem] * (3 + groups),
+        out_specs=vmem,
+        scratch_shapes=[pltpu.VMEM((8, split, 2 * half), bf16)],
+        compiler_params=params,
+        name="update_first",
+    )(left_own, left_other, weight[:, :split], *rights[::xs])
+    others = [rights[i] for i in range(groups * xs) if i % xs > 0]
     outs = pl.pallas_call(
-        functools.partial(update_kernel, groups, xs, seq_total),
+        functools.partial(update_kernel, groups, own_rows, seq_total, True),
         out_shape=[jax.ShapeDtypeStruct((own_rows, half, pair_channels), bf16)] * 2
         + [jax.ShapeDtypeStruct((2 * own_rows, run, pair_channels), bf16)] * groups,
-        in_specs=[smem] + [vmem] * (count - 1),
+        in_specs=[vmem] * 2 + [smem] + [vmem] * (3 + len(others)),
         out_specs=[vmem] * (2 + groups),
         scratch_shapes=[
-            pltpu.VMEM((8, channels * channels // 2, 2 * half), bf16),
+            pltpu.VMEM((8, (xs - 1) * split, 2 * half), bf16),
             pltpu.VMEM((2 * own_rows, half, pair_channels), bf16),
         ],
-        compiler_params=pltpu.CompilerParams(vmem_limit_bytes=40 * 1024 * 1024),
-        name="update",
-    )(place, left_own, left_other, *rights, weight, proj_bias.reshape(1, pair_channels))
+        compiler_params=params,
+        name="update_last",
+    )(
+        left_own,
+        left_other,
+        place,
+        proj_bias.reshape(1, pair_channels),
+        partial,
+        weight[:, split:],
+        *others,
+    )
     update_own, update_other = outs[:2]
     update_other = swap(update_other, "row", rows, 1)
 

time: 86.4 us -> 78.5 us (0.909)
  the two profiles are of different devices: /device:TPU:12 before, /device:TPU:10 now
where the time goes in v2:
time: 78.5 us; the launch traced here: 78.2 us
  waiting for transfers between devices  32.7 us (42%)
  starting transfers between devices  27.7 us (35%)
  Pallas kernels  12.2 us (16%)
  local copies, waits for them, and re-layouts  3.99 us (5%)
  other arithmetic  1.14 us (1%)
    ppermute x4, waiting for transfers between devices, on_device(): mirrors.append(lax.ppermute(outs[2 + dz], axes, pairs))  11.3 us
    ppermute x4, starting transfers between devices, on_device(): mirrors.append(lax.ppermute(outs[2 + dz], axes, pairs))  9.62 us
    ppermute x12, starting transfers between devices, swap(): return lax.ppermute(value, name, [(i, i ^ flip) for i in range(size)])  9.2 us
    ppermute x12, waiting for transfers between devices, swap(): return lax.ppermute(value, name, [(i, i ^ flip) for i in range(size)])  8.6 us
    pallas_call x2, Pallas kernels, on_device(): pl.pallas_call(functools.partial(update_kernel, groups, own_rows, seq_tot...  7.46 us
    ppermute x1, waiting for transfers between devices, on_device(): across = lax.ppermute(near, 'seq', [(1, 2), (2, 1)])  5.05 us
    pallas_call x1, Pallas kernels, on_device(): pl.pallas_call(functools.partial(finish_kernel, groups), out_shape=jax.Sh...  4.77 us
    ppermute x1, waiting for transfers between devices, on_device(): inner = lax.ppermute(base, 'seq', [(1, 2), (2, 1)])  4.57 us
  transfers between devices with their start and end apart: 20, of which 11 were waited for; matrix products, arithmetic and copies ran while one was open for 3% of the time, Pallas kernels for 4%

profile of v2, /device:TPU:10, one launch (start us, length us, event | category | flops | bytes accessed | tf_op | source)
XLA Modules:
  0.0 78.2 jit_solution(18218776865890383029)
XLA Ops:
  0.0 1.4 %copy.16 = bf16[64,32,128]{2,1,0:T(8,128)(2,1)S(1)} copy(bf16[64,32,128]{2,0,1:T(8,128)(2,1)} %bitcast.72) | data formatting | bytes 1048576 | tf_op jit(solution)/shard_map/transpose | solution.py:176
  1.5 1.6 %collective-permute-start.2 = (bf16[8,32,128]{2,1,0:T(8,128)(2,1)S(1)}, bf16[8,32,128]{2,1,0:T(8,128)(2,1)S(1)}, u32[]{:S(2)}, u32[]{:S(2)}) collective-permute-start(bf16[8,32,128]{2,1,0:T(8,128)(2,1)S(1)} %get-tuple-element.30), channel_id=1, source_target_pairs={{0,3},{1,2},{2,1},{3,0},{4,7},{5,6},{6,5},{7,4},{8,11},{9,10},{10,... | collective-permute-start | bytes 196616 | tf_op jit(solution)/shard_map/ppermute | solution.py:173
  3.1 1.2 %collective-permute-start.1 = (bf16[8,32,128]{2,1,0:T(8,128)(2,1)S(1)}, bf16[8,32,128]{2,1,0:T(8,128)(2,1)S(1)}, u32[]{:S(2)}, u32[]{:S(2)}) collective-permute-start(bf16[8,32,128]{2,1,0:T(8,128)(2,1)S(1)} %get-tuple-element.31), channel_id=1, source_target_pairs={{0,2},{1,3},{2,0},{3,1},{4,6},{5,7},{6,4},{7,5},{8,10},{9,11},{10,... | collective-permute-start | bytes 196616 | tf_op jit(solution)/shard_map/ppermute | solution.py:173
  4.3 1.2 %collective-permute-start = (bf16[8,32,128]{2,1,0:T(8,128)(2,1)S(1)}, bf16[8,32,128]{2,1,0:T(8,128)(2,1)S(1)}, u32[]{:S(2)}, u32[]{:S(2)}) collective-permute-start(bf16[8,32,128]{2,1,0:T(8,128)(2,1)S(1)} %get-tuple-element.32), channel_id=1, source_target_pairs={{0,1},{1,0},{2,3},{3,2},{4,5},{5,4},{6,7},{7,6},{8,9},{9,8},{10,11... | collective-permute-start | bytes 196616 | tf_op jit(solution)/shard_map/ppermute | solution.py:173
  5.6 0.2 copy.22
  5.9 0.1 copy.25
  6.0 0.1 collective-permute-start.5
  6.1 0.7 copy-done.8
  6.8 0.2 constant_dynamic-slice_fusion.5
  7.0 0.1 copy_bitcast_fusion.1
  7.1 0.1 copy_bitcast_fusion.3
  7.2 0.5 pad_maximum_fusion.2
  7.8 0.1 copy.24
  7.9 0.6 collective-permute-done.2
  8.5 0.6 collective-permute-done.1
  9.1 1.1 %collective-permute-done = bf16[8,32,128]{2,1,0:T(8,128)(2,1)S(1)} collective-permute-done((bf16[8,32,128]{2,1,0:T(8,128)(2,1)S(1)}, bf16[8,32,128]{2,1,0:T(8,128)(2,1)S(1)}, u32[]{:S(2)}, u32[]{:S(2)}) %collective-permute-start) | collective-permute-done | bytes 65568 | tf_op jit(solution)/shard_map/ppermute | solution.py:173
  10.3 1.6 %collective-permute-start.3 = (bf16[4,8,32,128]{3,2,1,0:T(8,128)(2,1)S(1)}, bf16[4,8,32,128]{3,2,1,0:T(8,128)(2,1)S(1)}, u32[]{:S(2)}, u32[]{:S(2)}) collective-permute-start(bf16[4,8,32,128]{3,2,1,0:T(8,128)(2,1)S(1)} %get-tuple-element.41), channel_id=1, source_target_pairs={{0,4},{4,0},{1,5},{5,1},{2,6},{6,2},{3,7},{7,3},{8,12},{12,8},{9,1... | collective-permute-start | bytes 786440 | tf_op jit(solution)/shard_map/ppermute | solution.py:173
  11.9 1.0 %collective-permute-start.6 = (bf16[8,128,128]{2,1,0:T(8,128)(2,1)S(1)}, bf16[8,128,128]{2,1,0:T(8,128)(2,1)S(1)}, u32[]{:S(2)}, u32[]{:S(2)}) collective-permute-start(bf16[8,128,128]{2,1,0:T(8,128)(2,1)S(1)} %pad_maximum_fusion.3.refs_3_), channel_id=1, source_target_pairs={{0,1},{1,0},{2,3},{3,2},{4,5},{5,4},{6,7},{7,6},{8,9},{9,8},{10,11... | collective-permute-start | bytes 786440 | tf_op jit(solution)/shard_map/ppermute | solution.py:173
  12.9 3.7 %collective-permute-start.8 = (bf16[8,128,128]{2,1,0:T(8,128)(2,1)S(1)}, bf16[8,128,128]{2,1,0:T(8,128)(2,1)S(1)}, u32[]{:S(2)}, u32[]{:S(2)}) collective-permute-start(bf16[8,128,128]{2,1,0:T(8,128)(2,1)S(1)} %pad_maximum_fusion.3.refs_3_), channel_id=1, source_target_pairs={{1,2},{2,1},{5,6},{6,5},{9,10},{10,9},{13,14},{14,13},{17,18},{18,... | collective-permute-start | bytes 786440 | tf_op jit(solution)/shard_map/ppermute | solution.py:203
  16.7 0.1 copy.31.refs_2_
  16.8 0.1 copy.32.refs_5_
  16.9 0.1 pad_add_fusion.refs_2_.refs_0_
  17.0 0.5 collective-permute-start.7
  17.5 0.2 fusion.3
  17.7 4.6 %collective-permute-done.8 = bf16[8,128,128]{2,1,0:T(8,128)(2,1)S(1)} collective-permute-done((bf16[8,128,128]{2,1,0:T(8,128)(2,1)S(1)}, bf16[8,128,128]{2,1,0:T(8,128)(2,1)S(1)}, u32[]{:S(2)}, u32[]{:S(2)}) %collective-permute-start.8) | collective-permute-done | bytes 262176 | tf_op jit(solution)/shard_map/ppermute | solution.py:203
  22.3 1.3 %collective-permute-start.9 = (bf16[8,128,128]{2,1,0:T(8,128)(2,1)S(1)}, bf16[8,128,128]{2,1,0:T(8,128)(2,1)S(1)}, u32[]{:S(2)}, u32[]{:S(2)}) collective-permute-start(bf16[8,128,128]{2,1,0:T(8,128)(2,1)S(1)} %collective-permute-done.8), channel_id=1, source_target_pairs={{1,0},{2,3},{5,4},{6,7},{9,8},{10,11},{13,12},{14,15},{17,16},{18,... | collective-permute-start | bytes 786440 | tf_op jit(solution)/shard_map/ppermute | solution.py:207
  23.6 2.6 %collective-permute-start.11 = (bf16[8,128,128]{2,1,0:T(8,128)(2,1)S(1)}, bf16[8,128,128]{2,1,0:T(8,128)(2,1)S(1)}, u32[]{:S(2)}, u32[]{:S(2)}) collective-permute-start(bf16[8,128,128]{2,1,0:T(8,128)(2,1)S(1)} %collective-permute-done.6.refs_4_), channel_id=1, source_target_pairs={{1,2},{2,1},{5,6},{6,5},{9,10},{10,9},{13,14},{14,13},{17,18},{18,... | collective-permute-start | bytes 786440 | tf_op jit(solution)/shard_map/ppermute | solution.py:206
  26.3 0.6 collective-permute-start.10
  27.0 5.0 %collective-permute-done.11 = bf16[8,128,128]{2,1,0:T(8,128)(2,1)S(1)} collective-permute-done((bf16[8,128,128]{2,1,0:T(8,128)(2,1)S(1)}, bf16[8,128,128]{2,1,0:T(8,128)(2,1)S(1)}, u32[]{:S(2)}, u32[]{:S(2)}) %collective-permute-start.11) | collective-permute-done | bytes 262176 | tf_op jit(solution)/shard_map/ppermute | solution.py:206
  32.1 1.3 %collective-permute-start.12 = (bf16[8,128,128]{2,1,0:T(8,128)(2,1)S(1)}, bf16[8,128,128]{2,1,0:T(8,128)(2,1)S(1)}, u32[]{:S(2)}, u32[]{:S(2)}) collective-permute-start(bf16[8,128,128]{2,1,0:T(8,128)(2,1)S(1)} %collective-permute-done.11), channel_id=1, source_target_pairs={{1,0},{2,3},{5,4},{6,7},{9,8},{10,11},{13,12},{14,15},{17,16},{18,... | collective-permute-start | bytes 786440 | tf_op jit(solution)/shard_map/ppermute | solution.py:209
  33.4 0.6 collective-permute-start.13
  34.0 0.1 maximum_select_fusion.refs_0_
  34.1 3.1 %collective-permute-done.12 = bf16[8,128,128]{2,1,0:T(8,128)(2,1)S(1)} collective-permute-done((bf16[8,128,128]{2,1,0:T(8,128)(2,1)S(1)}, bf16[8,128,128]{2,1,0:T(8,128)(2,1)S(1)}, u32[]{:S(2)}, u32[]{:S(2)}) %collective-permute-start.12) | collective-permute-done | bytes 262176 | tf_op jit(solution)/shard_map/ppermute | solution.py:209
  37.3 3.6 %collective-permute-done.13.refs_8_ = bf16[8,128,128]{2,1,0:T(8,128)(2,1)S(1)} collective-permute-done((bf16[8,128,128]{2,1,0:T(8,128)(2,1)S(1)}, bf16[8,128,128]{2,1,0:T(8,128)(2,1)S(1)}, u32[]{:S(2)}, u32[]{:S(2)}) %collective-permute-start.13) | collective-permute-done | bytes 262176 | tf_op jit(solution)/shard_map/ppermute | solution.py:173
  40.9 0.5 collective-permute-start.14
  41.5 0.1 maximum_select_fusion.1.refs_1_
  41.6 3.1 %update_first.1.refs_4_ = f32[16,128,128]{2,1,0:T(8,128)S(1)} custom-call(bf16[4,16,32,128]{3,2,1,0:T(8,128)(2,1)S(1)} %maximum_select_fusion.refs_0_, bf16[4,16,32,128]{3,2,1,0:T(8,128)(2,1)S(1)} %maximum_select_fusion.1.refs_1_, bf16[256,256]{1,0:T(8,128)(2,1)S(1)} %copy.31.refs_2_, bf16[8,128,128]{2,1,0:T(8,128)(2,1)S(1)} %pad_maximum_fusion.3.refs_3_, ...), custom_call_target="tpu_custom_call" | custom-call | tf_op jit(solution)/shard_map/update_first/pallas_call | solution.py:240
  44.7 2.6 %collective-permute-done.14.refs_9_ = bf16[8,128,128]{2,1,0:T(8,128)(2,1)S(1)} collective-permute-done((bf16[8,128,128]{2,1,0:T(8,128)(2,1)S(1)}, bf16[8,128,128]{2,1,0:T(8,128)(2,1)S(1)}, u32[]{:S(2)}, u32[]{:S(2)}) %collective-permute-start.14) | collective-permute-done | bytes 262176 | tf_op jit(solution)/shard_map/ppermute | solution.py:173
  47.3 4.4 %update_last.1 = (bf16[16,64,128]{2,1,0:T(8,128)(2,1)S(1)}, bf16[16,64,128]{2,1,0:T(8,128)(2,1)S(1)}, bf16[32,16,128]{2,1,0:T(8,128)(2,1)S(1)}, bf16[32,16,128]{...) custom-call(bf16[4,16,32,128]{3,2,1,0:T(8,128)(2,1)S(1)} %maximum_select_fusion.refs_0_, ...), custom_call_target="tpu_custom_call" | custom-call | tf_op jit(solution)/shard_map/update_last/pallas_call | solution.py:250
  51.8 1.9 %collective-permute-start.16 = (bf16[32,16,128]{2,1,0:T(8,128)(2,1)S(1)}, bf16[32,16,128]{2,1,0:T(8,128)(2,1)S(1)}, u32[]{:S(2)}, u32[]{:S(2)}) collective-permute-start(bf16[32,16,128]{2,1,0:T(8,128)(2,1)S(1)} %get-tuple-element.19), channel_id=1, source_target_pairs={{0,0},{1,1},{2,2},{3,3},{4,16},{5,17},{6,18},{7,19},{8,8},{9,9},{1... | collective-permute-start | bytes 393224 | tf_op jit(solution)/shard_map/ppermute | solution.py:283
  53.7 1.3 %collective-permute-start.17 = (bf16[32,16,128]{2,1,0:T(8,128)(2,1)S(1)}, bf16[32,16,128]{2,1,0:T(8,128)(2,1)S(1)}, u32[]{:S(2)}, u32[]{:S(2)}) collective-permute-start(bf16[32,16,128]{2,1,0:T(8,128)(2,1)S(1)} %get-tuple-element.20), channel_id=1, source_target_pairs={{0,1},{1,0},{2,3},{3,2},{4,17},{5,16},{6,19},{7,18},{8,9},{9,8},{1... | collective-permute-start | bytes 393224 | tf_op jit(solution)/shard_map/ppermute | solution.py:283
  55.0 3.1 %collective-permute-start.18 = (bf16[32,16,128]{2,1,0:T(8,128)(2,1)S(1)}, bf16[32,16,128]{2,1,0:T(8,128)(2,1)S(1)}, u32[]{:S(2)}, u32[]{:S(2)}) collective-permute-start(bf16[32,16,128]{2,1,0:T(8,128)(2,1)S(1)} %get-tuple-element.21), channel_id=1, source_target_pairs={{0,2},{1,3},{2,0},{3,1},{4,18},{5,19},{6,16},{7,17},{8,10},{9,11},... | collective-permute-start | bytes 393224 | tf_op jit(solution)/shard_map/ppermute | solution.py:283
  58.1 3.3 %collective-permute-start.19 = (bf16[32,16,128]{2,1,0:T(8,128)(2,1)S(1)}, bf16[32,16,128]{2,1,0:T(8,128)(2,1)S(1)}, u32[]{:S(2)}, u32[]{:S(2)}) collective-permute-start(bf16[32,16,128]{2,1,0:T(8,128)(2,1)S(1)} %get-tuple-element.22), channel_id=1, source_target_pairs={{0,3},{1,2},{2,1},{3,0},{4,19},{5,18},{6,17},{7,16},{8,11},{9,10},... | collective-permute-start | bytes 393224 | tf_op jit(solution)/shard_map/ppermute | solution.py:283
  61.4 4.7 %collective-permute-done.16.refs_4_ = bf16[32,16,128]{2,1,0:T(8,128)(2,1)S(1)} collective-permute-done((bf16[32,16,128]{2,1,0:T(8,128)(2,1)S(1)}, bf16[32,16,128]{2,1,0:T(8,128)(2,1)S(1)}, u32[]{:S(2)}, u32[]{:S(2)}) %collective-permute-start.16) | collective-permute-done | bytes 131104 | tf_op jit(solution)/shard_map/ppermute | solution.py:283
  66.1 0.8 collective-permute-done.18.refs_6_
  66.8 5.9 %collective-permute-done.19.refs_7_ = bf16[32,16,128]{2,1,0:T(8,128)(2,1)S(1)} collective-permute-done((bf16[32,16,128]{2,1,0:T(8,128)(2,1)S(1)}, bf16[32,16,128]{2,1,0:T(8,128)(2,1)S(1)}, u32[]{:S(2)}, u32[]{:S(2)}) %collective-permute-start.19) | collective-permute-done | bytes 131104 | tf_op jit(solution)/shard_map/ppermute | solution.py:283
  72.8 0.6 copy-done.3
  73.4 4.8 %finish.1 = bf16[16,128,128]{2,1,0:T(8,128)(2,1)} custom-call(s32[2]{0:T(128)S(1)} %pad_add_fusion.refs_2_.refs_0_, bf16[16,128,128]{2,1,0:T(8,128)(2,1)S(1)} %copy-done, bf16[16,64,128]{2,1,0:T(8,128)(2,1)S(1)} %get-tuple-element.17.refs_2_, bf16[16,64,128]{2,1,0:T(8,128)(2,1)S(1)} %collective-permute-done.15.refs_3_, ...), custom_call_target="tpu_custom_call" | custom-call | tf_op jit(solution)/shard_map/finish/pallas_call | solution.py:285
  (41 shorter events, 0.6 us)
Async XLA Ops:
  1.4 4.2 %copy-start.7 = (bf16[128,8,128]{2,1,0:T(8,128)(2,1)S(1)}, bf16[128,8,128]{2,1,0:T(8,128)(2,1)}, u32[]{:S(2)}) copy-start(bf16[128,8,128]{2,1,0:T(8,128)(2,1)} %param.11) | copy-start | bytes 786436
  1.5 7.1 %collective-permute-start.2 = (bf16[8,32,128]{2,1,0:T(8,128)(2,1)S(1)}, bf16[8,32,128]{2,1,0:T(8,128)(2,1)S(1)}, u32[]{:S(2)}, u32[]{:S(2)}) collective-permute-start(bf16[8,32,128]{2,1,0:T(8,128)(2,1)S(1)} %get-tuple-element.30), channel_id=1, source_target_pairs={{0,3},{1,2},{2,1},{3,0},{4,7},{5,6},{6,5},{7,4},{8,11},{9,10},{10,... | collective-permute-start | bytes 196616 | tf_op jit(solution)/shard_map/ppermute | solution.py:173
  3.1 6.0 %collective-permute-start.1 = (bf16[8,32,128]{2,1,0:T(8,128)(2,1)S(1)}, bf16[8,32,128]{2,1,0:T(8,128)(2,1)S(1)}, u32[]{:S(2)}, u32[]{:S(2)}) collective-permute-start(bf16[8,32,128]{2,1,0:T(8,128)(2,1)S(1)} %get-tuple-element.31), channel_id=1, source_target_pairs={{0,2},{1,3},{2,0},{3,1},{4,6},{5,7},{6,4},{7,5},{8,10},{9,11},{10,... | collective-permute-start | bytes 196616 | tf_op jit(solution)/shard_map/ppermute | solution.py:173
  4.3 5.9 %collective-permute-start = (bf16[8,32,128]{2,1,0:T(8,128)(2,1)S(1)}, bf16[8,32,128]{2,1,0:T(8,128)(2,1)S(1)}, u32[]{:S(2)}, u32[]{:S(2)}) collective-permute-start(bf16[8,32,128]{2,1,0:T(8,128)(2,1)S(1)} %get-tuple-element.32), channel_id=1, source_target_pairs={{0,1},{1,0},{2,3},{3,2},{4,5},{5,4},{6,7},{7,6},{8,9},{9,8},{10,11... | collective-permute-start | bytes 196616 | tf_op jit(solution)/shard_map/ppermute | solution.py:173
  5.9 1.0 %copy-start.8 = (bf16[1024,128]{1,0:T(8,128)(2,1)S(1)}, bf16[1024,128]{1,0:T(8,128)(2,1)}, u32[]{:S(2)}) copy-start(bf16[1024,128]{1,0:T(8,128)(2,1)} %param.12) | copy-start | bytes 786436
  6.0 5.8 %collective-permute-start.5 = (bf16[4,128,128]{2,1,0:T(8,128)(2,1)S(1)}, bf16[4,128,128]{2,1,0:T(8,128)(2,1)S(1)}, u32[]{:S(2)}, u32[]{:S(2)}) collective-permute-start(bf16[4,128,128]{2,1,0:T(8,128)(2,1)S(1)} %bitcast.78), channel_id=1, source_target_pairs={{0,8},{8,0},{16,24},{24,16},{1,9},{9,1},{17,25},{25,17},{2,10},{10... | collective-permute-start | bytes 393224 | tf_op jit(solution)/shard_map/ppermute | solution.py:173
  10.3 7.2 %collective-permute-start.3 = (bf16[4,8,32,128]{3,2,1,0:T(8,128)(2,1)S(1)}, bf16[4,8,32,128]{3,2,1,0:T(8,128)(2,1)S(1)}, u32[]{:S(2)}, u32[]{:S(2)}) collective-permute-start(bf16[4,8,32,128]{3,2,1,0:T(8,128)(2,1)S(1)} %get-tuple-element.41), channel_id=1, source_target_pairs={{0,4},{4,0},{1,5},{5,1},{2,6},{6,2},{3,7},{7,3},{8,12},{12,8},{9,1... | collective-permute-start | bytes 786440 | tf_op jit(solution)/shard_map/ppermute | solution.py:173
  11.9 11.7 %collective-permute-start.6 = (bf16[8,128,128]{2,1,0:T(8,128)(2,1)S(1)}, bf16[8,128,128]{2,1,0:T(8,128)(2,1)S(1)}, u32[]{:S(2)}, u32[]{:S(2)}) collective-permute-start(bf16[8,128,128]{2,1,0:T(8,128)(2,1)S(1)} %pad_maximum_fusion.3.refs_3_), channel_id=1, source_target_pairs={{0,1},{1,0},{2,3},{3,2},{4,5},{5,4},{6,7},{7,6},{8,9},{9,8},{10,11... | collective-permute-start | bytes 786440 | tf_op jit(solution)/shard_map/ppermute | solution.py:173
  12.9 9.4 %collective-permute-start.8 = (bf16[8,128,128]{2,1,0:T(8,128)(2,1)S(1)}, bf16[8,128,128]{2,1,0:T(8,128)(2,1)S(1)}, u32[]{:S(2)}, u32[]{:S(2)}) collective-permute-start(bf16[8,128,128]{2,1,0:T(8,128)(2,1)S(1)} %pad_maximum_fusion.3.refs_3_), channel_id=1, source_target_pairs={{1,2},{2,1},{5,6},{6,5},{9,10},{10,9},{13,14},{14,13},{17,18},{18,... | collective-permute-start | bytes 786440 | tf_op jit(solution)/shard_map/ppermute | solution.py:203
  17.0 9.3 %collective-permute-start.7 = (bf16[8,128,128]{2,1,0:T(8,128)(2,1)S(1)}, bf16[8,128,128]{2,1,0:T(8,128)(2,1)S(1)}, u32[]{:S(2)}, u32[]{:S(2)}) collective-permute-start(bf16[8,128,128]{2,1,0:T(8,128)(2,1)S(1)} %pad_maximum_fusion.3.refs_3_), channel_id=1, source_target_pairs={{0,16},{8,24},{16,0},{24,8},{1,17},{9,25},{17,1},{25,9},{2,18},{10... | collective-permute-start | bytes 786440 | tf_op jit(solution)/shard_map/ppermute | solution.py:173
  22.3 11.1 %collective-permute-start.9 = (bf16[8,128,128]{2,1,0:T(8,128)(2,1)S(1)}, bf16[8,128,128]{2,1,0:T(8,128)(2,1)S(1)}, u32[]{:S(2)}, u32[]{:S(2)}) collective-permute-start(bf16[8,128,128]{2,1,0:T(8,128)(2,1)S(1)} %collective-permute-done.8), channel_id=1, source_target_pairs={{1,0},{2,3},{5,4},{6,7},{9,8},{10,11},{13,12},{14,15},{17,16},{18,... | collective-permute-start | bytes 786440 | tf_op jit(solution)/shard_map/ppermute | solution.py:207
  23.6 8.5 %collective-permute-start.11 = (bf16[8,128,128]{2,1,0:T(8,128)(2,1)S(1)}, bf16[8,128,128]{2,1,0:T(8,128)(2,1)S(1)}, u32[]{:S(2)}, u32[]{:S(2)}) collective-permute-start(bf16[8,128,128]{2,1,0:T(8,128)(2,1)S(1)} %collective-permute-done.6.refs_4_), channel_id=1, source_target_pairs={{1,2},{2,1},{5,6},{6,5},{9,10},{10,9},{13,14},{14,13},{17,18},{18,... | collective-permute-start | bytes 786440 | tf_op jit(solution)/shard_map/ppermute | solution.py:206
  26.3 7.1 %collective-permute-start.10 = (bf16[8,128,128]{2,1,0:T(8,128)(2,1)S(1)}, bf16[8,128,128]{2,1,0:T(8,128)(2,1)S(1)}, u32[]{:S(2)}, u32[]{:S(2)}) collective-permute-start(bf16[8,128,128]{2,1,0:T(8,128)(2,1)S(1)} %collective-permute-done.6.refs_4_), channel_id=1, source_target_pairs={{0,16},{8,24},{16,0},{24,8},{1,17},{9,25},{17,1},{25,9},{2,18},{10... | collective-permute-start | bytes 786440 | tf_op jit(solution)/shard_map/ppermute | solution.py:173
  27.0 14.5 %collective-permute-start.4 = (bf16[4,16,32,128]{3,2,1,0:T(8,128)(2,1)S(1)}, bf16[4,16,32,128]{3,2,1,0:T(8,128)(2,1)S(1)}, u32[]{:S(2)}, u32[]{:S(2)}) collective-permute-start(bf16[4,16,32,128]{3,2,1,0:T(8,128)(2,1)S(1)} %bitcast.64), channel_id=1, source_target_pairs={{0,8},{8,0},{16,24},{24,16},{1,9},{9,1},{17,25},{25,17},{2,10},{10... | collective-permute-start | bytes 1572872 | tf_op jit(solution)/shard_map/ppermute | solution.py:173
  32.1 5.2 %collective-permute-start.12 = (bf16[8,128,128]{2,1,0:T(8,128)(2,1)S(1)}, bf16[8,128,128]{2,1,0:T(8,128)(2,1)S(1)}, u32[]{:S(2)}, u32[]{:S(2)}) collective-permute-start(bf16[8,128,128]{2,1,0:T(8,128)(2,1)S(1)} %collective-permute-done.11), channel_id=1, source_target_pairs={{1,0},{2,3},{5,4},{6,7},{9,8},{10,11},{13,12},{14,15},{17,16},{18,... | collective-permute-start | bytes 786440 | tf_op jit(solution)/shard_map/ppermute | solution.py:209
  33.4 7.5 %collective-permute-start.13 = (bf16[8,128,128]{2,1,0:T(8,128)(2,1)S(1)}, bf16[8,128,128]{2,1,0:T(8,128)(2,1)S(1)}, u32[]{:S(2)}, u32[]{:S(2)}) collective-permute-start(bf16[8,128,128]{2,1,0:T(8,128)(2,1)S(1)} %broadcast_select_fusion.1.refs_5_), channel_id=1, source_target_pairs={{0,16},{8,24},{16,0},{24,8},{1,17},{9,25},{17,1},{25,9},{2,18},{10... | collective-permute-start | bytes 786440 | tf_op jit(solution)/shard_map/ppermute | solution.py:173
  40.9 6.4 %collective-permute-start.14 = (bf16[8,128,128]{2,1,0:T(8,128)(2,1)S(1)}, bf16[8,128,128]{2,1,0:T(8,128)(2,1)S(1)}, u32[]{:S(2)}, u32[]{:S(2)}) collective-permute-start(bf16[8,128,128]{2,1,0:T(8,128)(2,1)S(1)} %broadcast_select_fusion.refs_6_), channel_id=1, source_target_pairs={{0,16},{8,24},{16,0},{24,8},{1,17},{9,25},{17,1},{25,9},{2,18},{10... | collective-permute-start | bytes 786440 | tf_op jit(solution)/shard_map/ppermute | solution.py:173
  44.7 2.6 %copy-start.4 = (f32[128]{0:T(128)S(1)}, f32[128]{0:T(128)}, u32[]{:S(2)}) copy-start(f32[128]{0:T(128)} %param.13) | copy-start | bytes 1540
  47.3 25.4 %copy-start = (bf16[16,128,128]{2,1,0:T(8,128)(2,1)S(1)}, bf16[16,128,128]{2,1,0:T(8,128)(2,1)}, u32[]{:S(2)}) copy-start(bf16[16,128,128]{2,1,0:T(8,128)(2,1)} %refs_1_.1) | copy-start | bytes 1572868
  47.3 25.5 %copy-start.1 = (bf16[128,512]{1,0:T(8,128)(2,1)S(1)}, bf16[128,512]{1,0:T(8,128)(2,1)}, u32[]{:S(2)}) copy-start(bf16[128,512]{1,0:T(8,128)(2,1)} %refs_9_.1) | copy-start | bytes 393220
  47.3 25.5 %copy-start.2 = (bf16[512,128]{1,0:T(8,128)(2,1)S(1)}, bf16[512,128]{1,0:T(8,128)(2,1)}, u32[]{:S(2)}) copy-start(bf16[512,128]{1,0:T(8,128)(2,1)} %refs_11_.1) | copy-start | bytes 393220
  51.7 21.0 %collective-permute-start.15 = (bf16[16,64,128]{2,1,0:T(8,128)(2,1)S(1)}, bf16[16,64,128]{2,1,0:T(8,128)(2,1)S(1)}, u32[]{:S(2)}, u32[]{:S(2)}) collective-permute-start(bf16[16,64,128]{2,1,0:T(8,128)(2,1)S(1)} %get-tuple-element.18), channel_id=1, source_target_pairs={{0,8},{8,0},{16,24},{24,16},{1,9},{9,1},{17,25},{25,17},{2,10},{10... | collective-permute-start | bytes 786440 | tf_op jit(solution)/shard_map/ppermute | solution.py:173
  51.8 14.3 %collective-permute-start.16 = (bf16[32,16,128]{2,1,0:T(8,128)(2,1)S(1)}, bf16[32,16,128]{2,1,0:T(8,128)(2,1)S(1)}, u32[]{:S(2)}, u32[]{:S(2)}) collective-permute-start(bf16[32,16,128]{2,1,0:T(8,128)(2,1)S(1)} %get-tuple-element.19), channel_id=1, source_target_pairs={{0,0},{1,1},{2,2},{3,3},{4,16},{5,17},{6,18},{7,19},{8,8},{9,9},{1... | collective-permute-start | bytes 393224 | tf_op jit(solution)/shard_map/ppermute | solution.py:283
  53.7 12.4 %collective-permute-start.17 = (bf16[32,16,128]{2,1,0:T(8,128)(2,1)S(1)}, bf16[32,16,128]{2,1,0:T(8,128)(2,1)S(1)}, u32[]{:S(2)}, u32[]{:S(2)}) collective-permute-start(bf16[32,16,128]{2,1,0:T(8,128)(2,1)S(1)} %get-tuple-element.20), channel_id=1, source_target_pairs={{0,1},{1,0},{2,3},{3,2},{4,17},{5,16},{6,19},{7,18},{8,9},{9,8},{1... | collective-permute-start | bytes 393224 | tf_op jit(solution)/shard_map/ppermute | solution.py:283
  55.0 11.8 %collective-permute-start.18 = (bf16[32,16,128]{2,1,0:T(8,128)(2,1)S(1)}, bf16[32,16,128]{2,1,0:T(8,128)(2,1)S(1)}, u32[]{:S(2)}, u32[]{:S(2)}) collective-permute-start(bf16[32,16,128]{2,1,0:T(8,128)(2,1)S(1)} %get-tuple-element.21), channel_id=1, source_target_pairs={{0,2},{1,3},{2,0},{3,1},{4,18},{5,19},{6,16},{7,17},{8,10},{9,11},... | collective-permute-start | bytes 393224 | tf_op jit(solution)/shard_map/ppermute | solution.py:283
  58.1 14.6 %collective-permute-start.19 = (bf16[32,16,128]{2,1,0:T(8,128)(2,1)S(1)}, bf16[32,16,128]{2,1,0:T(8,128)(2,1)S(1)}, u32[]{:S(2)}, u32[]{:S(2)}) collective-permute-start(bf16[32,16,128]{2,1,0:T(8,128)(2,1)S(1)} %get-tuple-element.22), channel_id=1, source_target_pairs={{0,3},{1,2},{2,1},{3,0},{4,19},{5,18},{6,17},{7,16},{8,11},{9,10},... | collective-permute-start | bytes 393224 | tf_op jit(solution)/shard_map/ppermute | solution.py:283
  72.7 0.7 copy-start.3
  72.7 0.7 copy-start.5
  72.7 0.7 copy-start.6

commit v3 on v0

v3 whole, which is shorter than its diff:
```python
import functools

import jax
import jax.numpy as jnp
from jax import lax
from jax.experimental import pallas as pl
from jax.experimental.pallas import tpu as pltpu
from jax.sharding import PartitionSpec as P

epsilon = 1e-05
axes = ("row", "col", "seq")


def update_kernel(groups, shares, low, last, scale, *refs):
    refs = list(refs)
    place_ref = refs.pop(0)
    left_refs = [refs.pop(0) for _ in range(groups * shares)]
    bias_ref, partial_ref = (refs.pop(0), refs.pop(0)) if last else (None, None)
    weight_ref = refs.pop(0)
    update_ref = refs.pop() if last else None
    outer_ref = refs.pop()
    lhs_ref = refs.pop()
    outs = 2 + 2 * low if last else 1
    right_refs, out_refs = refs[:-outs], refs[-outs:]
    share, channels, group_len = left_refs[0].shape
    per, _, lanes = right_refs[0].shape
    sources = len(right_refs) // groups
    half = lanes // 2
    pair_channels = weight_ref.shape[0] // 2
    block = 8
    row_count = share * shares
    lane_low = lax.broadcasted_iota(jnp.int32, (pair_channels, lanes), 1) < half
    for dy in range(shares):
        begin = pl.multiple_of((place_ref[2] ^ dy) * share * channels, share * channels)
        for dz in range(groups):
            lhs_ref[pl.ds(begin, share * channels), dz * group_len : (dz + 1) * group_len] = (
                left_refs[dz * shares + dy][...].reshape(share * channels, group_len)
            )

    def right_tile(item):
        source, rest = divmod(item, per)
        return jnp.concatenate(
            [right_refs[dz * sources + source][rest] for dz in range(groups)], axis=0
        )

    @pl.loop(0, row_count // block)
    def _(step):
        start = step * block
        left = lhs_ref[pl.ds(start * channels, block * channels)]
        for pair in range(sources * per // 2):
            right = jnp.concatenate([right_tile(2 * pair), right_tile(2 * pair + 1)], axis=1)
            outer = jnp.dot(left, right, preferred_element_type=jnp.float32)
            outer = outer.astype(jnp.bfloat16)
            for part in range(2):
                item = 2 * pair + part
                outer_ref[:, item * channels : (item + 1) * channels, :] = outer[
                    :, part * lanes : (part + 1) * lanes
                ].reshape(block, channels, lanes)
        for two in range(block // 2):
            both = jnp.concatenate([outer_ref[2 * two], outer_ref[2 * two + 1]], axis=1)
            proj = jnp.dot(weight_ref[...], both, preferred_element_type=jnp.float32)
            a0 = proj[:pair_channels, :lanes]
            a1 = proj[:pair_channels, lanes:]
            b0 = proj[pair_channels:, :lanes]
            b1 = proj[pair_channels:, lanes:]
            cell = jnp.where(lane_low, a0, b1) + pltpu.roll(
                jnp.where(lane_low, a1, b0), half, 1
            )
            index = start // 2 + two
            if last:
                cell = (cell + partial_ref[index]) * scale + bias_ref[...]
                update_ref[pl.ds(2 * index, 2)] = (
                    cell.astype(jnp.bfloat16).T.reshape(2, half, pair_channels)
                )
            else:
                out_refs[0][index] = cell

    if last:
        core, z_low, z_high = place_ref[0], place_ref[1], place_ref[3]
        run = row_count // 2
        out_refs[0][...] = update_ref[pl.ds(z_high * run, run)]
        out_refs[1][...] = update_ref[pl.ds((1 - z_high) * run, run)]
        for flip in range(2):
            for dz in range(low):
                begin = (core ^ flip) * (half // 2) + (z_low ^ dz) * run
                out_refs[2 + flip * low + dz][...] = update_ref[
                    :, pl.ds(pl.multiple_of(begin, run), run), :
                ]


def finish_kernel(low, *refs):
    place_ref, pair_ref, own_ref, other_ref = refs[:4]
    mirror_refs = refs[4 : 4 + 2 * low]
    gain_ref, up_ref, up_bias_ref, down_ref, down_bias_ref, out_ref = refs[4 + 2 * low :]
    run, columns, pair_channels = pair_ref.shape
    half = columns // 2
    core, z_low, z_high = place_ref[0], place_ref[1], place_ref[3]
    cells = run * run
    to = lax.broadcasted_iota(jnp.int32, (cells, cells), 0)
    of = lax.broadcasted_iota(jnp.int32, (cells, cells), 1)
    swap_cells = jnp.where(
        jnp.logical_and(to // run == of % run, to % run == of // run), 1.0, 0.0
    ).astype(jnp.bfloat16)
    ones = jnp.full((2 * pair_channels, pair_channels), 1.0 / pair_channels, jnp.bfloat16)
    for dz in range(low):
        for flip in range(2):
            for part in range(2):
                local = (core ^ flip) * (half // 2) + (z_low ^ dz) * run
                local = pl.multiple_of(local, run)
                begin = (core ^ flip) * half + (part * low + (z_low ^ dz)) * run
                begin = pl.multiple_of(begin, run)
                piece = mirror_refs[flip * low + dz][part * run : (part + 1) * run]
                mirrored = jnp.dot(
                    swap_cells,
                    piece.reshape(cells, pair_channels),
                    preferred_element_type=jnp.float32,
                )
                direct = jnp.where(
                    z_high == part,
                    own_ref[:, pl.ds(local, run), :],
                    other_ref[:, pl.ds(local, run), :],
                ).reshape(cells, pair_channels)
                residual = pair_ref[:, pl.ds(begin, run), :].reshape(cells, pair_channels)
                middle = (
                    residual.astype(jnp.float32) + 0.5 * (direct.astype(jnp.float32) + mirrored)
                ).astype(jnp.bfloat16)
                values = middle.astype(jnp.float32)
                center = jnp.dot(
                    middle, ones[:pair_channels], preferred_element_type=jnp.float32
                )
                moved = values - center
                square = jnp.square(moved)
                high = square.astype(jnp.bfloat16)
                rest = (square - high.astype(jnp.float32)).astype(jnp.bfloat16)
                spread = jnp.dot(
                    jnp.concatenate([high, rest], axis=1),
                    ones,
                    preferred_element_type=jnp.float32,
                )
                normed = moved * lax.rsqrt(spread + epsilon) * gain_ref[...]
                hidden = jnp.dot(
                    normed.astype(jnp.bfloat16), up_ref[...], preferred_element_type=jnp.float32
                )
                hidden = jnp.maximum(hidden + up_bias_ref[...], 0.0).astype(jnp.bfloat16)
                result = (
                    values
                    + jnp.dot(hidden, down_ref[...], preferred_element_type=jnp.float32)
                    + down_bias_ref[...]
                )
                out_ref[:, pl.ds(begin, run), :] = result.astype(jnp.bfloat16).reshape(
                    run, run, pair_channels
                )


def on_device(
    left_piece,
    right_piece,
    proj_weight,
    proj_bias,
    pair_rep,
    norm_gain,
    up_weight,
    up_bias,
    down_weight,
    down_bias,
):
    rows = lax.axis_size("row")
    cols = lax.axis_size("col")
    groups = lax.axis_size("seq")
    xs = rows // 2
    low = groups // 2
    row, col, seq = (lax.axis_index(name) for name in axes)
    core, z_low, z_high = row % 2, seq % low, seq // low
    run, columns, pair_channels = pair_rep.shape
    group_len, channels, _ = left_piece.shape
    e1 = right_piece.shape[1] // 2
    half = columns // 2
    bf16 = jnp.bfloat16

    def pick(value, index, axis=0):
        return lax.dynamic_index_in_dim(value, index, axis, False)

    def swap(value, name, size, flip):
        return lax.ppermute(value, name, [(i, i ^ flip) for i in range(size)])

    right = right_piece.reshape(group_len, e1, 2, 2, 2, half // 2).transpose(4, 1, 0, 2, 3, 5)
    right = right.reshape(2, e1, group_len, 2 * half)
    mine = pick(right, z_high)
    theirs = pick(right, 1 - z_high)
    blocks = [mine]
    for dz in range(1, groups):
        blocks.append(swap(theirs if dz >= low else mine, "seq", groups, dz))
    firsts, others = [], []
    chain = None
    for block in blocks:
        firsts += [block, swap(block, "row", rows, 1)]
        for dx in range(1, xs):
            if chain is not None:
                block, _ = lax.optimization_barrier((block, chain))
            chain = swap(block, "row", rows, 2 * dx)
            others += [chain, swap(chain, "row", rows, 1)]

    share = 2 * run // cols
    left_piece, _ = lax.optimization_barrier((left_piece, mine))
    left = left_piece.transpose(2, 1, 0).reshape(2, low, run, channels, group_len)
    left = left.transpose(1, 0, 2, 3, 4).reshape(low, cols, share, channels, group_len)
    left = pick(left, col, 1)
    lefts = []
    for dz in range(groups):
        piece = pick(left, z_low ^ (dz % low))
        piece = swap(piece, "seq", groups, dz) if dz > 0 else piece
        lefts += [piece] + [swap(piece, "col", cols, dy) for dy in range(1, cols)]

    weight = proj_weight.reshape(channels, rows, e1, 2, pair_channels)
    weight = weight.transpose(1, 3, 4, 2, 0)
    weight = jnp.stack([pick(weight, row ^ m) for m in range(rows)], axis=2)
    weight = weight.reshape(2 * pair_channels, channels * channels // 2)
    split = channels * channels // 2 // xs

    place = jnp.stack([core, z_low, col, z_high]).astype(jnp.int32)
    vmem = pl.BlockSpec(memory_space=pltpu.VMEM)
    smem = pl.BlockSpec(memory_space=pltpu.SMEM)
    params = pltpu.CompilerParams(vmem_limit_bytes=40 * 1024 * 1024)
    scale = 1.0 / (group_len * groups)
    lhs = pltpu.VMEM((2 * run * channels, groups * group_len), bf16)
    partial = pl.pallas_call(
        functools.partial(update_kernel, groups, cols, low, False, scale),
        out_shape=jax.ShapeDtypeStruct((run, pair_channels, 2 * half), jnp.float32),
        in_specs=[smem] + [vmem] * (len(lefts) + 1 + len(firsts)),
        out_specs=vmem,
        scratch_shapes=[lhs, pltpu.VMEM((8, split, 2 * half), bf16)],
        compiler_params=params,
        name="update_first",
    )(place, *lefts, weight[:, :split], *firsts)
    bias = jnp.broadcast_to(proj_bias[:, None], (pair_channels, 2 * half))
    outs = pl.pallas_call(
        functools.partial(update_kernel, groups, cols, low, True, scale),
        out_shape=[jax.ShapeDtypeStruct((run, half, pair_channels), bf16)] * 2
        + [jax.ShapeDtypeStruct((2 * run, run, pair_channels), bf16)] * (2 * low),
        in_specs=[smem] + [vmem] * (len(lefts) + 3 + len(others)),
        out_specs=[vmem] * (2 + 2 * low),
        scratch_shapes=[
            lhs,
            pltpu.VMEM((8, (xs - 1) * split, 2 * half), bf16),
            pltpu.VMEM((2 * run, half, pair_channels), bf16),
        ],
        compiler_params=params,
        name="update_last",
    )(place, *lefts, bias, partial, weight[:, split:], *others)

    mirrors = []
    for flip in range(2):
        for dz in range(low):
            pairs = []
            for r in range(rows):
                for c in range(cols):
                    for q in range(groups):
                        source = (r * cols + c) * groups + q
                        target = 2 * c + (r % 2 ^ flip)
                        target = (target * cols + r // 2) * groups + (q ^ dz)
                        pairs.append((source, target))
            mirrors.append(lax.ppermute(outs[2 + flip * low + dz], axes, pairs))
    update_other = swap(outs[1], "seq", groups, low)

    return pl.pallas_call(
        functools.partial(finish_kernel, low),
        out_shape=jax.ShapeDtypeStruct(pair_rep.shape, bf16),
        in_specs=[smem] + [vmem] * (8 + 2 * low),
        out_specs=vmem,
        compiler_params=params,
        name="finish",
    )(
        place,
        pair_rep,
        outs[0],
        update_other,
        *mirrors,
        norm_gain.reshape(1, -1),
        up_weight,
        up_bias.reshape(1, -1),
        down_weight,
        down_bias.reshape(1, -1),
    )


def solution(mesh):
    in_specs = (
        P("seq", None, "row"),
        P("seq", "row", "col"),
        P(),
        P(),
        P(("row", "seq"), "col", None),
        P(),
        P(),
        P(),
        P(),
        P(),
    )
    out_specs = P(("row", "seq"), "col", None)
    return jax.shard_map(
        on_device, mesh=mesh, in_specs=in_specs, out_specs=out_specs, check_vma=False
    )
```

time: 158 us -> 74.4 us (0.47); the launches traced: 155 us -> 74.1 us
  blocking collectives: 42 us -> 0 us
  waiting for transfers between devices: 60.8 us -> 22.7 us
  starting transfers between devices: 3.51 us -> 33.4 us
  matrix products: 21.8 us -> 0 us
  Pallas kernels: 0 us -> 14.2 us
  between operations: 13.6 us -> 0.33 us
  local copies, waits for them, and re-layouts: 9.86 us -> 2.95 us
  other arithmetic: 3.76 us -> 0.55 us
    all_gather x2 -> x0, waiting for transfers between devices: 46.1 us -> none  [the longest x1 30.7 us: on_device(): right_seq = lax.all_gather(right_piece, 'seq', axis=0, tiled=True)]
    all_to_all x3 -> x0, blocking collectives: 42 us -> none  [the longest x1 21.6 us: on_device(): lax.all_to_all(section_one.reshape(run_len, rowseq_count, own_rows, chann...]
    ppermute x0 -> x27, starting transfers between devices: none -> 33.4 us  [the longest x23 23.5 us: swap(): return lax.ppermute(value, name, [(i, i ^ flip) for i in range(size)])]
    ppermute x0 -> x27, waiting for transfers between devices: none -> 22.7 us  [the longest x23 13 us: swap(): return lax.ppermute(value, name, [(i, i ^ flip) for i in range(size)])]
    dot_general x17 -> x0, matrix products: 21.8 us -> none  [the longest x8 10.3 us: project_block(): lax.dot_general(left_mat, right_mat, (((0,), (0,)), ((), ())), preferred_...]
    pallas_call x0 -> x3, Pallas kernels: none -> 14.2 us  [the longest x1 6.24 us: on_device(): pl.pallas_call(functools.partial(finish_kernel, low), out_shape=jax.Shape...]
    all_to_all x1 -> x0, waiting for transfers between devices: 14 us -> none  [on_device(): lax.all_to_all(split_left, 'seq', split_axis=2, concat_axis=0, tiled=True)]
    slice x1, local copies, waits for them, and re-layouts: 3.97 us -> 0.02 us  [on_device(): weight[:, split:]]
  transfers between devices with their start and end apart: 3 -> 27, of which waited for: 3 -> 10; matrix products, arithmetic and copies ran while one was open for 2% -> 2% of each run, Pallas kernels for 0% -> 5%
where the time goes in v3:
time: 74.4 us; the launch traced here: 74.1 us
  starting transfers between devices  33.4 us (45%)
  waiting for transfers between devices  22.7 us (31%)
  Pallas kernels  14.2 us (19%)
  local copies, waits for them, and re-layouts  2.95 us (4%)
    ppermute x23, starting transfers between devices, swap(): return lax.ppermute(value, name, [(i, i ^ flip) for i in range(size)])  23.5 us
    ppermute x23, waiting for transfers between devices, swap(): return lax.ppermute(value, name, [(i, i ^ flip) for i in range(size)])  13 us
    ppermute x4, starting transfers between devices, on_device(): mirrors.append(lax.ppermute(outs[2 + flip * low + dz], axes, pairs))  9.84 us
    ppermute x4, waiting for transfers between devices, on_device(): mirrors.append(lax.ppermute(outs[2 + flip * low + dz], axes, pairs))  9.67 us
    pallas_call x1, Pallas kernels, on_device(): pl.pallas_call(functools.partial(finish_kernel, low), out_shape=jax.Shape...  6.24 us
    pallas_call x1, Pallas kernels, on_device(): pl.pallas_call(functools.partial(update_kernel, groups, cols, low, True,...  4.17 us
    pallas_call x1, Pallas kernels, on_device(): pl.pallas_call(functools.partial(update_kernel, groups, cols, low, False,...  3.8 us
    unnamed x24, local copies, waits for them, and re-layouts  2.14 us
  transfers between devices with their start and end apart: 27, of which 10 were waited for; matrix products, arithmetic and copies ran while one was open for 2% of the time, Pallas kernels for 5%

profile of v3, /device:TPU:3, one launch (start us, length us, event | category | flops | bytes accessed | tf_op | source)
XLA Modules:
  0.0 74.1 jit_solution(8424729086398639036)
XLA Ops:
  0.0 1.1 %copy.18 = bf16[128,8,128]{0,2,1:T(8,128)(2,1)S(1)} copy(bf16[128,8,128]{2,1,0:T(8,128)(2,1)} %param.11) | data formatting | bytes 524288 | tf_op args[1]
  1.2 0.1 copy.20
  1.4 1.4 %collective-permute-start.8 = (bf16[4,128,128]{2,1,0:T(8,128)(2,1)S(1)}, bf16[4,128,128]{2,1,0:T(8,128)(2,1)S(1)}, u32[]{:S(2)}, u32[]{:S(2)}) collective-permute-start(bf16[4,128,128]{2,1,0:T(8,128)(2,1)S(1)} %bitcast.50), channel_id=1, source_target_pairs={{0,1},{1,0},{2,3},{3,2},{4,5},{5,4},{6,7},{7,6},{8,9},{9,8},{10,11... | collective-permute-start | bytes 393224 | tf_op jit(solution)/shard_map/ppermute | solution.py:184
  2.7 0.3 collective-permute-start.14
  3.0 0.1 copy.28
  3.1 2.4 %collective-permute-start.10 = (bf16[4,128,128]{2,1,0:T(8,128)(2,1)S(1)}, bf16[4,128,128]{2,1,0:T(8,128)(2,1)S(1)}, u32[]{:S(2)}, u32[]{:S(2)}) collective-permute-start(bf16[4,128,128]{2,1,0:T(8,128)(2,1)S(1)} %bitcast.63), channel_id=1, source_target_pairs={{0,2},{1,3},{2,0},{3,1},{4,6},{5,7},{6,4},{7,5},{8,10},{9,11},{10,... | collective-permute-start | bytes 393224 | tf_op jit(solution)/shard_map/ppermute | solution.py:184
  5.5 0.3 collective-permute-done.8.refs_12_
  5.8 1.0 %collective-permute-done.14.refs_12_ = bf16[4,128,128]{2,1,0:T(8,128)(2,1)S(1)} collective-permute-done((bf16[4,128,128]{2,1,0:T(8,128)(2,1)S(1)}, bf16[4,128,128]{2,1,0:T(8,128)(2,1)S(1)}, u32[]{:S(2)}, u32[]{:S(2)}) %collective-permute-start.14) | collective-permute-done | bytes 131104 | tf_op jit(solution)/shard_map/ppermute | solution.py:184
  6.8 0.2 collective-permute-start.16
  7.0 3.2 %collective-permute-start.12 = (bf16[4,128,128]{2,1,0:T(8,128)(2,1)S(1)}, bf16[4,128,128]{2,1,0:T(8,128)(2,1)S(1)}, u32[]{:S(2)}, u32[]{:S(2)}) collective-permute-start(bf16[4,128,128]{2,1,0:T(8,128)(2,1)S(1)} %bitcast.64), channel_id=1, source_target_pairs={{0,3},{1,2},{2,1},{3,0},{4,7},{5,6},{6,5},{7,4},{8,11},{9,10},{10,... | collective-permute-start | bytes 393224 | tf_op jit(solution)/shard_map/ppermute | solution.py:184
  10.3 0.1 collective-permute-start.1
  10.4 0.5 collective-permute-done.16.refs_14_
  11.0 1.7 %collective-permute-start.18 = (bf16[4,128,128]{2,1,0:T(8,128)(2,1)S(1)}, bf16[4,128,128]{2,1,0:T(8,128)(2,1)S(1)}, u32[]{:S(2)}, u32[]{:S(2)}) collective-permute-start(bf16[4,128,128]{2,1,0:T(8,128)(2,1)S(1)} %collective-permute-done.10.refs_14_), channel_id=1, source_target_pairs={{0,16},{8,24},{16,0},{24,8},{1,17},{9,25},{17,1},{25,9},{2,18},{10... | collective-permute-start | bytes 393224 | tf_op jit(solution)/shard_map/ppermute | solution.py:184
  12.7 2.1 %collective-permute-start.5 = (bf16[16,32,128]{2,1,0:T(8,128)(2,1)S(1)}, bf16[16,32,128]{2,1,0:T(8,128)(2,1)S(1)}, u32[]{:S(2)}, u32[]{:S(2)}) collective-permute-start(bf16[16,32,128]{2,1,0:T(8,128)(2,1)S(1)} %bitcast.66), channel_id=1, source_target_pairs={{0,3},{1,2},{2,1},{3,0},{4,7},{5,6},{6,5},{7,4},{8,11},{9,10},{10,... | collective-permute-start | bytes 393224 | tf_op jit(solution)/shard_map/ppermute | solution.py:184
  14.8 0.1 collective-permute-start.3
  14.9 0.2 constant_dynamic-slice_fusion.4
  15.1 2.0 %collective-permute-done.1.refs_3_ = bf16[16,32,128]{2,1,0:T(8,128)(2,1)S(1)} collective-permute-done((bf16[16,32,128]{2,1,0:T(8,128)(2,1)S(1)}, bf16[16,32,128]{2,1,0:T(8,128)(2,1)S(1)}, u32[]{:S(2)}, u32[]{:S(2)}) %collective-permute-start.1) | collective-permute-done | bytes 131104 | tf_op jit(solution)/shard_map/ppermute | solution.py:184
  17.1 1.2 %collective-permute-start = (bf16[16,32,128]{2,1,0:T(8,128)(2,1)S(1)}, bf16[16,32,128]{2,1,0:T(8,128)(2,1)S(1)}, u32[]{:S(2)}, u32[]{:S(2)}) collective-permute-start(bf16[16,32,128]{2,1,0:T(8,128)(2,1)S(1)} %bitcast.47), channel_id=1, source_target_pairs={{0,4},{4,0},{1,5},{5,1},{2,6},{6,2},{3,7},{7,3},{8,12},{12,8},{9,1... | collective-permute-start | bytes 393224 | tf_op jit(solution)/shard_map/ppermute | solution.py:184
  18.3 3.1 %collective-permute-start.7 = (bf16[4,128,128]{2,1,0:T(8,128)(2,1)S(1)}, bf16[4,128,128]{2,1,0:T(8,128)(2,1)S(1)}, u32[]{:S(2)}, u32[]{:S(2)}) collective-permute-start(bf16[4,128,128]{2,1,0:T(8,128)(2,1)S(1)} %bitcast.52), channel_id=1, source_target_pairs={{0,8},{8,0},{16,24},{24,16},{1,9},{9,1},{17,25},{25,17},{2,10},{10... | collective-permute-start | bytes 393224 | tf_op jit(solution)/shard_map/ppermute | solution.py:184
  21.4 0.2 collective-permute-start.2
  21.6 0.1 copy_bitcast_fusion.3
  21.7 7.1 %collective-permute-done.3.refs_5_ = bf16[16,32,128]{2,1,0:T(8,128)(2,1)S(1)} collective-permute-done((bf16[16,32,128]{2,1,0:T(8,128)(2,1)S(1)}, bf16[16,32,128]{2,1,0:T(8,128)(2,1)S(1)}, u32[]{:S(2)}, u32[]{:S(2)}) %collective-permute-start.3) | collective-permute-done | bytes 131104 | tf_op jit(solution)/shard_map/ppermute | solution.py:184
  28.8 0.9 %collective-permute-start.11 = (bf16[4,128,128]{2,1,0:T(8,128)(2,1)S(1)}, bf16[4,128,128]{2,1,0:T(8,128)(2,1)S(1)}, u32[]{:S(2)}, u32[]{:S(2)}) collective-permute-start(bf16[4,128,128]{2,1,0:T(8,128)(2,1)S(1)} %collective-permute-done.10.refs_14_), channel_id=1, source_target_pairs={{0,8},{8,0},{16,24},{24,16},{1,9},{9,1},{17,25},{25,17},{2,10},{10... | collective-permute-start | bytes 393224 | tf_op jit(solution)/shard_map/ppermute | solution.py:184
  29.7 1.3 %collective-permute-start.4 = (bf16[16,32,128]{2,1,0:T(8,128)(2,1)S(1)}, bf16[16,32,128]{2,1,0:T(8,128)(2,1)S(1)}, u32[]{:S(2)}, u32[]{:S(2)}) collective-permute-start(bf16[16,32,128]{2,1,0:T(8,128)(2,1)S(1)} %collective-permute-done.3.refs_5_), channel_id=1, source_target_pairs={{0,4},{4,0},{1,5},{5,1},{2,6},{6,2},{3,7},{7,3},{8,12},{12,8},{9,1... | collective-permute-start | bytes 393224 | tf_op jit(solution)/shard_map/ppermute | solution.py:184
  31.0 0.2 collective-permute-start.6
  31.3 1.2 %collective-permute-start.20 = (bf16[4,128,128]{2,1,0:T(8,128)(2,1)S(1)}, bf16[4,128,128]{2,1,0:T(8,128)(2,1)S(1)}, u32[]{:S(2)}, u32[]{:S(2)}) collective-permute-start(bf16[4,128,128]{2,1,0:T(8,128)(2,1)S(1)} %collective-permute-done.12.refs_16_), channel_id=1, source_target_pairs={{0,16},{8,24},{16,0},{24,8},{1,17},{9,25},{17,1},{25,9},{2,18},{10... | collective-permute-start | bytes 393224 | tf_op jit(solution)/shard_map/ppermute | solution.py:184
  32.4 0.1 copy_bitcast_fusion.5
  32.5 0.5 pad_maximum_fusion
  33.0 1.4 %collective-permute-done.4.refs_6_ = bf16[16,32,128]{2,1,0:T(8,128)(2,1)S(1)} collective-permute-done((bf16[16,32,128]{2,1,0:T(8,128)(2,1)S(1)}, bf16[16,32,128]{2,1,0:T(8,128)(2,1)S(1)}, u32[]{:S(2)}, u32[]{:S(2)}) %collective-permute-start.4) | collective-permute-done | bytes 131104 | tf_op jit(solution)/shard_map/ppermute | solution.py:184
  34.4 2.2 %collective-permute-start.9 = (bf16[4,128,128]{2,1,0:T(8,128)(2,1)S(1)}, bf16[4,128,128]{2,1,0:T(8,128)(2,1)S(1)}, u32[]{:S(2)}, u32[]{:S(2)}) collective-permute-start(bf16[4,128,128]{2,1,0:T(8,128)(2,1)S(1)} %collective-permute-done.8.refs_12_), channel_id=1, source_target_pairs={{0,8},{8,0},{16,24},{24,16},{1,9},{9,1},{17,25},{25,17},{2,10},{10... | collective-permute-start | bytes 393224 | tf_op jit(solution)/shard_map/ppermute | solution.py:184
  36.6 0.6 collective-permute-done.6.refs_8_
  37.2 1.3 %collective-permute-start.15 = (bf16[4,128,128]{2,1,0:T(8,128)(2,1)S(1)}, bf16[4,128,128]{2,1,0:T(8,128)(2,1)S(1)}, u32[]{:S(2)}, u32[]{:S(2)}) collective-permute-start(bf16[4,128,128]{2,1,0:T(8,128)(2,1)S(1)} %collective-permute-done.14.refs_12_), channel_id=1, source_target_pairs={{0,8},{8,0},{16,24},{24,16},{1,9},{9,1},{17,25},{25,17},{2,10},{10... | collective-permute-start | bytes 393224 | tf_op jit(solution)/shard_map/ppermute | solution.py:184
  38.5 0.5 collective-permute-start.19
  39.1 0.1 copy.36.refs_9_
  39.2 0.1 copy.37.refs_11_
  39.4 0.1 pad_add_fusion.refs_0_
  39.4 3.8 %update_first.1.refs_10_ = f32[16,128,128]{2,1,0:T(8,128)S(1)} custom-call(s32[4]{0:T(128)S(1)} %pad_add_fusion.refs_0_, bf16[16,32,128]{2,1,0:T(8,128)(2,1)S(1)} %bitcast.48, bf16[16,32,128]{2,1,0:T(8,128)(2,1)S(1)} %collective-permute-done.refs_2_, bf16[16,32,128]{2,1,0:T(8,128)(2,1)S(1)} %collective-permute-done.1.refs_3_, ...), custom_call_target="tpu_custom_call" | custom-call | tf_op jit(solution)/shard_map/update_first/pallas_call | solution.py:226
  43.3 0.1 broadcast_in_dim.2.refs_9_
  43.4 4.2 %update_last.1 = (bf16[16,64,128]{2,1,0:T(8,128)(2,1)S(1)}, bf16[16,64,128]{2,1,0:T(8,128)(2,1)S(1)}, bf16[32,16,128]{2,1,0:T(8,128)(2,1)S(1)}, bf16[32,16,128]{...) custom-call(s32[4]{0:T(128)S(1)} %pad_add_fusion.refs_0_, ...), custom_call_target="tpu_custom_call" | custom-call | tf_op jit(solution)/shard_map/update_last/pallas_call | solution.py:236
  47.6 0.1 collective-permute-start.22
  47.7 4.0 %collective-permute-start.23 = (bf16[32,16,128]{2,1,0:T(8,128)(2,1)S(1)}, bf16[32,16,128]{2,1,0:T(8,128)(2,1)S(1)}, u32[]{:S(2)}, u32[]{:S(2)}) collective-permute-start(bf16[32,16,128]{2,1,0:T(8,128)(2,1)S(1)} %get-tuple-element.21), channel_id=1, source_target_pairs={{0,0},{1,1},{2,2},{3,3},{4,16},{5,17},{6,18},{7,19},{8,8},{9,9},{1... | collective-permute-start | bytes 393224 | tf_op jit(solution)/shard_map/ppermute | solution.py:262
  51.7 2.5 %collective-permute-start.24 = (bf16[32,16,128]{2,1,0:T(8,128)(2,1)S(1)}, bf16[32,16,128]{2,1,0:T(8,128)(2,1)S(1)}, u32[]{:S(2)}, u32[]{:S(2)}) collective-permute-start(bf16[32,16,128]{2,1,0:T(8,128)(2,1)S(1)} %get-tuple-element.22), channel_id=1, source_target_pairs={{0,1},{1,0},{2,3},{3,2},{4,17},{5,16},{6,19},{7,18},{8,9},{9,8},{1... | collective-permute-start | bytes 393224 | tf_op jit(solution)/shard_map/ppermute | solution.py:262
  54.2 3.3 %collective-permute-start.25 = (bf16[32,16,128]{2,1,0:T(8,128)(2,1)S(1)}, bf16[32,16,128]{2,1,0:T(8,128)(2,1)S(1)}, u32[]{:S(2)}, u32[]{:S(2)}) collective-permute-start(bf16[32,16,128]{2,1,0:T(8,128)(2,1)S(1)} %get-tuple-element.23), channel_id=1, source_target_pairs={{0,8},{1,9},{2,10},{3,11},{4,24},{5,25},{6,26},{7,27},{8,0},{9,1},... | collective-permute-start | bytes 393224 | tf_op jit(solution)/shard_map/ppermute | solution.py:262
  57.5 0.4 collective-permute-done.24.refs_5_
  57.9 3.9 %collective-permute-done.25.refs_6_ = bf16[32,16,128]{2,1,0:T(8,128)(2,1)S(1)} collective-permute-done((bf16[32,16,128]{2,1,0:T(8,128)(2,1)S(1)}, bf16[32,16,128]{2,1,0:T(8,128)(2,1)S(1)}, u32[]{:S(2)}, u32[]{:S(2)}) %collective-permute-start.25) | collective-permute-done | bytes 131104 | tf_op jit(solution)/shard_map/ppermute | solution.py:262
  61.8 5.4 %collective-permute-done.26.refs_7_ = bf16[32,16,128]{2,1,0:T(8,128)(2,1)S(1)} collective-permute-done((bf16[32,16,128]{2,1,0:T(8,128)(2,1)S(1)}, bf16[32,16,128]{2,1,0:T(8,128)(2,1)S(1)}, u32[]{:S(2)}, u32[]{:S(2)}) %collective-permute-start.26) | collective-permute-done | bytes 131104 | tf_op jit(solution)/shard_map/ppermute | solution.py:262
  67.2 0.6 copy-done.3
  67.9 6.2 %finish.1 = bf16[16,128,128]{2,1,0:T(8,128)(2,1)} custom-call(s32[4]{0:T(128)S(1)} %pad_add_fusion.refs_0_, bf16[16,128,128]{2,1,0:T(8,128)(2,1)S(1)} %copy-done, bf16[16,64,128]{2,1,0:T(8,128)(2,1)S(1)} %get-tuple-element.19.refs_2_, bf16[16,64,128]{2,1,0:T(8,128)(2,1)S(1)} %collective-permute-done.22.refs_3_, ...), custom_call_target="tpu_custom_call" | custom-call | tf_op jit(solution)/shard_map/finish/pallas_call | solution.py:265
  (45 shorter events, 0.4 us)
Async XLA Ops:
  1.2 9.1 %copy-start.7 = (bf16[128,32,64]{0,2,1:T(8,128)(2,1)S(1)}, bf16[128,32,64]{0,2,1:T(8,128)(2,1)}, u32[]{:S(2)}) copy-start(bf16[128,32,64]{0,2,1:T(8,128)(2,1)} %param.10) | copy-start | bytes 1572868
  1.4 4.4 %collective-permute-start.8 = (bf16[4,128,128]{2,1,0:T(8,128)(2,1)S(1)}, bf16[4,128,128]{2,1,0:T(8,128)(2,1)S(1)}, u32[]{:S(2)}, u32[]{:S(2)}) collective-permute-start(bf16[4,128,128]{2,1,0:T(8,128)(2,1)S(1)} %bitcast.50), channel_id=1, source_target_pairs={{0,1},{1,0},{2,3},{3,2},{4,5},{5,4},{6,7},{7,6},{8,9},{9,8},{10,11... | collective-permute-start | bytes 393224 | tf_op jit(solution)/shard_map/ppermute | solution.py:184
  2.7 4.1 %collective-permute-start.14 = (bf16[4,128,128]{2,1,0:T(8,128)(2,1)S(1)}, bf16[4,128,128]{2,1,0:T(8,128)(2,1)S(1)}, u32[]{:S(2)}, u32[]{:S(2)}) collective-permute-start(bf16[4,128,128]{2,1,0:T(8,128)(2,1)S(1)} %bitcast.51), channel_id=1, source_target_pairs={{0,16},{8,24},{16,0},{24,8},{1,17},{9,25},{17,1},{25,9},{2,18},{10... | collective-permute-start | bytes 393224 | tf_op jit(solution)/shard_map/ppermute | solution.py:184
  3.1 7.3 %collective-permute-start.10 = (bf16[4,128,128]{2,1,0:T(8,128)(2,1)S(1)}, bf16[4,128,128]{2,1,0:T(8,128)(2,1)S(1)}, u32[]{:S(2)}, u32[]{:S(2)}) collective-permute-start(bf16[4,128,128]{2,1,0:T(8,128)(2,1)S(1)} %bitcast.63), channel_id=1, source_target_pairs={{0,2},{1,3},{2,0},{3,1},{4,6},{5,7},{6,4},{7,5},{8,10},{9,11},{10,... | collective-permute-start | bytes 393224 | tf_op jit(solution)/shard_map/ppermute | solution.py:184
  6.8 4.1 %collective-permute-start.16 = (bf16[4,128,128]{2,1,0:T(8,128)(2,1)S(1)}, bf16[4,128,128]{2,1,0:T(8,128)(2,1)S(1)}, u32[]{:S(2)}, u32[]{:S(2)}) collective-permute-start(bf16[4,128,128]{2,1,0:T(8,128)(2,1)S(1)} %collective-permute-done.8.refs_12_), channel_id=1, source_target_pairs={{0,16},{8,24},{16,0},{24,8},{1,17},{9,25},{17,1},{25,9},{2,18},{10... | collective-permute-start | bytes 393224 | tf_op jit(solution)/shard_map/ppermute | solution.py:184
  7.0 11.3 %collective-permute-start.12 = (bf16[4,128,128]{2,1,0:T(8,128)(2,1)S(1)}, bf16[4,128,128]{2,1,0:T(8,128)(2,1)S(1)}, u32[]{:S(2)}, u32[]{:S(2)}) collective-permute-start(bf16[4,128,128]{2,1,0:T(8,128)(2,1)S(1)} %bitcast.64), channel_id=1, source_target_pairs={{0,3},{1,2},{2,1},{3,0},{4,7},{5,6},{6,5},{7,4},{8,11},{9,10},{10,... | collective-permute-start | bytes 393224 | tf_op jit(solution)/shard_map/ppermute | solution.py:184
  10.3 4.6 %copy-start.6 = (bf16[1024,128]{1,0:T(8,128)(2,1)S(1)}, bf16[1024,128]{1,0:T(8,128)(2,1)}, u32[]{:S(2)}) copy-start(bf16[1024,128]{1,0:T(8,128)(2,1)} %param.12) | copy-start | bytes 786436
  10.3 6.7 %collective-permute-start.1 = (bf16[16,32,128]{2,1,0:T(8,128)(2,1)S(1)}, bf16[16,32,128]{2,1,0:T(8,128)(2,1)S(1)}, u32[]{:S(2)}, u32[]{:S(2)}) collective-permute-start(bf16[16,32,128]{2,1,0:T(8,128)(2,1)S(1)} %bitcast.65), channel_id=1, source_target_pairs={{0,1},{1,0},{2,3},{3,2},{4,5},{5,4},{6,7},{7,6},{8,9},{9,8},{10,11... | collective-permute-start | bytes 393224 | tf_op jit(solution)/shard_map/ppermute | solution.py:184
  11.0 10.4 %collective-permute-start.18 = (bf16[4,128,128]{2,1,0:T(8,128)(2,1)S(1)}, bf16[4,128,128]{2,1,0:T(8,128)(2,1)S(1)}, u32[]{:S(2)}, u32[]{:S(2)}) collective-permute-start(bf16[4,128,128]{2,1,0:T(8,128)(2,1)S(1)} %collective-permute-done.10.refs_14_), channel_id=1, source_target_pairs={{0,16},{8,24},{16,0},{24,8},{1,17},{9,25},{17,1},{25,9},{2,18},{10... | collective-permute-start | bytes 393224 | tf_op jit(solution)/shard_map/ppermute | solution.py:184
  12.7 17.0 %collective-permute-start.5 = (bf16[16,32,128]{2,1,0:T(8,128)(2,1)S(1)}, bf16[16,32,128]{2,1,0:T(8,128)(2,1)S(1)}, u32[]{:S(2)}, u32[]{:S(2)}) collective-permute-start(bf16[16,32,128]{2,1,0:T(8,128)(2,1)S(1)} %bitcast.66), channel_id=1, source_target_pairs={{0,3},{1,2},{2,1},{3,0},{4,7},{5,6},{6,5},{7,4},{8,11},{9,10},{10,... | collective-permute-start | bytes 393224 | tf_op jit(solution)/shard_map/ppermute | solution.py:184
  14.8 14.0 %collective-permute-start.3 = (bf16[16,32,128]{2,1,0:T(8,128)(2,1)S(1)}, bf16[16,32,128]{2,1,0:T(8,128)(2,1)S(1)}, u32[]{:S(2)}, u32[]{:S(2)}) collective-permute-start(bf16[16,32,128]{2,1,0:T(8,128)(2,1)S(1)} %bitcast.46), channel_id=1, source_target_pairs={{0,2},{1,3},{2,0},{3,1},{4,6},{5,7},{6,4},{7,5},{8,10},{9,11},{10,... | collective-permute-start | bytes 393224 | tf_op jit(solution)/shard_map/ppermute | solution.py:184
  17.1 12.6 %collective-permute-start = (bf16[16,32,128]{2,1,0:T(8,128)(2,1)S(1)}, bf16[16,32,128]{2,1,0:T(8,128)(2,1)S(1)}, u32[]{:S(2)}, u32[]{:S(2)}) collective-permute-start(bf16[16,32,128]{2,1,0:T(8,128)(2,1)S(1)} %bitcast.47), channel_id=1, source_target_pairs={{0,4},{4,0},{1,5},{5,1},{2,6},{6,2},{3,7},{7,3},{8,12},{12,8},{9,1... | collective-permute-start | bytes 393224 | tf_op jit(solution)/shard_map/ppermute | solution.py:184
  18.3 12.7 %collective-permute-start.7 = (bf16[4,128,128]{2,1,0:T(8,128)(2,1)S(1)}, bf16[4,128,128]{2,1,0:T(8,128)(2,1)S(1)}, u32[]{:S(2)}, u32[]{:S(2)}) collective-permute-start(bf16[4,128,128]{2,1,0:T(8,128)(2,1)S(1)} %bitcast.52), channel_id=1, source_target_pairs={{0,8},{8,0},{16,24},{24,16},{1,9},{9,1},{17,25},{25,17},{2,10},{10... | collective-permute-start | bytes 393224 | tf_op jit(solution)/shard_map/ppermute | solution.py:184
  21.4 9.9 %collective-permute-start.2 = (bf16[16,32,128]{2,1,0:T(8,128)(2,1)S(1)}, bf16[16,32,128]{2,1,0:T(8,128)(2,1)S(1)}, u32[]{:S(2)}, u32[]{:S(2)}) collective-permute-start(bf16[16,32,128]{2,1,0:T(8,128)(2,1)S(1)} %collective-permute-done.1.refs_3_), channel_id=1, source_target_pairs={{0,4},{4,0},{1,5},{5,1},{2,6},{6,2},{3,7},{7,3},{8,12},{12,8},{9,1... | collective-permute-start | bytes 393224 | tf_op jit(solution)/shard_map/ppermute | solution.py:184
  28.8 9.7 %collective-permute-start.11 = (bf16[4,128,128]{2,1,0:T(8,128)(2,1)S(1)}, bf16[4,128,128]{2,1,0:T(8,128)(2,1)S(1)}, u32[]{:S(2)}, u32[]{:S(2)}) collective-permute-start(bf16[4,128,128]{2,1,0:T(8,128)(2,1)S(1)} %collective-permute-done.10.refs_14_), channel_id=1, source_target_pairs={{0,8},{8,0},{16,24},{24,16},{1,9},{9,1},{17,25},{25,17},{2,10},{10... | collective-permute-start | bytes 393224 | tf_op jit(solution)/shard_map/ppermute | solution.py:184
  29.7 8.8 %collective-permute-start.13 = (bf16[4,128,128]{2,1,0:T(8,128)(2,1)S(1)}, bf16[4,128,128]{2,1,0:T(8,128)(2,1)S(1)}, u32[]{:S(2)}, u32[]{:S(2)}) collective-permute-start(bf16[4,128,128]{2,1,0:T(8,128)(2,1)S(1)} %collective-permute-done.12.refs_16_), channel_id=1, source_target_pairs={{0,8},{8,0},{16,24},{24,16},{1,9},{9,1},{17,25},{25,17},{2,10},{10... | collective-permute-start | bytes 393224 | tf_op jit(solution)/shard_map/ppermute | solution.py:184
  29.7 4.7 %collective-permute-start.4 = (bf16[16,32,128]{2,1,0:T(8,128)(2,1)S(1)}, bf16[16,32,128]{2,1,0:T(8,128)(2,1)S(1)}, u32[]{:S(2)}, u32[]{:S(2)}) collective-permute-start(bf16[16,32,128]{2,1,0:T(8,128)(2,1)S(1)} %collective-permute-done.3.refs_5_), channel_id=1, source_target_pairs={{0,4},{4,0},{1,5},{5,1},{2,6},{6,2},{3,7},{7,3},{8,12},{12,8},{9,1... | collective-permute-start | bytes 393224 | tf_op jit(solution)/shard_map/ppermute | solution.py:184
  31.0 6.2 %collective-permute-start.6 = (bf16[16,32,128]{2,1,0:T(8,128)(2,1)S(1)}, bf16[16,32,128]{2,1,0:T(8,128)(2,1)S(1)}, u32[]{:S(2)}, u32[]{:S(2)}) collective-permute-start(bf16[16,32,128]{2,1,0:T(8,128)(2,1)S(1)} %collective-permute-done.5.refs_7_), channel_id=1, source_target_pairs={{0,4},{4,0},{1,5},{5,1},{2,6},{6,2},{3,7},{7,3},{8,12},{12,8},{9,1... | collective-permute-start | bytes 393224 | tf_op jit(solution)/shard_map/ppermute | solution.py:184
  31.3 7.8 %collective-permute-start.20 = (bf16[4,128,128]{2,1,0:T(8,128)(2,1)S(1)}, bf16[4,128,128]{2,1,0:T(8,128)(2,1)S(1)}, u32[]{:S(2)}, u32[]{:S(2)}) collective-permute-start(bf16[4,128,128]{2,1,0:T(8,128)(2,1)S(1)} %collective-permute-done.12.refs_16_), channel_id=1, source_target_pairs={{0,16},{8,24},{16,0},{24,8},{1,17},{9,25},{17,1},{25,9},{2,18},{10... | collective-permute-start | bytes 393224 | tf_op jit(solution)/shard_map/ppermute | solution.py:184
  34.4 5.0 %collective-permute-start.9 = (bf16[4,128,128]{2,1,0:T(8,128)(2,1)S(1)}, bf16[4,128,128]{2,1,0:T(8,128)(2,1)S(1)}, u32[]{:S(2)}, u32[]{:S(2)}) collective-permute-start(bf16[4,128,128]{2,1,0:T(8,128)(2,1)S(1)} %collective-permute-done.8.refs_12_), channel_id=1, source_target_pairs={{0,8},{8,0},{16,24},{24,16},{1,9},{9,1},{17,25},{25,17},{2,10},{10... | collective-permute-start | bytes 393224 | tf_op jit(solution)/shard_map/ppermute | solution.py:184
  37.2 6.0 %collective-permute-start.15 = (bf16[4,128,128]{2,1,0:T(8,128)(2,1)S(1)}, bf16[4,128,128]{2,1,0:T(8,128)(2,1)S(1)}, u32[]{:S(2)}, u32[]{:S(2)}) collective-permute-start(bf16[4,128,128]{2,1,0:T(8,128)(2,1)S(1)} %collective-permute-done.14.refs_12_), channel_id=1, source_target_pairs={{0,8},{8,0},{16,24},{24,16},{1,9},{9,1},{17,25},{25,17},{2,10},{10... | collective-permute-start | bytes 393224 | tf_op jit(solution)/shard_map/ppermute | solution.py:184
  38.5 4.7 %collective-permute-start.17 = (bf16[4,128,128]{2,1,0:T(8,128)(2,1)S(1)}, bf16[4,128,128]{2,1,0:T(8,128)(2,1)S(1)}, u32[]{:S(2)}, u32[]{:S(2)}) collective-permute-start(bf16[4,128,128]{2,1,0:T(8,128)(2,1)S(1)} %collective-permute-done.16.refs_14_), channel_id=1, source_target_pairs={{0,8},{8,0},{16,24},{24,16},{1,9},{9,1},{17,25},{25,17},{2,10},{10... | collective-permute-start | bytes 393224 | tf_op jit(solution)/shard_map/ppermute | solution.py:184
  38.5 4.7 %collective-permute-start.19 = (bf16[4,128,128]{2,1,0:T(8,128)(2,1)S(1)}, bf16[4,128,128]{2,1,0:T(8,128)(2,1)S(1)}, u32[]{:S(2)}, u32[]{:S(2)}) collective-permute-start(bf16[4,128,128]{2,1,0:T(8,128)(2,1)S(1)} %collective-permute-done.18.refs_16_), channel_id=1, source_target_pairs={{0,8},{8,0},{16,24},{24,16},{1,9},{9,1},{17,25},{25,17},{2,10},{10... | collective-permute-start | bytes 393224 | tf_op jit(solution)/shard_map/ppermute | solution.py:184
  39.0 4.2 %collective-permute-start.21 = (bf16[4,128,128]{2,1,0:T(8,128)(2,1)S(1)}, bf16[4,128,128]{2,1,0:T(8,128)(2,1)S(1)}, u32[]{:S(2)}, u32[]{:S(2)}) collective-permute-start(bf16[4,128,128]{2,1,0:T(8,128)(2,1)S(1)} %collective-permute-done.20.refs_18_), channel_id=1, source_target_pairs={{0,8},{8,0},{16,24},{24,16},{1,9},{9,1},{17,25},{25,17},{2,10},{10... | collective-permute-start | bytes 393224 | tf_op jit(solution)/shard_map/ppermute | solution.py:184
  39.4 3.9 %copy-start.8 = (f32[128]{0:T(128)S(1)}, f32[128]{0:T(128)}, u32[]{:S(2)}) copy-start(f32[128]{0:T(128)} %param.13) | copy-start | bytes 1540
  43.4 23.8 %copy-start = (bf16[16,128,128]{2,1,0:T(8,128)(2,1)S(1)}, bf16[16,128,128]{2,1,0:T(8,128)(2,1)}, u32[]{:S(2)}) copy-start(bf16[16,128,128]{2,1,0:T(8,128)(2,1)} %refs_1_.1) | copy-start | bytes 1572868
  43.4 23.8 %copy-start.1 = (bf16[128,512]{1,0:T(8,128)(2,1)S(1)}, bf16[128,512]{1,0:T(8,128)(2,1)}, u32[]{:S(2)}) copy-start(bf16[128,512]{1,0:T(8,128)(2,1)} %refs_9_.1) | copy-start | bytes 393220
  43.4 23.8 %copy-start.2 = (bf16[512,128]{1,0:T(8,128)(2,1)S(1)}, bf16[512,128]{1,0:T(8,128)(2,1)}, u32[]{:S(2)}) copy-start(bf16[512,128]{1,0:T(8,128)(2,1)} %refs_11_.1) | copy-start | bytes 393220
  47.6 19.6 %collective-permute-start.22 = (bf16[16,64,128]{2,1,0:T(8,128)(2,1)S(1)}, bf16[16,64,128]{2,1,0:T(8,128)(2,1)S(1)}, u32[]{:S(2)}, u32[]{:S(2)}) collective-permute-start(bf16[16,64,128]{2,1,0:T(8,128)(2,1)S(1)} %get-tuple-element.20), channel_id=1, source_target_pairs={{0,2},{1,3},{2,0},{3,1},{4,6},{5,7},{6,4},{7,5},{8,10},{9,11},{10,... | collective-permute-start | bytes 786440 | tf_op jit(solution)/shard_map/ppermute | solution.py:184
  47.7 9.9 %collective-permute-start.23 = (bf16[32,16,128]{2,1,0:T(8,128)(2,1)S(1)}, bf16[32,16,128]{2,1,0:T(8,128)(2,1)S(1)}, u32[]{:S(2)}, u32[]{:S(2)}) collective-permute-start(bf16[32,16,128]{2,1,0:T(8,128)(2,1)S(1)} %get-tuple-element.21), channel_id=1, source_target_pairs={{0,0},{1,1},{2,2},{3,3},{4,16},{5,17},{6,18},{7,19},{8,8},{9,9},{1... | collective-permute-start | bytes 393224 | tf_op jit(solution)/shard_map/ppermute | solution.py:262
  51.7 6.2 %collective-permute-start.24 = (bf16[32,16,128]{2,1,0:T(8,128)(2,1)S(1)}, bf16[32,16,128]{2,1,0:T(8,128)(2,1)S(1)}, u32[]{:S(2)}, u32[]{:S(2)}) collective-permute-start(bf16[32,16,128]{2,1,0:T(8,128)(2,1)S(1)} %get-tuple-element.22), channel_id=1, source_target_pairs={{0,1},{1,0},{2,3},{3,2},{4,17},{5,16},{6,19},{7,18},{8,9},{9,8},{1... | collective-permute-start | bytes 393224 | tf_op jit(solution)/shard_map/ppermute | solution.py:262
  54.2 7.6 %collective-permute-start.25 = (bf16[32,16,128]{2,1,0:T(8,128)(2,1)S(1)}, bf16[32,16,128]{2,1,0:T(8,128)(2,1)S(1)}, u32[]{:S(2)}, u32[]{:S(2)}) collective-permute-start(bf16[32,16,128]{2,1,0:T(8,128)(2,1)S(1)} %get-tuple-element.23), channel_id=1, source_target_pairs={{0,8},{1,9},{2,10},{3,11},{4,24},{5,25},{6,26},{7,27},{8,0},{9,1},... | collective-permute-start | bytes 393224 | tf_op jit(solution)/shard_map/ppermute | solution.py:262
  57.5 9.7 %collective-permute-start.26 = (bf16[32,16,128]{2,1,0:T(8,128)(2,1)S(1)}, bf16[32,16,128]{2,1,0:T(8,128)(2,1)S(1)}, u32[]{:S(2)}, u32[]{:S(2)}) collective-permute-start(bf16[32,16,128]{2,1,0:T(8,128)(2,1)S(1)} %get-tuple-element.24), channel_id=1, source_target_pairs={{0,9},{1,8},{2,11},{3,10},{4,25},{5,24},{6,27},{7,26},{8,1},{9,0},... | collective-permute-start | bytes 393224 | tf_op jit(solution)/shard_map/ppermute | solution.py:262
  67.2 0.7 copy-start.3
  67.2 0.7 copy-start.4
  67.2 0.7 copy-start.5

commit v4 on v3

v4 whole, which is shorter than its diff:
```python
import functools

import jax
import jax.numpy as jnp
from jax import lax
from jax.experimental import pallas as pl
from jax.experimental.pallas import tpu as pltpu
from jax.sharding import PartitionSpec as P

epsilon = 1e-05
axes = ("row", "col", "seq")


def update_kernel(places, shares, low, last, scale, *refs):
    left_places, right_places, share_rows, source_rows, group_len, operands = places
    refs = list(refs)
    place_ref = refs.pop(0)
    data_refs = [refs.pop(0) for _ in range(operands)]
    bias_ref, partial_ref = (refs.pop(0), refs.pop(0)) if last else (None, None)
    weight_ref = refs.pop(0)
    update_ref = refs.pop() if last else None
    outer_ref = refs.pop()
    lhs_ref = refs.pop()
    out_refs = refs
    groups = len(left_places)
    row_count, _, lanes = outer_ref.shape
    channels = share_rows * shares // row_count
    per = source_rows // group_len
    sources = len(right_places[0])
    half = lanes // 2
    pair_channels = weight_ref.shape[0] // 2
    lane_low = lax.broadcasted_iota(jnp.int32, (pair_channels, lanes), 1) < half
    for dy in range(shares):
        begin = pl.multiple_of((place_ref[2] ^ dy) * share_rows, share_rows)
        for dz in range(groups):
            operand, first = left_places[dz][dy]
            lhs_ref[pl.ds(begin, share_rows), dz * group_len : (dz + 1) * group_len] = data_refs[
                operand
            ][first : first + share_rows]

    def right_tile(item):
        source, rest = divmod(item, per)
        tiles = []
        for dz in range(groups):
            operand, first = right_places[dz][source]
            first += rest * group_len
            tiles.append(data_refs[operand][first : first + group_len])
        return jnp.concatenate(tiles, axis=0)

    for pair in range(sources * per // 2):
        right = jnp.concatenate([right_tile(2 * pair), right_tile(2 * pair + 1)], axis=1)
        outer = jnp.dot(lhs_ref[...], right, preferred_element_type=jnp.float32)
        outer = outer.astype(jnp.bfloat16)
        for part in range(2):
            item = 2 * pair + part
            outer_ref[:, item * channels : (item + 1) * channels, :] = outer[
                :, part * lanes : (part + 1) * lanes
            ].reshape(row_count, channels, lanes)

    @pl.loop(0, row_count // 8)
    def _(step):
        for two in range(4):
            index = step * 4 + two
            both = jnp.concatenate([outer_ref[2 * index], outer_ref[2 * index + 1]], axis=1)
            proj = jnp.dot(weight_ref[...], both, preferred_element_type=jnp.float32)
            a0 = proj[:pair_channels, :lanes]
            a1 = proj[:pair_channels, lanes:]
            b0 = proj[pair_channels:, :lanes]
            b1 = proj[pair_channels:, lanes:]
            cell = jnp.where(lane_low, a0, b1) + pltpu.roll(
                jnp.where(lane_low, a1, b0), half, 1
            )
            if last:
                cell = (cell + partial_ref[index]) * scale + bias_ref[...]
                update_ref[pl.ds(2 * index, 2)] = (
                    cell.astype(jnp.bfloat16).T.reshape(2, half, pair_channels)
                )
            else:
                out_refs[0][index] = cell

    if last:
        core, z_low, z_high = place_ref[0], place_ref[1], place_ref[3]
        run = row_count // 2
        out_refs[0][...] = update_ref[pl.ds(z_high * run, run)]
        out_refs[1][...] = update_ref[pl.ds((1 - z_high) * run, run)]
        for dz in range(low):
            for flip in range(2):
                begin = (core ^ flip) * (half // 2) + (z_low ^ dz) * run
                out_refs[2 + 2 * dz + flip][...] = update_ref[
                    :, pl.ds(pl.multiple_of(begin, run), run), :
                ]


def finish_kernel(low, dz, *refs):
    place_ref, pair_ref, own_ref, other_ref, mirror_low, mirror_high = refs[:6]
    gain_ref, up_ref, up_bias_ref, down_ref, down_bias_ref = refs[6:11]
    out_ref, middle_ref, done_ref, sems = refs[-4:]
    mirror_refs = (mirror_low, mirror_high)
    run, columns, pair_channels = pair_ref.shape
    half = columns // 2
    core, z_low, z_high = place_ref[0], place_ref[1], place_ref[3]
    cells = run * run
    to = lax.broadcasted_iota(jnp.int32, (cells, cells), 0)
    of = lax.broadcasted_iota(jnp.int32, (cells, cells), 1)
    swap_cells = jnp.where(
        jnp.logical_and(to // run == of % run, to % run == of // run), 1.0, 0.0
    ).astype(jnp.bfloat16)
    begins = []
    for flip in range(2):
        for part in range(2):
            index = 2 * flip + part
            local = (core ^ flip) * (half // 2) + (z_low ^ dz) * run
            local = pl.multiple_of(local, run)
            begin = (core ^ flip) * half + (part * low + (z_low ^ dz)) * run
            begin = pl.multiple_of(begin, run)
            begins.append(begin)
            piece = mirror_refs[flip][part * run : (part + 1) * run]
            mirrored = jnp.dot(
                swap_cells,
                piece.reshape(cells, pair_channels),
                preferred_element_type=jnp.float32,
            )
            direct = jnp.where(
                z_high == part,
                own_ref[:, pl.ds(local, run), :],
                other_ref[:, pl.ds(local, run), :],
            ).reshape(cells, pair_channels)
            residual = pair_ref[:, pl.ds(begin, run), :].reshape(cells, pair_channels)
            middle_ref[index * cells : (index + 1) * cells] = (
                residual.astype(jnp.float32) + 0.5 * (direct.astype(jnp.float32) + mirrored)
            ).astype(jnp.bfloat16)

    values = middle_ref[...].astype(jnp.float32)
    center = jnp.mean(values, axis=1, keepdims=True)
    moved = values - center
    spread = jnp.mean(jnp.square(moved), axis=1, keepdims=True)
    normed = moved * lax.rsqrt(spread + epsilon) * gain_ref[...]
    hidden = jnp.dot(
        normed.astype(jnp.bfloat16), up_ref[...], preferred_element_type=jnp.float32
    )
    hidden = jnp.maximum(hidden + up_bias_ref[...], 0.0).astype(jnp.bfloat16)
    result = jnp.dot(hidden, down_ref[...], preferred_element_type=jnp.float32)
    result = (values + result + down_bias_ref[...]).astype(jnp.bfloat16)
    done_ref[...] = result.reshape(4, run, run, pair_channels)
    copies = [
        pltpu.make_async_copy(
            done_ref.at[index], out_ref.at[:, pl.ds(begins[index], run), :], sems.at[index]
        )
        for index in range(4)
    ]
    for copy in copies:
        copy.start()
    for copy in copies:
        copy.wait()


def on_device(
    left_piece,
    right_piece,
    proj_weight,
    proj_bias,
    pair_rep,
    norm_gain,
    up_weight,
    up_bias,
    down_weight,
    down_bias,
):
    rows = lax.axis_size("row")
    cols = lax.axis_size("col")
    groups = lax.axis_size("seq")
    xs = rows // 2
    low = groups // 2
    row, col, seq = (lax.axis_index(name) for name in axes)
    core, z_low, z_high = row % 2, seq % low, seq // low
    run, columns, pair_channels = pair_rep.shape
    group_len, channels, _ = left_piece.shape
    e1 = right_piece.shape[1] // 2
    half = columns // 2
    bf16 = jnp.bfloat16

    def pick(value, index, axis=0):
        return lax.dynamic_index_in_dim(value, index, axis, False)

    def swap(value, name, size, flip):
        return lax.ppermute(value, name, [(i, i ^ flip) for i in range(size)])

    right = right_piece.reshape(group_len, e1, 2, 2, 2, half // 2).transpose(4, 1, 0, 2, 3, 5)
    source_rows = e1 * group_len
    right = right.reshape(2, source_rows, 2 * half)
    share_rows = 2 * run // cols * channels
    left = left_piece.transpose(2, 1, 0).reshape(2, low, run, channels, group_len)
    left = left.transpose(1, 0, 2, 3, 4).reshape(low, cols, share_rows, group_len)
    left = pick(left, col, 1)

    def packed(dz):
        return jnp.concatenate(
            [pick(right, z_high ^ (dz // low)), pick(left, z_low ^ (dz % low))], axis=0
        )

    order = [0, 1] + list(range(groups - 1, 1, -1))
    held = {dz: packed(dz) if dz == 0 else swap(packed(dz), "seq", groups, dz) for dz in order}
    bundles = [order[:2]] + [[dz] for dz in order[2:]]
    data, left_places, right_places, other_places = [], {}, {}, {}
    for dz in range(groups):
        left_places[dz] = [(len(data), source_rows)]
        right_places[dz] = [(len(data), 0)]
        other_places[dz] = []
        data.append(held[dz])
    others = []
    for bundle in bundles:
        rights = jnp.concatenate([held[dz][:source_rows] for dz in bundle], axis=0)
        lefts = jnp.concatenate([held[dz][source_rows:] for dz in bundle], axis=0)
        for position, dz in enumerate(bundle):
            right_places[dz].append((len(data), position * source_rows))
        data.append(swap(rights, "row", rows, 1))
        for dy in range(1, cols):
            for position, dz in enumerate(bundle):
                left_places[dz].append((len(data), position * share_rows))
            data.append(swap(lefts, "col", cols, dy))
        for dx in range(1, xs):
            crossed = swap(rights, "row", rows, 2 * dx)
            for value in (crossed, swap(crossed, "row", rows, 1)):
                for position, dz in enumerate(bundle):
                    other_places[dz].append((len(others), position * source_rows))
                others.append(value)

    weight = proj_weight.reshape(channels, rows, e1, 2, pair_channels)
    weight = weight.transpose(1, 3, 4, 2, 0)
    weight = jnp.stack([pick(weight, row ^ m) for m in range(rows)], axis=2)
    weight = weight.reshape(2 * pair_channels, channels * channels // 2)
    split = channels * channels // 2 // xs

    place = jnp.stack([core, z_low, col, z_high]).astype(jnp.int32)
    vmem = pl.BlockSpec(memory_space=pltpu.VMEM)
    smem = pl.BlockSpec(memory_space=pltpu.SMEM)
    params = pltpu.CompilerParams(vmem_limit_bytes=40 * 1024 * 1024)
    scale = 1.0 / (group_len * groups)
    lhs = pltpu.VMEM((2 * run * channels, groups * group_len), bf16)

    def tabled(table):
        return [table[dz] for dz in range(groups)]

    sizes = (share_rows, source_rows, group_len)
    places = (tabled(left_places), tabled(right_places)) + sizes + (len(data),)
    partial = pl.pallas_call(
        functools.partial(update_kernel, places, cols, low, False, scale),
        out_shape=jax.ShapeDtypeStruct((run, pair_channels, 2 * half), jnp.float32),
        in_specs=[smem] + [vmem] * (len(data) + 1),
        out_specs=vmem,
        scratch_shapes=[lhs, pltpu.VMEM((2 * run, split, 2 * half), bf16)],
        compiler_params=params,
        name="update_first",
    )(place, *data, weight[:, :split])
    shifted = [[(o + len(data), f) for o, f in other_places[dz]] for dz in range(groups)]
    places = (tabled(left_places), shifted) + sizes + (len(data) + len(others),)
    bias = jnp.broadcast_to(proj_bias[:, None], (pair_channels, 2 * half))
    outs = pl.pallas_call(
        functools.partial(update_kernel, places, cols, low, True, scale),
        out_shape=[jax.ShapeDtypeStruct((run, half, pair_channels), bf16)] * 2
        + [jax.ShapeDtypeStruct((2 * run, run, pair_channels), bf16)] * (2 * low),
        in_specs=[smem] + [vmem] * (len(data) + len(others) + 3),
        out_specs=[vmem] * (2 + 2 * low),
        scratch_shapes=[
            lhs,
            pltpu.VMEM((2 * run, (xs - 1) * split, 2 * half), bf16),
            pltpu.VMEM((2 * run, half, pair_channels), bf16),
        ],
        compiler_params=params,
        name="update_last",
    )(place, *data, *others, bias, partial, weight[:, split:])

    update_other = swap(outs[1], "seq", groups, low)
    mirrors = []
    for dz in range(low):
        for flip in range(2):
            pairs = []
            for r in range(rows):
                for c in range(cols):
                    for q in range(groups):
                        source = (r * cols + c) * groups + q
                        target = 2 * c + (r % 2 ^ flip)
                        target = (target * cols + r // 2) * groups + (q ^ dz)
                        pairs.append((source, target))
            mirrors.append(lax.ppermute(outs[2 + 2 * dz + flip], axes, pairs))

    anywhere = pl.BlockSpec(memory_space=pl.ANY)
    result = None
    for dz in range(low):
        operands = [
            place,
            pair_rep,
            outs[0],
            update_other,
            mirrors[2 * dz],
            mirrors[2 * dz + 1],
            norm_gain.reshape(1, -1),
            up_weight,
            up_bias.reshape(1, -1),
            down_weight,
            down_bias.reshape(1, -1),
        ]
        extra = [] if result is None else [result]
        result = pl.pallas_call(
            functools.partial(finish_kernel, low, dz),
            out_shape=jax.ShapeDtypeStruct(pair_rep.shape, bf16),
            in_specs=[smem] + [vmem] * 10 + [anywhere] * len(extra),
            out_specs=anywhere,
            scratch_shapes=[
                pltpu.VMEM((4 * run * run, pair_channels), bf16),
                pltpu.VMEM((4, run, run, pair_channels), bf16),
                pltpu.SemaphoreType.DMA((4,)),
            ],
            input_output_aliases={11: 0} if extra else {},
            compiler_params=params,
            name="finish",
        )(*operands, *extra)
    return result


def solution(mesh):
    in_specs = (
        P("seq", None, "row"),
        P("seq", "row", "col"),
        P(),
        P(),
        P(("row", "seq"), "col", None),
        P(),
        P(),
        P(),
        P(),
        P(),
    )
    out_specs = P(("row", "seq"), "col", None)
    return jax.shard_map(
        on_device, mesh=mesh, in_specs=in_specs, out_specs=out_specs, check_vma=False
    )
```

time: 74.4 us -> 78.9 us (1.060)
  waiting for transfers between devices: 22.7 us -> 26.4 us
  local copies, waits for them, and re-layouts: 2.95 us -> 5.07 us
  Pallas kernels: 14.2 us -> 12.6 us
    ppermute x23 -> x16, waiting for transfers between devices: 13 us -> 19.8 us  [swap(): return lax.ppermute(value, name, [(i, i ^ flip) for i in range(size)])]
    ppermute x4, waiting for transfers between devices: 9.67 us -> 6.64 us  [on_device(): mirrors.append(lax.ppermute(outs[2 + 2 * dz + flip], axes, pairs))]
    pallas_call x3 -> x4, Pallas kernels: 14.2 us -> 12.6 us  [the longest x2 5.3 us: on_device(): pl.pallas_call(functools.partial(finish_kernel, low, dz), out_shape=jax.S...]
    ppermute x23 -> x16, starting transfers between devices: 23.5 us -> 24.6 us  [swap(): return lax.ppermute(value, name, [(i, i ^ flip) for i in range(size)])]
    ppermute x4, starting transfers between devices: 9.84 us -> 8.91 us  [on_device(): mirrors.append(lax.ppermute(outs[2 + 2 * dz + flip], axes, pairs))]
    unnamed x24 -> x22, local copies, waits for them, and re-layouts: 2.14 us -> 2.94 us
  transfers between devices with their start and end apart: 27 -> 20, of which waited for: 10 -> 8; matrix products, arithmetic and copies ran while one was open for 2% -> 3% of each run, Pallas kernels for 5% -> 8%
where the time goes in v4:
time: 78.9 us; the launch traced here: 78.7 us
  starting transfers between devices  33.5 us (42%)
  waiting for transfers between devices  26.4 us (33%)
  Pallas kernels  12.6 us (16%)
  local copies, waits for them, and re-layouts  5.07 us (6%)
    ppermute x16, starting transfers between devices, swap(): return lax.ppermute(value, name, [(i, i ^ flip) for i in range(size)])  24.6 us
    ppermute x16, waiting for transfers between devices, swap(): return lax.ppermute(value, name, [(i, i ^ flip) for i in range(size)])  19.8 us
    ppermute x4, starting transfers between devices, on_device(): mirrors.append(lax.ppermute(outs[2 + 2 * dz + flip], axes, pairs))  8.91 us
    ppermute x4, waiting for transfers between devices, on_device(): mirrors.append(lax.ppermute(outs[2 + 2 * dz + flip], axes, pairs))  6.64 us
    pallas_call x2, Pallas kernels, on_device(): pl.pallas_call(functools.partial(finish_kernel, low, dz), out_shape=jax.S...  5.3 us
    pallas_call x1, Pallas kernels, on_device(): pl.pallas_call(functools.partial(update_kernel, places, cols, low, True,...  3.87 us
    pallas_call x1, Pallas kernels, on_device(): pl.pallas_call(functools.partial(update_kernel, places, cols, low, False,...  3.45 us
    unnamed x22, local copies, waits for them, and re-layouts  2.94 us
  transfers between devices with their start and end apart: 20, of which 8 were waited for; matrix products, arithmetic and copies ran while one was open for 3% of the time, Pallas kernels for 8%

profile of v4, /device:TPU:3, one launch (start us, length us, event | category | flops | bytes accessed | tf_op | source)
XLA Modules:
  0.0 78.7 jit_solution(14145287158340224084)
XLA Ops:
  0.0 1.1 %copy.18 = bf16[128,8,128]{0,2,1:T(8,128)(2,1)S(1)} copy(bf16[128,8,128]{2,1,0:T(8,128)(2,1)} %param.11) | data formatting | bytes 524288 | tf_op args[1]
  1.2 0.2 copy.19
  1.4 0.1 reshape.40
  1.5 0.1 copy.20
  1.7 0.9 %copy-done.6 = bf16[128,32,64]{0,2,1:T(8,128)(2,1)S(1)} copy-done((bf16[128,32,64]{0,2,1:T(8,128)(2,1)S(1)}, bf16[128,32,64]{0,2,1:T(8,128)(2,1)}, u32[]{:S(2)}) %copy-start.6) | copy-done | bytes 524312
  2.5 0.3 copy.21
  2.9 1.4 %collective-permute-start = (bf16[1024,128]{1,0:T(8,128)(2,1)S(1)}, bf16[1024,128]{1,0:T(8,128)(2,1)S(1)}, u32[]{:S(2)}, u32[]{:S(2)}) collective-permute-start(bf16[1024,128]{1,0:T(8,128)(2,1)S(1)} %pad_maximum_fusion.1), channel_id=1, source_target_pairs={{0,1},{1,0},{2,3},{3,2},{4,5},{5,4},{6,7},{7,6},{8,9},{9,8},{10,11... | collective-permute-start | bytes 786440 | tf_op jit(solution)/shard_map/ppermute | solution.py:186
  4.3 0.1 copy.22
  4.4 5.7 %collective-permute-done.refs_2_ = bf16[1024,128]{1,0:T(8,128)(2,1)S(1)} collective-permute-done((bf16[1024,128]{1,0:T(8,128)(2,1)S(1)}, bf16[1024,128]{1,0:T(8,128)(2,1)S(1)}, u32[]{:S(2)}, u32[]{:S(2)}) %collective-permute-start) | collective-permute-done | bytes 262176 | tf_op jit(solution)/shard_map/ppermute | solution.py:186
  10.2 0.1 pad_maximum_fusion.5
  10.3 2.4 %collective-permute-start.1 = (bf16[1024,128]{1,0:T(8,128)(2,1)S(1)}, bf16[1024,128]{1,0:T(8,128)(2,1)S(1)}, u32[]{:S(2)}, u32[]{:S(2)}) collective-permute-start(bf16[1024,128]{1,0:T(8,128)(2,1)S(1)} %get-tuple-element.34), channel_id=1, source_target_pairs={{0,2},{1,3},{2,0},{3,1},{4,6},{5,7},{6,4},{7,5},{8,10},{9,11},{10,... | collective-permute-start | bytes 786440 | tf_op jit(solution)/shard_map/ppermute | solution.py:186
  12.7 0.2 constant_dynamic-slice_fusion.3
  12.9 1.8 %collective-permute-start.2 = (bf16[1024,128]{1,0:T(8,128)(2,1)S(1)}, bf16[1024,128]{1,0:T(8,128)(2,1)S(1)}, u32[]{:S(2)}, u32[]{:S(2)}) collective-permute-start(bf16[1024,128]{1,0:T(8,128)(2,1)S(1)} %get-tuple-element.35), channel_id=1, source_target_pairs={{0,3},{1,2},{2,1},{3,0},{4,7},{5,6},{6,5},{7,4},{8,11},{9,10},{10,... | collective-permute-start | bytes 786440 | tf_op jit(solution)/shard_map/ppermute | solution.py:186
  14.7 0.1 copy_bitcast_fusion.3
  14.8 0.3 collective-permute-start.9
  15.1 2.1 %collective-permute-start.3 = (bf16[1024,128]{1,0:T(8,128)(2,1)S(1)}, bf16[1024,128]{1,0:T(8,128)(2,1)S(1)}, u32[]{:S(2)}, u32[]{:S(2)}) collective-permute-start(bf16[1024,128]{1,0:T(8,128)(2,1)S(1)} %get-tuple-element.37), channel_id=1, source_target_pairs={{0,8},{8,0},{16,24},{24,16},{1,9},{9,1},{17,25},{25,17},{2,10},{10... | collective-permute-start | bytes 786440 | tf_op jit(solution)/shard_map/ppermute | solution.py:186
  17.2 1.2 %collective-permute-start.4 = (bf16[1024,128]{1,0:T(8,128)(2,1)S(1)}, bf16[1024,128]{1,0:T(8,128)(2,1)S(1)}, u32[]{:S(2)}, u32[]{:S(2)}) collective-permute-start(bf16[1024,128]{1,0:T(8,128)(2,1)S(1)} %get-tuple-element.33), channel_id=1, source_target_pairs={{0,4},{4,0},{1,5},{5,1},{2,6},{6,2},{3,7},{7,3},{8,12},{12,8},{9,1... | collective-permute-start | bytes 786440 | tf_op jit(solution)/shard_map/ppermute | solution.py:186
  18.5 11.2 %collective-permute-done.1.refs_3_ = bf16[1024,128]{1,0:T(8,128)(2,1)S(1)} collective-permute-done((bf16[1024,128]{1,0:T(8,128)(2,1)S(1)}, bf16[1024,128]{1,0:T(8,128)(2,1)S(1)}, u32[]{:S(2)}, u32[]{:S(2)}) %collective-permute-start.1) | collective-permute-done | bytes 262176 | tf_op jit(solution)/shard_map/ppermute | solution.py:186
  29.7 0.6 collective-permute-start.13
  30.3 2.7 %collective-permute-start.7 = (bf16[512,128]{1,0:T(8,128)(2,1)S(1)}, bf16[512,128]{1,0:T(8,128)(2,1)S(1)}, u32[]{:S(2)}, u32[]{:S(2)}) collective-permute-start(bf16[512,128]{1,0:T(8,128)(2,1)S(1)} %get-tuple-element.26), channel_id=1, source_target_pairs={{0,8},{8,0},{16,24},{24,16},{1,9},{9,1},{17,25},{25,17},{2,10},{10... | collective-permute-start | bytes 393224 | tf_op jit(solution)/shard_map/ppermute | solution.py:186
  33.1 0.7 fusion.2
  33.8 1.2 %collective-permute-start.8 = (bf16[512,128]{1,0:T(8,128)(2,1)S(1)}, bf16[512,128]{1,0:T(8,128)(2,1)S(1)}, u32[]{:S(2)}, u32[]{:S(2)}) collective-permute-start(bf16[512,128]{1,0:T(8,128)(2,1)S(1)} %get-tuple-element.25), channel_id=1, source_target_pairs={{0,4},{4,0},{1,5},{5,1},{2,6},{6,2},{3,7},{7,3},{8,12},{12,8},{9,1... | collective-permute-start | bytes 393224 | tf_op jit(solution)/shard_map/ppermute | solution.py:186
  35.0 1.2 %collective-permute-start.11 = (bf16[512,128]{1,0:T(8,128)(2,1)}, bf16[512,128]{1,0:T(8,128)(2,1)S(1)}, u32[]{:S(2)}, u32[]{:S(2)}) collective-permute-start(bf16[512,128]{1,0:T(8,128)(2,1)} %get-tuple-element.28), channel_id=1, source_target_pairs={{0,16},{8,24},{16,0},{24,8},{1,17},{9,25},{17,1},{25,9},{2,18},{10... | collective-permute-start | bytes 393224 | tf_op jit(solution)/shard_map/ppermute | solution.py:186
  36.2 0.1 copy_bitcast_fusion.1
  36.3 0.5 pad_maximum_fusion.6
  36.9 0.6 collective-permute-start.5
  37.5 1.4 %collective-permute-done.8.refs_10_ = bf16[512,128]{1,0:T(8,128)(2,1)S(1)} collective-permute-done((bf16[512,128]{1,0:T(8,128)(2,1)S(1)}, bf16[512,128]{1,0:T(8,128)(2,1)S(1)}, u32[]{:S(2)}, u32[]{:S(2)}) %collective-permute-start.8) | collective-permute-done | bytes 131104 | tf_op jit(solution)/shard_map/ppermute | solution.py:186
  38.9 1.2 %collective-permute-start.6 = (bf16[512,128]{1,0:T(8,128)(2,1)}, bf16[512,128]{1,0:T(8,128)(2,1)S(1)}, u32[]{:S(2)}, u32[]{:S(2)}) collective-permute-start(bf16[512,128]{1,0:T(8,128)(2,1)} %get-tuple-element.27), channel_id=1, source_target_pairs={{0,4},{4,0},{1,5},{5,1},{2,6},{6,2},{3,7},{7,3},{8,12},{12,8},{9,1... | collective-permute-start | bytes 393224 | tf_op jit(solution)/shard_map/ppermute | solution.py:186
  40.1 1.1 %collective-permute-start.10 = (bf16[1024,128]{1,0:T(8,128)(2,1)S(1)}, bf16[1024,128]{1,0:T(8,128)(2,1)S(1)}, u32[]{:S(2)}, u32[]{:S(2)}) collective-permute-start(bf16[1024,128]{1,0:T(8,128)(2,1)S(1)} %collective-permute-done.9.refs_11_), channel_id=1, source_target_pairs={{0,8},{8,0},{16,24},{24,16},{1,9},{9,1},{17,25},{25,17},{2,10},{10... | collective-permute-start | bytes 786440 | tf_op jit(solution)/shard_map/ppermute | solution.py:186
  41.2 0.1 collective-permute-start.14
  41.3 0.4 collective-permute-start.12
  41.8 0.1 copy.34.refs_19_
  41.9 0.1 copy.33.refs_11_
  42.0 0.1 pad_add_fusion.refs_0_
  42.1 1.3 %collective-permute-done.6.refs_8_ = bf16[512,128]{1,0:T(8,128)(2,1)S(1)} collective-permute-done((bf16[512,128]{1,0:T(8,128)(2,1)}, bf16[512,128]{1,0:T(8,128)(2,1)S(1)}, u32[]{:S(2)}, u32[]{:S(2)}) %collective-permute-start.6) | collective-permute-done | bytes 131104 | tf_op jit(solution)/shard_map/ppermute | solution.py:186
  43.4 3.5 %update_first.1.refs_18_ = f32[16,128,128]{2,1,0:T(8,128)S(1)} custom-call(s32[4]{0:T(128)S(1)} %pad_add_fusion.refs_0_, bf16[1024,128]{1,0:T(8,128)(2,1)S(1)} %get-tuple-element.36.refs_1_, bf16[1024,128]{1,0:T(8,128)(2,1)S(1)} %collective-permute-done.refs_2_, bf16[1024,128]{1,0:T(8,128)(2,1)S(1)} %collective-permute-done.1.refs_3_, ...), custom_call_target="tpu_custom_call" | custom-call | tf_op jit(solution)/shard_map/update_first/pallas_call | solution.py:246
  46.9 0.1 broadcast_in_dim.2.refs_17_
  47.0 3.9 %update_last.1 = (bf16[16,64,128]{2,1,0:T(8,128)(2,1)S(1)}, bf16[16,64,128]{2,1,0:T(8,128)(2,1)S(1)}, bf16[32,16,128]{2,1,0:T(8,128)(2,1)S(1)}, bf16[32,16,128]{...) custom-call(s32[4]{0:T(128)S(1)} %pad_add_fusion.refs_0_, ...), custom_call_target="tpu_custom_call" | custom-call | tf_op jit(solution)/shard_map/update_last/pallas_call | solution.py:258
  50.8 6.2 %collective-permute-start.15 = (bf16[16,64,128]{2,1,0:T(8,128)(2,1)S(1)}, bf16[16,64,128]{2,1,0:T(8,128)(2,1)S(1)}, u32[]{:S(2)}, u32[]{:S(2)}) collective-permute-start(bf16[16,64,128]{2,1,0:T(8,128)(2,1)S(1)} %get-tuple-element.12), channel_id=1, source_target_pairs={{0,2},{1,3},{2,0},{3,1},{4,6},{5,7},{6,4},{7,5},{8,10},{9,11},{10,... | collective-permute-start | bytes 786440 | tf_op jit(solution)/shard_map/ppermute | solution.py:186
  57.0 3.1 %collective-permute-start.18 = (bf16[32,16,128]{2,1,0:T(8,128)(2,1)S(1)}, bf16[32,16,128]{2,1,0:T(8,128)(2,1)S(1)}, u32[]{:S(2)}, u32[]{:S(2)}) collective-permute-start(bf16[32,16,128]{2,1,0:T(8,128)(2,1)S(1)} %get-tuple-element.15), channel_id=1, source_target_pairs={{0,0},{1,1},{2,2},{3,3},{4,16},{5,17},{6,18},{7,19},{8,8},{9,9},{1... | collective-permute-start | bytes 393224 | tf_op jit(solution)/shard_map/ppermute | solution.py:285
  60.1 3.4 %collective-permute-start.19 = (bf16[32,16,128]{2,1,0:T(8,128)(2,1)S(1)}, bf16[32,16,128]{2,1,0:T(8,128)(2,1)S(1)}, u32[]{:S(2)}, u32[]{:S(2)}) collective-permute-start(bf16[32,16,128]{2,1,0:T(8,128)(2,1)S(1)} %get-tuple-element.16), channel_id=1, source_target_pairs={{0,8},{1,9},{2,10},{3,11},{4,24},{5,25},{6,26},{7,27},{8,0},{9,1},... | collective-permute-start | bytes 393224 | tf_op jit(solution)/shard_map/ppermute | solution.py:285
  63.5 2.5 %collective-permute-start.17 = (bf16[32,16,128]{2,1,0:T(8,128)(2,1)S(1)}, bf16[32,16,128]{2,1,0:T(8,128)(2,1)S(1)}, u32[]{:S(2)}, u32[]{:S(2)}) collective-permute-start(bf16[32,16,128]{2,1,0:T(8,128)(2,1)S(1)} %get-tuple-element.14), channel_id=1, source_target_pairs={{0,9},{1,8},{2,11},{3,10},{4,25},{5,24},{6,27},{7,26},{8,1},{9,0},... | collective-permute-start | bytes 393224 | tf_op jit(solution)/shard_map/ppermute | solution.py:285
  66.0 3.3 %collective-permute-done.19.refs_5_ = bf16[32,16,128]{2,1,0:T(8,128)(2,1)S(1)} collective-permute-done((bf16[32,16,128]{2,1,0:T(8,128)(2,1)S(1)}, bf16[32,16,128]{2,1,0:T(8,128)(2,1)S(1)}, u32[]{:S(2)}, u32[]{:S(2)}) %collective-permute-start.19) | collective-permute-done | bytes 131104 | tf_op jit(solution)/shard_map/ppermute | solution.py:285
  69.3 0.7 copy-done.3
  70.0 2.6 %finish.2.refs_11_ = bf16[16,128,128]{2,1,0:T(8,128)(2,1)} custom-call(s32[4]{0:T(128)S(1)} %pad_add_fusion.refs_0_, bf16[16,128,128]{2,1,0:T(8,128)(2,1)S(1)} %copy-done, bf16[16,64,128]{2,1,0:T(8,128)(2,1)S(1)} %get-tuple-element.11.refs_2_, bf16[16,64,128]{2,1,0:T(8,128)(2,1)S(1)} %collective-permute-done.15.refs_3_, ...), custom_call_target="tpu_custom_call" | custom-call | tf_op jit(solution)/shard_map/finish/pallas_call | solution.py:304
  72.7 0.5 collective-permute-done.16.refs_4_
  73.2 2.8 %collective-permute-done.17.refs_5_ = bf16[32,16,128]{2,1,0:T(8,128)(2,1)S(1)} collective-permute-done((bf16[32,16,128]{2,1,0:T(8,128)(2,1)S(1)}, bf16[32,16,128]{2,1,0:T(8,128)(2,1)S(1)}, u32[]{:S(2)}, u32[]{:S(2)}) %collective-permute-start.17) | collective-permute-done | bytes 131104 | tf_op jit(solution)/shard_map/ppermute | solution.py:285
  76.0 2.7 %finish.3 = bf16[16,128,128]{2,1,0:T(8,128)(2,1)} custom-call(s32[4]{0:T(128)S(1)} %pad_add_fusion.refs_0_, bf16[16,128,128]{2,1,0:T(8,128)(2,1)S(1)} %copy-done, bf16[16,64,128]{2,1,0:T(8,128)(2,1)S(1)} %get-tuple-element.11.refs_2_, bf16[16,64,128]{2,1,0:T(8,128)(2,1)S(1)} %collective-permute-done.15.refs_3_, ...), custom_call_target="tpu_custom_call", output_to_operand_aliasing={{}: (11, {})} | custom-call | tf_op jit(solution)/shard_map/finish/pallas_call | solution.py:304
  (37 shorter events, 0.3 us)
Async XLA Ops:
  1.5 1.0 %copy-start.6 = (bf16[128,32,64]{0,2,1:T(8,128)(2,1)S(1)}, bf16[128,32,64]{0,2,1:T(8,128)(2,1)}, u32[]{:S(2)}) copy-start(bf16[128,32,64]{0,2,1:T(8,128)(2,1)} %param.10) | copy-start | bytes 1572868
  2.9 7.2 %collective-permute-start = (bf16[1024,128]{1,0:T(8,128)(2,1)S(1)}, bf16[1024,128]{1,0:T(8,128)(2,1)S(1)}, u32[]{:S(2)}, u32[]{:S(2)}) collective-permute-start(bf16[1024,128]{1,0:T(8,128)(2,1)S(1)} %pad_maximum_fusion.1), channel_id=1, source_target_pairs={{0,1},{1,0},{2,3},{3,2},{4,5},{5,4},{6,7},{7,6},{8,9},{9,8},{10,11... | collective-permute-start | bytes 786440 | tf_op jit(solution)/shard_map/ppermute | solution.py:186
  10.2 2.5 %copy-start.7 = (bf16[1024,128]{1,0:T(8,128)(2,1)S(1)}, bf16[1024,128]{1,0:T(8,128)(2,1)}, u32[]{:S(2)}) copy-start(bf16[1024,128]{1,0:T(8,128)(2,1)} %param.12) | copy-start | bytes 786436
  10.3 19.3 %collective-permute-start.1 = (bf16[1024,128]{1,0:T(8,128)(2,1)S(1)}, bf16[1024,128]{1,0:T(8,128)(2,1)S(1)}, u32[]{:S(2)}, u32[]{:S(2)}) collective-permute-start(bf16[1024,128]{1,0:T(8,128)(2,1)S(1)} %get-tuple-element.34), channel_id=1, source_target_pairs={{0,2},{1,3},{2,0},{3,1},{4,6},{5,7},{6,4},{7,5},{8,10},{9,11},{10,... | collective-permute-start | bytes 786440 | tf_op jit(solution)/shard_map/ppermute | solution.py:186
  12.9 17.4 %collective-permute-start.2 = (bf16[1024,128]{1,0:T(8,128)(2,1)S(1)}, bf16[1024,128]{1,0:T(8,128)(2,1)S(1)}, u32[]{:S(2)}, u32[]{:S(2)}) collective-permute-start(bf16[1024,128]{1,0:T(8,128)(2,1)S(1)} %get-tuple-element.35), channel_id=1, source_target_pairs={{0,3},{1,2},{2,1},{3,0},{4,7},{5,6},{6,5},{7,4},{8,11},{9,10},{10,... | collective-permute-start | bytes 786440 | tf_op jit(solution)/shard_map/ppermute | solution.py:186
  14.8 20.2 %collective-permute-start.9 = (bf16[1024,128]{1,0:T(8,128)(2,1)S(1)}, bf16[1024,128]{1,0:T(8,128)(2,1)S(1)}, u32[]{:S(2)}, u32[]{:S(2)}) collective-permute-start(bf16[1024,128]{1,0:T(8,128)(2,1)S(1)} %get-tuple-element.37), channel_id=1, source_target_pairs={{0,16},{8,24},{16,0},{24,8},{1,17},{9,25},{17,1},{25,9},{2,18},{10... | collective-permute-start | bytes 786440 | tf_op jit(solution)/shard_map/ppermute | solution.py:186
  15.1 21.7 %collective-permute-start.3 = (bf16[1024,128]{1,0:T(8,128)(2,1)S(1)}, bf16[1024,128]{1,0:T(8,128)(2,1)S(1)}, u32[]{:S(2)}, u32[]{:S(2)}) collective-permute-start(bf16[1024,128]{1,0:T(8,128)(2,1)S(1)} %get-tuple-element.37), channel_id=1, source_target_pairs={{0,8},{8,0},{16,24},{24,16},{1,9},{9,1},{17,25},{25,17},{2,10},{10... | collective-permute-start | bytes 786440 | tf_op jit(solution)/shard_map/ppermute | solution.py:186
  17.2 16.5 %collective-permute-start.4 = (bf16[1024,128]{1,0:T(8,128)(2,1)S(1)}, bf16[1024,128]{1,0:T(8,128)(2,1)S(1)}, u32[]{:S(2)}, u32[]{:S(2)}) collective-permute-start(bf16[1024,128]{1,0:T(8,128)(2,1)S(1)} %get-tuple-element.33), channel_id=1, source_target_pairs={{0,4},{4,0},{1,5},{5,1},{2,6},{6,2},{3,7},{7,3},{8,12},{12,8},{9,1... | collective-permute-start | bytes 786440 | tf_op jit(solution)/shard_map/ppermute | solution.py:186
  29.7 10.4 %collective-permute-start.13 = (bf16[512,128]{1,0:T(8,128)(2,1)S(1)}, bf16[512,128]{1,0:T(8,128)(2,1)S(1)}, u32[]{:S(2)}, u32[]{:S(2)}) collective-permute-start(bf16[512,128]{1,0:T(8,128)(2,1)S(1)} %get-tuple-element.26), channel_id=1, source_target_pairs={{0,16},{8,24},{16,0},{24,8},{1,17},{9,25},{17,1},{25,9},{2,18},{10... | collective-permute-start | bytes 393224 | tf_op jit(solution)/shard_map/ppermute | solution.py:186
  30.3 10.9 %collective-permute-start.7 = (bf16[512,128]{1,0:T(8,128)(2,1)S(1)}, bf16[512,128]{1,0:T(8,128)(2,1)S(1)}, u32[]{:S(2)}, u32[]{:S(2)}) collective-permute-start(bf16[512,128]{1,0:T(8,128)(2,1)S(1)} %get-tuple-element.26), channel_id=1, source_target_pairs={{0,8},{8,0},{16,24},{24,16},{1,9},{9,1},{17,25},{25,17},{2,10},{10... | collective-permute-start | bytes 393224 | tf_op jit(solution)/shard_map/ppermute | solution.py:186
  33.8 5.1 %collective-permute-start.8 = (bf16[512,128]{1,0:T(8,128)(2,1)S(1)}, bf16[512,128]{1,0:T(8,128)(2,1)S(1)}, u32[]{:S(2)}, u32[]{:S(2)}) collective-permute-start(bf16[512,128]{1,0:T(8,128)(2,1)S(1)} %get-tuple-element.25), channel_id=1, source_target_pairs={{0,4},{4,0},{1,5},{5,1},{2,6},{6,2},{3,7},{7,3},{8,12},{12,8},{9,1... | collective-permute-start | bytes 393224 | tf_op jit(solution)/shard_map/ppermute | solution.py:186
  35.0 6.3 %collective-permute-start.11 = (bf16[512,128]{1,0:T(8,128)(2,1)}, bf16[512,128]{1,0:T(8,128)(2,1)S(1)}, u32[]{:S(2)}, u32[]{:S(2)}) collective-permute-start(bf16[512,128]{1,0:T(8,128)(2,1)} %get-tuple-element.28), channel_id=1, source_target_pairs={{0,16},{8,24},{16,0},{24,8},{1,17},{9,25},{17,1},{25,9},{2,18},{10... | collective-permute-start | bytes 393224 | tf_op jit(solution)/shard_map/ppermute | solution.py:186
  36.9 6.5 %collective-permute-start.5 = (bf16[512,128]{1,0:T(8,128)(2,1)}, bf16[512,128]{1,0:T(8,128)(2,1)S(1)}, u32[]{:S(2)}, u32[]{:S(2)}) collective-permute-start(bf16[512,128]{1,0:T(8,128)(2,1)} %get-tuple-element.28), channel_id=1, source_target_pairs={{0,8},{8,0},{16,24},{24,16},{1,9},{9,1},{17,25},{25,17},{2,10},{10... | collective-permute-start | bytes 393224 | tf_op jit(solution)/shard_map/ppermute | solution.py:186
  38.9 4.5 %collective-permute-start.6 = (bf16[512,128]{1,0:T(8,128)(2,1)}, bf16[512,128]{1,0:T(8,128)(2,1)S(1)}, u32[]{:S(2)}, u32[]{:S(2)}) collective-permute-start(bf16[512,128]{1,0:T(8,128)(2,1)} %get-tuple-element.27), channel_id=1, source_target_pairs={{0,4},{4,0},{1,5},{5,1},{2,6},{6,2},{3,7},{7,3},{8,12},{12,8},{9,1... | collective-permute-start | bytes 393224 | tf_op jit(solution)/shard_map/ppermute | solution.py:186
  40.1 6.7 %collective-permute-start.10 = (bf16[1024,128]{1,0:T(8,128)(2,1)S(1)}, bf16[1024,128]{1,0:T(8,128)(2,1)S(1)}, u32[]{:S(2)}, u32[]{:S(2)}) collective-permute-start(bf16[1024,128]{1,0:T(8,128)(2,1)S(1)} %collective-permute-done.9.refs_11_), channel_id=1, source_target_pairs={{0,8},{8,0},{16,24},{24,16},{1,9},{9,1},{17,25},{25,17},{2,10},{10... | collective-permute-start | bytes 786440 | tf_op jit(solution)/shard_map/ppermute | solution.py:186
  41.2 5.6 %collective-permute-start.14 = (bf16[512,128]{1,0:T(8,128)(2,1)S(1)}, bf16[512,128]{1,0:T(8,128)(2,1)S(1)}, u32[]{:S(2)}, u32[]{:S(2)}) collective-permute-start(bf16[512,128]{1,0:T(8,128)(2,1)S(1)} %collective-permute-done.13.refs_15_), channel_id=1, source_target_pairs={{0,8},{8,0},{16,24},{24,16},{1,9},{9,1},{17,25},{25,17},{2,10},{10... | collective-permute-start | bytes 393224 | tf_op jit(solution)/shard_map/ppermute | solution.py:186
  41.3 5.6 %collective-permute-start.12 = (bf16[512,128]{1,0:T(8,128)(2,1)S(1)}, bf16[512,128]{1,0:T(8,128)(2,1)S(1)}, u32[]{:S(2)}, u32[]{:S(2)}) collective-permute-start(bf16[512,128]{1,0:T(8,128)(2,1)S(1)} %collective-permute-done.11.refs_13_), channel_id=1, source_target_pairs={{0,8},{8,0},{16,24},{24,16},{1,9},{9,1},{17,25},{25,17},{2,10},{10... | collective-permute-start | bytes 393224 | tf_op jit(solution)/shard_map/ppermute | solution.py:186
  43.4 3.5 %copy-start.8 = (f32[128]{0:T(128)S(1)}, f32[128]{0:T(128)}, u32[]{:S(2)}) copy-start(f32[128]{0:T(128)} %param.13) | copy-start | bytes 1540
  46.9 22.4 %copy-start = (bf16[16,128,128]{2,1,0:T(8,128)(2,1)S(1)}, bf16[16,128,128]{2,1,0:T(8,128)(2,1)}, u32[]{:S(2)}) copy-start(bf16[16,128,128]{2,1,0:T(8,128)(2,1)} %refs_1_.3) | copy-start | bytes 1572868
  46.9 22.4 %copy-start.1 = (bf16[128,512]{1,0:T(8,128)(2,1)S(1)}, bf16[128,512]{1,0:T(8,128)(2,1)}, u32[]{:S(2)}) copy-start(bf16[128,512]{1,0:T(8,128)(2,1)} %refs_7_.3) | copy-start | bytes 393220
  47.0 22.4 %copy-start.2 = (bf16[512,128]{1,0:T(8,128)(2,1)S(1)}, bf16[512,128]{1,0:T(8,128)(2,1)}, u32[]{:S(2)}) copy-start(bf16[512,128]{1,0:T(8,128)(2,1)} %refs_9_.3) | copy-start | bytes 393220
  50.8 18.5 %collective-permute-start.15 = (bf16[16,64,128]{2,1,0:T(8,128)(2,1)S(1)}, bf16[16,64,128]{2,1,0:T(8,128)(2,1)S(1)}, u32[]{:S(2)}, u32[]{:S(2)}) collective-permute-start(bf16[16,64,128]{2,1,0:T(8,128)(2,1)S(1)} %get-tuple-element.12), channel_id=1, source_target_pairs={{0,2},{1,3},{2,0},{3,1},{4,6},{5,7},{6,4},{7,5},{8,10},{9,11},{10,... | collective-permute-start | bytes 786440 | tf_op jit(solution)/shard_map/ppermute | solution.py:186
  57.0 8.9 %collective-permute-start.18 = (bf16[32,16,128]{2,1,0:T(8,128)(2,1)S(1)}, bf16[32,16,128]{2,1,0:T(8,128)(2,1)S(1)}, u32[]{:S(2)}, u32[]{:S(2)}) collective-permute-start(bf16[32,16,128]{2,1,0:T(8,128)(2,1)S(1)} %get-tuple-element.15), channel_id=1, source_target_pairs={{0,0},{1,1},{2,2},{3,3},{4,16},{5,17},{6,18},{7,19},{8,8},{9,9},{1... | collective-permute-start | bytes 393224 | tf_op jit(solution)/shard_map/ppermute | solution.py:285
  60.1 9.1 %collective-permute-start.19 = (bf16[32,16,128]{2,1,0:T(8,128)(2,1)S(1)}, bf16[32,16,128]{2,1,0:T(8,128)(2,1)S(1)}, u32[]{:S(2)}, u32[]{:S(2)}) collective-permute-start(bf16[32,16,128]{2,1,0:T(8,128)(2,1)S(1)} %get-tuple-element.16), channel_id=1, source_target_pairs={{0,8},{1,9},{2,10},{3,11},{4,24},{5,25},{6,26},{7,27},{8,0},{9,1},... | collective-permute-start | bytes 393224 | tf_op jit(solution)/shard_map/ppermute | solution.py:285
  63.5 9.7 %collective-permute-start.16 = (bf16[32,16,128]{2,1,0:T(8,128)(2,1)S(1)}, bf16[32,16,128]{2,1,0:T(8,128)(2,1)S(1)}, u32[]{:S(2)}, u32[]{:S(2)}) collective-permute-start(bf16[32,16,128]{2,1,0:T(8,128)(2,1)S(1)} %get-tuple-element.13), channel_id=1, source_target_pairs={{0,1},{1,0},{2,3},{3,2},{4,17},{5,16},{6,19},{7,18},{8,9},{9,8},{1... | collective-permute-start | bytes 393224 | tf_op jit(solution)/shard_map/ppermute | solution.py:285
  63.5 12.5 %collective-permute-start.17 = (bf16[32,16,128]{2,1,0:T(8,128)(2,1)S(1)}, bf16[32,16,128]{2,1,0:T(8,128)(2,1)S(1)}, u32[]{:S(2)}, u32[]{:S(2)}) collective-permute-start(bf16[32,16,128]{2,1,0:T(8,128)(2,1)S(1)} %get-tuple-element.14), channel_id=1, source_target_pairs={{0,9},{1,8},{2,11},{3,10},{4,25},{5,24},{6,27},{7,26},{8,1},{9,0},... | collective-permute-start | bytes 393224 | tf_op jit(solution)/shard_map/ppermute | solution.py:285
  69.3 0.7 copy-start.3
  69.3 0.7 copy-start.4
  69.3 0.7 copy-start.5

commit v5 on v4

--- a/solution.py
+++ b/solution.py
@@ -93,18 +93,16 @@
 
 def finish_kernel(low, dz, *refs):
     place_ref, pair_ref, own_ref, other_ref, mirror_low, mirror_high = refs[:6]
-    gain_ref, up_ref, up_bias_ref, down_ref, down_bias_ref = refs[6:11]
+    up_ref, down_ref, vector_ref, swap_ref = refs[6:10]
     out_ref, middle_ref, done_ref, sems = refs[-4:]
     mirror_refs = (mirror_low, mirror_high)
     run, columns, pair_channels = pair_ref.shape
     half = columns // 2
     core, z_low, z_high = place_ref[0], place_ref[1], place_ref[3]
     cells = run * run
-    to = lax.broadcasted_iota(jnp.int32, (cells, cells), 0)
-    of = lax.broadcasted_iota(jnp.int32, (cells, cells), 1)
-    swap_cells = jnp.where(
-        jnp.logical_and(to // run == of % run, to % run == of // run), 1.0, 0.0
-    ).astype(jnp.bfloat16)
+    gain = vector_ref[:, :pair_channels]
+    down_bias = vector_ref[:, pair_channels : 2 * pair_channels]
+    up_bias = vector_ref[:, 2 * pair_channels :]
     begins = []
     for flip in range(2):
         for part in range(2):
@@ -116,7 +114,7 @@
             begins.append(begin)
             piece = mirror_refs[flip][part * run : (part + 1) * run]
             mirrored = jnp.dot(
-                swap_cells,
+                swap_ref[...],
                 piece.reshape(cells, pair_channels),
                 preferred_element_type=jnp.float32,
             )
@@ -134,13 +132,13 @@
     center = jnp.mean(values, axis=1, keepdims=True)
     moved = values - center
     spread = jnp.mean(jnp.square(moved), axis=1, keepdims=True)
-    normed = moved * lax.rsqrt(spread + epsilon) * gain_ref[...]
+    normed = moved * lax.rsqrt(spread + epsilon) * gain
     hidden = jnp.dot(
         normed.astype(jnp.bfloat16), up_ref[...], preferred_element_type=jnp.float32
     )
-    hidden = jnp.maximum(hidden + up_bias_ref[...], 0.0).astype(jnp.bfloat16)
+    hidden = jnp.maximum(hidden + up_bias, 0.0).astype(jnp.bfloat16)
     result = jnp.dot(hidden, down_ref[...], preferred_element_type=jnp.float32)
-    result = (values + result + down_bias_ref[...]).astype(jnp.bfloat16)
+    result = (values + result + down_bias).astype(jnp.bfloat16)
     done_ref[...] = result.reshape(4, run, run, pair_channels)
     copies = [
         pltpu.make_async_copy(
@@ -193,37 +191,66 @@
     left = left.transpose(1, 0, 2, 3, 4).reshape(low, cols, share_rows, group_len)
     left = pick(left, col, 1)
 
-    def packed(dz):
-        return jnp.concatenate(
-            [pick(right, z_high ^ (dz // low)), pick(left, z_low ^ (dz % low))], axis=0
-        )
-
-    order = [0, 1] + list(range(groups - 1, 1, -1))
-    held = {dz: packed(dz) if dz == 0 else swap(packed(dz), "seq", groups, dz) for dz in order}
-    bundles = [order[:2]] + [[dz] for dz in order[2:]]
-    data, left_places, right_places, other_places = [], {}, {}, {}
-    for dz in range(groups):
-        left_places[dz] = [(len(data), source_rows)]
-        right_places[dz] = [(len(data), 0)]
-        other_places[dz] = []
+    blocks = [
+        (pick(right, z_high ^ (dz // low)), pick(left, z_low ^ (dz % low))) for dz in range(groups)
+    ]
+    packs = [jnp.concatenate(pair, axis=0) for pair in blocks[:2] + blocks[3:]]
+    packs = lax.optimization_barrier(packs + list(blocks[2]))
+    own, packs, (final_right, final_left) = packs[0], packs[1:-2], packs[-2:]
+    partners = [1] + list(range(3, groups))
+    held = {dz: swap(pack, "seq", groups, dz) for dz, pack in zip(partners, packs)}
+    final_left = swap(final_left, "seq", groups, 2)
+    final_right = swap(final_right, "seq", groups, 2)
+    held[0], _ = lax.optimization_barrier((own, held[1]))
+    data, others = [], []
+    left_places = {dz: [] for dz in range(groups)}
+    right_places = {dz: [] for dz in range(groups)}
+    other_places = {dz: [] for dz in range(groups)}
+
+    def place_in(store, table, value, bundle, size):
+        for position, dz in enumerate(bundle):
+            table[dz].append((len(store), position * size))
+        store.append(value)
+
+    for dz in [0] + partners:
+        left_places[dz].append((len(data), source_rows))
+        right_places[dz].append((len(data), 0))
         data.append(held[dz])
-    others = []
+    place_in(data, left_places, final_left, [2], share_rows)
+    place_in(data, right_places, final_right, [2], source_rows)
+
+    bundles = [[0, 1]] + [[dz] for dz in partners[1:]] + [[2]]
+    rights, crosses = [], {dx: [] for dx in range(1, xs)}
+    chain = None
     for bundle in bundles:
-        rights = jnp.concatenate([held[dz][:source_rows] for dz in bundle], axis=0)
-        lefts = jnp.concatenate([held[dz][source_rows:] for dz in bundle], axis=0)
-        for position, dz in enumerate(bundle):
-            right_places[dz].append((len(data), position * source_rows))
-        data.append(swap(rights, "row", rows, 1))
+        if bundle == [2]:
+            value, lefts = final_right, final_left
+        elif len(bundle) > 1:
+            value = jnp.concatenate([held[dz][:source_rows] for dz in bundle], axis=0)
+            lefts = jnp.concatenate([held[dz][source_rows:] for dz in bundle], axis=0)
+        else:
+            value, lefts = held[bundle[0]][:source_rows], held[bundle[0]][source_rows:]
+        rights.append(value)
         for dy in range(1, cols):
-            for position, dz in enumerate(bundle):
-                left_places[dz].append((len(data), position * share_rows))
-            data.append(swap(lefts, "col", cols, dy))
+            place_in(data, left_places, swap(lefts, "col", cols, dy), bundle, share_rows)
         for dx in range(1, xs):
-            crossed = swap(rights, "row", rows, 2 * dx)
-            for value in (crossed, swap(crossed, "row", rows, 1)):
-                for position, dz in enumerate(bundle):
-                    other_places[dz].append((len(others), position * source_rows))
-                others.append(value)
+            if chain is not None:
+                value, _ = lax.optimization_barrier((value, chain))
+            chain = swap(value, "row", rows, 2 * dx)
+            crosses[dx].append(chain)
+
+    early = [dz for bundle in bundles[:-1] for dz in bundle]
+    place_in(
+        data, right_places, swap(jnp.concatenate(rights[:-1], axis=0), "row", rows, 1), early,
+        source_rows,
+    )
+    place_in(data, right_places, swap(rights[-1], "row", rows, 1), [2], source_rows)
+    for dx in range(1, xs):
+        for value, bundle in zip(crosses[dx], bundles):
+            place_in(others, other_places, value, bundle, source_rows)
+        value = swap(jnp.concatenate(crosses[dx][:-1], axis=0), "row", rows, 1)
+        place_in(others, other_places, value, early, source_rows)
+        place_in(others, other_places, swap(crosses[dx][-1], "row", rows, 1), [2], source_rows)
 
     weight = proj_weight.reshape(channels, rows, e1, 2, pair_channels)
     weight = weight.transpose(1, 3, 4, 2, 0)
@@ -284,6 +311,10 @@
                         pairs.append((source, target))
             mirrors.append(lax.ppermute(outs[2 + 2 * dz + flip], axes, pairs))
 
+    vectors = jnp.concatenate([norm_gain, down_bias, up_bias]).reshape(1, -1)
+    cell = jnp.arange(run * run)
+    mirror_cell = cell % run * run + cell // run
+    swap_cells = (mirror_cell[:, None] == cell[None, :]).astype(bf16)
     anywhere = pl.BlockSpec(memory_space=pl.ANY)
     result = None
     for dz in range(low):
@@ -294,24 +325,23 @@
             update_other,
             mirrors[2 * dz],
             mirrors[2 * dz + 1],
-            norm_gain.reshape(1, -1),
             up_weight,
-            up_bias.reshape(1, -1),
             down_weight,
-            down_bias.reshape(1, -1),
+            vectors,
+            swap_cells,
         ]
         extra = [] if result is None else [result]
         result = pl.pallas_call(
             functools.partial(finish_kernel, low, dz),
             out_shape=jax.ShapeDtypeStruct(pair_rep.shape, bf16),
-            in_specs=[smem] + [vmem] * 10 + [anywhere] * len(extra),
+            in_specs=[smem] + [vmem] * 9 + [anywhere] * len(extra),
             out_specs=anywhere,
             scratch_shapes=[
                 pltpu.VMEM((4 * run * run, pair_channels), bf16),
                 pltpu.VMEM((4, run, run, pair_channels), bf16),
                 pltpu.SemaphoreType.DMA((4,)),
             ],
-            input_output_aliases={11: 0} if extra else {},
+            input_output_aliases={10: 0} if extra else {},
             compiler_params=params,
             name="finish",
         )(*operands, *extra)

time: 78.9 us -> 76.4 us (0.968)
  starting transfers between devices: 33.5 us -> 23.7 us
  waiting for transfers between devices: 26.4 us -> 31.2 us
  other arithmetic: 0.71 us -> 3.04 us
    ppermute x16 -> x15, starting transfers between devices: 24.6 us -> 14.2 us  [swap(): return lax.ppermute(value, name, [(i, i ^ flip) for i in range(size)])]
    ppermute x16 -> x15, waiting for transfers between devices: 19.8 us -> 25.9 us  [swap(): return lax.ppermute(value, name, [(i, i ^ flip) for i in range(size)])]
    concatenate x1 -> x5, other arithmetic: 0.02 us -> 1.66 us  [the longest x1 0.77 us: on_device(): value = swap(jnp.concatenate(crosses[dx][:-1], axis=0), 'row', rows, 1)]
    ppermute x4, waiting for transfers between devices: 6.64 us -> 5.32 us  [on_device(): mirrors.append(lax.ppermute(outs[2 + 2 * dz + flip], axes, pairs))]
  transfers between devices with their start and end apart: 20 -> 19, of which waited for: 8 -> 9; matrix products, arithmetic and copies ran while one was open for 3% -> 6% of each run, Pallas kernels for 8% -> 8%
where the time goes in v5:
time: 76.4 us; the launch traced here: 75.8 us
  waiting for transfers between devices  31.2 us (41%)
  starting transfers between devices  23.7 us (31%)
  Pallas kernels  12.6 us (16%)
  local copies, waits for them, and re-layouts  4.81 us (6%)
  other arithmetic  3.04 us (4%)
    ppermute x15, waiting for transfers between devices, swap(): return lax.ppermute(value, name, [(i, i ^ flip) for i in range(size)])  25.9 us
    ppermute x15, starting transfers between devices, swap(): return lax.ppermute(value, name, [(i, i ^ flip) for i in range(size)])  14.2 us
    ppermute x4, starting transfers between devices, on_device(): mirrors.append(lax.ppermute(outs[2 + 2 * dz + flip], axes, pairs))  9.54 us
    ppermute x4, waiting for transfers between devices, on_device(): mirrors.append(lax.ppermute(outs[2 + 2 * dz + flip], axes, pairs))  5.32 us
    pallas_call x2, Pallas kernels, on_device(): pl.pallas_call(functools.partial(finish_kernel, low, dz), out_shape=jax.S...  5.25 us
    pallas_call x1, Pallas kernels, on_device(): pl.pallas_call(functools.partial(update_kernel, places, cols, low, True,...  3.88 us
    pallas_call x1, Pallas kernels, on_device(): pl.pallas_call(functools.partial(update_kernel, places, cols, low, False,...  3.47 us
    unnamed x22, local copies, waits for them, and re-layouts  2.7 us
  transfers between devices with their start and end apart: 19, of which 9 were waited for; matrix products, arithmetic and copies ran while one was open for 6% of the time, Pallas kernels for 8%

profile of v5, /device:TPU:3, one launch (start us, length us, event | category | flops | bytes accessed | tf_op | source)
XLA Modules:
  0.0 75.8 jit_solution(5572910864371437766)
XLA Ops:
  0.0 1.1 %copy.18 = bf16[128,8,128]{0,2,1:T(8,128)(2,1)S(1)} copy(bf16[128,8,128]{2,1,0:T(8,128)(2,1)} %param.11) | data formatting | bytes 524288 | tf_op args[1]
  1.2 0.2 copy.19
  1.4 0.1 reshape.53
  1.5 0.1 copy.22
  1.7 0.1 copy.20
  1.8 0.7 copy-done.3
  2.5 0.3 copy.21
  3.0 1.4 %collective-permute-start = (bf16[1024,128]{1,0:T(8,128)(2,1)S(1)}, bf16[1024,128]{1,0:T(8,128)(2,1)S(1)}, u32[]{:S(2)}, u32[]{:S(2)}) collective-permute-start(bf16[1024,128]{1,0:T(8,128)(2,1)S(1)} %get-tuple-element.20), channel_id=1, source_target_pairs={{0,1},{1,0},{2,3},{3,2},{4,5},{5,4},{6,7},{7,6},{8,9},{9,8},{10,11... | collective-permute-start | bytes 786440 | tf_op jit(solution)/shard_map/ppermute | solution.py:184
  4.4 2.2 %collective-permute-start.1 = (bf16[1024,128]{1,0:T(8,128)(2,1)S(1)}, bf16[1024,128]{1,0:T(8,128)(2,1)S(1)}, u32[]{:S(2)}, u32[]{:S(2)}) collective-permute-start(bf16[1024,128]{1,0:T(8,128)(2,1)S(1)} %get-tuple-element.22), channel_id=1, source_target_pairs={{0,3},{1,2},{2,1},{3,0},{4,7},{5,6},{6,5},{7,4},{8,11},{9,10},{10,... | collective-permute-start | bytes 786440 | tf_op jit(solution)/shard_map/ppermute | solution.py:184
  6.6 0.1 collective-permute-start.2
  6.7 2.2 %collective-permute-start.3 = (bf16[512,128]{1,0:T(8,128)(2,1)S(1)}, bf16[512,128]{1,0:T(8,128)(2,1)S(1)}, u32[]{:S(2)}, u32[]{:S(2)}) collective-permute-start(bf16[512,128]{1,0:T(8,128)(2,1)S(1)} %bitcast.50), channel_id=1, source_target_pairs={{0,2},{1,3},{2,0},{3,1},{4,6},{5,7},{6,4},{7,5},{8,10},{9,11},{10,... | collective-permute-start | bytes 393224 | tf_op jit(solution)/shard_map/ppermute | solution.py:184
  8.9 0.2 constant_dynamic-slice_fusion.3
  9.1 0.1 copy_bitcast_fusion.1
  9.3 0.9 %collective-permute-done.refs_2_ = bf16[1024,128]{1,0:T(8,128)(2,1)S(1)} collective-permute-done((bf16[1024,128]{1,0:T(8,128)(2,1)S(1)}, bf16[1024,128]{1,0:T(8,128)(2,1)S(1)}, u32[]{:S(2)}, u32[]{:S(2)}) %collective-permute-start) | collective-permute-done | bytes 262176 | tf_op jit(solution)/shard_map/ppermute | solution.py:184
  10.3 0.5 collective-permute-start.9
  10.8 0.5 pad_maximum_fusion.7
  11.3 15.1 %collective-permute-done.2.refs_4_ = bf16[512,128]{1,0:T(8,128)(2,1)S(1)} collective-permute-done((bf16[512,128]{1,0:T(8,128)(2,1)S(1)}, bf16[512,128]{1,0:T(8,128)(2,1)S(1)}, u32[]{:S(2)}, u32[]{:S(2)}) %collective-permute-start.2) | collective-permute-done | bytes 131104 | tf_op jit(solution)/shard_map/ppermute | solution.py:184
  26.4 1.2 %collective-permute-start.6 = (bf16[512,128]{1,0:T(8,128)(2,1)S(1)}, bf16[512,128]{1,0:T(8,128)(2,1)S(1)}, u32[]{:S(2)}, u32[]{:S(2)}) collective-permute-start(bf16[512,128]{1,0:T(8,128)(2,1)S(1)} %collective-permute-done.2.refs_4_), channel_id=1, source_target_pairs={{0,4},{4,0},{1,5},{5,1},{2,6},{6,2},{3,7},{7,3},{8,12},{12,8},{9,1... | collective-permute-start | bytes 393224 | tf_op jit(solution)/shard_map/ppermute | solution.py:184
  27.7 1.6 %collective-permute-done.3.refs_5_ = bf16[512,128]{1,0:T(8,128)(2,1)S(1)} collective-permute-done((bf16[512,128]{1,0:T(8,128)(2,1)S(1)}, bf16[512,128]{1,0:T(8,128)(2,1)S(1)}, u32[]{:S(2)}, u32[]{:S(2)}) %collective-permute-start.3) | collective-permute-done | bytes 131104 | tf_op jit(solution)/shard_map/ppermute | solution.py:184
  29.3 1.5 %collective-permute-start.8 = (bf16[512,128]{1,0:T(8,128)(2,1)S(1)}, bf16[512,128]{1,0:T(8,128)(2,1)S(1)}, u32[]{:S(2)}, u32[]{:S(2)}) collective-permute-start(bf16[512,128]{1,0:T(8,128)(2,1)S(1)} %collective-permute-done.3.refs_5_), channel_id=1, source_target_pairs={{0,8},{8,0},{16,24},{24,16},{1,9},{9,1},{17,25},{25,17},{2,10},{10... | collective-permute-start | bytes 393224 | tf_op jit(solution)/shard_map/ppermute | solution.py:184
  30.8 0.7 fusion.8
  31.5 0.3 collective-permute-start.10
  31.7 0.8 %pad_maximum_fusion = bf16[1536,128]{1,0:T(8,128)(2,1)} fusion(bf16[512,128]{1,0:T(8,128)(2,1)S(1)} %get-tuple-element.25, bf16[512,128]{1,0:T(8,128)(2,1)S(1)} %get-tuple-element.53, bf16[512,128]{1,0:T(8,128)(2,1)S(1)} %get-tuple-element.41), kind=kLoop, calls=%fused_computation | loop fusion | flops 1179648 | bytes 786432 | tf_op jit(solution)/shard_map/concatenate | solution.py:244
  32.5 0.3 collective-permute-start.7
  32.8 0.7 pad_maximum_fusion.5
  33.5 1.2 %collective-permute-start.4 = (bf16[1024,128]{1,0:T(8,128)(2,1)}, bf16[1024,128]{1,0:T(8,128)(2,1)S(1)}, u32[]{:S(2)}, u32[]{:S(2)}) collective-permute-start(bf16[1024,128]{1,0:T(8,128)(2,1)} %pad_maximum_fusion.5), channel_id=1, source_target_pairs={{0,4},{4,0},{1,5},{5,1},{2,6},{6,2},{3,7},{7,3},{8,12},{12,8},{9,1... | collective-permute-start | bytes 786440 | tf_op jit(solution)/shard_map/ppermute | solution.py:184
  34.8 1.8 %collective-permute-done.10.refs_12_ = bf16[512,128]{1,0:T(8,128)(2,1)S(1)} collective-permute-done((bf16[512,128]{1,0:T(8,128)(2,1)S(1)}, bf16[512,128]{1,0:T(8,128)(2,1)S(1)}, u32[]{:S(2)}, u32[]{:S(2)}) %collective-permute-start.10) | collective-permute-done | bytes 131104 | tf_op jit(solution)/shard_map/ppermute | solution.py:184
  36.6 0.8 %pad_maximum_fusion.1 = bf16[1536,128]{1,0:T(8,128)(2,1)} fusion(bf16[512,128]{1,0:T(8,128)(2,1)S(1)} %collective-permute-done.10.refs_12_, bf16[1024,128]{1,0:T(8,128)(2,1)S(1)} %collective-permute-done.9.refs_11_), kind=kLoop, calls=%fused_computation.1 | loop fusion | flops 786432 | bytes 786432 | tf_op jit(solution)/shard_map/concatenate | solution.py:251
  37.4 0.8 %collective-permute-start.12 = (bf16[1536,128]{1,0:T(8,128)(2,1)}, bf16[1536,128]{1,0:T(8,128)(2,1)S(1)}, u32[]{:S(2)}, u32[]{:S(2)}) collective-permute-start(bf16[1536,128]{1,0:T(8,128)(2,1)} %pad_maximum_fusion.1), channel_id=1, source_target_pairs={{0,8},{8,0},{16,24},{24,16},{1,9},{9,1},{17,25},{25,17},{2,10},{10... | collective-permute-start | bytes 1179656 | tf_op jit(solution)/shard_map/ppermute | solution.py:184
  38.2 0.3 collective-permute-start.11
  38.5 1.3 %collective-permute-start.5 = (bf16[512,128]{1,0:T(8,128)(2,1)}, bf16[512,128]{1,0:T(8,128)(2,1)S(1)}, u32[]{:S(2)}, u32[]{:S(2)}) collective-permute-start(bf16[512,128]{1,0:T(8,128)(2,1)} %get-tuple-element.46), channel_id=1, source_target_pairs={{0,4},{4,0},{1,5},{5,1},{2,6},{6,2},{3,7},{7,3},{8,12},{12,8},{9,1... | collective-permute-start | bytes 393224 | tf_op jit(solution)/shard_map/ppermute | solution.py:184
  39.8 3.5 %collective-permute-done.11.refs_13_ = bf16[512,128]{1,0:T(8,128)(2,1)S(1)} collective-permute-done((bf16[512,128]{1,0:T(8,128)(2,1)S(1)}, bf16[512,128]{1,0:T(8,128)(2,1)S(1)}, u32[]{:S(2)}, u32[]{:S(2)}) %collective-permute-start.11) | collective-permute-done | bytes 131104 | tf_op jit(solution)/shard_map/ppermute | solution.py:184
  43.3 0.8 %collective-permute-start.13 = (bf16[512,128]{1,0:T(8,128)(2,1)S(1)}, bf16[512,128]{1,0:T(8,128)(2,1)S(1)}, u32[]{:S(2)}, u32[]{:S(2)}) collective-permute-start(bf16[512,128]{1,0:T(8,128)(2,1)S(1)} %collective-permute-done.11.refs_13_), channel_id=1, source_target_pairs={{0,8},{8,0},{16,24},{24,16},{1,9},{9,1},{17,25},{25,17},{2,10},{10... | collective-permute-start | bytes 393224 | tf_op jit(solution)/shard_map/ppermute | solution.py:184
  44.2 0.1 copy.33.refs_11_
  44.3 0.1 copy.34.refs_18_
  44.4 0.5 copy-done.5
  45.0 3.5 %update_first.1.refs_17_ = f32[16,128,128]{2,1,0:T(8,128)S(1)} custom-call(s32[4]{0:T(128)S(1)} %pad_add_fusion.refs_0_, bf16[1024,128]{1,0:T(8,128)(2,1)S(1)} %get-tuple-element.21.refs_1_, bf16[1024,128]{1,0:T(8,128)(2,1)S(1)} %collective-permute-done.refs_2_, bf16[1024,128]{1,0:T(8,128)(2,1)S(1)} %collective-permute-done.1.refs_3_, ...), custom_call_target="tpu_custom_call" | custom-call | tf_op jit(solution)/shard_map/update_first/pallas_call | solution.py:273
  48.6 3.9 %update_last.1 = (bf16[16,64,128]{2,1,0:T(8,128)(2,1)S(1)}, bf16[16,64,128]{2,1,0:T(8,128)(2,1)S(1)}, bf16[32,16,128]{2,1,0:T(8,128)(2,1)S(1)}, bf16[32,16,128]{...) custom-call(s32[4]{0:T(128)S(1)} %pad_add_fusion.refs_0_, ...), custom_call_target="tpu_custom_call" | custom-call | tf_op jit(solution)/shard_map/update_last/pallas_call | solution.py:285
  52.6 3.4 %collective-permute-start.17 = (bf16[32,16,128]{2,1,0:T(8,128)(2,1)S(1)}, bf16[32,16,128]{2,1,0:T(8,128)(2,1)S(1)}, u32[]{:S(2)}, u32[]{:S(2)}) collective-permute-start(bf16[32,16,128]{2,1,0:T(8,128)(2,1)S(1)} %get-tuple-element.31), channel_id=1, source_target_pairs={{0,0},{1,1},{2,2},{3,3},{4,16},{5,17},{6,18},{7,19},{8,8},{9,9},{1... | collective-permute-start | bytes 393224 | tf_op jit(solution)/shard_map/ppermute | solution.py:312
  56.0 1.4 %collective-permute-start.18 = (bf16[32,16,128]{2,1,0:T(8,128)(2,1)S(1)}, bf16[32,16,128]{2,1,0:T(8,128)(2,1)S(1)}, u32[]{:S(2)}, u32[]{:S(2)}) collective-permute-start(bf16[32,16,128]{2,1,0:T(8,128)(2,1)S(1)} %get-tuple-element.32), channel_id=1, source_target_pairs={{0,8},{1,9},{2,10},{3,11},{4,24},{5,25},{6,26},{7,27},{8,0},{9,1},... | collective-permute-start | bytes 393224 | tf_op jit(solution)/shard_map/ppermute | solution.py:312
  57.4 4.8 %collective-permute-start.15 = (bf16[32,16,128]{2,1,0:T(8,128)(2,1)S(1)}, bf16[32,16,128]{2,1,0:T(8,128)(2,1)S(1)}, u32[]{:S(2)}, u32[]{:S(2)}) collective-permute-start(bf16[32,16,128]{2,1,0:T(8,128)(2,1)S(1)} %get-tuple-element.29), channel_id=1, source_target_pairs={{0,1},{1,0},{2,3},{3,2},{4,17},{5,16},{6,19},{7,18},{8,9},{9,8},{1... | collective-permute-start | bytes 393224 | tf_op jit(solution)/shard_map/ppermute | solution.py:312
  62.2 0.1 fusion.refs_9_
  62.3 2.1 %collective-permute-done.18.refs_5_ = bf16[32,16,128]{2,1,0:T(8,128)(2,1)S(1)} collective-permute-done((bf16[32,16,128]{2,1,0:T(8,128)(2,1)S(1)}, bf16[32,16,128]{2,1,0:T(8,128)(2,1)S(1)}, u32[]{:S(2)}, u32[]{:S(2)}) %collective-permute-start.18) | collective-permute-done | bytes 131104 | tf_op jit(solution)/shard_map/ppermute | solution.py:312
  64.3 2.9 %collective-permute-done.14.refs_3_ = bf16[16,64,128]{2,1,0:T(8,128)(2,1)S(1)} collective-permute-done((bf16[16,64,128]{2,1,0:T(8,128)(2,1)S(1)}, bf16[16,64,128]{2,1,0:T(8,128)(2,1)S(1)}, u32[]{:S(2)}, u32[]{:S(2)}) %collective-permute-start.14) | collective-permute-done | bytes 262176 | tf_op jit(solution)/shard_map/ppermute | solution.py:184
  67.2 2.6 %finish.2.refs_10_ = bf16[16,128,128]{2,1,0:T(8,128)(2,1)} custom-call(s32[4]{0:T(128)S(1)} %pad_add_fusion.refs_0_, bf16[16,128,128]{2,1,0:T(8,128)(2,1)S(1)} %copy-done, bf16[16,64,128]{2,1,0:T(8,128)(2,1)S(1)} %get-tuple-element.27.refs_2_, bf16[16,64,128]{2,1,0:T(8,128)(2,1)S(1)} %collective-permute-done.14.refs_3_, ...), custom_call_target="tpu_custom_call" | custom-call | tf_op jit(solution)/shard_map/finish/pallas_call | solution.py:334
  69.9 1.3 %collective-permute-done.15.refs_4_ = bf16[32,16,128]{2,1,0:T(8,128)(2,1)S(1)} collective-permute-done((bf16[32,16,128]{2,1,0:T(8,128)(2,1)S(1)}, bf16[32,16,128]{2,1,0:T(8,128)(2,1)S(1)}, u32[]{:S(2)}, u32[]{:S(2)}) %collective-permute-start.15) | collective-permute-done | bytes 131104 | tf_op jit(solution)/shard_map/ppermute | solution.py:312
  71.2 1.9 %collective-permute-done.16.refs_5_ = bf16[32,16,128]{2,1,0:T(8,128)(2,1)S(1)} collective-permute-done((bf16[32,16,128]{2,1,0:T(8,128)(2,1)S(1)}, bf16[32,16,128]{2,1,0:T(8,128)(2,1)S(1)}, u32[]{:S(2)}, u32[]{:S(2)}) %collective-permute-start.16) | collective-permute-done | bytes 131104 | tf_op jit(solution)/shard_map/ppermute | solution.py:312
  73.1 2.6 %finish.3 = bf16[16,128,128]{2,1,0:T(8,128)(2,1)} custom-call(s32[4]{0:T(128)S(1)} %pad_add_fusion.refs_0_, bf16[16,128,128]{2,1,0:T(8,128)(2,1)S(1)} %copy-done, bf16[16,64,128]{2,1,0:T(8,128)(2,1)S(1)} %get-tuple-element.27.refs_2_, bf16[16,64,128]{2,1,0:T(8,128)(2,1)S(1)} %collective-permute-done.14.refs_3_, ...), custom_call_target="tpu_custom_call", output_to_operand_aliasing={{}: (10, {})} | custom-call | tf_op jit(solution)/shard_map/finish/pallas_call | solution.py:334
  (41 shorter events, 0.7 us)
Async XLA Ops:
  1.5 1.0 %copy-start.3 = (bf16[128,32,64]{0,2,1:T(8,128)(2,1)S(1)}, bf16[128,32,64]{0,2,1:T(8,128)(2,1)}, u32[]{:S(2)}) copy-start(bf16[128,32,64]{0,2,1:T(8,128)(2,1)} %param.10) | copy-start | bytes 1572868
  2.9 6.0 %copy-start.4 = (bf16[1024,128]{1,0:T(8,128)(2,1)S(1)}, bf16[1024,128]{1,0:T(8,128)(2,1)}, u32[]{:S(2)}) copy-start(bf16[1024,128]{1,0:T(8,128)(2,1)} %param.12) | copy-start | bytes 786436
  3.0 7.2 %collective-permute-start = (bf16[1024,128]{1,0:T(8,128)(2,1)S(1)}, bf16[1024,128]{1,0:T(8,128)(2,1)S(1)}, u32[]{:S(2)}, u32[]{:S(2)}) collective-permute-start(bf16[1024,128]{1,0:T(8,128)(2,1)S(1)} %get-tuple-element.20), channel_id=1, source_target_pairs={{0,1},{1,0},{2,3},{3,2},{4,5},{5,4},{6,7},{7,6},{8,9},{9,8},{10,11... | collective-permute-start | bytes 786440 | tf_op jit(solution)/shard_map/ppermute | solution.py:184
  4.4 26.4 %collective-permute-start.1 = (bf16[1024,128]{1,0:T(8,128)(2,1)S(1)}, bf16[1024,128]{1,0:T(8,128)(2,1)S(1)}, u32[]{:S(2)}, u32[]{:S(2)}) collective-permute-start(bf16[1024,128]{1,0:T(8,128)(2,1)S(1)} %get-tuple-element.22), channel_id=1, source_target_pairs={{0,3},{1,2},{2,1},{3,0},{4,7},{5,6},{6,5},{7,4},{8,11},{9,10},{10,... | collective-permute-start | bytes 786440 | tf_op jit(solution)/shard_map/ppermute | solution.py:184
  6.6 19.9 %collective-permute-start.2 = (bf16[512,128]{1,0:T(8,128)(2,1)S(1)}, bf16[512,128]{1,0:T(8,128)(2,1)S(1)}, u32[]{:S(2)}, u32[]{:S(2)}) collective-permute-start(bf16[512,128]{1,0:T(8,128)(2,1)S(1)} %get-tuple-element.23), channel_id=1, source_target_pairs={{0,2},{1,3},{2,0},{3,1},{4,6},{5,7},{6,4},{7,5},{8,10},{9,11},{10,... | collective-permute-start | bytes 393224 | tf_op jit(solution)/shard_map/ppermute | solution.py:184
  6.7 22.6 %collective-permute-start.3 = (bf16[512,128]{1,0:T(8,128)(2,1)S(1)}, bf16[512,128]{1,0:T(8,128)(2,1)S(1)}, u32[]{:S(2)}, u32[]{:S(2)}) collective-permute-start(bf16[512,128]{1,0:T(8,128)(2,1)S(1)} %bitcast.50), channel_id=1, source_target_pairs={{0,2},{1,3},{2,0},{3,1},{4,6},{5,7},{6,4},{7,5},{8,10},{9,11},{10,... | collective-permute-start | bytes 393224 | tf_op jit(solution)/shard_map/ppermute | solution.py:184
  10.3 21.1 %collective-permute-start.9 = (bf16[1024,128]{1,0:T(8,128)(2,1)S(1)}, bf16[1024,128]{1,0:T(8,128)(2,1)S(1)}, u32[]{:S(2)}, u32[]{:S(2)}) collective-permute-start(bf16[1024,128]{1,0:T(8,128)(2,1)S(1)} %pad_maximum_fusion.6), channel_id=1, source_target_pairs={{0,16},{8,24},{16,0},{24,8},{1,17},{9,25},{17,1},{25,9},{2,18},{10... | collective-permute-start | bytes 786440 | tf_op jit(solution)/shard_map/ppermute | solution.py:184
  26.4 11.7 %collective-permute-start.6 = (bf16[512,128]{1,0:T(8,128)(2,1)S(1)}, bf16[512,128]{1,0:T(8,128)(2,1)S(1)}, u32[]{:S(2)}, u32[]{:S(2)}) collective-permute-start(bf16[512,128]{1,0:T(8,128)(2,1)S(1)} %collective-permute-done.2.refs_4_), channel_id=1, source_target_pairs={{0,4},{4,0},{1,5},{5,1},{2,6},{6,2},{3,7},{7,3},{8,12},{12,8},{9,1... | collective-permute-start | bytes 393224 | tf_op jit(solution)/shard_map/ppermute | solution.py:184
  29.3 9.2 %collective-permute-start.8 = (bf16[512,128]{1,0:T(8,128)(2,1)S(1)}, bf16[512,128]{1,0:T(8,128)(2,1)S(1)}, u32[]{:S(2)}, u32[]{:S(2)}) collective-permute-start(bf16[512,128]{1,0:T(8,128)(2,1)S(1)} %collective-permute-done.3.refs_5_), channel_id=1, source_target_pairs={{0,8},{8,0},{16,24},{24,16},{1,9},{9,1},{17,25},{25,17},{2,10},{10... | collective-permute-start | bytes 393224 | tf_op jit(solution)/shard_map/ppermute | solution.py:184
  31.5 5.1 %collective-permute-start.10 = (bf16[512,128]{1,0:T(8,128)(2,1)S(1)}, bf16[512,128]{1,0:T(8,128)(2,1)S(1)}, u32[]{:S(2)}, u32[]{:S(2)}) collective-permute-start(bf16[512,128]{1,0:T(8,128)(2,1)S(1)} %get-tuple-element.25), channel_id=1, source_target_pairs={{0,16},{8,24},{16,0},{24,8},{1,17},{9,25},{17,1},{25,9},{2,18},{10... | collective-permute-start | bytes 393224 | tf_op jit(solution)/shard_map/ppermute | solution.py:184
  32.5 12.5 %collective-permute-start.7 = (bf16[1536,128]{1,0:T(8,128)(2,1)}, bf16[1536,128]{1,0:T(8,128)(2,1)S(1)}, u32[]{:S(2)}, u32[]{:S(2)}) collective-permute-start(bf16[1536,128]{1,0:T(8,128)(2,1)} %pad_maximum_fusion), channel_id=1, source_target_pairs={{0,8},{8,0},{16,24},{24,16},{1,9},{9,1},{17,25},{25,17},{2,10},{10... | collective-permute-start | bytes 1179656 | tf_op jit(solution)/shard_map/ppermute | solution.py:184
  33.5 11.5 %collective-permute-start.4 = (bf16[1024,128]{1,0:T(8,128)(2,1)}, bf16[1024,128]{1,0:T(8,128)(2,1)S(1)}, u32[]{:S(2)}, u32[]{:S(2)}) collective-permute-start(bf16[1024,128]{1,0:T(8,128)(2,1)} %pad_maximum_fusion.5), channel_id=1, source_target_pairs={{0,4},{4,0},{1,5},{5,1},{2,6},{6,2},{3,7},{7,3},{8,12},{12,8},{9,1... | collective-permute-start | bytes 786440 | tf_op jit(solution)/shard_map/ppermute | solution.py:184
  37.4 11.1 %collective-permute-start.12 = (bf16[1536,128]{1,0:T(8,128)(2,1)}, bf16[1536,128]{1,0:T(8,128)(2,1)S(1)}, u32[]{:S(2)}, u32[]{:S(2)}) collective-permute-start(bf16[1536,128]{1,0:T(8,128)(2,1)} %pad_maximum_fusion.1), channel_id=1, source_target_pairs={{0,8},{8,0},{16,24},{24,16},{1,9},{9,1},{17,25},{25,17},{2,10},{10... | collective-permute-start | bytes 1179656 | tf_op jit(solution)/shard_map/ppermute | solution.py:184
  38.2 5.1 %collective-permute-start.11 = (bf16[512,128]{1,0:T(8,128)(2,1)S(1)}, bf16[512,128]{1,0:T(8,128)(2,1)S(1)}, u32[]{:S(2)}, u32[]{:S(2)}) collective-permute-start(bf16[512,128]{1,0:T(8,128)(2,1)S(1)} %collective-permute-done.3.refs_5_), channel_id=1, source_target_pairs={{0,16},{8,24},{16,0},{24,8},{1,17},{9,25},{17,1},{25,9},{2,18},{10... | collective-permute-start | bytes 393224 | tf_op jit(solution)/shard_map/ppermute | solution.py:184
  38.5 6.5 %collective-permute-start.5 = (bf16[512,128]{1,0:T(8,128)(2,1)}, bf16[512,128]{1,0:T(8,128)(2,1)S(1)}, u32[]{:S(2)}, u32[]{:S(2)}) collective-permute-start(bf16[512,128]{1,0:T(8,128)(2,1)} %get-tuple-element.46), channel_id=1, source_target_pairs={{0,4},{4,0},{1,5},{5,1},{2,6},{6,2},{3,7},{7,3},{8,12},{12,8},{9,1... | collective-permute-start | bytes 393224 | tf_op jit(solution)/shard_map/ppermute | solution.py:184
  43.3 5.2 %collective-permute-start.13 = (bf16[512,128]{1,0:T(8,128)(2,1)S(1)}, bf16[512,128]{1,0:T(8,128)(2,1)S(1)}, u32[]{:S(2)}, u32[]{:S(2)}) collective-permute-start(bf16[512,128]{1,0:T(8,128)(2,1)S(1)} %collective-permute-done.11.refs_13_), channel_id=1, source_target_pairs={{0,8},{8,0},{16,24},{24,16},{1,9},{9,1},{17,25},{25,17},{2,10},{10... | collective-permute-start | bytes 393224 | tf_op jit(solution)/shard_map/ppermute | solution.py:184
  44.3 0.7 copy-start.5
  44.3 0.7 copy-start.7
  44.3 0.7 copy-start.8
  45.0 3.5 %copy-start.6 = (f32[128]{0:T(128)S(1)}, f32[128]{0:T(128)}, u32[]{:S(2)}) copy-start(f32[128]{0:T(128)} %param.13) | copy-start | bytes 1540
  48.6 18.7 %copy-start = (bf16[16,128,128]{2,1,0:T(8,128)(2,1)S(1)}, bf16[16,128,128]{2,1,0:T(8,128)(2,1)}, u32[]{:S(2)}) copy-start(bf16[16,128,128]{2,1,0:T(8,128)(2,1)} %refs_1_.3) | copy-start | bytes 1572868
  48.6 18.6 %copy-start.2 = (bf16[512,128]{1,0:T(8,128)(2,1)S(1)}, bf16[512,128]{1,0:T(8,128)(2,1)}, u32[]{:S(2)}) copy-start(bf16[512,128]{1,0:T(8,128)(2,1)} %refs_7_.3) | copy-start | bytes 393220
  52.5 14.8 %copy-start.1 = (bf16[128,512]{1,0:T(8,128)(2,1)S(1)}, bf16[128,512]{1,0:T(8,128)(2,1)}, u32[]{:S(2)}) copy-start(bf16[128,512]{1,0:T(8,128)(2,1)} %refs_6_.3) | copy-start | bytes 393220
  52.5 14.7 %collective-permute-start.14 = (bf16[16,64,128]{2,1,0:T(8,128)(2,1)S(1)}, bf16[16,64,128]{2,1,0:T(8,128)(2,1)S(1)}, u32[]{:S(2)}, u32[]{:S(2)}) collective-permute-start(bf16[16,64,128]{2,1,0:T(8,128)(2,1)S(1)} %get-tuple-element.28), channel_id=1, source_target_pairs={{0,2},{1,3},{2,0},{3,1},{4,6},{5,7},{6,4},{7,5},{8,10},{9,11},{10,... | collective-permute-start | bytes 786440 | tf_op jit(solution)/shard_map/ppermute | solution.py:184
  52.6 9.7 %collective-permute-start.17 = (bf16[32,16,128]{2,1,0:T(8,128)(2,1)S(1)}, bf16[32,16,128]{2,1,0:T(8,128)(2,1)S(1)}, u32[]{:S(2)}, u32[]{:S(2)}) collective-permute-start(bf16[32,16,128]{2,1,0:T(8,128)(2,1)S(1)} %get-tuple-element.31), channel_id=1, source_target_pairs={{0,0},{1,1},{2,2},{3,3},{4,16},{5,17},{6,18},{7,19},{8,8},{9,9},{1... | collective-permute-start | bytes 393224 | tf_op jit(solution)/shard_map/ppermute | solution.py:312
  56.0 8.3 %collective-permute-start.18 = (bf16[32,16,128]{2,1,0:T(8,128)(2,1)S(1)}, bf16[32,16,128]{2,1,0:T(8,128)(2,1)S(1)}, u32[]{:S(2)}, u32[]{:S(2)}) collective-permute-start(bf16[32,16,128]{2,1,0:T(8,128)(2,1)S(1)} %get-tuple-element.32), channel_id=1, source_target_pairs={{0,8},{1,9},{2,10},{3,11},{4,24},{5,25},{6,26},{7,27},{8,0},{9,1},... | collective-permute-start | bytes 393224 | tf_op jit(solution)/shard_map/ppermute | solution.py:312
  57.4 13.8 %collective-permute-start.15 = (bf16[32,16,128]{2,1,0:T(8,128)(2,1)S(1)}, bf16[32,16,128]{2,1,0:T(8,128)(2,1)S(1)}, u32[]{:S(2)}, u32[]{:S(2)}) collective-permute-start(bf16[32,16,128]{2,1,0:T(8,128)(2,1)S(1)} %get-tuple-element.29), channel_id=1, source_target_pairs={{0,1},{1,0},{2,3},{3,2},{4,17},{5,16},{6,19},{7,18},{8,9},{9,8},{1... | collective-permute-start | bytes 393224 | tf_op jit(solution)/shard_map/ppermute | solution.py:312
  62.1 11.0 %collective-permute-start.16 = (bf16[32,16,128]{2,1,0:T(8,128)(2,1)S(1)}, bf16[32,16,128]{2,1,0:T(8,128)(2,1)S(1)}, u32[]{:S(2)}, u32[]{:S(2)}) collective-permute-start(bf16[32,16,128]{2,1,0:T(8,128)(2,1)S(1)} %get-tuple-element.30), channel_id=1, source_target_pairs={{0,9},{1,8},{2,11},{3,10},{4,25},{5,24},{6,27},{7,26},{8,1},{9,0},... | collective-permute-start | bytes 393224 | tf_op jit(solution)/shard_map/ppermute | solution.py:312

commit v6 on v5

--- a/solution.py
+++ b/solution.py
@@ -191,66 +191,71 @@
     left = left.transpose(1, 0, 2, 3, 4).reshape(low, cols, share_rows, group_len)
     left = pick(left, col, 1)
 
-    blocks = [
-        (pick(right, z_high ^ (dz // low)), pick(left, z_low ^ (dz % low))) for dz in range(groups)
-    ]
-    packs = [jnp.concatenate(pair, axis=0) for pair in blocks[:2] + blocks[3:]]
-    packs = lax.optimization_barrier(packs + list(blocks[2]))
-    own, packs, (final_right, final_left) = packs[0], packs[1:-2], packs[-2:]
-    partners = [1] + list(range(3, groups))
-    held = {dz: swap(pack, "seq", groups, dz) for dz, pack in zip(partners, packs)}
-    final_left = swap(final_left, "seq", groups, 2)
-    final_right = swap(final_right, "seq", groups, 2)
-    held[0], _ = lax.optimization_barrier((own, held[1]))
+    def after(value, *earlier):
+        return lax.optimization_barrier((value, earlier))[0] if earlier else value
+
+    right_sends = [pick(right, z_high ^ (dz // low)) for dz in range(groups)]
+    left_sends = [pick(left, z_low ^ (dz % low)) for dz in range(groups)]
+    rights, lefts = {0: right_sends[0]}, {0: left_sends[0]}
+    crossed = {dz: [] for dz in range(groups)}
+    shared = {dz: [] for dz in range(groups)}
+
+    def along(sends, dz, *earlier):
+        return swap(after(sends[dz], *earlier), "seq", groups, dz)
+
+    def over_x(dz, *earlier):
+        for dx in range(1, xs):
+            value = swap(after(rights[dz], *earlier), "row", rows, 2 * dx)
+            crossed[dz].append(value)
+            earlier = (value,)
+        return earlier
+
+    def over_y(dz, *earlier):
+        for dy in range(1, cols):
+            value = swap(after(lefts[dz], *earlier), "col", cols, dy)
+            shared[dz].append(value)
+            earlier = (value,)
+        return earlier
+
+    rights[3] = along(right_sends, 3)
+    rights[1] = along(right_sends, 1)
+    last_x = over_x(0, rights[1])
+    last_y = over_y(0)
+    lefts[3] = along(left_sends, 3, rights[1])
+    lefts[1] = along(left_sends, 1)
+    last_x = over_x(1, *last_x)
+    lefts[2] = along(left_sends, 2, rights[3])
+    last_x = over_x(3, *last_x)
+    last_y = over_y(1, *last_y)
+    rights[2] = along(right_sends, 2, lefts[3])
+    last_y = over_y(3, *last_y)
+    cored, cored_too = {}, {}
+    for dz in (0, 1, 3):
+        cored[dz] = swap(after(rights[dz], lefts[3]), "row", rows, 1)
+        cored_too[dz] = [swap(after(value, lefts[2]), "row", rows, 1) for value in crossed[dz]]
+    last_y = over_y(2, *last_y)
+    rights[2] = after(rights[2], *last_y)
+    over_x(2)
+    cored[2] = swap(rights[2], "row", rows, 1)
+    cored_too[2] = [swap(value, "row", rows, 1) for value in crossed[2]]
+
     data, others = [], []
     left_places = {dz: [] for dz in range(groups)}
     right_places = {dz: [] for dz in range(groups)}
     other_places = {dz: [] for dz in range(groups)}
 
-    def place_in(store, table, value, bundle, size):
-        for position, dz in enumerate(bundle):
-            table[dz].append((len(store), position * size))
+    def place_in(store, table, dz, value):
+        table[dz].append((len(store), 0))
         store.append(value)
 
-    for dz in [0] + partners:
-        left_places[dz].append((len(data), source_rows))
-        right_places[dz].append((len(data), 0))
-        data.append(held[dz])
-    place_in(data, left_places, final_left, [2], share_rows)
-    place_in(data, right_places, final_right, [2], source_rows)
-
-    bundles = [[0, 1]] + [[dz] for dz in partners[1:]] + [[2]]
-    rights, crosses = [], {dx: [] for dx in range(1, xs)}
-    chain = None
-    for bundle in bundles:
-        if bundle == [2]:
-            value, lefts = final_right, final_left
-        elif len(bundle) > 1:
-            value = jnp.concatenate([held[dz][:source_rows] for dz in bundle], axis=0)
-            lefts = jnp.concatenate([held[dz][source_rows:] for dz in bundle], axis=0)
-        else:
-            value, lefts = held[bundle[0]][:source_rows], held[bundle[0]][source_rows:]
-        rights.append(value)
-        for dy in range(1, cols):
-            place_in(data, left_places, swap(lefts, "col", cols, dy), bundle, share_rows)
-        for dx in range(1, xs):
-            if chain is not None:
-                value, _ = lax.optimization_barrier((value, chain))
-            chain = swap(value, "row", rows, 2 * dx)
-            crosses[dx].append(chain)
-
-    early = [dz for bundle in bundles[:-1] for dz in bundle]
-    place_in(
-        data, right_places, swap(jnp.concatenate(rights[:-1], axis=0), "row", rows, 1), early,
-        source_rows,
-    )
-    place_in(data, right_places, swap(rights[-1], "row", rows, 1), [2], source_rows)
-    for dx in range(1, xs):
-        for value, bundle in zip(crosses[dx], bundles):
-            place_in(others, other_places, value, bundle, source_rows)
-        value = swap(jnp.concatenate(crosses[dx][:-1], axis=0), "row", rows, 1)
-        place_in(others, other_places, value, early, source_rows)
-        place_in(others, other_places, swap(crosses[dx][-1], "row", rows, 1), [2], source_rows)
+    for dz in range(groups):
+        for value in [lefts[dz]] + shared[dz]:
+            place_in(data, left_places, dz, value)
+        for value in (rights[dz], cored[dz]):
+            place_in(data, right_places, dz, value)
+        for pair in zip(crossed[dz], cored_too[dz]):
+            for value in pair:
+                place_in(others, other_places, dz, value)
 
     weight = proj_weight.reshape(channels, rows, e1, 2, pair_channels)
     weight = weight.transpose(1, 3, 4, 2, 0)
@@ -270,6 +275,12 @@
 
     sizes = (share_rows, source_rows, group_len)
     places = (tabled(left_places), tabled(right_places)) + sizes + (len(data),)
+    outer_size = 4 * run * channels * split * half
+    cost = pl.CostEstimate(
+        flops=2 * outer_size * (groups * group_len + 2 * pair_channels),
+        bytes_accessed=2 * outer_size,
+        transcendentals=0,
+    )
     partial = pl.pallas_call(
         functools.partial(update_kernel, places, cols, low, False, scale),
         out_shape=jax.ShapeDtypeStruct((run, pair_channels, 2 * half), jnp.float32),
@@ -277,6 +288,7 @@
         out_specs=vmem,
         scratch_shapes=[lhs, pltpu.VMEM((2 * run, split, 2 * half), bf16)],
         compiler_params=params,
+        cost_estimate=cost,
         name="update_first",
     )(place, *data, weight[:, :split])
     shifted = [[(o + len(data), f) for o, f in other_places[dz]] for dz in range(groups)]
@@ -294,6 +306,7 @@
             pltpu.VMEM((2 * run, half, pair_channels), bf16),
         ],
         compiler_params=params,
+        cost_estimate=cost,
         name="update_last",
     )(place, *data, *others, bias, partial, weight[:, split:])
 

time: 76.4 us -> 72 us (0.942)
  waiting for transfers between devices: 31.2 us -> 16.9 us
  starting transfers between devices: 23.7 us -> 37.4 us
  other arithmetic: 3.04 us -> 0.66 us
  local copies, waits for them, and re-layouts: 4.81 us -> 3.38 us
    ppermute x15 -> x23, waiting for transfers between devices: 25.9 us -> 10.6 us  [swap(): return lax.ppermute(value, name, [(i, i ^ flip) for i in range(size)])]
    ppermute x15 -> x23, starting transfers between devices: 14.2 us -> 29.3 us  [swap(): return lax.ppermute(value, name, [(i, i ^ flip) for i in range(size)])]
    concatenate x5 -> x0, other arithmetic: 2.38 us -> none  [the longest x1 0.77 us: on_device(): value = swap(jnp.concatenate(crosses[dx][:-1], axis=0), 'row', rows, 1)]
    ppermute x4, starting transfers between devices: 9.54 us -> 8.15 us  [on_device(): mirrors.append(lax.ppermute(outs[2 + 2 * dz + flip], axes, pairs))]
    ppermute x4, waiting for transfers between devices: 5.32 us -> 6.23 us  [on_device(): mirrors.append(lax.ppermute(outs[2 + 2 * dz + flip], axes, pairs))]
  transfers between devices with their start and end apart: 19 -> 27, of which waited for: 9 -> 9; matrix products, arithmetic and copies ran while one was open for 6% -> 2% of each run, Pallas kernels for 8% -> 9%
where the time goes in v6:
time: 72 us; the launch traced here: 71.3 us
  starting transfers between devices  37.4 us (52%)
  waiting for transfers between devices  16.9 us (23%)
  Pallas kernels  12.7 us (18%)
  local copies, waits for them, and re-layouts  3.38 us (5%)
    ppermute x23, starting transfers between devices, swap(): return lax.ppermute(value, name, [(i, i ^ flip) for i in range(size)])  29.3 us
    ppermute x23, waiting for transfers between devices, swap(): return lax.ppermute(value, name, [(i, i ^ flip) for i in range(size)])  10.6 us
    ppermute x4, starting transfers between devices, on_device(): mirrors.append(lax.ppermute(outs[2 + 2 * dz + flip], axes, pairs))  8.15 us
    ppermute x4, waiting for transfers between devices, on_device(): mirrors.append(lax.ppermute(outs[2 + 2 * dz + flip], axes, pairs))  6.23 us
    pallas_call x2, Pallas kernels, on_device(): pl.pallas_call(functools.partial(finish_kernel, low, dz), out_shape=jax.S...  5.26 us
    pallas_call x1, Pallas kernels, on_device(): pl.pallas_call(functools.partial(update_kernel, places, cols, low, True,...  3.98 us
    pallas_call x1, Pallas kernels, on_device(): pl.pallas_call(functools.partial(update_kernel, places, cols, low, False,...  3.47 us
    unnamed x22, local copies, waits for them, and re-layouts  1.98 us
  transfers between devices with their start and end apart: 27, of which 9 were waited for; matrix products, arithmetic and copies ran while one was open for 2% of the time, Pallas kernels for 9%

profile of v6, /device:TPU:3, one launch (start us, length us, event | category | flops | bytes accessed | tf_op | source)
XLA Modules:
  0.0 71.3 jit_solution(12209234085287405434)
XLA Ops:
  0.0 1.1 %copy.19 = bf16[128,8,128]{0,2,1:T(8,128)(2,1)S(1)} copy(bf16[128,8,128]{2,1,0:T(8,128)(2,1)} %param.11) | data formatting | bytes 524288 | tf_op args[1]
  1.2 0.2 copy.20
  1.4 0.1 reshape.55
  1.5 0.1 copy.21
  1.7 1.4 %collective-permute-start.1 = (bf16[512,128]{1,0:T(8,128)(2,1)S(1)}, bf16[512,128]{1,0:T(8,128)(2,1)S(1)}, u32[]{:S(2)}, u32[]{:S(2)}) collective-permute-start(bf16[512,128]{1,0:T(8,128)(2,1)S(1)} %bitcast.45), channel_id=1, source_target_pairs={{0,1},{1,0},{2,3},{3,2},{4,5},{5,4},{6,7},{7,6},{8,9},{9,8},{10,11... | collective-permute-start | bytes 393224 | tf_op jit(solution)/shard_map/ppermute | solution.py:184
  3.0 0.3 copy.18
  3.4 1.3 %collective-permute-start = (bf16[512,128]{1,0:T(8,128)(2,1)S(1)}, bf16[512,128]{1,0:T(8,128)(2,1)S(1)}, u32[]{:S(2)}, u32[]{:S(2)}) collective-permute-start(bf16[512,128]{1,0:T(8,128)(2,1)S(1)} %get-tuple-element.31.refs_1_), channel_id=1, source_target_pairs={{0,4},{4,0},{1,5},{5,1},{2,6},{6,2},{3,7},{7,3},{8,12},{12,8},{9,1... | collective-permute-start | bytes 393224 | tf_op jit(solution)/shard_map/ppermute | solution.py:184
  4.7 0.8 %collective-permute-start.4 = (bf16[512,128]{1,0:T(8,128)(2,1)S(1)}, bf16[512,128]{1,0:T(8,128)(2,1)S(1)}, u32[]{:S(2)}, u32[]{:S(2)}) collective-permute-start(bf16[512,128]{1,0:T(8,128)(2,1)S(1)} %get-tuple-element.27), channel_id=1, source_target_pairs={{0,1},{1,0},{2,3},{3,2},{4,5},{5,4},{6,7},{7,6},{8,9},{9,8},{10,11... | collective-permute-start | bytes 393224 | tf_op jit(solution)/shard_map/ppermute | solution.py:184
  5.5 0.1 copy.22
  5.6 2.8 %collective-permute-start.7 = (bf16[512,128]{1,0:T(8,128)(2,1)S(1)}, bf16[512,128]{1,0:T(8,128)(2,1)S(1)}, u32[]{:S(2)}, u32[]{:S(2)}) collective-permute-start(bf16[512,128]{1,0:T(8,128)(2,1)S(1)} %bitcast.56), channel_id=1, source_target_pairs={{0,3},{1,2},{2,1},{3,0},{4,7},{5,6},{6,5},{7,4},{8,11},{9,10},{10,... | collective-permute-start | bytes 393224 | tf_op jit(solution)/shard_map/ppermute | solution.py:184
  8.4 0.2 constant_dynamic-slice_fusion.3
  8.6 0.8 %collective-permute-start.2 = (bf16[512,128]{1,0:T(8,128)(2,1)S(1)}, bf16[512,128]{1,0:T(8,128)(2,1)S(1)}, u32[]{:S(2)}, u32[]{:S(2)}) collective-permute-start(bf16[512,128]{1,0:T(8,128)(2,1)S(1)} %get-tuple-element.27), channel_id=1, source_target_pairs={{0,3},{1,2},{2,1},{3,0},{4,7},{5,6},{6,5},{7,4},{8,11},{9,10},{10,... | collective-permute-start | bytes 393224 | tf_op jit(solution)/shard_map/ppermute | solution.py:184
  9.4 1.2 %collective-permute-start.5 = (bf16[512,128]{1,0:T(8,128)(2,1)S(1)}, bf16[512,128]{1,0:T(8,128)(2,1)S(1)}, u32[]{:S(2)}, u32[]{:S(2)}) collective-permute-start(bf16[512,128]{1,0:T(8,128)(2,1)S(1)} %collective-permute-done.4.refs_5_), channel_id=1, source_target_pairs={{0,4},{4,0},{1,5},{5,1},{2,6},{6,2},{3,7},{7,3},{8,12},{12,8},{9,1... | collective-permute-start | bytes 393224 | tf_op jit(solution)/shard_map/ppermute | solution.py:184
  10.7 0.3 collective-permute-start.14
  11.0 2.0 %collective-permute-done.7.refs_15_ = bf16[512,128]{1,0:T(8,128)(2,1)S(1)} collective-permute-done((bf16[512,128]{1,0:T(8,128)(2,1)S(1)}, bf16[512,128]{1,0:T(8,128)(2,1)S(1)}, u32[]{:S(2)}, u32[]{:S(2)}) %collective-permute-start.7) | collective-permute-done | bytes 131104 | tf_op jit(solution)/shard_map/ppermute | solution.py:184
  13.1 3.0 %collective-permute-done.2.refs_13_ = bf16[512,128]{1,0:T(8,128)(2,1)S(1)} collective-permute-done((bf16[512,128]{1,0:T(8,128)(2,1)S(1)}, bf16[512,128]{1,0:T(8,128)(2,1)S(1)}, u32[]{:S(2)}, u32[]{:S(2)}) %collective-permute-start.2) | collective-permute-done | bytes 131104 | tf_op jit(solution)/shard_map/ppermute | solution.py:184
  16.1 1.9 %collective-permute-start.9 = (bf16[512,128]{1,0:T(8,128)(2,1)S(1)}, bf16[512,128]{1,0:T(8,128)(2,1)S(1)}, u32[]{:S(2)}, u32[]{:S(2)}) collective-permute-start(bf16[512,128]{1,0:T(8,128)(2,1)S(1)} %collective-permute-done.2.refs_13_), channel_id=1, source_target_pairs={{0,4},{4,0},{1,5},{5,1},{2,6},{6,2},{3,7},{7,3},{8,12},{12,8},{9,1... | collective-permute-start | bytes 393224 | tf_op jit(solution)/shard_map/ppermute | solution.py:184
  18.0 0.3 collective-permute-start.16
  18.4 0.5 pad_maximum_fusion
  18.9 4.0 %collective-permute-start.11 = (bf16[512,128]{1,0:T(8,128)(2,1)S(1)}, bf16[512,128]{1,0:T(8,128)(2,1)S(1)}, u32[]{:S(2)}, u32[]{:S(2)}) collective-permute-start(bf16[512,128]{1,0:T(8,128)(2,1)S(1)} %bitcast.57), channel_id=1, source_target_pairs={{0,2},{1,3},{2,0},{3,1},{4,6},{5,7},{6,4},{7,5},{8,10},{9,11},{10,... | collective-permute-start | bytes 393224 | tf_op jit(solution)/shard_map/ppermute | solution.py:184
  22.9 0.2 collective-permute-done.8.refs_9_
  23.1 1.1 %collective-permute-start.10 = (bf16[512,128]{1,0:T(8,128)(2,1)S(1)}, bf16[512,128]{1,0:T(8,128)(2,1)S(1)}, u32[]{:S(2)}, u32[]{:S(2)}) collective-permute-start(bf16[512,128]{1,0:T(8,128)(2,1)S(1)} %collective-permute-done.8.refs_9_), channel_id=1, source_target_pairs={{0,4},{4,0},{1,5},{5,1},{2,6},{6,2},{3,7},{7,3},{8,12},{12,8},{9,1... | collective-permute-start | bytes 393224 | tf_op jit(solution)/shard_map/ppermute | solution.py:184
  24.2 1.2 %collective-permute-start.20 = (bf16[512,128]{1,0:T(8,128)(2,1)S(1)}, bf16[512,128]{1,0:T(8,128)(2,1)S(1)}, u32[]{:S(2)}, u32[]{:S(2)}) collective-permute-start(bf16[512,128]{1,0:T(8,128)(2,1)S(1)} %collective-permute-done.7.refs_15_), channel_id=1, source_target_pairs={{0,16},{8,24},{16,0},{24,8},{1,17},{9,25},{17,1},{25,9},{2,18},{10... | collective-permute-start | bytes 393224 | tf_op jit(solution)/shard_map/ppermute | solution.py:184
  25.4 4.9 %collective-permute-start.13 = (bf16[512,128]{1,0:T(8,128)(2,1)S(1)}, bf16[512,128]{1,0:T(8,128)(2,1)S(1)}, u32[]{:S(2)}, u32[]{:S(2)}) collective-permute-start(bf16[512,128]{1,0:T(8,128)(2,1)S(1)} %collective-permute-done.7.refs_15_), channel_id=1, source_target_pairs={{0,8},{8,0},{16,24},{24,16},{1,9},{9,1},{17,25},{25,17},{2,10},{10... | collective-permute-start | bytes 393224 | tf_op jit(solution)/shard_map/ppermute | solution.py:184
  30.4 0.8 %collective-permute-done.11.refs_11_ = bf16[512,128]{1,0:T(8,128)(2,1)S(1)} collective-permute-done((bf16[512,128]{1,0:T(8,128)(2,1)S(1)}, bf16[512,128]{1,0:T(8,128)(2,1)S(1)}, u32[]{:S(2)}, u32[]{:S(2)}) %collective-permute-start.11) | collective-permute-done | bytes 131104 | tf_op jit(solution)/shard_map/ppermute | solution.py:184
  31.2 1.6 %collective-permute-start.3 = (bf16[512,128]{1,0:T(8,128)(2,1)S(1)}, bf16[512,128]{1,0:T(8,128)(2,1)S(1)}, u32[]{:S(2)}, u32[]{:S(2)}) collective-permute-start(bf16[512,128]{1,0:T(8,128)(2,1)S(1)} %bitcast.47), channel_id=1, source_target_pairs={{0,8},{8,0},{16,24},{24,16},{1,9},{9,1},{17,25},{25,17},{2,10},{10... | collective-permute-start | bytes 393224 | tf_op jit(solution)/shard_map/ppermute | solution.py:184
  32.8 1.9 %collective-permute-start.12 = (bf16[512,128]{1,0:T(8,128)(2,1)S(1)}, bf16[512,128]{1,0:T(8,128)(2,1)S(1)}, u32[]{:S(2)}, u32[]{:S(2)}) collective-permute-start(bf16[512,128]{1,0:T(8,128)(2,1)S(1)} %collective-permute-done.11.refs_11_), channel_id=1, source_target_pairs={{0,8},{8,0},{16,24},{24,16},{1,9},{9,1},{17,25},{25,17},{2,10},{10... | collective-permute-start | bytes 393224 | tf_op jit(solution)/shard_map/ppermute | solution.py:184
  34.8 0.1 copy.33.refs_17_
  34.9 0.1 copy.34.refs_27_
  35.0 0.5 copy-done.5
  35.6 0.5 collective-permute-start.15
  36.2 0.4 collective-permute-start.21
  36.7 3.1 %collective-permute-done.18.refs_21_ = bf16[512,128]{1,0:T(8,128)(2,1)S(1)} collective-permute-done((bf16[512,128]{1,0:T(8,128)(2,1)S(1)}, bf16[512,128]{1,0:T(8,128)(2,1)S(1)}, u32[]{:S(2)}, u32[]{:S(2)}) %collective-permute-start.18) | collective-permute-done | bytes 131104 | tf_op jit(solution)/shard_map/ppermute | solution.py:184
  39.8 0.9 %collective-permute-start.19 = (bf16[512,128]{1,0:T(8,128)(2,1)S(1)}, bf16[512,128]{1,0:T(8,128)(2,1)S(1)}, u32[]{:S(2)}, u32[]{:S(2)}) collective-permute-start(bf16[512,128]{1,0:T(8,128)(2,1)S(1)} %collective-permute-done.18.refs_21_), channel_id=1, source_target_pairs={{0,8},{8,0},{16,24},{24,16},{1,9},{9,1},{17,25},{25,17},{2,10},{10... | collective-permute-start | bytes 393224 | tf_op jit(solution)/shard_map/ppermute | solution.py:184
  40.6 3.5 %update_first.1.refs_26_ = f32[16,128,128]{2,1,0:T(8,128)S(1)} custom-call(s32[4]{0:T(128)S(1)} %pad_add_fusion.refs_0_, bf16[512,128]{1,0:T(8,128)(2,1)S(1)} %get-tuple-element.31.refs_1_, bf16[512,128]{1,0:T(8,128)(2,1)S(1)} %collective-permute-done.refs_2_, bf16[512,128]{1,0:T(8,128)(2,1)S(1)} %bitcast.48, ...), custom_call_target="tpu_custom_call" | custom-call | flops 51539607552 | bytes 67108864 | tf_op jit(solution)/shard_map/update_first/pallas_call | solution.py:284
  44.2 4.0 %update_last.1 = (bf16[16,64,128]{2,1,0:T(8,128)(2,1)S(1)}, bf16[16,64,128]{2,1,0:T(8,128)(2,1)S(1)}, bf16[32,16,128]{2,1,0:T(8,128)(2,1)S(1)}, bf16[32,16,128]{...) custom-call(s32[4]{0:T(128)S(1)} %pad_add_fusion.refs_0_, ...), custom_call_target="tpu_custom_call" | custom-call | flops 51539607552 | bytes 67108864 | tf_op jit(solution)/shard_map/update_last/pallas_call | solution.py:297
  48.2 1.8 %collective-permute-start.22 = (bf16[16,64,128]{2,1,0:T(8,128)(2,1)S(1)}, bf16[16,64,128]{2,1,0:T(8,128)(2,1)S(1)}, u32[]{:S(2)}, u32[]{:S(2)}) collective-permute-start(bf16[16,64,128]{2,1,0:T(8,128)(2,1)S(1)} %get-tuple-element.44), channel_id=1, source_target_pairs={{0,2},{1,3},{2,0},{3,1},{4,6},{5,7},{6,4},{7,5},{8,10},{9,11},{10,... | collective-permute-start | bytes 786440 | tf_op jit(solution)/shard_map/ppermute | solution.py:184
  50.1 2.7 %collective-permute-start.25 = (bf16[32,16,128]{2,1,0:T(8,128)(2,1)S(1)}, bf16[32,16,128]{2,1,0:T(8,128)(2,1)S(1)}, u32[]{:S(2)}, u32[]{:S(2)}) collective-permute-start(bf16[32,16,128]{2,1,0:T(8,128)(2,1)S(1)} %get-tuple-element.47), channel_id=1, source_target_pairs={{0,0},{1,1},{2,2},{3,3},{4,16},{5,17},{6,18},{7,19},{8,8},{9,9},{1... | collective-permute-start | bytes 393224 | tf_op jit(solution)/shard_map/ppermute | solution.py:325
  52.8 2.1 %collective-permute-start.26 = (bf16[32,16,128]{2,1,0:T(8,128)(2,1)S(1)}, bf16[32,16,128]{2,1,0:T(8,128)(2,1)S(1)}, u32[]{:S(2)}, u32[]{:S(2)}) collective-permute-start(bf16[32,16,128]{2,1,0:T(8,128)(2,1)S(1)} %get-tuple-element.48), channel_id=1, source_target_pairs={{0,8},{1,9},{2,10},{3,11},{4,24},{5,25},{6,26},{7,27},{8,0},{9,1},... | collective-permute-start | bytes 393224 | tf_op jit(solution)/shard_map/ppermute | solution.py:325
  54.9 1.6 %collective-permute-start.23 = (bf16[32,16,128]{2,1,0:T(8,128)(2,1)S(1)}, bf16[32,16,128]{2,1,0:T(8,128)(2,1)S(1)}, u32[]{:S(2)}, u32[]{:S(2)}) collective-permute-start(bf16[32,16,128]{2,1,0:T(8,128)(2,1)S(1)} %get-tuple-element.45), channel_id=1, source_target_pairs={{0,1},{1,0},{2,3},{3,2},{4,17},{5,16},{6,19},{7,18},{8,9},{9,8},{1... | collective-permute-start | bytes 393224 | tf_op jit(solution)/shard_map/ppermute | solution.py:325
  56.5 1.8 %collective-permute-start.24 = (bf16[32,16,128]{2,1,0:T(8,128)(2,1)S(1)}, bf16[32,16,128]{2,1,0:T(8,128)(2,1)S(1)}, u32[]{:S(2)}, u32[]{:S(2)}) collective-permute-start(bf16[32,16,128]{2,1,0:T(8,128)(2,1)S(1)} %get-tuple-element.46), channel_id=1, source_target_pairs={{0,9},{1,8},{2,11},{3,10},{4,25},{5,24},{6,27},{7,26},{8,1},{9,0},... | collective-permute-start | bytes 393224 | tf_op jit(solution)/shard_map/ppermute | solution.py:325
  58.3 0.1 fusion.refs_9_
  58.4 2.9 %collective-permute-done.26.refs_5_ = bf16[32,16,128]{2,1,0:T(8,128)(2,1)S(1)} collective-permute-done((bf16[32,16,128]{2,1,0:T(8,128)(2,1)S(1)}, bf16[32,16,128]{2,1,0:T(8,128)(2,1)S(1)}, u32[]{:S(2)}, u32[]{:S(2)}) %collective-permute-start.26) | collective-permute-done | bytes 131104 | tf_op jit(solution)/shard_map/ppermute | solution.py:325
  61.3 1.4 %collective-permute-done.22.refs_3_ = bf16[16,64,128]{2,1,0:T(8,128)(2,1)S(1)} collective-permute-done((bf16[16,64,128]{2,1,0:T(8,128)(2,1)S(1)}, bf16[16,64,128]{2,1,0:T(8,128)(2,1)S(1)}, u32[]{:S(2)}, u32[]{:S(2)}) %collective-permute-start.22) | collective-permute-done | bytes 262176 | tf_op jit(solution)/shard_map/ppermute | solution.py:184
  62.8 2.6 %finish.2.refs_10_ = bf16[16,128,128]{2,1,0:T(8,128)(2,1)} custom-call(s32[4]{0:T(128)S(1)} %pad_add_fusion.refs_0_, bf16[16,128,128]{2,1,0:T(8,128)(2,1)S(1)} %copy-done, bf16[16,64,128]{2,1,0:T(8,128)(2,1)S(1)} %get-tuple-element.43.refs_2_, bf16[16,64,128]{2,1,0:T(8,128)(2,1)S(1)} %collective-permute-done.22.refs_3_, ...), custom_call_target="tpu_custom_call" | custom-call | tf_op jit(solution)/shard_map/finish/pallas_call | solution.py:347
  65.4 0.5 collective-permute-done.23.refs_4_
  65.9 2.8 %collective-permute-done.24.refs_5_ = bf16[32,16,128]{2,1,0:T(8,128)(2,1)S(1)} collective-permute-done((bf16[32,16,128]{2,1,0:T(8,128)(2,1)S(1)}, bf16[32,16,128]{2,1,0:T(8,128)(2,1)S(1)}, u32[]{:S(2)}, u32[]{:S(2)}) %collective-permute-start.24) | collective-permute-done | bytes 131104 | tf_op jit(solution)/shard_map/ppermute | solution.py:325
  68.7 2.6 %finish.3 = bf16[16,128,128]{2,1,0:T(8,128)(2,1)} custom-call(s32[4]{0:T(128)S(1)} %pad_add_fusion.refs_0_, bf16[16,128,128]{2,1,0:T(8,128)(2,1)S(1)} %copy-done, bf16[16,64,128]{2,1,0:T(8,128)(2,1)S(1)} %get-tuple-element.43.refs_2_, bf16[16,64,128]{2,1,0:T(8,128)(2,1)S(1)} %collective-permute-done.22.refs_3_, ...), custom_call_target="tpu_custom_call", output_to_operand_aliasing={{}: (10, {})} | custom-call | tf_op jit(solution)/shard_map/finish/pallas_call | solution.py:347
  (50 shorter events, 0.8 us)
Async XLA Ops:
  1.5 1.5 %copy-start.3 = (bf16[128,32,64]{0,2,1:T(8,128)(2,1)S(1)}, bf16[128,32,64]{0,2,1:T(8,128)(2,1)}, u32[]{:S(2)}) copy-start(bf16[128,32,64]{0,2,1:T(8,128)(2,1)} %param.10) | copy-start | bytes 1572868
  1.7 6.9 %collective-permute-start.1 = (bf16[512,128]{1,0:T(8,128)(2,1)S(1)}, bf16[512,128]{1,0:T(8,128)(2,1)S(1)}, u32[]{:S(2)}, u32[]{:S(2)}) collective-permute-start(bf16[512,128]{1,0:T(8,128)(2,1)S(1)} %bitcast.45), channel_id=1, source_target_pairs={{0,1},{1,0},{2,3},{3,2},{4,5},{5,4},{6,7},{7,6},{8,9},{9,8},{10,11... | collective-permute-start | bytes 393224 | tf_op jit(solution)/shard_map/ppermute | solution.py:184
  3.4 5.0 %copy-start.4 = (bf16[1024,128]{1,0:T(8,128)(2,1)S(1)}, bf16[1024,128]{1,0:T(8,128)(2,1)}, u32[]{:S(2)}) copy-start(bf16[1024,128]{1,0:T(8,128)(2,1)} %param.12) | copy-start | bytes 786436
  3.4 6.0 %collective-permute-start = (bf16[512,128]{1,0:T(8,128)(2,1)S(1)}, bf16[512,128]{1,0:T(8,128)(2,1)S(1)}, u32[]{:S(2)}, u32[]{:S(2)}) collective-permute-start(bf16[512,128]{1,0:T(8,128)(2,1)S(1)} %get-tuple-element.31.refs_1_), channel_id=1, source_target_pairs={{0,4},{4,0},{1,5},{5,1},{2,6},{6,2},{3,7},{7,3},{8,12},{12,8},{9,1... | collective-permute-start | bytes 393224 | tf_op jit(solution)/shard_map/ppermute | solution.py:184
  4.7 4.7 %collective-permute-start.4 = (bf16[512,128]{1,0:T(8,128)(2,1)S(1)}, bf16[512,128]{1,0:T(8,128)(2,1)S(1)}, u32[]{:S(2)}, u32[]{:S(2)}) collective-permute-start(bf16[512,128]{1,0:T(8,128)(2,1)S(1)} %get-tuple-element.27), channel_id=1, source_target_pairs={{0,1},{1,0},{2,3},{3,2},{4,5},{5,4},{6,7},{7,6},{8,9},{9,8},{10,11... | collective-permute-start | bytes 393224 | tf_op jit(solution)/shard_map/ppermute | solution.py:184
  5.6 7.4 %collective-permute-start.7 = (bf16[512,128]{1,0:T(8,128)(2,1)S(1)}, bf16[512,128]{1,0:T(8,128)(2,1)S(1)}, u32[]{:S(2)}, u32[]{:S(2)}) collective-permute-start(bf16[512,128]{1,0:T(8,128)(2,1)S(1)} %bitcast.56), channel_id=1, source_target_pairs={{0,3},{1,2},{2,1},{3,0},{4,7},{5,6},{6,5},{7,4},{8,11},{9,10},{10,... | collective-permute-start | bytes 393224 | tf_op jit(solution)/shard_map/ppermute | solution.py:184
  8.6 7.5 %collective-permute-start.2 = (bf16[512,128]{1,0:T(8,128)(2,1)S(1)}, bf16[512,128]{1,0:T(8,128)(2,1)S(1)}, u32[]{:S(2)}, u32[]{:S(2)}) collective-permute-start(bf16[512,128]{1,0:T(8,128)(2,1)S(1)} %get-tuple-element.27), channel_id=1, source_target_pairs={{0,3},{1,2},{2,1},{3,0},{4,7},{5,6},{6,5},{7,4},{8,11},{9,10},{10,... | collective-permute-start | bytes 393224 | tf_op jit(solution)/shard_map/ppermute | solution.py:184
  9.4 6.7 %collective-permute-start.5 = (bf16[512,128]{1,0:T(8,128)(2,1)S(1)}, bf16[512,128]{1,0:T(8,128)(2,1)S(1)}, u32[]{:S(2)}, u32[]{:S(2)}) collective-permute-start(bf16[512,128]{1,0:T(8,128)(2,1)S(1)} %collective-permute-done.4.refs_5_), channel_id=1, source_target_pairs={{0,4},{4,0},{1,5},{5,1},{2,6},{6,2},{3,7},{7,3},{8,12},{12,8},{9,1... | collective-permute-start | bytes 393224 | tf_op jit(solution)/shard_map/ppermute | solution.py:184
  10.7 7.4 %collective-permute-start.14 = (bf16[512,128]{1,0:T(8,128)(2,1)S(1)}, bf16[512,128]{1,0:T(8,128)(2,1)S(1)}, u32[]{:S(2)}, u32[]{:S(2)}) collective-permute-start(bf16[512,128]{1,0:T(8,128)(2,1)S(1)} %bitcast.46), channel_id=1, source_target_pairs={{0,16},{8,24},{16,0},{24,8},{1,17},{9,25},{17,1},{25,9},{2,18},{10... | collective-permute-start | bytes 393224 | tf_op jit(solution)/shard_map/ppermute | solution.py:184
  13.0 10.1 %collective-permute-start.8 = (bf16[512,128]{1,0:T(8,128)(2,1)S(1)}, bf16[512,128]{1,0:T(8,128)(2,1)S(1)}, u32[]{:S(2)}, u32[]{:S(2)}) collective-permute-start(bf16[512,128]{1,0:T(8,128)(2,1)S(1)} %get-tuple-element.31.refs_1_), channel_id=1, source_target_pairs={{0,2},{1,3},{2,0},{3,1},{4,6},{5,7},{6,4},{7,5},{8,10},{9,11},{10,... | collective-permute-start | bytes 393224 | tf_op jit(solution)/shard_map/ppermute | solution.py:184
  16.1 7.0 %collective-permute-start.9 = (bf16[512,128]{1,0:T(8,128)(2,1)S(1)}, bf16[512,128]{1,0:T(8,128)(2,1)S(1)}, u32[]{:S(2)}, u32[]{:S(2)}) collective-permute-start(bf16[512,128]{1,0:T(8,128)(2,1)S(1)} %collective-permute-done.2.refs_13_), channel_id=1, source_target_pairs={{0,4},{4,0},{1,5},{5,1},{2,6},{6,2},{3,7},{7,3},{8,12},{12,8},{9,1... | collective-permute-start | bytes 393224 | tf_op jit(solution)/shard_map/ppermute | solution.py:184
  18.0 6.2 %collective-permute-start.16 = (bf16[512,128]{1,0:T(8,128)(2,1)S(1)}, bf16[512,128]{1,0:T(8,128)(2,1)S(1)}, u32[]{:S(2)}, u32[]{:S(2)}) collective-permute-start(bf16[512,128]{1,0:T(8,128)(2,1)S(1)} %collective-permute-done.1.refs_7_), channel_id=1, source_target_pairs={{0,16},{8,24},{16,0},{24,8},{1,17},{9,25},{17,1},{25,9},{2,18},{10... | collective-permute-start | bytes 393224 | tf_op jit(solution)/shard_map/ppermute | solution.py:184
  18.9 12.3 %collective-permute-start.11 = (bf16[512,128]{1,0:T(8,128)(2,1)S(1)}, bf16[512,128]{1,0:T(8,128)(2,1)S(1)}, u32[]{:S(2)}, u32[]{:S(2)}) collective-permute-start(bf16[512,128]{1,0:T(8,128)(2,1)S(1)} %bitcast.57), channel_id=1, source_target_pairs={{0,2},{1,3},{2,0},{3,1},{4,6},{5,7},{6,4},{7,5},{8,10},{9,11},{10,... | collective-permute-start | bytes 393224 | tf_op jit(solution)/shard_map/ppermute | solution.py:184
  23.1 9.7 %collective-permute-start.10 = (bf16[512,128]{1,0:T(8,128)(2,1)S(1)}, bf16[512,128]{1,0:T(8,128)(2,1)S(1)}, u32[]{:S(2)}, u32[]{:S(2)}) collective-permute-start(bf16[512,128]{1,0:T(8,128)(2,1)S(1)} %collective-permute-done.8.refs_9_), channel_id=1, source_target_pairs={{0,4},{4,0},{1,5},{5,1},{2,6},{6,2},{3,7},{7,3},{8,12},{12,8},{9,1... | collective-permute-start | bytes 393224 | tf_op jit(solution)/shard_map/ppermute | solution.py:184
  24.2 10.5 %collective-permute-start.20 = (bf16[512,128]{1,0:T(8,128)(2,1)S(1)}, bf16[512,128]{1,0:T(8,128)(2,1)S(1)}, u32[]{:S(2)}, u32[]{:S(2)}) collective-permute-start(bf16[512,128]{1,0:T(8,128)(2,1)S(1)} %collective-permute-done.7.refs_15_), channel_id=1, source_target_pairs={{0,16},{8,24},{16,0},{24,8},{1,17},{9,25},{17,1},{25,9},{2,18},{10... | collective-permute-start | bytes 393224 | tf_op jit(solution)/shard_map/ppermute | solution.py:184
  25.4 10.2 %collective-permute-start.13 = (bf16[512,128]{1,0:T(8,128)(2,1)S(1)}, bf16[512,128]{1,0:T(8,128)(2,1)S(1)}, u32[]{:S(2)}, u32[]{:S(2)}) collective-permute-start(bf16[512,128]{1,0:T(8,128)(2,1)S(1)} %collective-permute-done.7.refs_15_), channel_id=1, source_target_pairs={{0,8},{8,0},{16,24},{24,16},{1,9},{9,1},{17,25},{25,17},{2,10},{10... | collective-permute-start | bytes 393224 | tf_op jit(solution)/shard_map/ppermute | solution.py:184
  30.3 5.9 %collective-permute-start.6 = (bf16[512,128]{1,0:T(8,128)(2,1)S(1)}, bf16[512,128]{1,0:T(8,128)(2,1)S(1)}, u32[]{:S(2)}, u32[]{:S(2)}) collective-permute-start(bf16[512,128]{1,0:T(8,128)(2,1)S(1)} %collective-permute-done.1.refs_7_), channel_id=1, source_target_pairs={{0,8},{8,0},{16,24},{24,16},{1,9},{9,1},{17,25},{25,17},{2,10},{10... | collective-permute-start | bytes 393224 | tf_op jit(solution)/shard_map/ppermute | solution.py:184
  31.2 5.0 %collective-permute-start.3 = (bf16[512,128]{1,0:T(8,128)(2,1)S(1)}, bf16[512,128]{1,0:T(8,128)(2,1)S(1)}, u32[]{:S(2)}, u32[]{:S(2)}) collective-permute-start(bf16[512,128]{1,0:T(8,128)(2,1)S(1)} %bitcast.47), channel_id=1, source_target_pairs={{0,8},{8,0},{16,24},{24,16},{1,9},{9,1},{17,25},{25,17},{2,10},{10... | collective-permute-start | bytes 393224 | tf_op jit(solution)/shard_map/ppermute | solution.py:184
  32.8 7.8 %collective-permute-start.12 = (bf16[512,128]{1,0:T(8,128)(2,1)S(1)}, bf16[512,128]{1,0:T(8,128)(2,1)S(1)}, u32[]{:S(2)}, u32[]{:S(2)}) collective-permute-start(bf16[512,128]{1,0:T(8,128)(2,1)S(1)} %collective-permute-done.11.refs_11_), channel_id=1, source_target_pairs={{0,8},{8,0},{16,24},{24,16},{1,9},{9,1},{17,25},{25,17},{2,10},{10... | collective-permute-start | bytes 393224 | tf_op jit(solution)/shard_map/ppermute | solution.py:184
  34.7 5.1 %collective-permute-start.18 = (bf16[512,128]{1,0:T(8,128)(2,1)S(1)}, bf16[512,128]{1,0:T(8,128)(2,1)S(1)}, u32[]{:S(2)}, u32[]{:S(2)}) collective-permute-start(bf16[512,128]{1,0:T(8,128)(2,1)S(1)} %collective-permute-done.11.refs_11_), channel_id=1, source_target_pairs={{0,16},{8,24},{16,0},{24,8},{1,17},{9,25},{17,1},{25,9},{2,18},{10... | collective-permute-start | bytes 393224 | tf_op jit(solution)/shard_map/ppermute | solution.py:184
  34.9 0.7 copy-start.5
  34.9 0.7 copy-start.7
  34.9 0.7 copy-start.8
  35.6 8.5 %copy-start.6 = (f32[128]{0:T(128)S(1)}, f32[128]{0:T(128)}, u32[]{:S(2)}) copy-start(f32[128]{0:T(128)} %param.13) | copy-start | bytes 1540
  35.6 8.5 %collective-permute-start.15 = (bf16[512,128]{1,0:T(8,128)(2,1)S(1)}, bf16[512,128]{1,0:T(8,128)(2,1)S(1)}, u32[]{:S(2)}, u32[]{:S(2)}) collective-permute-start(bf16[512,128]{1,0:T(8,128)(2,1)S(1)} %collective-permute-done.14.refs_17_), channel_id=1, source_target_pairs={{0,8},{8,0},{16,24},{24,16},{1,9},{9,1},{17,25},{25,17},{2,10},{10... | collective-permute-start | bytes 393224 | tf_op jit(solution)/shard_map/ppermute | solution.py:184
  36.2 8.0 %collective-permute-start.17 = (bf16[512,128]{1,0:T(8,128)(2,1)S(1)}, bf16[512,128]{1,0:T(8,128)(2,1)S(1)}, u32[]{:S(2)}, u32[]{:S(2)}) collective-permute-start(bf16[512,128]{1,0:T(8,128)(2,1)S(1)} %collective-permute-done.16.refs_19_), channel_id=1, source_target_pairs={{0,8},{8,0},{16,24},{24,16},{1,9},{9,1},{17,25},{25,17},{2,10},{10... | collective-permute-start | bytes 393224 | tf_op jit(solution)/shard_map/ppermute | solution.py:184
  36.2 7.9 %collective-permute-start.21 = (bf16[512,128]{1,0:T(8,128)(2,1)S(1)}, bf16[512,128]{1,0:T(8,128)(2,1)S(1)}, u32[]{:S(2)}, u32[]{:S(2)}) collective-permute-start(bf16[512,128]{1,0:T(8,128)(2,1)S(1)} %collective-permute-done.20.refs_23_), channel_id=1, source_target_pairs={{0,8},{8,0},{16,24},{24,16},{1,9},{9,1},{17,25},{25,17},{2,10},{10... | collective-permute-start | bytes 393224 | tf_op jit(solution)/shard_map/ppermute | solution.py:184
  39.8 4.4 %collective-permute-start.19 = (bf16[512,128]{1,0:T(8,128)(2,1)S(1)}, bf16[512,128]{1,0:T(8,128)(2,1)S(1)}, u32[]{:S(2)}, u32[]{:S(2)}) collective-permute-start(bf16[512,128]{1,0:T(8,128)(2,1)S(1)} %collective-permute-done.18.refs_21_), channel_id=1, source_target_pairs={{0,8},{8,0},{16,24},{24,16},{1,9},{9,1},{17,25},{25,17},{2,10},{10... | collective-permute-start | bytes 393224 | tf_op jit(solution)/shard_map/ppermute | solution.py:184
  44.2 18.5 %copy-start = (bf16[16,128,128]{2,1,0:T(8,128)(2,1)S(1)}, bf16[16,128,128]{2,1,0:T(8,128)(2,1)}, u32[]{:S(2)}) copy-start(bf16[16,128,128]{2,1,0:T(8,128)(2,1)} %refs_1_.3) | copy-start | bytes 1572868
  44.2 18.5 %copy-start.2 = (bf16[512,128]{1,0:T(8,128)(2,1)S(1)}, bf16[512,128]{1,0:T(8,128)(2,1)}, u32[]{:S(2)}) copy-start(bf16[512,128]{1,0:T(8,128)(2,1)} %refs_7_.3) | copy-start | bytes 393220
  48.2 14.5 %copy-start.1 = (bf16[128,512]{1,0:T(8,128)(2,1)S(1)}, bf16[128,512]{1,0:T(8,128)(2,1)}, u32[]{:S(2)}) copy-start(bf16[128,512]{1,0:T(8,128)(2,1)} %refs_6_.3) | copy-start | bytes 393220
  48.2 14.5 %collective-permute-start.22 = (bf16[16,64,128]{2,1,0:T(8,128)(2,1)S(1)}, bf16[16,64,128]{2,1,0:T(8,128)(2,1)S(1)}, u32[]{:S(2)}, u32[]{:S(2)}) collective-permute-start(bf16[16,64,128]{2,1,0:T(8,128)(2,1)S(1)} %get-tuple-element.44), channel_id=1, source_target_pairs={{0,2},{1,3},{2,0},{3,1},{4,6},{5,7},{6,4},{7,5},{8,10},{9,11},{10,... | collective-permute-start | bytes 786440 | tf_op jit(solution)/shard_map/ppermute | solution.py:184
  50.1 8.3 %collective-permute-start.25 = (bf16[32,16,128]{2,1,0:T(8,128)(2,1)S(1)}, bf16[32,16,128]{2,1,0:T(8,128)(2,1)S(1)}, u32[]{:S(2)}, u32[]{:S(2)}) collective-permute-start(bf16[32,16,128]{2,1,0:T(8,128)(2,1)S(1)} %get-tuple-element.47), channel_id=1, source_target_pairs={{0,0},{1,1},{2,2},{3,3},{4,16},{5,17},{6,18},{7,19},{8,8},{9,9},{1... | collective-permute-start | bytes 393224 | tf_op jit(solution)/shard_map/ppermute | solution.py:325
  52.8 8.5 %collective-permute-start.26 = (bf16[32,16,128]{2,1,0:T(8,128)(2,1)S(1)}, bf16[32,16,128]{2,1,0:T(8,128)(2,1)S(1)}, u32[]{:S(2)}, u32[]{:S(2)}) collective-permute-start(bf16[32,16,128]{2,1,0:T(8,128)(2,1)S(1)} %get-tuple-element.48), channel_id=1, source_target_pairs={{0,8},{1,9},{2,10},{3,11},{4,24},{5,25},{6,26},{7,27},{8,0},{9,1},... | collective-permute-start | bytes 393224 | tf_op jit(solution)/shard_map/ppermute | solution.py:325
  54.9 11.0 %collective-permute-start.23 = (bf16[32,16,128]{2,1,0:T(8,128)(2,1)S(1)}, bf16[32,16,128]{2,1,0:T(8,128)(2,1)S(1)}, u32[]{:S(2)}, u32[]{:S(2)}) collective-permute-start(bf16[32,16,128]{2,1,0:T(8,128)(2,1)S(1)} %get-tuple-element.45), channel_id=1, source_target_pairs={{0,1},{1,0},{2,3},{3,2},{4,17},{5,16},{6,19},{7,18},{8,9},{9,8},{1... | collective-permute-start | bytes 393224 | tf_op jit(solution)/shard_map/ppermute | solution.py:325
  56.5 12.2 %collective-permute-start.24 = (bf16[32,16,128]{2,1,0:T(8,128)(2,1)S(1)}, bf16[32,16,128]{2,1,0:T(8,128)(2,1)S(1)}, u32[]{:S(2)}, u32[]{:S(2)}) collective-permute-start(bf16[32,16,128]{2,1,0:T(8,128)(2,1)S(1)} %get-tuple-element.46), channel_id=1, source_target_pairs={{0,9},{1,8},{2,11},{3,10},{4,25},{5,24},{6,27},{7,26},{8,1},{9,0},... | collective-permute-start | bytes 393224 | tf_op jit(solution)/shard_map/ppermute | solution.py:325

commit v7 on v6

--- a/solution.py
+++ b/solution.py
@@ -12,39 +12,40 @@
 
 
 def update_kernel(places, shares, low, last, scale, *refs):
-    left_places, right_places, share_rows, source_rows, group_len, operands = places
+    left_count, right_places, share_rows, source_rows, group_len, run = places
+    groups = len(right_places)
+    sources = len(right_places[0])
     refs = list(refs)
     place_ref = refs.pop(0)
-    data_refs = [refs.pop(0) for _ in range(operands)]
-    bias_ref, partial_ref = (refs.pop(0), refs.pop(0)) if last else (None, None)
-    weight_ref = refs.pop(0)
-    update_ref = refs.pop() if last else None
+    left_refs = [refs.pop(0) for _ in range(left_count)]
+    data_refs = [refs.pop(0) for _ in range(groups * sources)]
+    bias_ref, weight_ref = refs.pop(0), refs.pop(0)
+    first_ref = refs.pop(0) if last else None
+    update_ref = refs.pop() if last else refs[0]
     outer_ref = refs.pop()
     lhs_ref = refs.pop()
     out_refs = refs
-    groups = len(left_places)
     row_count, _, lanes = outer_ref.shape
-    channels = share_rows * shares // row_count
+    blocks = left_count // groups
+    channels = share_rows * blocks // row_count
+    share = share_rows // channels
     per = source_rows // group_len
-    sources = len(right_places[0])
     half = lanes // 2
     pair_channels = weight_ref.shape[0] // 2
     lane_low = lax.broadcasted_iota(jnp.int32, (pair_channels, lanes), 1) < half
-    for dy in range(shares):
-        begin = pl.multiple_of((place_ref[2] ^ dy) * share_rows, share_rows)
+    for block in range(blocks):
         for dz in range(groups):
-            operand, first = left_places[dz][dy]
-            lhs_ref[pl.ds(begin, share_rows), dz * group_len : (dz + 1) * group_len] = data_refs[
-                operand
-            ][first : first + share_rows]
+            lhs_ref[
+                block * share_rows : (block + 1) * share_rows,
+                dz * group_len : (dz + 1) * group_len,
+            ] = left_refs[dz * blocks + block][...]
 
     def right_tile(item):
         source, rest = divmod(item, per)
         tiles = []
         for dz in range(groups):
-            operand, first = right_places[dz][source]
-            first += rest * group_len
-            tiles.append(data_refs[operand][first : first + group_len])
+            first = rest * group_len
+            tiles.append(data_refs[right_places[dz][source]][first : first + group_len])
         return jnp.concatenate(tiles, axis=0)
 
     for pair in range(sources * per // 2):
@@ -57,10 +58,12 @@
                 :, part * lanes : (part + 1) * lanes
             ].reshape(row_count, channels, lanes)
 
-    @pl.loop(0, row_count // 8)
+    unroll = min(4, row_count // 2)
+
+    @pl.loop(0, row_count // (2 * unroll))
     def _(step):
-        for two in range(4):
-            index = step * 4 + two
+        for two in range(unroll):
+            index = step * unroll + two
             both = jnp.concatenate([outer_ref[2 * index], outer_ref[2 * index + 1]], axis=1)
             proj = jnp.dot(weight_ref[...], both, preferred_element_type=jnp.float32)
             a0 = proj[:pair_channels, :lanes]
@@ -70,17 +73,15 @@
             cell = jnp.where(lane_low, a0, b1) + pltpu.roll(
                 jnp.where(lane_low, a1, b0), half, 1
             )
+            cell = (cell * scale + bias_ref[...]).astype(jnp.bfloat16)
+            begin = 2 * index
             if last:
-                cell = (cell + partial_ref[index]) * scale + bias_ref[...]
-                update_ref[pl.ds(2 * index, 2)] = (
-                    cell.astype(jnp.bfloat16).T.reshape(2, half, pair_channels)
-                )
-            else:
-                out_refs[0][index] = cell
+                begin = (place_ref[2] ^ (1 + begin // share)) * share + begin % share
+            update_ref[pl.ds(begin, 2)] = cell.T.reshape(2, half, pair_channels)
 
     if last:
+        update_ref[pl.ds(place_ref[2] * share, share)] = first_ref[...]
         core, z_low, z_high = place_ref[0], place_ref[1], place_ref[3]
-        run = row_count // 2
         out_refs[0][...] = update_ref[pl.ds(z_high * run, run)]
         out_refs[1][...] = update_ref[pl.ds((1 - z_high) * run, run)]
         for dz in range(low):
@@ -219,96 +220,82 @@
 
     rights[3] = along(right_sends, 3)
     rights[1] = along(right_sends, 1)
-    last_x = over_x(0, rights[1])
-    last_y = over_y(0)
+    last_x = over_x(0)
+    last_x = over_x(1, *last_x)
     lefts[3] = along(left_sends, 3, rights[1])
-    lefts[1] = along(left_sends, 1)
-    last_x = over_x(1, *last_x)
+    lefts[1] = along(left_sends, 1, rights[1])
+    last_y = over_y(0, rights[1])
     lefts[2] = along(left_sends, 2, rights[3])
+    rights[2] = swap(rights[3], "seq", groups, 1)
     last_x = over_x(3, *last_x)
     last_y = over_y(1, *last_y)
-    rights[2] = along(right_sends, 2, lefts[3])
     last_y = over_y(3, *last_y)
+    over_x(2, lefts[3], *last_x)
+    over_y(2, *last_y)
     cored, cored_too = {}, {}
-    for dz in (0, 1, 3):
-        cored[dz] = swap(after(rights[dz], lefts[3]), "row", rows, 1)
-        cored_too[dz] = [swap(after(value, lefts[2]), "row", rows, 1) for value in crossed[dz]]
-    last_y = over_y(2, *last_y)
-    rights[2] = after(rights[2], *last_y)
-    over_x(2)
-    cored[2] = swap(rights[2], "row", rows, 1)
-    cored_too[2] = [swap(value, "row", rows, 1) for value in crossed[2]]
-
-    data, others = [], []
-    left_places = {dz: [] for dz in range(groups)}
-    right_places = {dz: [] for dz in range(groups)}
-    other_places = {dz: [] for dz in range(groups)}
-
-    def place_in(store, table, dz, value):
-        table[dz].append((len(store), 0))
-        store.append(value)
-
+    for dz in (0, 1, 3, 2):
+        behind = (shared[3], lefts[2]) if dz == 2 else (rights[3], lefts[3])
+        cored[dz] = swap(after(rights[dz], behind[0]), "row", rows, 1)
+        cored_too[dz] = [swap(after(value, behind[1]), "row", rows, 1) for value in crossed[dz]]
+
+    data, right_places = [], []
     for dz in range(groups):
-        for value in [lefts[dz]] + shared[dz]:
-            place_in(data, left_places, dz, value)
-        for value in (rights[dz], cored[dz]):
-            place_in(data, right_places, dz, value)
+        values = [rights[dz], cored[dz]]
         for pair in zip(crossed[dz], cored_too[dz]):
-            for value in pair:
-                place_in(others, other_places, dz, value)
+            values += pair
+        right_places.append(list(range(len(data), len(data) + len(values))))
+        data += values
+    first_lefts = [lefts[dz] for dz in range(groups)]
+    last_lefts = [value for dz in range(groups) for value in shared[dz]]
 
     weight = proj_weight.reshape(channels, rows, e1, 2, pair_channels)
     weight = weight.transpose(1, 3, 4, 2, 0)
     weight = jnp.stack([pick(weight, row ^ m) for m in range(rows)], axis=2)
     weight = weight.reshape(2 * pair_channels, channels * channels // 2)
-    split = channels * channels // 2 // xs
 
     place = jnp.stack([core, z_low, col, z_high]).astype(jnp.int32)
     vmem = pl.BlockSpec(memory_space=pltpu.VMEM)
     smem = pl.BlockSpec(memory_space=pltpu.SMEM)
     params = pltpu.CompilerParams(vmem_limit_bytes=40 * 1024 * 1024)
     scale = 1.0 / (group_len * groups)
-    lhs = pltpu.VMEM((2 * run * channels, groups * group_len), bf16)
-
-    def tabled(table):
-        return [table[dz] for dz in range(groups)]
-
-    sizes = (share_rows, source_rows, group_len)
-    places = (tabled(left_places), tabled(right_places)) + sizes + (len(data),)
-    outer_size = 4 * run * channels * split * half
-    cost = pl.CostEstimate(
-        flops=2 * outer_size * (groups * group_len + 2 * pair_channels),
-        bytes_accessed=2 * outer_size,
-        transcendentals=0,
-    )
-    partial = pl.pallas_call(
-        functools.partial(update_kernel, places, cols, low, False, scale),
-        out_shape=jax.ShapeDtypeStruct((run, pair_channels, 2 * half), jnp.float32),
-        in_specs=[smem] + [vmem] * (len(data) + 1),
-        out_specs=vmem,
-        scratch_shapes=[lhs, pltpu.VMEM((2 * run, split, 2 * half), bf16)],
-        compiler_params=params,
-        cost_estimate=cost,
-        name="update_first",
-    )(place, *data, weight[:, :split])
-    shifted = [[(o + len(data), f) for o, f in other_places[dz]] for dz in range(groups)]
-    places = (tabled(left_places), shifted) + sizes + (len(data) + len(others),)
     bias = jnp.broadcast_to(proj_bias[:, None], (pair_channels, 2 * half))
-    outs = pl.pallas_call(
-        functools.partial(update_kernel, places, cols, low, True, scale),
-        out_shape=[jax.ShapeDtypeStruct((run, half, pair_channels), bf16)] * 2
+    share = share_rows // channels
+
+    def update_call(last, left_values, extra, out_shape, out_specs, scratch):
+        row_count = share * len(left_values) // groups
+        outer_size = row_count * channels * channels * half
+        places = (len(left_values), right_places, share_rows, source_rows, group_len, run)
+        return pl.pallas_call(
+            functools.partial(update_kernel, places, cols, low, last, scale),
+            out_shape=out_shape,
+            in_specs=[smem] + [vmem] * (len(left_values) + len(data) + 2 + len(extra)),
+            out_specs=out_specs,
+            scratch_shapes=[
+                pltpu.VMEM((row_count * channels, groups * group_len), bf16),
+                pltpu.VMEM((row_count, channels * channels // 2, 2 * half), bf16),
+            ]
+            + scratch,
+            compiler_params=params,
+            cost_estimate=pl.CostEstimate(
+                flops=2 * outer_size * (groups * group_len + 2 * pair_channels),
+                bytes_accessed=2 * outer_size,
+                transcendentals=0,
+            ),
+            name="update_last" if last else "update_first",
+        )(place, *left_values, *data, bias, weight, *extra)
+
+    first = update_call(
+        False, first_lefts, [], jax.ShapeDtypeStruct((share, half, pair_channels), bf16), vmem, []
+    )
+    outs = update_call(
+        True,
+        last_lefts,
+        [first],
+        [jax.ShapeDtypeStruct((run, half, pair_channels), bf16)] * 2
         + [jax.ShapeDtypeStruct((2 * run, run, pair_channels), bf16)] * (2 * low),
-        in_specs=[smem] + [vmem] * (len(data) + len(others) + 3),
-        out_specs=[vmem] * (2 + 2 * low),
-        scratch_shapes=[
-            lhs,
-            pltpu.VMEM((2 * run, (xs - 1) * split, 2 * half), bf16),
-            pltpu.VMEM((2 * run, half, pair_channels), bf16),
-        ],
-        compiler_params=params,
-        cost_estimate=cost,
-        name="update_last",
-    )(place, *data, *others, bias, partial, weight[:, split:])
+        [vmem] * (2 + 2 * low),
+        [pltpu.VMEM((2 * run, half, pair_channels), bf16)],
+    )
 
     update_other = swap(outs[1], "seq", groups, low)
     mirrors = []

time: 72 us -> 66.6 us (0.925)
  the two profiles are of different devices: /device:TPU:3 before, /device:TPU:11 now
where the time goes in v7:
time: 66.6 us; the launch traced here: 66.4 us
  starting transfers between devices  38.6 us (58%)
  waiting for transfers between devices  12.2 us (18%)
  Pallas kernels  11.4 us (17%)
  local copies, waits for them, and re-layouts  3.26 us (5%)
    ppermute x23, starting transfers between devices, swap(): return lax.ppermute(value, name, [(i, i ^ flip) for i in range(size)])  30.3 us
    ppermute x4, waiting for transfers between devices, on_device(): mirrors.append(lax.ppermute(outs[2 + 2 * dz + flip], axes, pairs))  8.55 us
    ppermute x4, starting transfers between devices, on_device(): mirrors.append(lax.ppermute(outs[2 + 2 * dz + flip], axes, pairs))  8.38 us
    pallas_call x2, Pallas kernels, update_call(): pl.pallas_call(functools.partial(update_kernel, places, cols, low, last,...  6.13 us
    pallas_call x2, Pallas kernels, on_device(): pl.pallas_call(functools.partial(finish_kernel, low, dz), out_shape=jax.S...  5.27 us
    ppermute x23, waiting for transfers between devices, swap(): return lax.ppermute(value, name, [(i, i ^ flip) for i in range(size)])  3.63 us
    unnamed x20, local copies, waits for them, and re-layouts  1.74 us
  transfers between devices with their start and end apart: 27, of which 4 were waited for; matrix products, arithmetic and copies ran while one was open for 3% of the time, Pallas kernels for 8%

profile of v7, /device:TPU:11, one launch (start us, length us, event | category | flops | bytes accessed | tf_op | source)
XLA Modules:
  0.0 66.4 jit_solution(7164898708042933924)
XLA Ops:
  0.0 1.1 %copy.19 = bf16[128,8,128]{0,2,1:T(8,128)(2,1)S(1)} copy(bf16[128,8,128]{2,1,0:T(8,128)(2,1)} %param.11) | data formatting | bytes 524288 | tf_op args[1]
  1.2 0.2 copy.20
  1.4 0.1 reshape.55
  1.5 0.1 copy.21
  1.7 0.2 collective-permute-start
  1.9 0.2 collective-permute-start.10
  2.1 0.1 copy.22
  2.2 2.6 %collective-permute-start.4 = (bf16[512,128]{1,0:T(8,128)(2,1)S(1)}, bf16[512,128]{1,0:T(8,128)(2,1)S(1)}, u32[]{:S(2)}, u32[]{:S(2)}) collective-permute-start(bf16[512,128]{1,0:T(8,128)(2,1)S(1)} %bitcast.56), channel_id=1, source_target_pairs={{0,3},{1,2},{2,1},{3,0},{4,7},{5,6},{6,5},{7,4},{8,11},{9,10},{10,... | collective-permute-start | bytes 393224 | tf_op jit(solution)/shard_map/ppermute | solution.py:185
  4.8 0.3 copy.18
  5.2 0.9 %collective-permute-done.refs_9_ = bf16[512,128]{1,0:T(8,128)(2,1)S(1)} collective-permute-done((bf16[512,128]{1,0:T(8,128)(2,1)S(1)}, bf16[512,128]{1,0:T(8,128)(2,1)S(1)}, u32[]{:S(2)}, u32[]{:S(2)}) %collective-permute-start) | collective-permute-done | bytes 131104 | tf_op jit(solution)/shard_map/ppermute | solution.py:185
  6.1 0.4 collective-permute-start.13
  6.5 1.1 %collective-permute-start.2 = (bf16[512,128]{1,0:T(8,128)(2,1)S(1)}, bf16[512,128]{1,0:T(8,128)(2,1)S(1)}, u32[]{:S(2)}, u32[]{:S(2)}) collective-permute-start(bf16[512,128]{1,0:T(8,128)(2,1)S(1)} %get-tuple-element.29), channel_id=1, source_target_pairs={{0,1},{1,0},{2,3},{3,2},{4,5},{5,4},{6,7},{7,6},{8,9},{9,8},{10,11... | collective-permute-start | bytes 393224 | tf_op jit(solution)/shard_map/ppermute | solution.py:185
  7.5 1.3 %collective-permute-start.1 = (bf16[512,128]{1,0:T(8,128)(2,1)S(1)}, bf16[512,128]{1,0:T(8,128)(2,1)S(1)}, u32[]{:S(2)}, u32[]{:S(2)}) collective-permute-start(bf16[512,128]{1,0:T(8,128)(2,1)S(1)} %get-tuple-element.31.refs_1_), channel_id=1, source_target_pairs={{0,4},{4,0},{1,5},{5,1},{2,6},{6,2},{3,7},{7,3},{8,12},{12,8},{9,1... | collective-permute-start | bytes 393224 | tf_op jit(solution)/shard_map/ppermute | solution.py:185
  8.8 0.2 constant_dynamic-slice_fusion.3
  9.0 1.4 %collective-permute-start.6 = (bf16[512,128]{1,0:T(8,128)(2,1)S(1)}, bf16[512,128]{1,0:T(8,128)(2,1)S(1)}, u32[]{:S(2)}, u32[]{:S(2)}) collective-permute-start(bf16[512,128]{1,0:T(8,128)(2,1)S(1)} %get-tuple-element.29), channel_id=1, source_target_pairs={{0,3},{1,2},{2,1},{3,0},{4,7},{5,6},{6,5},{7,4},{8,11},{9,10},{10,... | collective-permute-start | bytes 393224 | tf_op jit(solution)/shard_map/ppermute | solution.py:185
  10.4 1.1 %collective-permute-start.5 = (bf16[512,128]{1,0:T(8,128)(2,1)S(1)}, bf16[512,128]{1,0:T(8,128)(2,1)S(1)}, u32[]{:S(2)}, u32[]{:S(2)}) collective-permute-start(bf16[512,128]{1,0:T(8,128)(2,1)S(1)} %get-tuple-element.31.refs_1_), channel_id=1, source_target_pairs={{0,2},{1,3},{2,0},{3,1},{4,6},{5,7},{6,4},{7,5},{8,10},{9,11},{10,... | collective-permute-start | bytes 393224 | tf_op jit(solution)/shard_map/ppermute | solution.py:185
  11.5 1.2 %collective-permute-start.15 = (bf16[512,128]{1,0:T(8,128)(2,1)S(1)}, bf16[512,128]{1,0:T(8,128)(2,1)S(1)}, u32[]{:S(2)}, u32[]{:S(2)}) collective-permute-start(bf16[512,128]{1,0:T(8,128)(2,1)S(1)} %collective-permute-done.4.refs_17_), channel_id=1, source_target_pairs={{0,1},{1,0},{2,3},{3,2},{4,5},{5,4},{6,7},{7,6},{8,9},{9,8},{10,11... | collective-permute-start | bytes 393224 | tf_op jit(solution)/shard_map/ppermute | solution.py:185
  12.7 1.5 %collective-permute-start.17 = (bf16[512,128]{1,0:T(8,128)(2,1)S(1)}, bf16[512,128]{1,0:T(8,128)(2,1)S(1)}, u32[]{:S(2)}, u32[]{:S(2)}) collective-permute-start(bf16[512,128]{1,0:T(8,128)(2,1)S(1)} %collective-permute-done.4.refs_17_), channel_id=1, source_target_pairs={{0,16},{8,24},{16,0},{24,8},{1,17},{9,25},{17,1},{25,9},{2,18},{10... | collective-permute-start | bytes 393224 | tf_op jit(solution)/shard_map/ppermute | solution.py:185
  14.2 1.2 %collective-permute-start.3 = (bf16[512,128]{1,0:T(8,128)(2,1)S(1)}, bf16[512,128]{1,0:T(8,128)(2,1)S(1)}, u32[]{:S(2)}, u32[]{:S(2)}) collective-permute-start(bf16[512,128]{1,0:T(8,128)(2,1)S(1)} %collective-permute-done.2.refs_2_), channel_id=1, source_target_pairs={{0,4},{4,0},{1,5},{5,1},{2,6},{6,2},{3,7},{7,3},{8,12},{12,8},{9,1... | collective-permute-start | bytes 393224 | tf_op jit(solution)/shard_map/ppermute | solution.py:185
  15.4 0.1 copy_bitcast_fusion.1
  15.5 6.7 %collective-permute-start.12 = (bf16[512,128]{1,0:T(8,128)(2,1)S(1)}, bf16[512,128]{1,0:T(8,128)(2,1)S(1)}, u32[]{:S(2)}, u32[]{:S(2)}) collective-permute-start(bf16[512,128]{1,0:T(8,128)(2,1)S(1)} %collective-permute-done.refs_9_), channel_id=1, source_target_pairs={{0,8},{8,0},{16,24},{24,16},{1,9},{9,1},{17,25},{25,17},{2,10},{10... | collective-permute-start | bytes 393224 | tf_op jit(solution)/shard_map/ppermute | solution.py:185
  22.2 0.5 collective-permute-start.9
  22.7 0.0 collective-permute-start.20
  22.7 1.2 %collective-permute-start.18 = (bf16[512,128]{1,0:T(8,128)(2,1)S(1)}, bf16[512,128]{1,0:T(8,128)(2,1)S(1)}, u32[]{:S(2)}, u32[]{:S(2)}) collective-permute-start(bf16[512,128]{1,0:T(8,128)(2,1)S(1)} %collective-permute-done.15.refs_13_), channel_id=1, source_target_pairs={{0,16},{8,24},{16,0},{24,8},{1,17},{9,25},{17,1},{25,9},{2,18},{10... | collective-permute-start | bytes 393224 | tf_op jit(solution)/shard_map/ppermute | solution.py:185
  24.0 0.8 %collective-permute-start.7 = (bf16[512,128]{1,0:T(8,128)(2,1)S(1)}, bf16[512,128]{1,0:T(8,128)(2,1)S(1)}, u32[]{:S(2)}, u32[]{:S(2)}) collective-permute-start(bf16[512,128]{1,0:T(8,128)(2,1)S(1)} %collective-permute-done.6.refs_4_), channel_id=1, source_target_pairs={{0,4},{4,0},{1,5},{5,1},{2,6},{6,2},{3,7},{7,3},{8,12},{12,8},{9,1... | collective-permute-start | bytes 393224 | tf_op jit(solution)/shard_map/ppermute | solution.py:185
  24.8 0.1 copy_bitcast_fusion.3
  24.9 0.5 pad_maximum_fusion
  25.4 2.0 %collective-permute-done.18.refs_15_ = bf16[512,128]{1,0:T(8,128)(2,1)S(1)} collective-permute-done((bf16[512,128]{1,0:T(8,128)(2,1)S(1)}, bf16[512,128]{1,0:T(8,128)(2,1)S(1)}, u32[]{:S(2)}, u32[]{:S(2)}) %collective-permute-start.18) | collective-permute-done | bytes 131104 | tf_op jit(solution)/shard_map/ppermute | solution.py:185
  27.4 1.3 %collective-permute-start.14 = (bf16[512,128]{1,0:T(8,128)(2,1)S(1)}, bf16[512,128]{1,0:T(8,128)(2,1)S(1)}, u32[]{:S(2)}, u32[]{:S(2)}) collective-permute-start(bf16[512,128]{1,0:T(8,128)(2,1)S(1)} %collective-permute-done.13.refs_11_), channel_id=1, source_target_pairs={{0,8},{8,0},{16,24},{24,16},{1,9},{9,1},{17,25},{25,17},{2,10},{10... | collective-permute-start | bytes 393224 | tf_op jit(solution)/shard_map/ppermute | solution.py:185
  28.7 1.2 %collective-permute-start.11 = (bf16[512,128]{1,0:T(8,128)(2,1)S(1)}, bf16[512,128]{1,0:T(8,128)(2,1)S(1)}, u32[]{:S(2)}, u32[]{:S(2)}) collective-permute-start(bf16[512,128]{1,0:T(8,128)(2,1)S(1)} %collective-permute-done.10.refs_7_), channel_id=1, source_target_pairs={{0,8},{8,0},{16,24},{24,16},{1,9},{9,1},{17,25},{25,17},{2,10},{10... | collective-permute-start | bytes 393224 | tf_op jit(solution)/shard_map/ppermute | solution.py:185
  29.9 0.5 collective-permute-start.19
  30.4 0.1 collective-permute-start.16
  30.5 0.1 pad_add_fusion.refs_0_
  30.6 0.1 copy.28.refs_22_
  30.8 0.5 copy-done.5
  31.3 0.9 %collective-permute-start.8 = (bf16[512,128]{1,0:T(8,128)(2,1)S(1)}, bf16[512,128]{1,0:T(8,128)(2,1)S(1)}, u32[]{:S(2)}, u32[]{:S(2)}) collective-permute-start(bf16[512,128]{1,0:T(8,128)(2,1)S(1)} %collective-permute-done.5.refs_3_), channel_id=1, source_target_pairs={{0,4},{4,0},{1,5},{5,1},{2,6},{6,2},{3,7},{7,3},{8,12},{12,8},{9,1... | collective-permute-start | bytes 393224 | tf_op jit(solution)/shard_map/ppermute | solution.py:185
  32.3 0.1 broadcast_in_dim.2.refs_21_
  32.3 3.0 %update_first.1.refs_23_ = bf16[16,64,128]{2,1,0:T(8,128)(2,1)S(1)} custom-call(s32[4]{0:T(128)S(1)} %pad_add_fusion.refs_0_, bf16[512,128]{1,0:T(8,128)(2,1)S(1)} %get-tuple-element.31.refs_1_, bf16[512,128]{1,0:T(8,128)(2,1)S(1)} %collective-permute-done.2.refs_2_, bf16[512,128]{1,0:T(8,128)(2,1)S(1)} %collective-permute-done.5.refs_3_, ...), custom_call_target="tpu_custom_call" | custom-call | flops 1610612736 | bytes 2097152 | tf_op jit(solution)/shard_map/update_first/pallas_call | solution.py:268
  35.4 0.7 collective-permute-done.8.refs_3_
  36.0 3.1 %update_last.1 = (bf16[16,64,128]{2,1,0:T(8,128)(2,1)S(1)}, bf16[16,64,128]{2,1,0:T(8,128)(2,1)S(1)}, bf16[32,16,128]{2,1,0:T(8,128)(2,1)S(1)}, bf16[32,16,128]{...) custom-call(s32[4]{0:T(128)S(1)} %pad_add_fusion.refs_0_, ...), custom_call_target="tpu_custom_call" | custom-call | flops 1610612736 | bytes 2097152 | tf_op jit(solution)/shard_map/update_last/pallas_call | solution.py:268
  39.2 4.9 %collective-permute-start.22 = (bf16[16,64,128]{2,1,0:T(8,128)(2,1)S(1)}, bf16[16,64,128]{2,1,0:T(8,128)(2,1)S(1)}, u32[]{:S(2)}, u32[]{:S(2)}) collective-permute-start(bf16[16,64,128]{2,1,0:T(8,128)(2,1)S(1)} %get-tuple-element.46), channel_id=1, source_target_pairs={{0,2},{1,3},{2,0},{3,1},{4,6},{5,7},{6,4},{7,5},{8,10},{9,11},{10,... | collective-permute-start | bytes 786440 | tf_op jit(solution)/shard_map/ppermute | solution.py:185
  44.0 3.0 %collective-permute-start.25 = (bf16[32,16,128]{2,1,0:T(8,128)(2,1)S(1)}, bf16[32,16,128]{2,1,0:T(8,128)(2,1)S(1)}, u32[]{:S(2)}, u32[]{:S(2)}) collective-permute-start(bf16[32,16,128]{2,1,0:T(8,128)(2,1)S(1)} %get-tuple-element.49), channel_id=1, source_target_pairs={{0,0},{1,1},{2,2},{3,3},{4,16},{5,17},{6,18},{7,19},{8,8},{9,9},{1... | collective-permute-start | bytes 393224 | tf_op jit(solution)/shard_map/ppermute | solution.py:312
  47.0 3.1 %collective-permute-start.26 = (bf16[32,16,128]{2,1,0:T(8,128)(2,1)S(1)}, bf16[32,16,128]{2,1,0:T(8,128)(2,1)S(1)}, u32[]{:S(2)}, u32[]{:S(2)}) collective-permute-start(bf16[32,16,128]{2,1,0:T(8,128)(2,1)S(1)} %get-tuple-element.50), channel_id=1, source_target_pairs={{0,8},{1,9},{2,10},{3,11},{4,24},{5,25},{6,26},{7,27},{8,0},{9,1},... | collective-permute-start | bytes 393224 | tf_op jit(solution)/shard_map/ppermute | solution.py:312
  50.1 2.3 %collective-permute-start.24 = (bf16[32,16,128]{2,1,0:T(8,128)(2,1)S(1)}, bf16[32,16,128]{2,1,0:T(8,128)(2,1)S(1)}, u32[]{:S(2)}, u32[]{:S(2)}) collective-permute-start(bf16[32,16,128]{2,1,0:T(8,128)(2,1)S(1)} %get-tuple-element.48), channel_id=1, source_target_pairs={{0,9},{1,8},{2,11},{3,10},{4,25},{5,24},{6,27},{7,26},{8,1},{9,0},... | collective-permute-start | bytes 393224 | tf_op jit(solution)/shard_map/ppermute | solution.py:312
  52.4 0.1 fusion.refs_9_
  52.6 8.5 %collective-permute-done.26.refs_5_ = bf16[32,16,128]{2,1,0:T(8,128)(2,1)S(1)} collective-permute-done((bf16[32,16,128]{2,1,0:T(8,128)(2,1)S(1)}, bf16[32,16,128]{2,1,0:T(8,128)(2,1)S(1)}, u32[]{:S(2)}, u32[]{:S(2)}) %collective-permute-start.26) | collective-permute-done | bytes 131104 | tf_op jit(solution)/shard_map/ppermute | solution.py:312
  61.1 2.6 %finish.2.refs_10_ = bf16[16,128,128]{2,1,0:T(8,128)(2,1)} custom-call(s32[4]{0:T(128)S(1)} %pad_add_fusion.refs_0_, bf16[16,128,128]{2,1,0:T(8,128)(2,1)S(1)} %copy-done, bf16[16,64,128]{2,1,0:T(8,128)(2,1)S(1)} %get-tuple-element.45.refs_2_, bf16[16,64,128]{2,1,0:T(8,128)(2,1)S(1)} %collective-permute-done.22.refs_3_, ...), custom_call_target="tpu_custom_call" | custom-call | tf_op jit(solution)/shard_map/finish/pallas_call | solution.py:334
  63.8 2.6 %finish.3 = bf16[16,128,128]{2,1,0:T(8,128)(2,1)} custom-call(s32[4]{0:T(128)S(1)} %pad_add_fusion.refs_0_, bf16[16,128,128]{2,1,0:T(8,128)(2,1)S(1)} %copy-done, bf16[16,64,128]{2,1,0:T(8,128)(2,1)S(1)} %get-tuple-element.45.refs_2_, bf16[16,64,128]{2,1,0:T(8,128)(2,1)S(1)} %collective-permute-done.22.refs_3_, ...), custom_call_target="tpu_custom_call", output_to_operand_aliasing={{}: (10, {})} | custom-call | tf_op jit(solution)/shard_map/finish/pallas_call | solution.py:334
  (48 shorter events, 0.2 us)
Async XLA Ops:
  1.5 3.3 %copy-start.3 = (bf16[128,32,64]{0,2,1:T(8,128)(2,1)S(1)}, bf16[128,32,64]{0,2,1:T(8,128)(2,1)}, u32[]{:S(2)}) copy-start(bf16[128,32,64]{0,2,1:T(8,128)(2,1)} %param.10) | copy-start | bytes 1572868
  1.7 4.4 %collective-permute-start = (bf16[512,128]{1,0:T(8,128)(2,1)S(1)}, bf16[512,128]{1,0:T(8,128)(2,1)S(1)}, u32[]{:S(2)}, u32[]{:S(2)}) collective-permute-start(bf16[512,128]{1,0:T(8,128)(2,1)S(1)} %bitcast.45), channel_id=1, source_target_pairs={{0,1},{1,0},{2,3},{3,2},{4,5},{5,4},{6,7},{7,6},{8,9},{9,8},{10,11... | collective-permute-start | bytes 393224 | tf_op jit(solution)/shard_map/ppermute | solution.py:185
  1.9 4.2 %collective-permute-start.10 = (bf16[512,128]{1,0:T(8,128)(2,1)S(1)}, bf16[512,128]{1,0:T(8,128)(2,1)S(1)}, u32[]{:S(2)}, u32[]{:S(2)}) collective-permute-start(bf16[512,128]{1,0:T(8,128)(2,1)S(1)} %bitcast.46), channel_id=1, source_target_pairs={{0,16},{8,24},{16,0},{24,8},{1,17},{9,25},{17,1},{25,9},{2,18},{10... | collective-permute-start | bytes 393224 | tf_op jit(solution)/shard_map/ppermute | solution.py:185
  2.2 8.3 %collective-permute-start.4 = (bf16[512,128]{1,0:T(8,128)(2,1)S(1)}, bf16[512,128]{1,0:T(8,128)(2,1)S(1)}, u32[]{:S(2)}, u32[]{:S(2)}) collective-permute-start(bf16[512,128]{1,0:T(8,128)(2,1)S(1)} %bitcast.56), channel_id=1, source_target_pairs={{0,3},{1,2},{2,1},{3,0},{4,7},{5,6},{6,5},{7,4},{8,11},{9,10},{10,... | collective-permute-start | bytes 393224 | tf_op jit(solution)/shard_map/ppermute | solution.py:185
  5.1 3.7 %copy-start.4 = (bf16[1024,128]{1,0:T(8,128)(2,1)S(1)}, bf16[1024,128]{1,0:T(8,128)(2,1)}, u32[]{:S(2)}) copy-start(bf16[1024,128]{1,0:T(8,128)(2,1)} %param.12) | copy-start | bytes 786436
  6.1 5.4 %collective-permute-start.13 = (bf16[512,128]{1,0:T(8,128)(2,1)S(1)}, bf16[512,128]{1,0:T(8,128)(2,1)S(1)}, u32[]{:S(2)}, u32[]{:S(2)}) collective-permute-start(bf16[512,128]{1,0:T(8,128)(2,1)S(1)} %collective-permute-done.refs_9_), channel_id=1, source_target_pairs={{0,16},{8,24},{16,0},{24,8},{1,17},{9,25},{17,1},{25,9},{2,18},{10... | collective-permute-start | bytes 393224 | tf_op jit(solution)/shard_map/ppermute | solution.py:185
  6.5 6.2 %collective-permute-start.2 = (bf16[512,128]{1,0:T(8,128)(2,1)S(1)}, bf16[512,128]{1,0:T(8,128)(2,1)S(1)}, u32[]{:S(2)}, u32[]{:S(2)}) collective-permute-start(bf16[512,128]{1,0:T(8,128)(2,1)S(1)} %get-tuple-element.29), channel_id=1, source_target_pairs={{0,1},{1,0},{2,3},{3,2},{4,5},{5,4},{6,7},{7,6},{8,9},{9,8},{10,11... | collective-permute-start | bytes 393224 | tf_op jit(solution)/shard_map/ppermute | solution.py:185
  7.5 6.7 %collective-permute-start.1 = (bf16[512,128]{1,0:T(8,128)(2,1)S(1)}, bf16[512,128]{1,0:T(8,128)(2,1)S(1)}, u32[]{:S(2)}, u32[]{:S(2)}) collective-permute-start(bf16[512,128]{1,0:T(8,128)(2,1)S(1)} %get-tuple-element.31.refs_1_), channel_id=1, source_target_pairs={{0,4},{4,0},{1,5},{5,1},{2,6},{6,2},{3,7},{7,3},{8,12},{12,8},{9,1... | collective-permute-start | bytes 393224 | tf_op jit(solution)/shard_map/ppermute | solution.py:185
  9.0 6.5 %collective-permute-start.6 = (bf16[512,128]{1,0:T(8,128)(2,1)S(1)}, bf16[512,128]{1,0:T(8,128)(2,1)S(1)}, u32[]{:S(2)}, u32[]{:S(2)}) collective-permute-start(bf16[512,128]{1,0:T(8,128)(2,1)S(1)} %get-tuple-element.29), channel_id=1, source_target_pairs={{0,3},{1,2},{2,1},{3,0},{4,7},{5,6},{6,5},{7,4},{8,11},{9,10},{10,... | collective-permute-start | bytes 393224 | tf_op jit(solution)/shard_map/ppermute | solution.py:185
  10.4 13.5 %collective-permute-start.5 = (bf16[512,128]{1,0:T(8,128)(2,1)S(1)}, bf16[512,128]{1,0:T(8,128)(2,1)S(1)}, u32[]{:S(2)}, u32[]{:S(2)}) collective-permute-start(bf16[512,128]{1,0:T(8,128)(2,1)S(1)} %get-tuple-element.31.refs_1_), channel_id=1, source_target_pairs={{0,2},{1,3},{2,0},{3,1},{4,6},{5,7},{6,4},{7,5},{8,10},{9,11},{10,... | collective-permute-start | bytes 393224 | tf_op jit(solution)/shard_map/ppermute | solution.py:185
  11.5 10.7 %collective-permute-start.15 = (bf16[512,128]{1,0:T(8,128)(2,1)S(1)}, bf16[512,128]{1,0:T(8,128)(2,1)S(1)}, u32[]{:S(2)}, u32[]{:S(2)}) collective-permute-start(bf16[512,128]{1,0:T(8,128)(2,1)S(1)} %collective-permute-done.4.refs_17_), channel_id=1, source_target_pairs={{0,1},{1,0},{2,3},{3,2},{4,5},{5,4},{6,7},{7,6},{8,9},{9,8},{10,11... | collective-permute-start | bytes 393224 | tf_op jit(solution)/shard_map/ppermute | solution.py:185
  12.7 10.0 %collective-permute-start.17 = (bf16[512,128]{1,0:T(8,128)(2,1)S(1)}, bf16[512,128]{1,0:T(8,128)(2,1)S(1)}, u32[]{:S(2)}, u32[]{:S(2)}) collective-permute-start(bf16[512,128]{1,0:T(8,128)(2,1)S(1)} %collective-permute-done.4.refs_17_), channel_id=1, source_target_pairs={{0,16},{8,24},{16,0},{24,8},{1,17},{9,25},{17,1},{25,9},{2,18},{10... | collective-permute-start | bytes 393224 | tf_op jit(solution)/shard_map/ppermute | solution.py:185
  14.2 8.6 %collective-permute-start.3 = (bf16[512,128]{1,0:T(8,128)(2,1)S(1)}, bf16[512,128]{1,0:T(8,128)(2,1)S(1)}, u32[]{:S(2)}, u32[]{:S(2)}) collective-permute-start(bf16[512,128]{1,0:T(8,128)(2,1)S(1)} %collective-permute-done.2.refs_2_), channel_id=1, source_target_pairs={{0,4},{4,0},{1,5},{5,1},{2,6},{6,2},{3,7},{7,3},{8,12},{12,8},{9,1... | collective-permute-start | bytes 393224 | tf_op jit(solution)/shard_map/ppermute | solution.py:185
  15.5 14.4 %collective-permute-start.12 = (bf16[512,128]{1,0:T(8,128)(2,1)S(1)}, bf16[512,128]{1,0:T(8,128)(2,1)S(1)}, u32[]{:S(2)}, u32[]{:S(2)}) collective-permute-start(bf16[512,128]{1,0:T(8,128)(2,1)S(1)} %collective-permute-done.refs_9_), channel_id=1, source_target_pairs={{0,8},{8,0},{16,24},{24,16},{1,9},{9,1},{17,25},{25,17},{2,10},{10... | collective-permute-start | bytes 393224 | tf_op jit(solution)/shard_map/ppermute | solution.py:185
  22.2 7.7 %collective-permute-start.9 = (bf16[512,128]{1,0:T(8,128)(2,1)S(1)}, bf16[512,128]{1,0:T(8,128)(2,1)S(1)}, u32[]{:S(2)}, u32[]{:S(2)}) collective-permute-start(bf16[512,128]{1,0:T(8,128)(2,1)S(1)} %bitcast.47), channel_id=1, source_target_pairs={{0,8},{8,0},{16,24},{24,16},{1,9},{9,1},{17,25},{25,17},{2,10},{10... | collective-permute-start | bytes 393224 | tf_op jit(solution)/shard_map/ppermute | solution.py:185
  22.7 7.7 %collective-permute-start.20 = (bf16[512,128]{1,0:T(8,128)(2,1)S(1)}, bf16[512,128]{1,0:T(8,128)(2,1)S(1)}, u32[]{:S(2)}, u32[]{:S(2)}) collective-permute-start(bf16[512,128]{1,0:T(8,128)(2,1)S(1)} %collective-permute-done.4.refs_17_), channel_id=1, source_target_pairs={{0,8},{8,0},{16,24},{24,16},{1,9},{9,1},{17,25},{25,17},{2,10},{10... | collective-permute-start | bytes 393224 | tf_op jit(solution)/shard_map/ppermute | solution.py:185
  22.7 4.7 %collective-permute-start.18 = (bf16[512,128]{1,0:T(8,128)(2,1)S(1)}, bf16[512,128]{1,0:T(8,128)(2,1)S(1)}, u32[]{:S(2)}, u32[]{:S(2)}) collective-permute-start(bf16[512,128]{1,0:T(8,128)(2,1)S(1)} %collective-permute-done.15.refs_13_), channel_id=1, source_target_pairs={{0,16},{8,24},{16,0},{24,8},{1,17},{9,25},{17,1},{25,9},{2,18},{10... | collective-permute-start | bytes 393224 | tf_op jit(solution)/shard_map/ppermute | solution.py:185
  24.0 4.7 %collective-permute-start.7 = (bf16[512,128]{1,0:T(8,128)(2,1)S(1)}, bf16[512,128]{1,0:T(8,128)(2,1)S(1)}, u32[]{:S(2)}, u32[]{:S(2)}) collective-permute-start(bf16[512,128]{1,0:T(8,128)(2,1)S(1)} %collective-permute-done.6.refs_4_), channel_id=1, source_target_pairs={{0,4},{4,0},{1,5},{5,1},{2,6},{6,2},{3,7},{7,3},{8,12},{12,8},{9,1... | collective-permute-start | bytes 393224 | tf_op jit(solution)/shard_map/ppermute | solution.py:185
  27.4 3.9 %collective-permute-start.14 = (bf16[512,128]{1,0:T(8,128)(2,1)S(1)}, bf16[512,128]{1,0:T(8,128)(2,1)S(1)}, u32[]{:S(2)}, u32[]{:S(2)}) collective-permute-start(bf16[512,128]{1,0:T(8,128)(2,1)S(1)} %collective-permute-done.13.refs_11_), channel_id=1, source_target_pairs={{0,8},{8,0},{16,24},{24,16},{1,9},{9,1},{17,25},{25,17},{2,10},{10... | collective-permute-start | bytes 393224 | tf_op jit(solution)/shard_map/ppermute | solution.py:185
  28.7 3.5 %collective-permute-start.11 = (bf16[512,128]{1,0:T(8,128)(2,1)S(1)}, bf16[512,128]{1,0:T(8,128)(2,1)S(1)}, u32[]{:S(2)}, u32[]{:S(2)}) collective-permute-start(bf16[512,128]{1,0:T(8,128)(2,1)S(1)} %collective-permute-done.10.refs_7_), channel_id=1, source_target_pairs={{0,8},{8,0},{16,24},{24,16},{1,9},{9,1},{17,25},{25,17},{2,10},{10... | collective-permute-start | bytes 393224 | tf_op jit(solution)/shard_map/ppermute | solution.py:185
  29.9 2.3 %collective-permute-start.21 = (bf16[512,128]{1,0:T(8,128)(2,1)S(1)}, bf16[512,128]{1,0:T(8,128)(2,1)S(1)}, u32[]{:S(2)}, u32[]{:S(2)}) collective-permute-start(bf16[512,128]{1,0:T(8,128)(2,1)S(1)} %collective-permute-done.17.refs_19_), channel_id=1, source_target_pairs={{0,8},{8,0},{16,24},{24,16},{1,9},{9,1},{17,25},{25,17},{2,10},{10... | collective-permute-start | bytes 393224 | tf_op jit(solution)/shard_map/ppermute | solution.py:185
  29.9 2.3 %collective-permute-start.19 = (bf16[512,128]{1,0:T(8,128)(2,1)S(1)}, bf16[512,128]{1,0:T(8,128)(2,1)S(1)}, u32[]{:S(2)}, u32[]{:S(2)}) collective-permute-start(bf16[512,128]{1,0:T(8,128)(2,1)S(1)} %collective-permute-done.18.refs_15_), channel_id=1, source_target_pairs={{0,8},{8,0},{16,24},{24,16},{1,9},{9,1},{17,25},{25,17},{2,10},{10... | collective-permute-start | bytes 393224 | tf_op jit(solution)/shard_map/ppermute | solution.py:185
  30.4 1.8 %collective-permute-start.16 = (bf16[512,128]{1,0:T(8,128)(2,1)S(1)}, bf16[512,128]{1,0:T(8,128)(2,1)S(1)}, u32[]{:S(2)}, u32[]{:S(2)}) collective-permute-start(bf16[512,128]{1,0:T(8,128)(2,1)S(1)} %collective-permute-done.15.refs_13_), channel_id=1, source_target_pairs={{0,8},{8,0},{16,24},{24,16},{1,9},{9,1},{17,25},{25,17},{2,10},{10... | collective-permute-start | bytes 393224 | tf_op jit(solution)/shard_map/ppermute | solution.py:185
  30.6 0.7 %copy-start.5 = (f32[512]{0:T(512)S(1)}, f32[512]{0:T(512)}, u32[]{:S(2)}) copy-start(f32[512]{0:T(512)} %param.17) | copy-start | bytes 6148
  30.6 0.7 %copy-start.7 = (f32[128]{0:T(128)S(1)}, f32[128]{0:T(128)}, u32[]{:S(2)}) copy-start(f32[128]{0:T(128)} %param.19) | copy-start | bytes 1540
  30.6 0.7 %copy-start.8 = (f32[128]{0:T(128)S(1)}, f32[128]{0:T(128)}, u32[]{:S(2)}) copy-start(f32[128]{0:T(128)} %param.15) | copy-start | bytes 1540
  31.3 1.0 %copy-start.6 = (f32[128]{0:T(128)S(1)}, f32[128]{0:T(128)}, u32[]{:S(2)}) copy-start(f32[128]{0:T(128)} %param.13) | copy-start | bytes 1540
  31.3 4.7 %collective-permute-start.8 = (bf16[512,128]{1,0:T(8,128)(2,1)S(1)}, bf16[512,128]{1,0:T(8,128)(2,1)S(1)}, u32[]{:S(2)}, u32[]{:S(2)}) collective-permute-start(bf16[512,128]{1,0:T(8,128)(2,1)S(1)} %collective-permute-done.5.refs_3_), channel_id=1, source_target_pairs={{0,4},{4,0},{1,5},{5,1},{2,6},{6,2},{3,7},{7,3},{8,12},{12,8},{9,1... | collective-permute-start | bytes 393224 | tf_op jit(solution)/shard_map/ppermute | solution.py:185
  35.4 25.8 %copy-start = (bf16[16,128,128]{2,1,0:T(8,128)(2,1)S(1)}, bf16[16,128,128]{2,1,0:T(8,128)(2,1)}, u32[]{:S(2)}) copy-start(bf16[16,128,128]{2,1,0:T(8,128)(2,1)} %refs_1_.3) | copy-start | bytes 1572868
  36.0 25.1 %copy-start.2 = (bf16[512,128]{1,0:T(8,128)(2,1)S(1)}, bf16[512,128]{1,0:T(8,128)(2,1)}, u32[]{:S(2)}) copy-start(bf16[512,128]{1,0:T(8,128)(2,1)} %refs_7_.3) | copy-start | bytes 393220
  39.1 22.0 %copy-start.1 = (bf16[128,512]{1,0:T(8,128)(2,1)S(1)}, bf16[128,512]{1,0:T(8,128)(2,1)}, u32[]{:S(2)}) copy-start(bf16[128,512]{1,0:T(8,128)(2,1)} %refs_6_.3) | copy-start | bytes 393220
  39.2 21.9 %collective-permute-start.22 = (bf16[16,64,128]{2,1,0:T(8,128)(2,1)S(1)}, bf16[16,64,128]{2,1,0:T(8,128)(2,1)S(1)}, u32[]{:S(2)}, u32[]{:S(2)}) collective-permute-start(bf16[16,64,128]{2,1,0:T(8,128)(2,1)S(1)} %get-tuple-element.46), channel_id=1, source_target_pairs={{0,2},{1,3},{2,0},{3,1},{4,6},{5,7},{6,4},{7,5},{8,10},{9,11},{10,... | collective-permute-start | bytes 786440 | tf_op jit(solution)/shard_map/ppermute | solution.py:185
  44.0 8.5 %collective-permute-start.25 = (bf16[32,16,128]{2,1,0:T(8,128)(2,1)S(1)}, bf16[32,16,128]{2,1,0:T(8,128)(2,1)S(1)}, u32[]{:S(2)}, u32[]{:S(2)}) collective-permute-start(bf16[32,16,128]{2,1,0:T(8,128)(2,1)S(1)} %get-tuple-element.49), channel_id=1, source_target_pairs={{0,0},{1,1},{2,2},{3,3},{4,16},{5,17},{6,18},{7,19},{8,8},{9,9},{1... | collective-permute-start | bytes 393224 | tf_op jit(solution)/shard_map/ppermute | solution.py:312
  47.0 14.1 %collective-permute-start.26 = (bf16[32,16,128]{2,1,0:T(8,128)(2,1)S(1)}, bf16[32,16,128]{2,1,0:T(8,128)(2,1)S(1)}, u32[]{:S(2)}, u32[]{:S(2)}) collective-permute-start(bf16[32,16,128]{2,1,0:T(8,128)(2,1)S(1)} %get-tuple-element.50), channel_id=1, source_target_pairs={{0,8},{1,9},{2,10},{3,11},{4,24},{5,25},{6,26},{7,27},{8,0},{9,1},... | collective-permute-start | bytes 393224 | tf_op jit(solution)/shard_map/ppermute | solution.py:312
  50.1 13.7 %collective-permute-start.23 = (bf16[32,16,128]{2,1,0:T(8,128)(2,1)S(1)}, bf16[32,16,128]{2,1,0:T(8,128)(2,1)S(1)}, u32[]{:S(2)}, u32[]{:S(2)}) collective-permute-start(bf16[32,16,128]{2,1,0:T(8,128)(2,1)S(1)} %get-tuple-element.47), channel_id=1, source_target_pairs={{0,1},{1,0},{2,3},{3,2},{4,17},{5,16},{6,19},{7,18},{8,9},{9,8},{1... | collective-permute-start | bytes 393224 | tf_op jit(solution)/shard_map/ppermute | solution.py:312
  50.1 13.7 %collective-permute-start.24 = (bf16[32,16,128]{2,1,0:T(8,128)(2,1)S(1)}, bf16[32,16,128]{2,1,0:T(8,128)(2,1)S(1)}, u32[]{:S(2)}, u32[]{:S(2)}) collective-permute-start(bf16[32,16,128]{2,1,0:T(8,128)(2,1)S(1)} %get-tuple-element.48), channel_id=1, source_target_pairs={{0,9},{1,8},{2,11},{3,10},{4,25},{5,24},{6,27},{7,26},{8,1},{9,0},... | collective-permute-start | bytes 393224 | tf_op jit(solution)/shard_map/ppermute | solution.py:312

commit v8 on v7

--- a/solution.py
+++ b/solution.py
@@ -92,63 +92,69 @@
                 ]
 
 
-def finish_kernel(low, dz, *refs):
-    place_ref, pair_ref, own_ref, other_ref, mirror_low, mirror_high = refs[:6]
-    up_ref, down_ref, vector_ref, swap_ref = refs[6:10]
-    out_ref, middle_ref, done_ref, sems = refs[-4:]
-    mirror_refs = (mirror_low, mirror_high)
+def finish_kernel(low, other, *refs):
+    place_ref, pair_ref, direct_ref = refs[:3]
+    mirror_refs = refs[3 : 3 + 2 * low]
+    up_ref, down_ref, vector_ref, swap_ref = refs[3 + 2 * low : 7 + 2 * low]
+    out_ref, done_ref, sems = refs[-3:]
     run, columns, pair_channels = pair_ref.shape
     half = columns // 2
-    core, z_low, z_high = place_ref[0], place_ref[1], place_ref[3]
+    core, z_low, part = place_ref[0], place_ref[1], place_ref[3] ^ other
     cells = run * run
     gain = vector_ref[:, :pair_channels]
     down_bias = vector_ref[:, pair_channels : 2 * pair_channels]
     up_bias = vector_ref[:, 2 * pair_channels :]
-    begins = []
-    for flip in range(2):
-        for part in range(2):
-            index = 2 * flip + part
+    ones = jnp.full((2 * pair_channels, pair_channels), 1.0 / pair_channels, jnp.bfloat16)
+    copies = []
+    for dz in range(low):
+        middles = []
+        begins = []
+        for flip in range(2):
             local = (core ^ flip) * (half // 2) + (z_low ^ dz) * run
             local = pl.multiple_of(local, run)
             begin = (core ^ flip) * half + (part * low + (z_low ^ dz)) * run
             begin = pl.multiple_of(begin, run)
             begins.append(begin)
-            piece = mirror_refs[flip][part * run : (part + 1) * run]
+            piece = mirror_refs[2 * dz + flip][pl.ds(part * run, run)]
             mirrored = jnp.dot(
                 swap_ref[...],
                 piece.reshape(cells, pair_channels),
                 preferred_element_type=jnp.float32,
             )
-            direct = jnp.where(
-                z_high == part,
-                own_ref[:, pl.ds(local, run), :],
-                other_ref[:, pl.ds(local, run), :],
-            ).reshape(cells, pair_channels)
+            direct = direct_ref[:, pl.ds(local, run), :].reshape(cells, pair_channels)
             residual = pair_ref[:, pl.ds(begin, run), :].reshape(cells, pair_channels)
-            middle_ref[index * cells : (index + 1) * cells] = (
-                residual.astype(jnp.float32) + 0.5 * (direct.astype(jnp.float32) + mirrored)
-            ).astype(jnp.bfloat16)
-
-    values = middle_ref[...].astype(jnp.float32)
-    center = jnp.mean(values, axis=1, keepdims=True)
-    moved = values - center
-    spread = jnp.mean(jnp.square(moved), axis=1, keepdims=True)
-    normed = moved * lax.rsqrt(spread + epsilon) * gain
-    hidden = jnp.dot(
-        normed.astype(jnp.bfloat16), up_ref[...], preferred_element_type=jnp.float32
-    )
-    hidden = jnp.maximum(hidden + up_bias, 0.0).astype(jnp.bfloat16)
-    result = jnp.dot(hidden, down_ref[...], preferred_element_type=jnp.float32)
-    result = (values + result + down_bias).astype(jnp.bfloat16)
-    done_ref[...] = result.reshape(4, run, run, pair_channels)
-    copies = [
-        pltpu.make_async_copy(
-            done_ref.at[index], out_ref.at[:, pl.ds(begins[index], run), :], sems.at[index]
+            middles.append(
+                (
+                    residual.astype(jnp.float32) + 0.5 * (direct.astype(jnp.float32) + mirrored)
+                ).astype(jnp.bfloat16)
+            )
+        middle = jnp.concatenate(middles, axis=0)
+        values = middle.astype(jnp.float32)
+        center = jnp.dot(middle, ones[:pair_channels], preferred_element_type=jnp.float32)
+        moved = values - center
+        square = jnp.square(moved)
+        high = square.astype(jnp.bfloat16)
+        rest = (square - high.astype(jnp.float32)).astype(jnp.bfloat16)
+        spread = jnp.dot(
+            jnp.concatenate([high, rest], axis=1), ones, preferred_element_type=jnp.float32
         )
-        for index in range(4)
-    ]
-    for copy in copies:
-        copy.start()
+        normed = moved * lax.rsqrt(spread + epsilon) * gain
+        hidden = jnp.dot(
+            normed.astype(jnp.bfloat16), up_ref[...], preferred_element_type=jnp.float32
+        )
+        hidden = jnp.maximum(hidden + up_bias, 0.0).astype(jnp.bfloat16)
+        result = jnp.dot(hidden, down_ref[...], preferred_element_type=jnp.float32)
+        result = (values + result + down_bias).astype(jnp.bfloat16)
+        for flip in range(2):
+            index = 2 * dz + flip
+            done_ref[index] = result[flip * cells : (flip + 1) * cells].reshape(
+                run, run, pair_channels
+            )
+            copy = pltpu.make_async_copy(
+                done_ref.at[index], out_ref.at[:, pl.ds(begins[flip], run), :], sems.at[index]
+            )
+            copy.start()
+            copies.append(copy)
     for copy in copies:
         copy.wait()
 
@@ -195,8 +201,9 @@
     def after(value, *earlier):
         return lax.optimization_barrier((value, earlier))[0] if earlier else value
 
-    right_sends = [pick(right, z_high ^ (dz // low)) for dz in range(groups)]
+    mine, theirs = lax.optimization_barrier((pick(right, z_high), pick(right, 1 - z_high)))
     left_sends = [pick(left, z_low ^ (dz % low)) for dz in range(groups)]
+    right_sends = [theirs if dz >= low else mine for dz in range(groups)]
     rights, lefts = {0: right_sends[0]}, {0: left_sends[0]}
     crossed = {dz: [] for dz in range(groups)}
     shared = {dz: [] for dz in range(groups)}
@@ -223,8 +230,8 @@
     last_x = over_x(0)
     last_x = over_x(1, *last_x)
     lefts[3] = along(left_sends, 3, rights[1])
-    lefts[1] = along(left_sends, 1, rights[1])
-    last_y = over_y(0, rights[1])
+    last_y = over_y(0)
+    lefts[1] = along(left_sends, 1, *last_y)
     lefts[2] = along(left_sends, 2, rights[3])
     rights[2] = swap(rights[3], "seq", groups, 1)
     last_x = over_x(3, *last_x)
@@ -297,7 +304,6 @@
         [pltpu.VMEM((2 * run, half, pair_channels), bf16)],
     )
 
-    update_other = swap(outs[1], "seq", groups, low)
     mirrors = []
     for dz in range(low):
         for flip in range(2):
@@ -310,6 +316,7 @@
                         target = (target * cols + r // 2) * groups + (q ^ dz)
                         pairs.append((source, target))
             mirrors.append(lax.ppermute(outs[2 + 2 * dz + flip], axes, pairs))
+    update_other = swap(outs[1], "seq", groups, low)
 
     vectors = jnp.concatenate([norm_gain, down_bias, up_bias]).reshape(1, -1)
     cell = jnp.arange(run * run)
@@ -317,14 +324,12 @@
     swap_cells = (mirror_cell[:, None] == cell[None, :]).astype(bf16)
     anywhere = pl.BlockSpec(memory_space=pl.ANY)
     result = None
-    for dz in range(low):
+    for other in range(2):
         operands = [
             place,
             pair_rep,
-            outs[0],
-            update_other,
-            mirrors[2 * dz],
-            mirrors[2 * dz + 1],
+            update_other if other else outs[0],
+            *mirrors,
             up_weight,
             down_weight,
             vectors,
@@ -332,17 +337,21 @@
         ]
         extra = [] if result is None else [result]
         result = pl.pallas_call(
-            functools.partial(finish_kernel, low, dz),
+            functools.partial(finish_kernel, low, other),
             out_shape=jax.ShapeDtypeStruct(pair_rep.shape, bf16),
-            in_specs=[smem] + [vmem] * 9 + [anywhere] * len(extra),
+            in_specs=[smem] + [vmem] * (len(operands) - 1) + [anywhere] * len(extra),
             out_specs=anywhere,
             scratch_shapes=[
-                pltpu.VMEM((4 * run * run, pair_channels), bf16),
-                pltpu.VMEM((4, run, run, pair_channels), bf16),
-                pltpu.SemaphoreType.DMA((4,)),
+                pltpu.VMEM((2 * low, run, run, pair_channels), bf16),
+                pltpu.SemaphoreType.DMA((2 * low,)),
             ],
-            input_output_aliases={10: 0} if extra else {},
+            input_output_aliases={len(operands): 0} if extra else {},
             compiler_params=params,
+            cost_estimate=pl.CostEstimate(
+                flops=64 * run * columns * pair_channels * up_bias.size,
+                bytes_accessed=2 * pair_rep.size,
+                transcendentals=0,
+            ),
             name="finish",
         )(*operands, *extra)
     return result

time: 66.6 us -> 69.2 us (1.039)
  the two profiles are of different devices: /device:TPU:11 before, /device:TPU:3 now
where the time goes in v8:
time: 69.2 us; the launch traced here: 68 us
  starting transfers between devices  37.8 us (55%)
  waiting for transfers between devices  15 us (22%)
  Pallas kernels  11.4 us (16%)
  local copies, waits for them, and re-layouts  2.77 us (4%)
    ppermute x23, starting transfers between devices, swap(): return lax.ppermute(value, name, [(i, i ^ flip) for i in range(size)])  29.5 us
    ppermute x4, waiting for transfers between devices, on_device(): mirrors.append(lax.ppermute(outs[2 + 2 * dz + flip], axes, pairs))  8.67 us
    ppermute x4, starting transfers between devices, on_device(): mirrors.append(lax.ppermute(outs[2 + 2 * dz + flip], axes, pairs))  8.29 us
    ppermute x23, waiting for transfers between devices, swap(): return lax.ppermute(value, name, [(i, i ^ flip) for i in range(size)])  6.35 us
    pallas_call x2, Pallas kernels, update_call(): pl.pallas_call(functools.partial(update_kernel, places, cols, low, last,...  6.13 us
    pallas_call x2, Pallas kernels, on_device(): pl.pallas_call(functools.partial(finish_kernel, low, other), out_shape=ja...  5.3 us
  transfers between devices with their start and end apart: 27, of which 8 were waited for; matrix products, arithmetic and copies ran while one was open for 2% of the time, Pallas kernels for 8%

profile of v8, /device:TPU:3, one launch (start us, length us, event | category | flops | bytes accessed | tf_op | source)
XLA Modules:
  0.0 68.0 jit_solution(8927040920981672822)
XLA Ops:
  0.0 1.1 %copy.19 = bf16[128,8,128]{0,2,1:T(8,128)(2,1)S(1)} copy(bf16[128,8,128]{2,1,0:T(8,128)(2,1)} %param.11) | data formatting | bytes 524288 | tf_op args[1]
  1.2 0.2 copy.20
  1.4 0.1 reshape.55
  1.5 0.1 copy.21
  1.7 0.1 copy.22
  1.8 0.1 collective-permute-start.10
  1.9 1.5 %collective-permute-start.5 = (bf16[512,128]{1,0:T(8,128)(2,1)S(1)}, bf16[512,128]{1,0:T(8,128)(2,1)S(1)}, u32[]{:S(2)}, u32[]{:S(2)}) collective-permute-start(bf16[512,128]{1,0:T(8,128)(2,1)S(1)} %bitcast.46), channel_id=1, source_target_pairs={{0,1},{1,0},{2,3},{3,2},{4,5},{5,4},{6,7},{7,6},{8,9},{9,8},{10,11... | collective-permute-start | bytes 393224 | tf_op jit(solution)/shard_map/ppermute | solution.py:191
  3.4 0.3 copy.18
  3.8 1.3 %collective-permute-start = (bf16[512,128]{1,0:T(8,128)(2,1)S(1)}, bf16[512,128]{1,0:T(8,128)(2,1)S(1)}, u32[]{:S(2)}, u32[]{:S(2)}) collective-permute-start(bf16[512,128]{1,0:T(8,128)(2,1)S(1)} %get-tuple-element.33.refs_1_), channel_id=1, source_target_pairs={{0,4},{4,0},{1,5},{5,1},{2,6},{6,2},{3,7},{7,3},{8,12},{12,8},{9,1... | collective-permute-start | bytes 393224 | tf_op jit(solution)/shard_map/ppermute | solution.py:191
  5.1 2.4 %collective-permute-start.3 = (bf16[512,128]{1,0:T(8,128)(2,1)S(1)}, bf16[512,128]{1,0:T(8,128)(2,1)S(1)}, u32[]{:S(2)}, u32[]{:S(2)}) collective-permute-start(bf16[512,128]{1,0:T(8,128)(2,1)S(1)} %bitcast.56), channel_id=1, source_target_pairs={{0,3},{1,2},{2,1},{3,0},{4,7},{5,6},{6,5},{7,4},{8,11},{9,10},{10,... | collective-permute-start | bytes 393224 | tf_op jit(solution)/shard_map/ppermute | solution.py:191
  7.6 0.2 constant_dynamic-slice_fusion.3
  7.8 1.0 %collective-permute-start.13 = (bf16[512,128]{1,0:T(8,128)(2,1)S(1)}, bf16[512,128]{1,0:T(8,128)(2,1)S(1)}, u32[]{:S(2)}, u32[]{:S(2)}) collective-permute-start(bf16[512,128]{1,0:T(8,128)(2,1)S(1)} %collective-permute-done.5.refs_9_), channel_id=1, source_target_pairs={{0,16},{8,24},{16,0},{24,8},{1,17},{9,25},{17,1},{25,9},{2,18},{10... | collective-permute-start | bytes 393224 | tf_op jit(solution)/shard_map/ppermute | solution.py:191
  8.8 0.4 collective-permute-start.1
  9.2 0.1 copy_bitcast_fusion.1
  9.3 2.1 %collective-permute-start.6 = (bf16[512,128]{1,0:T(8,128)(2,1)S(1)}, bf16[512,128]{1,0:T(8,128)(2,1)S(1)}, u32[]{:S(2)}, u32[]{:S(2)}) collective-permute-start(bf16[512,128]{1,0:T(8,128)(2,1)S(1)} %get-tuple-element.35), channel_id=1, source_target_pairs={{0,3},{1,2},{2,1},{3,0},{4,7},{5,6},{6,5},{7,4},{8,11},{9,10},{10,... | collective-permute-start | bytes 393224 | tf_op jit(solution)/shard_map/ppermute | solution.py:191
  11.3 2.0 %collective-permute-start.4 = (bf16[512,128]{1,0:T(8,128)(2,1)S(1)}, bf16[512,128]{1,0:T(8,128)(2,1)S(1)}, u32[]{:S(2)}, u32[]{:S(2)}) collective-permute-start(bf16[512,128]{1,0:T(8,128)(2,1)S(1)} %get-tuple-element.33.refs_1_), channel_id=1, source_target_pairs={{0,2},{1,3},{2,0},{3,1},{4,6},{5,7},{6,4},{7,5},{8,10},{9,11},{10,... | collective-permute-start | bytes 393224 | tf_op jit(solution)/shard_map/ppermute | solution.py:191
  13.4 0.2 collective-permute-start.15
  13.6 1.5 %collective-permute-start.17 = (bf16[512,128]{1,0:T(8,128)(2,1)S(1)}, bf16[512,128]{1,0:T(8,128)(2,1)S(1)}, u32[]{:S(2)}, u32[]{:S(2)}) collective-permute-start(bf16[512,128]{1,0:T(8,128)(2,1)S(1)} %collective-permute-done.3.refs_17_), channel_id=1, source_target_pairs={{0,16},{8,24},{16,0},{24,8},{1,17},{9,25},{17,1},{25,9},{2,18},{10... | collective-permute-start | bytes 393224 | tf_op jit(solution)/shard_map/ppermute | solution.py:191
  15.0 0.4 collective-permute-start.2
  15.5 0.1 copy_bitcast_fusion.3
  15.6 0.4 collective-permute-done.6.refs_4_
  16.0 7.3 %collective-permute-start.12 = (bf16[512,128]{1,0:T(8,128)(2,1)S(1)}, bf16[512,128]{1,0:T(8,128)(2,1)S(1)}, u32[]{:S(2)}, u32[]{:S(2)}) collective-permute-start(bf16[512,128]{1,0:T(8,128)(2,1)S(1)} %collective-permute-done.5.refs_9_), channel_id=1, source_target_pairs={{0,8},{8,0},{16,24},{24,16},{1,9},{9,1},{17,25},{25,17},{2,10},{10... | collective-permute-start | bytes 393224 | tf_op jit(solution)/shard_map/ppermute | solution.py:191
  23.2 0.2 collective-permute-start.9
  23.5 2.5 %collective-permute-start.20 = (bf16[512,128]{1,0:T(8,128)(2,1)S(1)}, bf16[512,128]{1,0:T(8,128)(2,1)S(1)}, u32[]{:S(2)}, u32[]{:S(2)}) collective-permute-start(bf16[512,128]{1,0:T(8,128)(2,1)S(1)} %collective-permute-done.3.refs_17_), channel_id=1, source_target_pairs={{0,8},{8,0},{16,24},{24,16},{1,9},{9,1},{17,25},{25,17},{2,10},{10... | collective-permute-start | bytes 393224 | tf_op jit(solution)/shard_map/ppermute | solution.py:191
  26.0 2.6 %collective-permute-start.18 = (bf16[512,128]{1,0:T(8,128)(2,1)S(1)}, bf16[512,128]{1,0:T(8,128)(2,1)S(1)}, u32[]{:S(2)}, u32[]{:S(2)}) collective-permute-start(bf16[512,128]{1,0:T(8,128)(2,1)S(1)} %collective-permute-done.15.refs_13_), channel_id=1, source_target_pairs={{0,16},{8,24},{16,0},{24,8},{1,17},{9,25},{17,1},{25,9},{2,18},{10... | collective-permute-start | bytes 393224 | tf_op jit(solution)/shard_map/ppermute | solution.py:191
  28.7 0.5 pad_maximum_fusion
  29.1 2.2 %collective-permute-done.18.refs_15_ = bf16[512,128]{1,0:T(8,128)(2,1)S(1)} collective-permute-done((bf16[512,128]{1,0:T(8,128)(2,1)S(1)}, bf16[512,128]{1,0:T(8,128)(2,1)S(1)}, u32[]{:S(2)}, u32[]{:S(2)}) %collective-permute-start.18) | collective-permute-done | bytes 131104 | tf_op jit(solution)/shard_map/ppermute | solution.py:191
  31.3 1.8 %collective-permute-start.14 = (bf16[512,128]{1,0:T(8,128)(2,1)S(1)}, bf16[512,128]{1,0:T(8,128)(2,1)S(1)}, u32[]{:S(2)}, u32[]{:S(2)}) collective-permute-start(bf16[512,128]{1,0:T(8,128)(2,1)S(1)} %collective-permute-done.13.refs_11_), channel_id=1, source_target_pairs={{0,8},{8,0},{16,24},{24,16},{1,9},{9,1},{17,25},{25,17},{2,10},{10... | collective-permute-start | bytes 393224 | tf_op jit(solution)/shard_map/ppermute | solution.py:191
  33.1 1.5 %collective-permute-start.11 = (bf16[512,128]{1,0:T(8,128)(2,1)S(1)}, bf16[512,128]{1,0:T(8,128)(2,1)S(1)}, u32[]{:S(2)}, u32[]{:S(2)}) collective-permute-start(bf16[512,128]{1,0:T(8,128)(2,1)S(1)} %collective-permute-done.10.refs_7_), channel_id=1, source_target_pairs={{0,8},{8,0},{16,24},{24,16},{1,9},{9,1},{17,25},{25,17},{2,10},{10... | collective-permute-start | bytes 393224 | tf_op jit(solution)/shard_map/ppermute | solution.py:191
  34.5 0.5 collective-permute-start.19
  35.1 0.1 pad_add_fusion.refs_0_
  35.2 0.1 copy.28.refs_22_
  35.5 0.4 collective-permute-done.21.refs_20_
  35.9 0.2 collective-permute-done.19.refs_16_
  36.1 0.3 collective-permute-done.16.refs_14_
  36.4 0.1 broadcast_in_dim.2.refs_21_
  36.5 3.0 %update_first.1.refs_23_ = bf16[16,64,128]{2,1,0:T(8,128)(2,1)S(1)} custom-call(s32[4]{0:T(128)S(1)} %pad_add_fusion.refs_0_, bf16[512,128]{1,0:T(8,128)(2,1)S(1)} %get-tuple-element.33.refs_1_, bf16[512,128]{1,0:T(8,128)(2,1)S(1)} %collective-permute-done.1.refs_2_, bf16[512,128]{1,0:T(8,128)(2,1)S(1)} %collective-permute-done.4.refs_3_, ...), custom_call_target="tpu_custom_call" | custom-call | flops 1610612736 | bytes 2097152 | tf_op jit(solution)/shard_map/update_first/pallas_call | solution.py:275
  39.5 0.6 collective-permute-done.8.refs_3_
  40.1 3.1 %update_last.1 = (bf16[16,64,128]{2,1,0:T(8,128)(2,1)S(1)}, bf16[16,64,128]{2,1,0:T(8,128)(2,1)S(1)}, bf16[32,16,128]{2,1,0:T(8,128)(2,1)S(1)}, bf16[32,16,128]{...) custom-call(s32[4]{0:T(128)S(1)} %pad_add_fusion.refs_0_, ...), custom_call_target="tpu_custom_call" | custom-call | flops 1610612736 | bytes 2097152 | tf_op jit(solution)/shard_map/update_last/pallas_call | solution.py:275
  43.3 2.6 %collective-permute-start.23 = (bf16[32,16,128]{2,1,0:T(8,128)(2,1)S(1)}, bf16[32,16,128]{2,1,0:T(8,128)(2,1)S(1)}, u32[]{:S(2)}, u32[]{:S(2)}) collective-permute-start(bf16[32,16,128]{2,1,0:T(8,128)(2,1)S(1)} %get-tuple-element.50), channel_id=1, source_target_pairs={{0,0},{1,1},{2,2},{3,3},{4,16},{5,17},{6,18},{7,19},{8,8},{9,9},{1... | collective-permute-start | bytes 393224 | tf_op jit(solution)/shard_map/ppermute | solution.py:318
  45.9 3.3 %collective-permute-start.24 = (bf16[32,16,128]{2,1,0:T(8,128)(2,1)S(1)}, bf16[32,16,128]{2,1,0:T(8,128)(2,1)S(1)}, u32[]{:S(2)}, u32[]{:S(2)}) collective-permute-start(bf16[32,16,128]{2,1,0:T(8,128)(2,1)S(1)} %get-tuple-element.51), channel_id=1, source_target_pairs={{0,8},{1,9},{2,10},{3,11},{4,24},{5,25},{6,26},{7,27},{8,0},{9,1},... | collective-permute-start | bytes 393224 | tf_op jit(solution)/shard_map/ppermute | solution.py:318
  49.2 1.4 %collective-permute-start.25 = (bf16[32,16,128]{2,1,0:T(8,128)(2,1)S(1)}, bf16[32,16,128]{2,1,0:T(8,128)(2,1)S(1)}, u32[]{:S(2)}, u32[]{:S(2)}) collective-permute-start(bf16[32,16,128]{2,1,0:T(8,128)(2,1)S(1)} %get-tuple-element.52), channel_id=1, source_target_pairs={{0,1},{1,0},{2,3},{3,2},{4,17},{5,16},{6,19},{7,18},{8,9},{9,8},{1... | collective-permute-start | bytes 393224 | tf_op jit(solution)/shard_map/ppermute | solution.py:318
  50.6 1.0 %collective-permute-start.26 = (bf16[32,16,128]{2,1,0:T(8,128)(2,1)S(1)}, bf16[32,16,128]{2,1,0:T(8,128)(2,1)S(1)}, u32[]{:S(2)}, u32[]{:S(2)}) collective-permute-start(bf16[32,16,128]{2,1,0:T(8,128)(2,1)S(1)} %get-tuple-element.53), channel_id=1, source_target_pairs={{0,9},{1,8},{2,11},{3,10},{4,25},{5,24},{6,27},{7,26},{8,1},{9,0},... | collective-permute-start | bytes 393224 | tf_op jit(solution)/shard_map/ppermute | solution.py:318
  51.6 0.1 fusion.refs_10_
  51.8 8.7 %collective-permute-done.24.refs_4_ = bf16[32,16,128]{2,1,0:T(8,128)(2,1)S(1)} collective-permute-done((bf16[32,16,128]{2,1,0:T(8,128)(2,1)S(1)}, bf16[32,16,128]{2,1,0:T(8,128)(2,1)S(1)}, u32[]{:S(2)}, u32[]{:S(2)}) %collective-permute-start.24) | collective-permute-done | bytes 131104 | tf_op jit(solution)/shard_map/ppermute | solution.py:318
  60.4 2.7 %finish.2.refs_11_ = bf16[16,128,128]{2,1,0:T(8,128)(2,1)} custom-call(s32[4]{0:T(128)S(1)} %pad_add_fusion.refs_0_, bf16[16,128,128]{2,1,0:T(8,128)(2,1)S(1)} %copy-done, bf16[16,64,128]{2,1,0:T(8,128)(2,1)S(1)} %get-tuple-element.54.refs_2_, bf16[32,16,128]{2,1,0:T(8,128)(2,1)S(1)} %collective-permute-done.23.refs_3_, ...), custom_call_target="tpu_custom_call" | custom-call | flops 8589934592 | bytes 524288 | tf_op jit(solution)/shard_map/finish/pallas_call | solution.py:339
  63.1 2.2 %collective-permute-done.22.refs_2_ = bf16[16,64,128]{2,1,0:T(8,128)(2,1)S(1)} collective-permute-done((bf16[16,64,128]{2,1,0:T(8,128)(2,1)S(1)}, bf16[16,64,128]{2,1,0:T(8,128)(2,1)S(1)}, u32[]{:S(2)}, u32[]{:S(2)}) %collective-permute-start.22) | collective-permute-done | bytes 262176 | tf_op jit(solution)/shard_map/ppermute | solution.py:191
  65.3 2.6 %finish.3 = bf16[16,128,128]{2,1,0:T(8,128)(2,1)} custom-call(s32[4]{0:T(128)S(1)} %pad_add_fusion.refs_0_, bf16[16,128,128]{2,1,0:T(8,128)(2,1)S(1)} %copy-done, bf16[16,64,128]{2,1,0:T(8,128)(2,1)S(1)} %collective-permute-done.22.refs_2_, bf16[32,16,128]{2,1,0:T(8,128)(2,1)S(1)} %collective-permute-done.23.refs_3_, ...), custom_call_target="tpu_custom_call", output_to_operand_aliasing={{}: (11, {})} | custom-call | flops 8589934592 | bytes 524288 | tf_op jit(solution)/shard_map/finish/pallas_call | solution.py:339
  (48 shorter events, 0.4 us)
Async XLA Ops:
  1.5 1.9 %copy-start.3 = (bf16[128,32,64]{0,2,1:T(8,128)(2,1)S(1)}, bf16[128,32,64]{0,2,1:T(8,128)(2,1)}, u32[]{:S(2)}) copy-start(bf16[128,32,64]{0,2,1:T(8,128)(2,1)} %param.10) | copy-start | bytes 1572868
  1.8 6.0 %collective-permute-start.10 = (bf16[512,128]{1,0:T(8,128)(2,1)S(1)}, bf16[512,128]{1,0:T(8,128)(2,1)S(1)}, u32[]{:S(2)}, u32[]{:S(2)}) collective-permute-start(bf16[512,128]{1,0:T(8,128)(2,1)S(1)} %bitcast.45), channel_id=1, source_target_pairs={{0,16},{8,24},{16,0},{24,8},{1,17},{9,25},{17,1},{25,9},{2,18},{10... | collective-permute-start | bytes 393224 | tf_op jit(solution)/shard_map/ppermute | solution.py:191
  1.9 5.9 %collective-permute-start.5 = (bf16[512,128]{1,0:T(8,128)(2,1)S(1)}, bf16[512,128]{1,0:T(8,128)(2,1)S(1)}, u32[]{:S(2)}, u32[]{:S(2)}) collective-permute-start(bf16[512,128]{1,0:T(8,128)(2,1)S(1)} %bitcast.46), channel_id=1, source_target_pairs={{0,1},{1,0},{2,3},{3,2},{4,5},{5,4},{6,7},{7,6},{8,9},{9,8},{10,11... | collective-permute-start | bytes 393224 | tf_op jit(solution)/shard_map/ppermute | solution.py:191
  3.7 3.8 %copy-start.4 = (bf16[1024,128]{1,0:T(8,128)(2,1)S(1)}, bf16[1024,128]{1,0:T(8,128)(2,1)}, u32[]{:S(2)}) copy-start(bf16[1024,128]{1,0:T(8,128)(2,1)} %param.12) | copy-start | bytes 786436
  3.8 5.0 %collective-permute-start = (bf16[512,128]{1,0:T(8,128)(2,1)S(1)}, bf16[512,128]{1,0:T(8,128)(2,1)S(1)}, u32[]{:S(2)}, u32[]{:S(2)}) collective-permute-start(bf16[512,128]{1,0:T(8,128)(2,1)S(1)} %get-tuple-element.33.refs_1_), channel_id=1, source_target_pairs={{0,4},{4,0},{1,5},{5,1},{2,6},{6,2},{3,7},{7,3},{8,12},{12,8},{9,1... | collective-permute-start | bytes 393224 | tf_op jit(solution)/shard_map/ppermute | solution.py:191
  5.1 6.2 %collective-permute-start.3 = (bf16[512,128]{1,0:T(8,128)(2,1)S(1)}, bf16[512,128]{1,0:T(8,128)(2,1)S(1)}, u32[]{:S(2)}, u32[]{:S(2)}) collective-permute-start(bf16[512,128]{1,0:T(8,128)(2,1)S(1)} %bitcast.56), channel_id=1, source_target_pairs={{0,3},{1,2},{2,1},{3,0},{4,7},{5,6},{6,5},{7,4},{8,11},{9,10},{10,... | collective-permute-start | bytes 393224 | tf_op jit(solution)/shard_map/ppermute | solution.py:191
  7.8 5.8 %collective-permute-start.13 = (bf16[512,128]{1,0:T(8,128)(2,1)S(1)}, bf16[512,128]{1,0:T(8,128)(2,1)S(1)}, u32[]{:S(2)}, u32[]{:S(2)}) collective-permute-start(bf16[512,128]{1,0:T(8,128)(2,1)S(1)} %collective-permute-done.5.refs_9_), channel_id=1, source_target_pairs={{0,16},{8,24},{16,0},{24,8},{1,17},{9,25},{17,1},{25,9},{2,18},{10... | collective-permute-start | bytes 393224 | tf_op jit(solution)/shard_map/ppermute | solution.py:191
  8.8 6.2 %collective-permute-start.1 = (bf16[512,128]{1,0:T(8,128)(2,1)S(1)}, bf16[512,128]{1,0:T(8,128)(2,1)S(1)}, u32[]{:S(2)}, u32[]{:S(2)}) collective-permute-start(bf16[512,128]{1,0:T(8,128)(2,1)S(1)} %get-tuple-element.35), channel_id=1, source_target_pairs={{0,1},{1,0},{2,3},{3,2},{4,5},{5,4},{6,7},{7,6},{8,9},{9,8},{10,11... | collective-permute-start | bytes 393224 | tf_op jit(solution)/shard_map/ppermute | solution.py:191
  9.3 6.7 %collective-permute-start.6 = (bf16[512,128]{1,0:T(8,128)(2,1)S(1)}, bf16[512,128]{1,0:T(8,128)(2,1)S(1)}, u32[]{:S(2)}, u32[]{:S(2)}) collective-permute-start(bf16[512,128]{1,0:T(8,128)(2,1)S(1)} %get-tuple-element.35), channel_id=1, source_target_pairs={{0,3},{1,2},{2,1},{3,0},{4,7},{5,6},{6,5},{7,4},{8,11},{9,10},{10,... | collective-permute-start | bytes 393224 | tf_op jit(solution)/shard_map/ppermute | solution.py:191
  11.3 17.3 %collective-permute-start.4 = (bf16[512,128]{1,0:T(8,128)(2,1)S(1)}, bf16[512,128]{1,0:T(8,128)(2,1)S(1)}, u32[]{:S(2)}, u32[]{:S(2)}) collective-permute-start(bf16[512,128]{1,0:T(8,128)(2,1)S(1)} %get-tuple-element.33.refs_1_), channel_id=1, source_target_pairs={{0,2},{1,3},{2,0},{3,1},{4,6},{5,7},{6,4},{7,5},{8,10},{9,11},{10,... | collective-permute-start | bytes 393224 | tf_op jit(solution)/shard_map/ppermute | solution.py:191
  13.4 9.9 %collective-permute-start.15 = (bf16[512,128]{1,0:T(8,128)(2,1)S(1)}, bf16[512,128]{1,0:T(8,128)(2,1)S(1)}, u32[]{:S(2)}, u32[]{:S(2)}) collective-permute-start(bf16[512,128]{1,0:T(8,128)(2,1)S(1)} %collective-permute-done.3.refs_17_), channel_id=1, source_target_pairs={{0,1},{1,0},{2,3},{3,2},{4,5},{5,4},{6,7},{7,6},{8,9},{9,8},{10,11... | collective-permute-start | bytes 393224 | tf_op jit(solution)/shard_map/ppermute | solution.py:191
  13.6 9.9 %collective-permute-start.17 = (bf16[512,128]{1,0:T(8,128)(2,1)S(1)}, bf16[512,128]{1,0:T(8,128)(2,1)S(1)}, u32[]{:S(2)}, u32[]{:S(2)}) collective-permute-start(bf16[512,128]{1,0:T(8,128)(2,1)S(1)} %collective-permute-done.3.refs_17_), channel_id=1, source_target_pairs={{0,16},{8,24},{16,0},{24,8},{1,17},{9,25},{17,1},{25,9},{2,18},{10... | collective-permute-start | bytes 393224 | tf_op jit(solution)/shard_map/ppermute | solution.py:191
  15.0 10.9 %collective-permute-start.2 = (bf16[512,128]{1,0:T(8,128)(2,1)S(1)}, bf16[512,128]{1,0:T(8,128)(2,1)S(1)}, u32[]{:S(2)}, u32[]{:S(2)}) collective-permute-start(bf16[512,128]{1,0:T(8,128)(2,1)S(1)} %collective-permute-done.1.refs_2_), channel_id=1, source_target_pairs={{0,4},{4,0},{1,5},{5,1},{2,6},{6,2},{3,7},{7,3},{8,12},{12,8},{9,1... | collective-permute-start | bytes 393224 | tf_op jit(solution)/shard_map/ppermute | solution.py:191
  15.5 13.2 %copy-start.5 = (f32[512]{0:T(512)S(1)}, f32[512]{0:T(512)}, u32[]{:S(2)}) copy-start(f32[512]{0:T(512)} %param.17) | copy-start | bytes 6148
  15.5 13.2 %copy-start.7 = (f32[128]{0:T(128)S(1)}, f32[128]{0:T(128)}, u32[]{:S(2)}) copy-start(f32[128]{0:T(128)} %param.19) | copy-start | bytes 1540
  15.5 13.2 %copy-start.8 = (f32[128]{0:T(128)S(1)}, f32[128]{0:T(128)}, u32[]{:S(2)}) copy-start(f32[128]{0:T(128)} %param.15) | copy-start | bytes 1540
  16.0 18.5 %collective-permute-start.12 = (bf16[512,128]{1,0:T(8,128)(2,1)S(1)}, bf16[512,128]{1,0:T(8,128)(2,1)S(1)}, u32[]{:S(2)}, u32[]{:S(2)}) collective-permute-start(bf16[512,128]{1,0:T(8,128)(2,1)S(1)} %collective-permute-done.5.refs_9_), channel_id=1, source_target_pairs={{0,8},{8,0},{16,24},{24,16},{1,9},{9,1},{17,25},{25,17},{2,10},{10... | collective-permute-start | bytes 393224 | tf_op jit(solution)/shard_map/ppermute | solution.py:191
  23.2 11.3 %collective-permute-start.9 = (bf16[512,128]{1,0:T(8,128)(2,1)S(1)}, bf16[512,128]{1,0:T(8,128)(2,1)S(1)}, u32[]{:S(2)}, u32[]{:S(2)}) collective-permute-start(bf16[512,128]{1,0:T(8,128)(2,1)S(1)} %bitcast.47), channel_id=1, source_target_pairs={{0,8},{8,0},{16,24},{24,16},{1,9},{9,1},{17,25},{25,17},{2,10},{10... | collective-permute-start | bytes 393224 | tf_op jit(solution)/shard_map/ppermute | solution.py:191
  23.5 11.6 %collective-permute-start.20 = (bf16[512,128]{1,0:T(8,128)(2,1)S(1)}, bf16[512,128]{1,0:T(8,128)(2,1)S(1)}, u32[]{:S(2)}, u32[]{:S(2)}) collective-permute-start(bf16[512,128]{1,0:T(8,128)(2,1)S(1)} %collective-permute-done.3.refs_17_), channel_id=1, source_target_pairs={{0,8},{8,0},{16,24},{24,16},{1,9},{9,1},{17,25},{25,17},{2,10},{10... | collective-permute-start | bytes 393224 | tf_op jit(solution)/shard_map/ppermute | solution.py:191
  26.0 5.3 %collective-permute-start.18 = (bf16[512,128]{1,0:T(8,128)(2,1)S(1)}, bf16[512,128]{1,0:T(8,128)(2,1)S(1)}, u32[]{:S(2)}, u32[]{:S(2)}) collective-permute-start(bf16[512,128]{1,0:T(8,128)(2,1)S(1)} %collective-permute-done.15.refs_13_), channel_id=1, source_target_pairs={{0,16},{8,24},{16,0},{24,8},{1,17},{9,25},{17,1},{25,9},{2,18},{10... | collective-permute-start | bytes 393224 | tf_op jit(solution)/shard_map/ppermute | solution.py:191
  28.6 4.5 %collective-permute-start.7 = (bf16[512,128]{1,0:T(8,128)(2,1)S(1)}, bf16[512,128]{1,0:T(8,128)(2,1)S(1)}, u32[]{:S(2)}, u32[]{:S(2)}) collective-permute-start(bf16[512,128]{1,0:T(8,128)(2,1)S(1)} %collective-permute-done.6.refs_4_), channel_id=1, source_target_pairs={{0,4},{4,0},{1,5},{5,1},{2,6},{6,2},{3,7},{7,3},{8,12},{12,8},{9,1... | collective-permute-start | bytes 393224 | tf_op jit(solution)/shard_map/ppermute | solution.py:191
  31.3 4.1 %collective-permute-start.14 = (bf16[512,128]{1,0:T(8,128)(2,1)S(1)}, bf16[512,128]{1,0:T(8,128)(2,1)S(1)}, u32[]{:S(2)}, u32[]{:S(2)}) collective-permute-start(bf16[512,128]{1,0:T(8,128)(2,1)S(1)} %collective-permute-done.13.refs_11_), channel_id=1, source_target_pairs={{0,8},{8,0},{16,24},{24,16},{1,9},{9,1},{17,25},{25,17},{2,10},{10... | collective-permute-start | bytes 393224 | tf_op jit(solution)/shard_map/ppermute | solution.py:191
  33.1 2.4 %collective-permute-start.11 = (bf16[512,128]{1,0:T(8,128)(2,1)S(1)}, bf16[512,128]{1,0:T(8,128)(2,1)S(1)}, u32[]{:S(2)}, u32[]{:S(2)}) collective-permute-start(bf16[512,128]{1,0:T(8,128)(2,1)S(1)} %collective-permute-done.10.refs_7_), channel_id=1, source_target_pairs={{0,8},{8,0},{16,24},{24,16},{1,9},{9,1},{17,25},{25,17},{2,10},{10... | collective-permute-start | bytes 393224 | tf_op jit(solution)/shard_map/ppermute | solution.py:191
  34.5 1.3 %collective-permute-start.21 = (bf16[512,128]{1,0:T(8,128)(2,1)S(1)}, bf16[512,128]{1,0:T(8,128)(2,1)S(1)}, u32[]{:S(2)}, u32[]{:S(2)}) collective-permute-start(bf16[512,128]{1,0:T(8,128)(2,1)S(1)} %collective-permute-done.17.refs_19_), channel_id=1, source_target_pairs={{0,8},{8,0},{16,24},{24,16},{1,9},{9,1},{17,25},{25,17},{2,10},{10... | collective-permute-start | bytes 393224 | tf_op jit(solution)/shard_map/ppermute | solution.py:191
  34.5 1.5 %collective-permute-start.19 = (bf16[512,128]{1,0:T(8,128)(2,1)S(1)}, bf16[512,128]{1,0:T(8,128)(2,1)S(1)}, u32[]{:S(2)}, u32[]{:S(2)}) collective-permute-start(bf16[512,128]{1,0:T(8,128)(2,1)S(1)} %collective-permute-done.18.refs_15_), channel_id=1, source_target_pairs={{0,8},{8,0},{16,24},{24,16},{1,9},{9,1},{17,25},{25,17},{2,10},{10... | collective-permute-start | bytes 393224 | tf_op jit(solution)/shard_map/ppermute | solution.py:191
  35.0 1.3 %collective-permute-start.16 = (bf16[512,128]{1,0:T(8,128)(2,1)S(1)}, bf16[512,128]{1,0:T(8,128)(2,1)S(1)}, u32[]{:S(2)}, u32[]{:S(2)}) collective-permute-start(bf16[512,128]{1,0:T(8,128)(2,1)S(1)} %collective-permute-done.15.refs_13_), channel_id=1, source_target_pairs={{0,8},{8,0},{16,24},{24,16},{1,9},{9,1},{17,25},{25,17},{2,10},{10... | collective-permute-start | bytes 393224 | tf_op jit(solution)/shard_map/ppermute | solution.py:191
  35.4 1.0 %copy-start.6 = (f32[128]{0:T(128)S(1)}, f32[128]{0:T(128)}, u32[]{:S(2)}) copy-start(f32[128]{0:T(128)} %param.13) | copy-start | bytes 1540
  35.4 4.7 %collective-permute-start.8 = (bf16[512,128]{1,0:T(8,128)(2,1)S(1)}, bf16[512,128]{1,0:T(8,128)(2,1)S(1)}, u32[]{:S(2)}, u32[]{:S(2)}) collective-permute-start(bf16[512,128]{1,0:T(8,128)(2,1)S(1)} %collective-permute-done.4.refs_3_), channel_id=1, source_target_pairs={{0,4},{4,0},{1,5},{5,1},{2,6},{6,2},{3,7},{7,3},{8,12},{12,8},{9,1... | collective-permute-start | bytes 393224 | tf_op jit(solution)/shard_map/ppermute | solution.py:191
  39.5 20.9 %copy-start = (bf16[16,128,128]{2,1,0:T(8,128)(2,1)S(1)}, bf16[16,128,128]{2,1,0:T(8,128)(2,1)}, u32[]{:S(2)}) copy-start(bf16[16,128,128]{2,1,0:T(8,128)(2,1)} %refs_1_.3) | copy-start | bytes 1572868
  40.1 20.3 %copy-start.2 = (bf16[512,128]{1,0:T(8,128)(2,1)S(1)}, bf16[512,128]{1,0:T(8,128)(2,1)}, u32[]{:S(2)}) copy-start(bf16[512,128]{1,0:T(8,128)(2,1)} %refs_8_.3) | copy-start | bytes 393220
  43.2 17.2 %copy-start.1 = (bf16[128,512]{1,0:T(8,128)(2,1)S(1)}, bf16[128,512]{1,0:T(8,128)(2,1)}, u32[]{:S(2)}) copy-start(bf16[128,512]{1,0:T(8,128)(2,1)} %refs_7_.3) | copy-start | bytes 393220
  43.3 8.5 %collective-permute-start.23 = (bf16[32,16,128]{2,1,0:T(8,128)(2,1)S(1)}, bf16[32,16,128]{2,1,0:T(8,128)(2,1)S(1)}, u32[]{:S(2)}, u32[]{:S(2)}) collective-permute-start(bf16[32,16,128]{2,1,0:T(8,128)(2,1)S(1)} %get-tuple-element.50), channel_id=1, source_target_pairs={{0,0},{1,1},{2,2},{3,3},{4,16},{5,17},{6,18},{7,19},{8,8},{9,9},{1... | collective-permute-start | bytes 393224 | tf_op jit(solution)/shard_map/ppermute | solution.py:318
  45.9 14.5 %collective-permute-start.24 = (bf16[32,16,128]{2,1,0:T(8,128)(2,1)S(1)}, bf16[32,16,128]{2,1,0:T(8,128)(2,1)S(1)}, u32[]{:S(2)}, u32[]{:S(2)}) collective-permute-start(bf16[32,16,128]{2,1,0:T(8,128)(2,1)S(1)} %get-tuple-element.51), channel_id=1, source_target_pairs={{0,8},{1,9},{2,10},{3,11},{4,24},{5,25},{6,26},{7,27},{8,0},{9,1},... | collective-permute-start | bytes 393224 | tf_op jit(solution)/shard_map/ppermute | solution.py:318
  49.2 11.2 %collective-permute-start.25 = (bf16[32,16,128]{2,1,0:T(8,128)(2,1)S(1)}, bf16[32,16,128]{2,1,0:T(8,128)(2,1)S(1)}, u32[]{:S(2)}, u32[]{:S(2)}) collective-permute-start(bf16[32,16,128]{2,1,0:T(8,128)(2,1)S(1)} %get-tuple-element.52), channel_id=1, source_target_pairs={{0,1},{1,0},{2,3},{3,2},{4,17},{5,16},{6,19},{7,18},{8,9},{9,8},{1... | collective-permute-start | bytes 393224 | tf_op jit(solution)/shard_map/ppermute | solution.py:318
  50.6 9.9 %collective-permute-start.26 = (bf16[32,16,128]{2,1,0:T(8,128)(2,1)S(1)}, bf16[32,16,128]{2,1,0:T(8,128)(2,1)S(1)}, u32[]{:S(2)}, u32[]{:S(2)}) collective-permute-start(bf16[32,16,128]{2,1,0:T(8,128)(2,1)S(1)} %get-tuple-element.53), channel_id=1, source_target_pairs={{0,9},{1,8},{2,11},{3,10},{4,25},{5,24},{6,27},{7,26},{8,1},{9,0},... | collective-permute-start | bytes 393224 | tf_op jit(solution)/shard_map/ppermute | solution.py:318
  51.7 13.7 %collective-permute-start.22 = (bf16[16,64,128]{2,1,0:T(8,128)(2,1)S(1)}, bf16[16,64,128]{2,1,0:T(8,128)(2,1)S(1)}, u32[]{:S(2)}, u32[]{:S(2)}) collective-permute-start(bf16[16,64,128]{2,1,0:T(8,128)(2,1)S(1)} %get-tuple-element.49), channel_id=1, source_target_pairs={{0,2},{1,3},{2,0},{3,1},{4,6},{5,7},{6,4},{7,5},{8,10},{9,11},{10,... | collective-permute-start | bytes 786440 | tf_op jit(solution)/shard_map/ppermute | solution.py:191
